TPU v7x, 256 devices: a whole 4x4x8 slice. The times are simulated.
256 devices in a mesh: tower: 2 (over core), shard: 128 (over x, y, z).
Axes of the slice: x: 4, y: 4, z: 8, core: 2. Of those that a mesh axis runs over, the one named last changes fastest.
Arguments:
- history: int32 [1024, 64], P(('tower', 'shard')), may hold values from 0 to 65663, as said below
- item_ids: int32 [1024], P(('tower', 'shard')), may hold values from 0 to 65663, as said below
- hot_table: float32 [128, 256], replicated, may hold values from -6 to 6
- rare_table: float32 [65536, 256], P('shard'), may hold values from -6 to 6
- in_proj: bfloat16 [256, 1024], replicated, may hold values from -0.375 to 0.375
- pos_embed: bfloat16 [64, 1024], replicated, may hold values from -3 to 3
- norm_gain: float32 [1024], replicated, may hold values from 0.5 to 1.5
- w_query: bfloat16 [1024, 1024], replicated, may hold values from -0.1875 to 0.1875
- w_key: bfloat16 [1024, 1024], replicated, may hold values from -0.1875 to 0.1875
- w_value: bfloat16 [1024, 1024], replicated, may hold values from -0.1875 to 0.1875
- w_out: bfloat16 [1024, 1024], replicated, may hold values from -0.1875 to 0.1875
- out_gain: float32 [1024], replicated, may hold values from 0.5 to 1.5
- item_w1: bfloat16 [256, 1024], replicated, may hold values from -0.375 to 0.375
- item_w2: bfloat16 [1024, 1024], replicated, may hold values from -0.1875 to 0.1875
- item_gain: float32 [1024], replicated, may hold values from 0.5 to 1.5
Outputs:
- grad_hot: float32 [128, 256], replicated
- grad_rare: float32 [65536, 256], P('shard')
- loss: float32 [], replicated
Inputs may be any that keep to these rules, and one draw needn't show every extreme that they name: An id below 128 names hot row id; another id i names rare row i - 128, held by shard index (i - 128) // 512. Among the history and item ids of one device's 4 users (aligned blocks) at most 5 rare ids fall on one shard index, and exactly 5 on one. `item_ids`: same rule as history, counted together with it.
All inputs are finite; a program needn't handle non-finite values.
Results may differ from a plain program's by a relative error of at most 0.019.
Values may be sent and summed in bfloat16 or wider, within the bound.
No kernel may reach another device: no remote copies, remote signals or barrier semaphores. Data moves between devices by JAX's collectives and lax.ppermute only.
A program may use at most 128 MiB of HBM per device.

v0:
```python
import math

import jax
import jax.numpy as jnp
from jax import lax
from jax.sharding import PartitionSpec as P

HEAD_DIM = 64


EPS = 1e-06


def rms_scale(values, gain):
    return values * lax.rsqrt(jnp.mean(values * values, axis=-1, keepdims=True) + EPS) * gain


def user_tower(rows, in_proj, pos_embed, norm_gain, w_query, w_key, w_value, w_out, out_gain):
    users, hist, emb = rows.shape
    width = in_proj.shape[1]
    heads = width // HEAD_DIM
    flat = rows.reshape(users * hist, emb).astype(jnp.bfloat16)
    hidden = jnp.dot(flat, in_proj, preferred_element_type=jnp.float32).reshape(users, hist, width)
    hidden = hidden + pos_embed.astype(jnp.float32)[None]
    normed = rms_scale(hidden, norm_gain).astype(jnp.bfloat16)
    flat_normed = normed.reshape(users * hist, width)
    keys = jnp.dot(flat_normed, w_key, preferred_element_type=jnp.float32).astype(jnp.bfloat16)
    keys = keys.reshape(users, hist, heads, HEAD_DIM)
    values = jnp.dot(flat_normed, w_value, preferred_element_type=jnp.float32).astype(jnp.bfloat16)
    values = values.reshape(users, hist, heads, HEAD_DIM)
    query = jnp.dot(normed[:, -1], w_query, preferred_element_type=jnp.float32).astype(jnp.bfloat16)
    query = query.reshape(users, heads, HEAD_DIM)
    scores = jnp.einsum(
        "uhd,ushd->uhs", query, keys, preferred_element_type=jnp.float32
    ) / math.sqrt(HEAD_DIM)
    weights = jax.nn.softmax(scores, axis=-1).astype(jnp.bfloat16)
    attended = jnp.einsum("uhs,ushd->uhd", weights, values, preferred_element_type=jnp.float32)
    attended = attended.astype(jnp.bfloat16).reshape(users, width)
    mixed = hidden[:, -1] + jnp.dot(attended, w_out, preferred_element_type=jnp.float32)
    return rms_scale(mixed, out_gain).astype(jnp.bfloat16)


def item_tower(rows, item_w1, item_w2, item_gain):
    inner = jax.nn.silu(
        jnp.dot(rows.astype(jnp.bfloat16), item_w1, preferred_element_type=jnp.float32)
    )
    outer = jnp.dot(inner.astype(jnp.bfloat16), item_w2, preferred_element_type=jnp.float32)
    return rms_scale(outer, item_gain).astype(jnp.bfloat16)


def shards(
    history,
    item_ids,
    hot_table,
    rare_table,
    in_proj,
    pos_embed,
    norm_gain,
    w_query,
    w_key,
    w_value,
    w_out,
    out_gain,
    item_w1,
    item_w2,
    item_gain,
):
    batch, hist = history.shape
    hot_count, emb = hot_table.shape
    rare_count = rare_table.shape[0]
    width = in_proj.shape[1]
    scale = 4.0 / math.sqrt(width)
    owners = lax.axis_size("shard")
    total_users = batch * lax.axis_size("tower") * owners
    span = batch * (hist + 1)
    slots = 3 * span // (2 * owners) + 2
    lookups = jnp.concatenate([history.reshape(-1), item_ids])
    is_rare = lookups >= hot_count
    rare_index = jnp.where(is_rare, lookups - hot_count, 0)
    owner = rare_index // rare_count
    local_row = rare_index % rare_count
    owner_hits = ((owner[:, None] == jnp.arange(owners)[None, :]) & is_rare[:, None]).astype(
        jnp.int32
    )
    earlier = jnp.cumsum(owner_hits, axis=0) - owner_hits
    position = jnp.sum(earlier * owner_hits, axis=1)
    slot_index = jnp.where(is_rare, owner * slots + position, owners * slots)
    request = jnp.zeros((owners * slots + 1,), jnp.int32).at[slot_index].set(local_row)
    request = request[:-1].reshape(owners, slots)
    asked = lax.all_to_all(request, "shard", split_axis=0, concat_axis=0, tiled=True)
    served = jnp.take(rare_table, asked, axis=0)
    fetched = lax.all_to_all(
        served.astype(jnp.bfloat16), "shard", split_axis=0, concat_axis=0, tiled=True
    ).astype(served.dtype)
    flat_fetched = fetched.reshape(owners * slots, emb)
    rare_rows = jnp.take(flat_fetched, jnp.minimum(slot_index, owners * slots - 1), axis=0)
    hot_hits = (lookups[:, None] == jnp.arange(hot_count)[None, :]).astype(jnp.float32)
    hot_rows = jnp.dot(
        hot_hits, hot_table, precision=lax.Precision.HIGHEST, preferred_element_type=jnp.float32
    )
    rows = jnp.where(is_rare[:, None], rare_rows, hot_rows)
    user_rows = rows[: batch * hist].reshape(batch, hist, emb)
    item_rows = rows[batch * hist :]

    def user_side(inputs):
        return user_tower(
            inputs, in_proj, pos_embed, norm_gain, w_query, w_key, w_value, w_out, out_gain
        )

    def item_side(inputs):
        return item_tower(inputs, item_w1, item_w2, item_gain)

    user_vec, pull_user = jax.vjp(user_side, user_rows)
    item_vec, pull_item = jax.vjp(item_side, item_rows)
    item_all = lax.all_gather(item_vec, ("tower", "shard"), axis=0, tiled=True)
    logits = scale * jnp.dot(user_vec, item_all.T, preferred_element_type=jnp.float32)
    top = jnp.max(logits, axis=1, keepdims=True)
    normalizer = top + jnp.log(jnp.sum(jnp.exp(logits - top), axis=1, keepdims=True))
    base = (lax.axis_index("tower") * owners + lax.axis_index("shard")) * batch
    mine = base + jnp.arange(batch)
    target = jnp.arange(total_users)[None, :] == mine[:, None]
    positive = jnp.sum(jnp.where(target, logits, 0.0), axis=1)
    loss_part = jnp.sum(normalizer[:, 0] - positive)
    slope = (jnp.exp(logits - normalizer) - target.astype(jnp.float32)).astype(jnp.bfloat16)
    d_user = (scale * jnp.dot(slope, item_all, preferred_element_type=jnp.float32)).astype(
        jnp.bfloat16
    )
    contract_rows = (((0,), (0,)), ((), ()))
    d_item = lax.psum_scatter(
        scale * lax.dot_general(slope, user_vec, contract_rows, preferred_element_type=jnp.float32),
        ("tower", "shard"),
        scatter_dimension=0,
        tiled=True,
    ).astype(jnp.bfloat16)
    (d_user_rows,) = pull_user(d_user)
    (d_item_rows,) = pull_item(d_item)
    d_rows = jnp.concatenate([d_user_rows.reshape(-1, emb), d_item_rows])
    hot_grad = jnp.dot(
        hot_hits.T, d_rows, precision=lax.Precision.HIGHEST, preferred_element_type=jnp.float32
    )
    outgoing = jnp.zeros((owners * slots + 1, emb), jnp.float32).at[slot_index].set(d_rows)
    outgoing = outgoing[:-1].reshape(owners, slots, emb)
    returned = lax.all_to_all(
        outgoing.astype(jnp.bfloat16), "shard", split_axis=0, concat_axis=0, tiled=True
    ).astype(outgoing.dtype)
    rare_part = (
        jnp.zeros((rare_count, emb), jnp.float32)
        .at[asked.reshape(-1)]
        .add(returned.reshape(-1, emb))
    )
    rare_grad = lax.psum(rare_part.astype(jnp.bfloat16), "tower").astype(jnp.float32)
    hot_total, loss_total = lax.psum((hot_grad, loss_part), ("tower", "shard"))
    return (hot_total, rare_grad, loss_total / total_users)


def solution(mesh):
    return jax.shard_map(
        shards,
        mesh=mesh,
        in_specs=(
            P(("tower", "shard"), None),
            P(("tower", "shard")),
            P(),
            P("shard", None),
            P(),
            P(),
            P(),
            P(),
            P(),
            P(),
            P(),
            P(),
            P(),
            P(),
            P(),
        ),
        out_specs=(P(), P("shard", None), P()),
        check_vma=False,
    )
```

profile of v0, /device:TPU:1, one launch (start us, length us, event | category | flops | bytes accessed | tf_op | source)
XLA Modules:
  0.0 675.3 jit_solution(15406295788380606110)
XLA Ops:
  11.0 2.9 scatter_custom_fusion
  14.1 26.7 %all_to_all.25 = s32[128,1,5]{2,1,0:T(1,128)S(1)} all-to-all(s32[128,1,5]{2,1,0:T(1,128)S(1)} %bitcast.92), channel_id=1, replica_groups=mesh['tower'=2,'shard'=128] {'shard'}, dimensions={0} | all-to-all | bytes 5120 | tf_op jit(solution)/shard_map/all_to_all | solution.py:90
  41.7 2.2 gather_fusion
  45.0 6.2 all-to-all-start.1
  51.5 17.9 %all-to-all-done.1 = bf16[128,5,256]{2,1,0:T(8,128)(2,1)S(1)} async-done(((bf16[128,5,256]{2,1,0:T(8,128)(2,1)}), bf16[128,5,256]{2,1,0:T(8,128)(2,1)S(1)}, u32[]{:S(2)}, u32[]{:S(2)}) %all-to-all-start.1) | async-done | bytes 327712 | tf_op jit(solution)/shard_map/all_to_all | solution.py:92
  83.0 2.5 reshape.438
  85.5 3.3 convolution_convert_fusion.2
  88.8 2.5 reshape.439
  104.5 73.4 %all-gather.3.cloned.1.call-done = bf16[256,4,1024]{2,1,0:T(4,128)(2,1)} async-done(((bf16[1,4,1024]{2,1,0:T(4,128)(2,1)}), bf16[256,4,1024]{2,1,0:T(4,128)(2,1)}) %all-gather.3.cloned.1.call-update) | async-done | bytes 2097168 | tf_op jit(solution)/shard_map/all_gather | solution.py:115
  177.9 4.0 reshape.497
  182.0 2.5 fusion.82
  187.9 2.7 convolution_multiply_fusion
  196.1 2.4 fusion.11
  202.5 2.3 fusion.9
  206.4 2.6 reshape.443
  209.0 2.6 reshape.444
  216.4 2.3 add_add_fusion
  219.3 132.2 %all-reduce.12 = (bf16[1024,1024]{1,0:T(8,128)(2,1)}, f32[]{:T(128)}) all-reduce(f32[1024,1024]{1,0:T(8,128)} %convolution_multiply_fusion, f32[]{:T(128)} %get-tuple-element.9), channel_id=2, replica_groups=mesh['tower'=2,'shard'=128] {'tower','shard'}, use_global_device_ids=true, to_apply=%region_14.15.clone | all-reduce | flops 1048577 | bytes 6291464
  352.4 2.5 convolution_convert_fusion.9
  357.6 9.7 %all-to-all-start.2 = ((bf16[128,5,256]{2,1,0:T(8,128)(2,1)}), bf16[128,5,256]{2,1,0:T(8,128)(2,1)S(1)}, u32[]{:S(2)}, u32[]{:S(2)}) async-start(bf16[128,5,256]{2,1,0:T(8,128)(2,1)} %convert_element_type.162), calls=%async_computation.2 | async-start | bytes 1048576 | tf_op jit(solution)/shard_map/all_to_all | solution.py:143
  369.0 17.3 %all-to-all-done.2 = bf16[128,5,256]{2,1,0:T(8,128)(2,1)S(1)} async-done(((bf16[128,5,256]{2,1,0:T(8,128)(2,1)}), bf16[128,5,256]{2,1,0:T(8,128)(2,1)S(1)}, u32[]{:S(2)}, u32[]{:S(2)}) %all-to-all-start.2) | async-done | bytes 327712 | tf_op jit(solution)/shard_map/all_to_all | solution.py:143
  386.4 5.8 scatter_custom_fusion.2
  394.8 23.1 %all-reduce.11.cloned.1.call-done = bf16[512,256]{1,0:T(8,128)(2,1)} async-done(((bf16[512,256]{1,0:T(8,128)(2,1)}), bf16[512,256]{1,0:T(8,128)(2,1)}) %all-reduce.11.cloned.1.call-update) | async-done | bytes 262160 | tf_op jit(solution)/shard_map/psum | solution.py:151
  419.7 246.4 %all-reduce.9.cloned.1.call-done = f32[128,256]{1,0:T(8,128)} async-done(((f32[128,256]{1,0:T(8,128)}), f32[128,256]{1,0:T(8,128)}) %all-reduce.9.cloned.1.call-update) | async-done | bytes 131088 | tf_op jit(solution)/shard_map/psum | solution.py:152
  (201 shorter events, 62.9 us)
Async XLA Ops:
  7.2 74.3 %copy-start = (bf16[1024,1024]{1,0:T(8,128)(2,1)S(1)}, bf16[1024,1024]{1,0:T(8,128)(2,1)}, u32[]{:S(2)}) copy-start(bf16[1024,1024]{1,0:T(8,128)(2,1)} %param.23) | copy-start | bytes 6291460
  7.2 34.5 %copy-start.1 = (f32[512,256]{1,0:T(8,128)S(1)}, f32[512,256]{1,0:T(8,128)}, u32[]{:S(2)}) copy-start(f32[512,256]{1,0:T(8,128)} %param.18) | copy-start | bytes 1572868
  9.6 61.9 %copy-start.38 = (s32[260]{0:T(512)}, s32[260]{0:T(512)S(1)}, u32[]{:S(2)}) copy-start(s32[260]{0:T(512)S(1)} %constant_dynamic-update-slice_fusion) | copy-start | bytes 3124
  44.0 29.4 %copy-start.7 = (bf16[256,1024]{1,0:T(8,128)(2,1)S(1)}, bf16[256,1024]{1,0:T(8,128)(2,1)}, u32[]{:S(2)}) copy-start(bf16[256,1024]{1,0:T(8,128)(2,1)} %param.27) | copy-start | bytes 1572868
  45.0 24.3 %all-to-all-start.1 = ((bf16[128,5,256]{2,1,0:T(8,128)(2,1)}), bf16[128,5,256]{2,1,0:T(8,128)(2,1)S(1)}, u32[]{:S(2)}, u32[]{:S(2)}) async-start(bf16[128,5,256]{2,1,0:T(8,128)(2,1)} %select_convert_fusion), calls=%async_computation.1 | async-start | bytes 1048576 | tf_op jit(solution)/shard_map/all_to_all | solution.py:92
  51.2 126.7 %all-gather.3.cloned.1.call-start = ((), (), s32[]{:S(2)}) async-start(), calls=%async_computation.5 | async-start | bytes 2105344 | tf_op jit(solution)/shard_map/all_gather | solution.py:115
  69.5 7.4 %copy-start.31 = (f32[1024]{0:T(1024)S(1)}, f32[1024]{0:T(1024)}, u32[]{:S(2)}) copy-start(f32[1024]{0:T(1024)} %param.29) | copy-start | bytes 12292
  69.5 8.1 %copy-start.27 = (bf16[64,1024]{1,0:T(8,128)(2,1)S(1)}, bf16[64,1024]{1,0:T(8,128)(2,1)}, u32[]{:S(2)}) copy-start(bf16[64,1024]{1,0:T(8,128)(2,1)} %param.20) | copy-start | bytes 393220
  74.2 4.1 copy-start.24
  74.2 6.3 copy-start.28
  181.9 4.0 copy-start.3
  181.9 4.0 copy-start.40
  196.1 8.6 %copy-start.15 = (f32[4,16,64]{1,2,0:T(8,128)S(1)}, f32[4,16,64]{1,2,0:T(8,128)}, u32[]{:S(2)}) copy-start(f32[4,16,64]{1,2,0:T(8,128)} %get-tuple-element.13) | copy-start | bytes 49156
  219.2 132.3 %copy-start.20 = (f32[4,1024]{1,0:T(4,128)S(1)}, f32[4,1024]{1,0:T(4,128)}, u32[]{:S(2)}) copy-start(f32[4,1024]{1,0:T(4,128)} %copy-done.19) | copy-start | bytes 49156
  219.2 132.3 %copy-start.32 = (f32[1024]{0:T(1024)S(1)}, f32[1024]{0:T(1024)}, u32[]{:S(2)}) copy-start(f32[1024]{0:T(1024)} %param.29) | copy-start | bytes 12292
  219.3 133.1 %copy-start.46 = (f32[4]{0:T(128)S(1)}, f32[4]{0:T(128)}, u32[]{:S(2)}) copy-start(f32[4]{0:T(128)} %copy-done.45) | copy-start | bytes 52
  219.3 133.1 %copy-start.8 = (bf16[256,1024]{1,0:T(8,128)(2,1)S(1)}, bf16[256,1024]{1,0:T(8,128)(2,1)}, u32[]{:S(2)}) copy-start(bf16[256,1024]{1,0:T(8,128)(2,1)} %param.27) | copy-start | bytes 1572868
  219.3 133.1 %copy-start.22 = (f32[4,1024]{1,0:T(4,128)S(1)}, f32[4,1024]{1,0:T(4,128)}, u32[]{:S(2)}) copy-start(f32[4,1024]{1,0:T(4,128)} %copy-done.21) | copy-start | bytes 49156
  219.3 133.1 %copy-start.43 = (f32[4]{0:T(128)S(1)}, f32[4]{0:T(128)}, u32[]{:S(2)}) copy-start(f32[4]{0:T(128)} %copy-done.42) | copy-start | bytes 52
  354.9 13.0 %copy-start.12 = (s32[128,1,5]{2,1,0:T(1,128)S(1)}, s32[128,1,5]{2,1,0:T(1,128)}, u32[]{:S(2)}) copy-start(s32[128,1,5]{2,1,0:T(1,128)} %copy-done.11) | copy-start | bytes 7684
  357.6 35.5 %copy-start.39 = (s32[260]{0:T(512)S(1)}, s32[260]{0:T(512)}, u32[]{:S(2)}) copy-start(s32[260]{0:T(512)} %copy-done.38) | copy-start | bytes 3124
  357.6 28.7 %all-to-all-start.2 = ((bf16[128,5,256]{2,1,0:T(8,128)(2,1)}), bf16[128,5,256]{2,1,0:T(8,128)(2,1)S(1)}, u32[]{:S(2)}, u32[]{:S(2)}) async-start(bf16[128,5,256]{2,1,0:T(8,128)(2,1)} %convert_element_type.162), calls=%async_computation.2 | async-start | bytes 1048576 | tf_op jit(solution)/shard_map/all_to_all | solution.py:143
  367.4 50.5 %all-reduce.11.cloned.1.call-start = ((), (), s32[]{:S(2)}) async-start(), calls=%async_computation.4 | async-start | bytes 524288 | tf_op jit(solution)/shard_map/psum | solution.py:151
  393.1 273.1 %all-reduce.9.cloned.1.call-start = ((), (), s32[]{:S(2)}) async-start(), calls=%async_computation.3 | async-start | bytes 262144 | tf_op jit(solution)/shard_map/psum | solution.py:152
  (31 other events, 57.5 us)
Sparse Core Ops, SparseCore 0:
  77.7 100.1 all-gather.2
  393.2 24.6 all-reduce.10
  424.9 241.1 all-reduce.8
where the time goes:
time: 677 us; the launch traced here: 675 us
  waiting for transfers between devices  378 us (56%)
  blocking collectives  159 us (23%)
  local copies, waits for them, and re-layouts  41.1 us (6%)
  other arithmetic  33.2 us (5%)
  matrix products  31.4 us (5%)
  between operations  16.3 us (2%)
  starting transfers between devices  16.2 us (2%)
    psum x1, waiting for transfers between devices, shards(): hot_total, loss_total = lax.psum((hot_grad, loss_part), ('tower', 'shard'))  246 us
    unnamed x1, blocking collectives  132 us
    all_gather x1, waiting for transfers between devices, shards(): item_all = lax.all_gather(item_vec, ('tower', 'shard'), axis=0, tiled=True)  73.4 us
    all_to_all x1, blocking collectives, shards(): lax.all_to_all(request, 'shard', split_axis=0, concat_axis=0, tiled=True)  26.7 us
    psum x1, waiting for transfers between devices, shards(): lax.psum(rare_part.astype(jnp.bfloat16), 'tower').astype(jnp.float32)  23.1 us
    all_to_all x1, waiting for transfers between devices, shards(): lax.all_to_all(served.astype(jnp.bfloat16), 'shard', split_axis=0, concat...  17.9 us
    all_to_all x1, waiting for transfers between devices, shards(): lax.all_to_all(outgoing.astype(jnp.bfloat16), 'shard', split_axis=0, conc...  17.3 us
  transfers between devices with their start and end apart: 5, of which 5 were waited for; matrix products, arithmetic and copies ran while one was open for 4% of the time, Pallas kernels for 0%

commit v1 on v0

v1 whole, which is shorter than its diff:
```python
import functools
import math

import jax
import jax.numpy as jnp
from jax import lax
from jax.experimental import pallas as pl
from jax.experimental.pallas import tpu as pltpu
from jax.sharding import PartitionSpec as P

HEAD_DIM = 64
EPS = 1e-06
SLOTS = 8
PAD = 16
BF = jnp.bfloat16
F32 = jnp.float32
VMEM = pl.BlockSpec(memory_space=pltpu.VMEM)
SMEM = pl.BlockSpec(memory_space=pltpu.SMEM)
HBM = pl.BlockSpec(memory_space=pl.ANY)
NT = (((1,), (1,)), ((), ()))
TN = (((0,), (0,)), ((), ()))


def dot(a, b):
    return jnp.dot(a, b, preferred_element_type=F32)


def dot_nt(a, b):
    return lax.dot_general(a, b, NT, preferred_element_type=F32)


def dot_tn(a, b):
    return lax.dot_general(a, b, TN, preferred_element_type=F32)


def iota(shape, axis):
    return lax.broadcasted_iota(jnp.int32, shape, axis)


def one_hot(mask):
    return jnp.where(mask, 1.0, 0.0).astype(BF)


def params(mib):
    return pltpu.CompilerParams(vmem_limit_bytes=mib * 1024 * 1024)


def index_kernel(hot_count, rare_count, owners, ids_ref, request_ref, row_ref, column_ref):
    ids = ids_ref[...]
    span = ids.shape[1]
    is_rare = ids >= hot_count
    index = ids - hot_count
    owner = jnp.where(is_rare, index // rare_count, -1)
    local = jnp.where(is_rare, index % rare_count, 0)
    hits = iota((owners, span), 0) == owner
    before = one_hot(iota((span, span), 0) < iota((span, span), 1))
    earlier = dot(one_hot(hits), before)
    position = jnp.sum(jnp.where(hits, earlier, 0.0), axis=0, keepdims=True).astype(jnp.int32)
    column = jnp.where(
        is_rare, owner * SLOTS + position, jnp.where(ids >= 0, owners * SLOTS + ids, -1)
    )
    row_ref[...] = jnp.broadcast_to(column, row_ref.shape)
    column_ref[...] = jnp.transpose(
        jnp.broadcast_to(column.astype(F32), (128, span))
    ).astype(jnp.int32)
    spread = one_hot(iota((owners * SLOTS, span), 0) == column)
    value = local + 1
    high = jnp.broadcast_to((value // 2).astype(F32), (128, span)).astype(BF)
    low = jnp.broadcast_to((value % 2).astype(F32), (128, span)).astype(BF)
    request_ref[...] = (2.0 * dot_nt(spread, high) + dot_nt(spread, low) - 1.0).astype(jnp.int32)


def serve_kernel(asked_ref, table_ref, served_ref, row_ref):
    asked = asked_ref[...]
    rows = table_ref.shape[0]
    lanes = iota(asked.shape, 1)
    picks = jnp.concatenate(
        [one_hot(asked == lanes + 128 * j) for j in range(rows // 128)], axis=1
    )
    served_ref[...] = dot(picks, table_ref[...].astype(BF)).astype(BF)
    row_ref[...] = jnp.transpose(asked.astype(F32))[0:8].astype(jnp.int32)


def head_mask(heads, width):
    return iota((heads, width), 1) // HEAD_DIM == iota((heads, width), 0)


def spread_heads(values, mask, users):
    return jnp.concatenate(
        [jnp.where(mask, values[u : u + 1], 0.0) for u in range(users)], axis=0
    ).astype(BF)


def join_heads(full, mask, users):
    heads = mask.shape[0]
    parts = [
        jnp.sum(
            jnp.where(mask, full[u * heads : (u + 1) * heads], 0.0), axis=0, keepdims=True
        )
        for u in range(users)
    ]
    return jnp.concatenate(parts + [jnp.zeros((PAD - users, full.shape[1]), F32)], axis=0)


def forward_kernel(
    users,
    fetched_ref,
    hot_ref,
    column_ref,
    pos_ref,
    norm_gain_ref,
    out_gain_ref,
    item_gain_ref,
    in_proj_hbm,
    w_query_hbm,
    w_key_hbm,
    w_value_hbm,
    w_out_hbm,
    item_w1_hbm,
    item_w2_hbm,
    user_vec_ref,
    item_vec_ref,
    hidden_ref,
    normed_ref,
    qk_ref,
    weights_ref,
    mixed_ref,
    inner_ref,
    outer_ref,
    in_proj,
    w_query,
    w_key,
    w_value,
    w_out,
    item_w1,
    item_w2,
    sems,
):
    sources = (in_proj_hbm, w_query_hbm, w_key_hbm, w_value_hbm, w_out_hbm, item_w1_hbm, item_w2_hbm)
    targets = (in_proj, w_query, w_key, w_value, w_out, item_w1, item_w2)
    copies = [
        pltpu.make_async_copy(s, t, sems.at[i]) for i, (s, t) in enumerate(zip(sources, targets))
    ]
    for copy in copies:
        copy.start()
    hist, width = pos_ref.shape
    heads = width // HEAD_DIM
    span = users * hist
    slots = fetched_ref.shape[0]
    column = column_ref[0 : span + PAD, :]
    lanes = iota(column.shape, 1)
    picks = jnp.concatenate(
        [one_hot(column == lanes + 128 * j) for j in range(slots // 128)], axis=1
    )
    hot_picks = one_hot(column == lanes + slots)
    rows = (dot(picks, fetched_ref[...]) + dot(hot_picks, hot_ref[...].astype(BF))).astype(BF)
    copies[0].wait()
    pos = pos_ref[...].astype(F32)
    hidden = dot(rows[0:span], in_proj[...]) + jnp.concatenate([pos] * users, axis=0)
    hidden_ref[...] = hidden
    scale = lax.rsqrt(jnp.mean(hidden * hidden, axis=-1, keepdims=True) + EPS)
    normed = (hidden * scale * norm_gain_ref[...]).astype(BF)
    normed_ref[...] = normed
    last = jnp.concatenate(
        [normed_ref[(u + 1) * hist - 1 : (u + 1) * hist, :].astype(F32) for u in range(users)]
        + [jnp.zeros((PAD - users, width), F32)],
        axis=0,
    ).astype(BF)
    mask = head_mask(heads, width)
    copies[1].wait()
    query = dot(last, w_query[...]).astype(BF).astype(F32)
    copies[2].wait()
    qk = dot_nt(spread_heads(query, mask, users), w_key[...]).astype(BF)
    qk_ref[...] = qk
    mixes = []
    for u in range(users):
        own = normed[u * hist : (u + 1) * hist]
        scores = dot_nt(qk[u * heads : (u + 1) * heads], own) * (1.0 / math.sqrt(HEAD_DIM))
        raised = jnp.exp(scores - jnp.max(scores, axis=1, keepdims=True))
        weights = raised / jnp.sum(raised, axis=1, keepdims=True)
        weights_ref[u * heads : (u + 1) * heads, :] = weights
        mixes.append(dot(weights.astype(BF), own))
    mixes = jnp.concatenate(mixes, axis=0).astype(BF)
    copies[3].wait()
    attended = join_heads(dot(mixes, w_value[...]), mask, users).astype(BF)
    copies[4].wait()
    hidden_last = jnp.concatenate(
        [hidden_ref[(u + 1) * hist - 1 : (u + 1) * hist, :] for u in range(users)]
        + [jnp.zeros((PAD - users, width), F32)],
        axis=0,
    )
    mixed = hidden_last + dot(attended, w_out[...])
    mixed_ref[...] = mixed
    scale = lax.rsqrt(jnp.mean(mixed * mixed, axis=-1, keepdims=True) + EPS)
    user_vec_ref[...] = (mixed * scale * out_gain_ref[...]).astype(BF)
    copies[5].wait()
    inner = dot(rows[span : span + PAD], item_w1[...])
    inner_ref[...] = inner
    copies[6].wait()
    outer = dot((inner * jax.nn.sigmoid(inner)).astype(BF), item_w2[...])
    outer_ref[...] = outer
    scale = lax.rsqrt(jnp.mean(outer * outer, axis=-1, keepdims=True) + EPS)
    item_vec_ref[...] = (outer * scale * item_gain_ref[...]).astype(BF)


def softmax_step(users, scale, base, user_all, item_all, user_vec, item_vec, logits, d_user, d_item, loss):
    total = user_all.shape[0]
    chunk = 256
    top = jnp.full((1, total), -jnp.inf, F32)
    for c in range(total // chunk):
        part = scale * dot_nt(item_all[c * chunk : (c + 1) * chunk, :], user_all[...])
        logits[c * chunk : (c + 1) * chunk, :] = part
        top = jnp.maximum(top, jnp.max(part, axis=0, keepdims=True))
    count = jnp.zeros((1, total), F32)
    for c in range(total // chunk):
        part = logits[c * chunk : (c + 1) * chunk, :]
        count = count + jnp.sum(jnp.exp(part - top), axis=0, keepdims=True)
    normalizer = top + jnp.log(count)
    rows = iota((PAD, total), 0)
    valid = rows < users
    target = iota((PAD, total), 1) == rows + base
    one = jnp.where(target, 1.0, 0.0)
    item_logits = scale * dot_nt(item_vec[...], user_all[...])
    slope = jnp.where(valid, jnp.exp(item_logits - normalizer) - one, 0.0).astype(BF)
    d_item[...] = (scale * dot(slope, user_all[...])).astype(BF).astype(F32)
    user_logits = scale * dot_nt(user_vec[...], item_all[...])
    top = jnp.max(user_logits, axis=1, keepdims=True)
    normalizer = top + jnp.log(jnp.sum(jnp.exp(user_logits - top), axis=1, keepdims=True))
    slope = jnp.where(valid, jnp.exp(user_logits - normalizer) - one, 0.0).astype(BF)
    d_user[...] = (scale * dot(slope, item_all[...])).astype(BF).astype(F32)
    each = jnp.sum(jnp.where(valid & target, normalizer - user_logits, 0.0), axis=1, keepdims=True)
    loss[...] = jnp.broadcast_to(jnp.sum(each, axis=0, keepdims=True), loss.shape)


def norm_backward(values, cotangent, gain):
    inverse = lax.rsqrt(jnp.mean(values * values, axis=-1, keepdims=True) + EPS)
    pulled = cotangent * gain
    along = jnp.mean(pulled * values, axis=-1, keepdims=True)
    return inverse * pulled - values * (inverse * inverse * inverse * along)


def backward_kernel(
    users,
    loss_scale,
    place_ref,
    gathered_ref,
    swapped_ref,
    user_vec_ref,
    item_vec_ref,
    hidden_ref,
    normed_ref,
    qk_ref,
    weights_ref,
    mixed_ref,
    inner_ref,
    outer_ref,
    row_ref,
    norm_gain_ref,
    out_gain_ref,
    item_gain_ref,
    in_proj_hbm,
    w_query_hbm,
    w_key_hbm,
    w_value_hbm,
    w_out_hbm,
    item_w1_hbm,
    item_w2_hbm,
    outgoing_ref,
    hot_ref,
    in_proj,
    w_query,
    w_key,
    w_value,
    w_out,
    item_w1,
    item_w2,
    logits,
    d_user,
    d_item,
    loss,
    d_normed,
    sems,
):
    sources = (in_proj_hbm, w_query_hbm, w_key_hbm, w_value_hbm, w_out_hbm, item_w1_hbm, item_w2_hbm)
    targets = (in_proj, w_query, w_key, w_value, w_out, item_w1, item_w2)
    copies = [
        pltpu.make_async_copy(s, t, sems.at[i]) for i, (s, t) in enumerate(zip(sources, targets))
    ]
    for copy in copies:
        copy.start()
    own = (user_vec_ref, item_vec_ref, logits, d_user, d_item, loss)

    @pl.when(place_ref[0] == 0)
    def _():
        softmax_step(users, loss_scale, place_ref[1], gathered_ref, swapped_ref, *own)

    @pl.when(place_ref[0] != 0)
    def _():
        softmax_step(users, loss_scale, place_ref[1], swapped_ref, gathered_ref, *own)

    for copy in copies:
        copy.wait()
    span, width = hidden_ref.shape
    hist = span // users
    heads = width // HEAD_DIM
    mask = head_mask(heads, width)
    d_mixed = norm_backward(mixed_ref[...], d_user[...], out_gain_ref[...])
    d_attended = dot_nt(d_mixed.astype(BF), w_out[...])
    d_mixes = dot_nt(spread_heads(d_attended, mask, users), w_value[...]).astype(BF)
    d_qk = []
    for u in range(users):
        own = normed_ref[u * hist : (u + 1) * hist, :]
        weights = weights_ref[u * heads : (u + 1) * heads, :]
        pulled = d_mixes[u * heads : (u + 1) * heads]
        d_weights = dot_nt(pulled, own)
        d_scores = weights * (d_weights - jnp.sum(weights * d_weights, axis=1, keepdims=True))
        d_scores = (d_scores * (1.0 / math.sqrt(HEAD_DIM))).astype(BF)
        d_normed[u * hist : (u + 1) * hist, :] = dot_tn(weights.astype(BF), pulled) + dot_tn(
            d_scores, qk_ref[u * heads : (u + 1) * heads, :]
        )
        d_qk.append(dot(d_scores, own))
    d_qk = jnp.concatenate(d_qk, axis=0).astype(BF)
    d_query = join_heads(dot(d_qk, w_key[...]), mask, users).astype(BF)
    d_last = dot_nt(d_query, w_query[...])
    for u in range(users):
        at = slice((u + 1) * hist - 1, (u + 1) * hist)
        d_normed[at, :] = d_normed[at, :] + d_last[u : u + 1]
    d_normed[...] = norm_backward(hidden_ref[...], d_normed[...], norm_gain_ref[...])
    for u in range(users):
        at = slice((u + 1) * hist - 1, (u + 1) * hist)
        d_normed[at, :] = d_normed[at, :] + d_mixed[u : u + 1]
    d_rows = dot_nt(d_normed[...].astype(BF), in_proj[...])
    d_outer = norm_backward(outer_ref[...], d_item[...], item_gain_ref[...])
    inner = inner_ref[...]
    gate = jax.nn.sigmoid(inner)
    d_inner = dot_nt(d_outer.astype(BF), item_w2[...]) * (gate * (1.0 + inner * (1.0 - gate)))
    d_items = dot_nt(d_inner.astype(BF), item_w1[...])
    wide = row_ref.shape[1]
    d_all = jnp.concatenate(
        [d_rows, d_items, jnp.zeros((wide - span - PAD, d_rows.shape[1]), F32)], axis=0
    ).astype(BF)
    slots = outgoing_ref.shape[0]
    hot_count = hot_ref.shape[0] - 16
    column = row_ref[0:1, :]
    outgoing_ref[...] = dot(one_hot(iota((slots, wide), 0) == column), d_all).astype(BF)
    hot = dot(one_hot(iota((hot_count, wide), 0) + slots == column), d_all)
    half = hot_count // 2
    hot_ref[0:half, :] = hot[0:half]
    hot_ref[half : half + 8, :] = loss[...]
    hot_ref[half + 8 : 2 * half + 8, :] = hot[half:]
    hot_ref[2 * half + 8 :, :] = jnp.zeros_like(loss)


def scatter_kernel(returned_ref, row_ref, part_ref):
    rows = part_ref.shape[0]
    slots = returned_ref.shape[0]
    picks = one_hot(iota((rows, slots), 0) == row_ref[0:1, :])
    part_ref[...] = dot(picks, returned_ref[...]).astype(BF)


def shards(
    history,
    item_ids,
    hot_table,
    rare_table,
    in_proj,
    pos_embed,
    norm_gain,
    w_query,
    w_key,
    w_value,
    w_out,
    out_gain,
    item_w1,
    item_w2,
    item_gain,
):
    users, hist = history.shape
    hot_count, emb = hot_table.shape
    rare_count = rare_table.shape[0]
    width = in_proj.shape[1]
    heads = width // HEAD_DIM
    scale = 4.0 / math.sqrt(width)
    owners = lax.axis_size("shard")
    towers = lax.axis_size("tower")
    tower = lax.axis_index("tower")
    total = users * towers * owners
    slots = owners * SLOTS
    span = users * hist
    wide = -(-(span + PAD) // 128) * 128
    swap = [(i, towers - 1 - i) for i in range(towers)]
    shape = jax.ShapeDtypeStruct

    ids = jnp.concatenate(
        [history.reshape(-1), item_ids, jnp.full((wide - span - users,), -1, jnp.int32)]
    ).reshape(1, wide)
    request, row, column = pl.pallas_call(
        functools.partial(index_kernel, hot_count, rare_count, owners),
        out_shape=(
            shape((slots, 128), jnp.int32),
            shape((8, wide), jnp.int32),
            shape((wide, 128), jnp.int32),
        ),
        in_specs=[VMEM],
        out_specs=(VMEM, VMEM, VMEM),
        compiler_params=params(24),
        name="index",
    )(ids)
    asked = lax.all_to_all(request, "shard", split_axis=0, concat_axis=0, tiled=True)
    served, asked_row = pl.pallas_call(
        serve_kernel,
        out_shape=(shape((slots, emb), BF), shape((8, slots), jnp.int32)),
        in_specs=[VMEM, VMEM],
        out_specs=(VMEM, VMEM),
        compiler_params=params(24),
        name="serve",
    )(asked, rare_table)
    fetched = lax.all_to_all(served, "shard", split_axis=0, concat_axis=0, tiled=True)

    weights = (in_proj, w_query, w_key, w_value, w_out, item_w1, item_w2)
    gains = tuple(g.reshape(1, width) for g in (norm_gain, out_gain, item_gain))
    weight_scratch = [pltpu.VMEM(w.shape, w.dtype) for w in weights]
    sems = pltpu.SemaphoreType.DMA((len(weights),))
    user_vec, item_vec, *kept = pl.pallas_call(
        functools.partial(forward_kernel, users),
        out_shape=(
            shape((PAD, width), BF),
            shape((PAD, width), BF),
            shape((span, width), F32),
            shape((span, width), BF),
            shape((users * heads, width), BF),
            shape((users * heads, hist), F32),
            shape((PAD, width), F32),
            shape((PAD, width), F32),
            shape((PAD, width), F32),
        ),
        in_specs=[VMEM] * 7 + [HBM] * 7,
        out_specs=(VMEM,) * 9,
        scratch_shapes=weight_scratch + [sems],
        compiler_params=params(40),
        name="forward",
    )(fetched, hot_table, column, pos_embed, *gains, *weights)

    is_first = tower == 0
    mine_user, mine_item = user_vec[:users], item_vec[:users]
    kept_vec = jnp.where(is_first, mine_user, mine_item)
    other_vec = lax.ppermute(jnp.where(is_first, mine_item, mine_user), "tower", swap)
    chip = jnp.concatenate(
        [jnp.where(is_first, kept_vec, other_vec), jnp.where(is_first, other_vec, kept_vec)], axis=0
    )
    spread = jnp.broadcast_to(chip[None], (owners, towers * users, width)).reshape(total, width)
    gathered = lax.all_to_all(spread, "shard", split_axis=0, concat_axis=0, tiled=True)
    swapped = lax.ppermute(gathered, "tower", swap)
    base = lax.axis_index("shard") * (towers * users) + tower * users
    place = jnp.stack([tower, base]).astype(jnp.int32)

    half = hot_count // 2 + 8
    outgoing, hot = pl.pallas_call(
        functools.partial(backward_kernel, users, scale),
        out_shape=(shape((slots, emb), BF), shape((2 * half, emb), F32)),
        in_specs=[SMEM] + [VMEM] * 15 + [HBM] * 7,
        out_specs=(VMEM, VMEM),
        scratch_shapes=weight_scratch
        + [
            pltpu.VMEM((total, total), F32),
            pltpu.VMEM((PAD, width), F32),
            pltpu.VMEM((PAD, width), F32),
            pltpu.VMEM((8, emb), F32),
            pltpu.VMEM((span, width), F32),
            sems,
        ],
        compiler_params=params(48),
        name="backward",
    )(place, gathered, swapped, user_vec, item_vec, *kept, row, *gains, *weights)

    returned = lax.all_to_all(outgoing, "shard", split_axis=0, concat_axis=0, tiled=True)

    lower, upper = hot[:half], hot[half:]
    mine = jnp.where(is_first, lower, upper)
    mine = mine + lax.ppermute(jnp.where(is_first, upper, lower), "tower", swap)
    step = 1
    while step < owners:
        mine = mine + lax.ppermute(mine, "shard", [(i, i ^ step) for i in range(owners)])
        step *= 2
    other = lax.ppermute(mine, "tower", swap)
    lower = jnp.where(is_first, mine, other)
    upper = jnp.where(is_first, other, mine)
    hot_total = jnp.concatenate([lower[: half - 8], upper[: half - 8]], axis=0)
    loss_total = lower[half - 8, 0]

    part = pl.pallas_call(
        scatter_kernel,
        out_shape=shape((rare_count, emb), BF),
        in_specs=[VMEM, VMEM],
        out_specs=VMEM,
        compiler_params=params(24),
        name="scatter",
    )(returned, asked_row)
    rare_grad = part.astype(F32) + lax.ppermute(part, "tower", swap).astype(F32)
    return (hot_total, rare_grad, loss_total / total)


def solution(mesh):
    return jax.shard_map(
        shards,
        mesh=mesh,
        in_specs=(
            P(("tower", "shard"), None),
            P(("tower", "shard")),
            P(),
            P("shard", None),
            P(),
            P(),
            P(),
            P(),
            P(),
            P(),
            P(),
            P(),
            P(),
            P(),
            P(),
        ),
        out_specs=(P(), P("shard", None), P()),
        check_vma=False,
    )
```

time: 677 us -> 235 us (0.35)
  waiting for transfers between devices: 378 us -> 50.8 us
  blocking collectives: 159 us -> 93.9 us
  matrix products: 31.4 us -> 0 us
  other arithmetic: 33.2 us -> 2.5 us
  starting transfers between devices: 16.2 us -> 44.2 us
  local copies, waits for them, and re-layouts: 41.1 us -> 19.3 us
  Pallas kernels: 0 us -> 20.7 us
  between operations: 16.3 us -> 2.75 us
    psum x2 -> x0, waiting for transfers between devices: 270 us -> none  [the longest x1 246 us: shards(): hot_total, loss_total = lax.psum((hot_grad, loss_part), ('tower', 'shard'))]
    unnamed x1 -> x0, blocking collectives: 132 us -> none
    all_gather x1 -> x0, waiting for transfers between devices: 73.4 us -> none  [shards(): item_all = lax.all_gather(item_vec, ('tower', 'shard'), axis=0, tiled=True)]
    all_to_all x0 -> x1, blocking collectives: none -> 58.7 us  [shards(): lax.all_to_all(spread, 'shard', split_axis=0, concat_axis=0, tiled=True)]
    ppermute x0 -> x12, waiting for transfers between devices: none -> 33.9 us  [the longest x7 27.8 us: shards(): lax.ppermute(mine, 'shard', [(i, i ^ step) for i in range(owners)])]
    dot_general x20 -> x0, matrix products: 31.4 us -> none  [the longest x2 4.04 us: user_tower(): jnp.dot(flat_normed, w_value, preferred_element_type=jnp.float32)]
    ppermute x0 -> x12, starting transfers between devices: none -> 30.5 us  [the longest x7 17.2 us: shards(): lax.ppermute(mine, 'shard', [(i, i ^ step) for i in range(owners)])]
    pallas_call x0 -> x5, Pallas kernels: none -> 20.7 us  [the longest x1 12 us: shards(): pl.pallas_call(functools.partial(backward_kernel, users, scale), out_shap...]
  transfers between devices with their start and end apart: 5 -> 14, of which waited for: 5 -> 12; matrix products, arithmetic and copies ran while one was open for 4% -> 1% of each run, Pallas kernels for 0% -> 0%
where the time goes in v1:
time: 235 us; the launch traced here: 234 us
  blocking collectives  93.9 us (40%)
  waiting for transfers between devices  50.8 us (22%)
  starting transfers between devices  44.2 us (19%)
  Pallas kernels  20.7 us (9%)
  local copies, waits for them, and re-layouts  19.3 us (8%)
  between operations  2.75 us (1%)
  other arithmetic  2.5 us (1%)
    all_to_all x1, blocking collectives, shards(): lax.all_to_all(spread, 'shard', split_axis=0, concat_axis=0, tiled=True)  58.7 us
    all_to_all x1, blocking collectives, shards(): lax.all_to_all(request, 'shard', split_axis=0, concat_axis=0, tiled=True)  35.2 us
    ppermute x7, waiting for transfers between devices, shards(): lax.ppermute(mine, 'shard', [(i, i ^ step) for i in range(owners)])  27.8 us
    unnamed x62, local copies, waits for them, and re-layouts  17.6 us
    ppermute x7, starting transfers between devices, shards(): lax.ppermute(mine, 'shard', [(i, i ^ step) for i in range(owners)])  17.2 us
    all_to_all x1, waiting for transfers between devices, shards(): lax.all_to_all(served, 'shard', split_axis=0, concat_axis=0, tiled=True)  16.9 us
    pallas_call x1, Pallas kernels, shards(): pl.pallas_call(functools.partial(backward_kernel, users, scale), out_shap...  12 us
    all_to_all x1, starting transfers between devices, shards(): lax.all_to_all(served, 'shard', split_axis=0, concat_axis=0, tiled=True)  7.3 us
  transfers between devices with their start and end apart: 14, of which 12 were waited for; matrix products, arithmetic and copies ran while one was open for 1% of the time, Pallas kernels for 0%

profile of v1, /device:TPU:1, one launch (start us, length us, event | category | flops | bytes accessed | tf_op | source)
XLA Modules:
  0.0 234.1 jit_solution(13787357163934650973)
XLA Ops:
  3.8 35.2 %all_to_all.41 = s32[128,8,128]{2,1,0:T(8,128)S(1)} all-to-all(s32[128,8,128]{2,1,0:T(8,128)S(1)} %bitcast.19), channel_id=1, replica_groups=mesh['tower'=2,'shard'=128] {'shard'}, dimensions={0} | all-to-all | bytes 1048576 | tf_op jit(solution)/shard_map/all_to_all | solution.py:409
  41.9 7.3 %all-to-all-start.1 = ((bf16[128,8,256]{2,1,0:T(8,128)(2,1)}), bf16[128,8,256]{2,1,0:T(8,128)(2,1)}, u32[]{:S(2)}, u32[]{:S(2)}) async-start(bf16[128,8,256]{2,1,0:T(8,128)(2,1)} %bitcast.18), calls=%async_computation.1 | async-start | bytes 1048576 | tf_op jit(solution)/shard_map/all_to_all | solution.py:418
  49.2 16.9 %all-to-all-done.1 = bf16[128,8,256]{2,1,0:T(8,128)(2,1)} async-done(((bf16[128,8,256]{2,1,0:T(8,128)(2,1)}), bf16[128,8,256]{2,1,0:T(8,128)(2,1)}, u32[]{:S(2)}, u32[]{:S(2)}) %all-to-all-start.1) | async-done | bytes 524320 | tf_op jit(solution)/shard_map/all_to_all | solution.py:418
  71.0 1.6 copy-done.4
  74.4 7.0 %forward.1 = (bf16[16,1024]{1,0:T(8,128)(2,1)S(1)}, bf16[16,1024]{1,0:T(8,128)(2,1)S(1)}, f32[256,1024]{1,0:T(8,128)S(1)}, bf16[256,1024]{1,0:T(8,128)(2,1)S(1)}...) custom-call(bf16[1024,256]{1,0:T(8,128)(2,1)} %bitcast.5.fetched_ref, ...), custom_call_target="tpu_custom_call" | custom-call | tf_op jit(solution)/shard_map/forward/pallas_call | solution.py:424
  81.4 4.4 %collective-permute-start = (bf16[4,1024]{1,0:T(4,128)(2,1)S(1)}, bf16[4,1024]{1,0:T(4,128)(2,1)S(1)}, u32[]{:S(2)}, u32[]{:S(2)}) collective-permute-start(bf16[4,1024]{1,0:T(4,128)(2,1)S(1)} %broadcast_select_fusion.3), channel_id=1, source_target_pairs={{0,128},{128,0},{1,129},{129,1},{2,130},{130,2},{3,131},{131,3},{4... | collective-permute-start | bytes 24584 | tf_op jit(solution)/shard_map/ppermute | solution.py:447
  86.9 58.7 %all_to_all.42 = bf16[128,8,1024]{2,1,0:T(8,128)(2,1)S(1)} all-to-all(bf16[128,8,1024]{2,1,0:T(8,128)(2,1)S(1)} %broadcast_in_dim.10), channel_id=1, replica_groups=mesh['tower'=2,'shard'=128] {'shard'}, dimensions={0} | all-to-all | bytes 4194304 | tf_op jit(solution)/shard_map/all_to_all | solution.py:452
  145.7 2.3 collective-permute-start.1
  148.0 3.8 %collective-permute-done.1.swapped_ref = bf16[1024,1024]{1,0:T(8,128)(2,1)} collective-permute-done((bf16[1024,1024]{1,0:T(8,128)(2,1)S(1)}, bf16[1024,1024]{1,0:T(8,128)(2,1)}, u32[]{:S(2)}, u32[]{:S(2)}) %collective-permute-start.1) | collective-permute-done | bytes 2097184 | tf_op jit(solution)/shard_map/ppermute | solution.py:453
  157.4 12.0 %backward.1 = (bf16[1024,256]{1,0:T(8,128)(2,1)S(1)}, f32[144,256]{1,0:T(8,128)S(1)}) custom-call(s32[2]{0:T(128)S(1)} %pad_add_fusion.1.place_ref, bf16[1024,1024]{1,0:T(8,128)(2,1)S(1)} %bitcast.14, bf16[1024,1024]{1,0:T(8,128)(2,1)} %collective-permute-done.1.swapped_ref, bf16[16,1024]{1,0:T(8,128)(2,1)S(1)} %get-tuple-element.22.user_vec_ref, ...), custom_call_target="tpu_custom_call" | custom-call | tf_op jit(solution)/shard_map/backward/pallas_call | solution.py:458
  170.7 6.4 %all-to-all-start.3 = ((bf16[128,8,256]{2,1,0:T(8,128)(2,1)}), bf16[128,8,256]{2,1,0:T(8,128)(2,1)S(1)}, u32[]{:S(2)}, u32[]{:S(2)}) async-start(bf16[128,8,256]{2,1,0:T(8,128)(2,1)} %bitcast.17), calls=%async_computation.3 | async-start | bytes 1048576 | tf_op jit(solution)/shard_map/all_to_all | solution.py:476
  177.7 12.7 %collective-permute-done.3 = f32[72,256]{1,0:T(8,128)S(1)} collective-permute-done((f32[72,256]{1,0:T(8,128)S(1)}, f32[72,256]{1,0:T(8,128)S(1)}, u32[]{:S(2)}, u32[]{:S(2)}) %collective-permute-start.3) | collective-permute-done | bytes 73760 | tf_op jit(solution)/shard_map/ppermute | solution.py:483
  191.5 4.3 %collective-permute-done.4 = f32[72,256]{1,0:T(8,128)S(1)} collective-permute-done((f32[72,256]{1,0:T(8,128)S(1)}, f32[72,256]{1,0:T(8,128)S(1)}, u32[]{:S(2)}, u32[]{:S(2)}) %collective-permute-start.4) | collective-permute-done | bytes 73760 | tf_op jit(solution)/shard_map/ppermute | solution.py:483
  195.8 3.5 %collective-permute-start.5 = (f32[72,256]{1,0:T(8,128)S(1)}, f32[72,256]{1,0:T(8,128)S(1)}, u32[]{:S(2)}, u32[]{:S(2)}) collective-permute-start(f32[72,256]{1,0:T(8,128)S(1)} %add.33), channel_id=1, source_target_pairs={{0,4},{1,5},{2,6},{3,7},{4,0},{5,1},{6,2},{7,3},{8,12},{9,13},{10,... | collective-permute-start | bytes 221192 | tf_op jit(solution)/shard_map/ppermute | solution.py:483
  199.3 3.7 %collective-permute-done.5 = f32[72,256]{1,0:T(8,128)S(1)} collective-permute-done((f32[72,256]{1,0:T(8,128)S(1)}, f32[72,256]{1,0:T(8,128)S(1)}, u32[]{:S(2)}, u32[]{:S(2)}) %collective-permute-start.5) | collective-permute-done | bytes 73760 | tf_op jit(solution)/shard_map/ppermute | solution.py:483
  203.0 4.2 %collective-permute-start.6 = (f32[72,256]{1,0:T(8,128)S(1)}, f32[72,256]{1,0:T(8,128)S(1)}, u32[]{:S(2)}, u32[]{:S(2)}) collective-permute-start(f32[72,256]{1,0:T(8,128)S(1)} %add.34), channel_id=1, source_target_pairs={{0,8},{1,9},{2,10},{3,11},{4,12},{5,13},{6,14},{7,15},{8,0},{9,1},... | collective-permute-start | bytes 221192 | tf_op jit(solution)/shard_map/ppermute | solution.py:483
  207.2 1.7 collective-permute-done.6
  209.0 3.1 %collective-permute-start.7 = (f32[72,256]{1,0:T(8,128)S(1)}, f32[72,256]{1,0:T(8,128)S(1)}, u32[]{:S(2)}, u32[]{:S(2)}) collective-permute-start(f32[72,256]{1,0:T(8,128)S(1)} %add.35), channel_id=1, source_target_pairs={{0,16},{1,17},{2,18},{3,19},{4,20},{5,21},{6,22},{7,23},{8,24},{9,... | collective-permute-start | bytes 221192 | tf_op jit(solution)/shard_map/ppermute | solution.py:483
  212.1 1.7 collective-permute-done.7
  213.9 1.6 collective-permute-start.8
  215.5 1.7 collective-permute-done.8
  217.2 3.3 %collective-permute-start.9 = (f32[72,256]{1,0:T(8,128)S(1)}, f32[72,256]{1,0:T(8,128)S(1)}, u32[]{:S(2)}, u32[]{:S(2)}) collective-permute-start(f32[72,256]{1,0:T(8,128)S(1)} %add.37), channel_id=1, source_target_pairs={{0,64},{1,65},{2,66},{3,67},{4,68},{5,69},{6,70},{7,71},{8,72},{9,... | collective-permute-start | bytes 221192 | tf_op jit(solution)/shard_map/ppermute | solution.py:483
  220.5 1.7 collective-permute-done.9
  222.3 5.7 %collective-permute-start.10 = (f32[72,256]{1,0:T(8,128)S(1)}, f32[72,256]{1,0:T(8,128)S(1)}, u32[]{:S(2)}, u32[]{:S(2)}) collective-permute-start(f32[72,256]{1,0:T(8,128)S(1)} %add.38), channel_id=1, source_target_pairs={{0,128},{128,0},{1,129},{129,1},{2,130},{130,2},{3,131},{131,3},{4... | collective-permute-start | bytes 221192 | tf_op jit(solution)/shard_map/ppermute | solution.py:485
  (97 shorter events, 26.6 us)
Async XLA Ops:
  0.6 65.5 %copy-start.6 = (bf16[256,1024]{1,0:T(8,128)(2,1)S(1)}, bf16[256,1024]{1,0:T(8,128)(2,1)}, u32[]{:S(2)}) copy-start(bf16[256,1024]{1,0:T(8,128)(2,1)} %item_w1_hbm.3) | copy-start | bytes 1572868
  0.6 65.5 %copy-start = (bf16[1024,1024]{1,0:T(8,128)(2,1)S(1)}, bf16[1024,1024]{1,0:T(8,128)(2,1)}, u32[]{:S(2)}) copy-start(bf16[1024,1024]{1,0:T(8,128)(2,1)} %w_query_hbm.3) | copy-start | bytes 6291460
  0.7 65.5 %copy-start.5 = (bf16[256,1024]{1,0:T(8,128)(2,1)S(1)}, bf16[256,1024]{1,0:T(8,128)(2,1)}, u32[]{:S(2)}) copy-start(bf16[256,1024]{1,0:T(8,128)(2,1)} %in_proj_hbm.3) | copy-start | bytes 1572868
  41.9 24.2 %all-to-all-start.1 = ((bf16[128,8,256]{2,1,0:T(8,128)(2,1)}), bf16[128,8,256]{2,1,0:T(8,128)(2,1)}, u32[]{:S(2)}, u32[]{:S(2)}) async-start(bf16[128,8,256]{2,1,0:T(8,128)(2,1)} %bitcast.18), calls=%async_computation.1 | async-start | bytes 1048576 | tf_op jit(solution)/shard_map/all_to_all | solution.py:418
  81.3 64.3 %copy-start.7 = (f32[256,1024]{1,0:T(8,128)}, f32[256,1024]{1,0:T(8,128)S(1)}, u32[]{:S(2)}) copy-start(f32[256,1024]{1,0:T(8,128)S(1)} %get-tuple-element.24.hidden_ref) | copy-start | bytes 3145732
  81.3 64.3 %copy-start.9 = (bf16[256,1024]{1,0:T(8,128)(2,1)}, bf16[256,1024]{1,0:T(8,128)(2,1)S(1)}, u32[]{:S(2)}) copy-start(bf16[256,1024]{1,0:T(8,128)(2,1)S(1)} %get-tuple-element.25.normed_ref) | copy-start | bytes 1572868
  81.4 64.3 %copy-start.16 = (f32[16,1024]{1,0:T(8,128)}, f32[16,1024]{1,0:T(8,128)S(1)}, u32[]{:S(2)}) copy-start(f32[16,1024]{1,0:T(8,128)S(1)} %get-tuple-element.28.mixed_ref) | copy-start | bytes 196612
  81.4 64.3 %copy-start.18 = (f32[16,1024]{1,0:T(8,128)}, f32[16,1024]{1,0:T(8,128)S(1)}, u32[]{:S(2)}) copy-start(f32[16,1024]{1,0:T(8,128)S(1)} %get-tuple-element.29.inner_ref) | copy-start | bytes 196612
  81.4 64.3 %copy-start.20 = (f32[16,1024]{1,0:T(8,128)}, f32[16,1024]{1,0:T(8,128)S(1)}, u32[]{:S(2)}) copy-start(f32[16,1024]{1,0:T(8,128)S(1)} %get-tuple-element.30.outer_ref) | copy-start | bytes 196612
  81.4 64.3 %copy-start.22 = (f32[64,64]{1,0:T(8,128)}, f32[64,64]{1,0:T(8,128)S(1)}, u32[]{:S(2)}) copy-start(f32[64,64]{1,0:T(8,128)S(1)} %get-tuple-element.27.weights_ref) | copy-start | bytes 49156
  81.4 5.2 %collective-permute-start = (bf16[4,1024]{1,0:T(4,128)(2,1)S(1)}, bf16[4,1024]{1,0:T(4,128)(2,1)S(1)}, u32[]{:S(2)}, u32[]{:S(2)}) collective-permute-start(bf16[4,1024]{1,0:T(4,128)(2,1)S(1)} %broadcast_select_fusion.3), channel_id=1, source_target_pairs={{0,128},{128,0},{1,129},{129,1},{2,130},{130,2},{3,131},{131,3},{4... | collective-permute-start | bytes 24584 | tf_op jit(solution)/shard_map/ppermute | solution.py:447
  86.9 65.0 %copy-start.30 = (s32[8,384]{1,0:T(8,128)S(1)}, s32[8,384]{1,0:T(8,128)}, u32[]{:S(2)}) copy-start(s32[8,384]{1,0:T(8,128)} %copy-done.29) | copy-start | bytes 36868
  145.7 6.2 %collective-permute-start.1 = (bf16[1024,1024]{1,0:T(8,128)(2,1)S(1)}, bf16[1024,1024]{1,0:T(8,128)(2,1)}, u32[]{:S(2)}, u32[]{:S(2)}) collective-permute-start(bf16[1024,1024]{1,0:T(8,128)(2,1)S(1)} %bitcast.13), channel_id=1, source_target_pairs={{0,128},{128,0},{1,129},{129,1},{2,130},{130,2},{3,131},{131,3},{4... | collective-permute-start | bytes 6291464 | tf_op jit(solution)/shard_map/ppermute | solution.py:453
  170.3 6.9 %collective-permute-start.2 = (f32[72,256]{1,0:T(8,128)S(1)}, f32[72,256]{1,0:T(8,128)S(1)}, u32[]{:S(2)}, u32[]{:S(2)}) collective-permute-start(f32[72,256]{1,0:T(8,128)S(1)} %slice_select_fusion), channel_id=1, source_target_pairs={{0,128},{128,0},{1,129},{129,1},{2,130},{130,2},{3,131},{131,3},{4... | collective-permute-start | bytes 221192 | tf_op jit(solution)/shard_map/ppermute | solution.py:480
  170.7 59.3 %all-to-all-start.3 = ((bf16[128,8,256]{2,1,0:T(8,128)(2,1)}), bf16[128,8,256]{2,1,0:T(8,128)(2,1)S(1)}, u32[]{:S(2)}, u32[]{:S(2)}) async-start(bf16[128,8,256]{2,1,0:T(8,128)(2,1)} %bitcast.17), calls=%async_computation.3 | async-start | bytes 1048576 | tf_op jit(solution)/shard_map/all_to_all | solution.py:476
  177.2 13.3 %collective-permute-start.3 = (f32[72,256]{1,0:T(8,128)S(1)}, f32[72,256]{1,0:T(8,128)S(1)}, u32[]{:S(2)}, u32[]{:S(2)}) collective-permute-start(f32[72,256]{1,0:T(8,128)S(1)} %select_add_fusion), channel_id=1, source_target_pairs={{0,1},{1,0},{2,3},{3,2},{4,5},{5,4},{6,7},{7,6},{8,9},{9,8},{10,11... | collective-permute-start | bytes 221192 | tf_op jit(solution)/shard_map/ppermute | solution.py:483
  190.5 5.4 %collective-permute-start.4 = (f32[72,256]{1,0:T(8,128)S(1)}, f32[72,256]{1,0:T(8,128)S(1)}, u32[]{:S(2)}, u32[]{:S(2)}) collective-permute-start(f32[72,256]{1,0:T(8,128)S(1)} %add.32), channel_id=1, source_target_pairs={{0,2},{1,3},{2,0},{3,1},{4,6},{5,7},{6,4},{7,5},{8,10},{9,11},{10,... | collective-permute-start | bytes 221192 | tf_op jit(solution)/shard_map/ppermute | solution.py:483
  195.8 7.2 %collective-permute-start.5 = (f32[72,256]{1,0:T(8,128)S(1)}, f32[72,256]{1,0:T(8,128)S(1)}, u32[]{:S(2)}, u32[]{:S(2)}) collective-permute-start(f32[72,256]{1,0:T(8,128)S(1)} %add.33), channel_id=1, source_target_pairs={{0,4},{1,5},{2,6},{3,7},{4,0},{5,1},{6,2},{7,3},{8,12},{9,13},{10,... | collective-permute-start | bytes 221192 | tf_op jit(solution)/shard_map/ppermute | solution.py:483
  203.0 5.9 %collective-permute-start.6 = (f32[72,256]{1,0:T(8,128)S(1)}, f32[72,256]{1,0:T(8,128)S(1)}, u32[]{:S(2)}, u32[]{:S(2)}) collective-permute-start(f32[72,256]{1,0:T(8,128)S(1)} %add.34), channel_id=1, source_target_pairs={{0,8},{1,9},{2,10},{3,11},{4,12},{5,13},{6,14},{7,15},{8,0},{9,1},... | collective-permute-start | bytes 221192 | tf_op jit(solution)/shard_map/ppermute | solution.py:483
  209.0 4.8 %collective-permute-start.7 = (f32[72,256]{1,0:T(8,128)S(1)}, f32[72,256]{1,0:T(8,128)S(1)}, u32[]{:S(2)}, u32[]{:S(2)}) collective-permute-start(f32[72,256]{1,0:T(8,128)S(1)} %add.35), channel_id=1, source_target_pairs={{0,16},{1,17},{2,18},{3,19},{4,20},{5,21},{6,22},{7,23},{8,24},{9,... | collective-permute-start | bytes 221192 | tf_op jit(solution)/shard_map/ppermute | solution.py:483
  213.9 3.3 %collective-permute-start.8 = (f32[72,256]{1,0:T(8,128)S(1)}, f32[72,256]{1,0:T(8,128)S(1)}, u32[]{:S(2)}, u32[]{:S(2)}) collective-permute-start(f32[72,256]{1,0:T(8,128)S(1)} %add.36), channel_id=1, source_target_pairs={{0,32},{1,33},{2,34},{3,35},{4,36},{5,37},{6,38},{7,39},{8,40},{9,... | collective-permute-start | bytes 221192 | tf_op jit(solution)/shard_map/ppermute | solution.py:483
  217.2 5.1 %collective-permute-start.9 = (f32[72,256]{1,0:T(8,128)S(1)}, f32[72,256]{1,0:T(8,128)S(1)}, u32[]{:S(2)}, u32[]{:S(2)}) collective-permute-start(f32[72,256]{1,0:T(8,128)S(1)} %add.37), channel_id=1, source_target_pairs={{0,64},{1,65},{2,66},{3,67},{4,68},{5,69},{6,70},{7,71},{8,72},{9,... | collective-permute-start | bytes 221192 | tf_op jit(solution)/shard_map/ppermute | solution.py:483
  222.3 6.6 %collective-permute-start.10 = (f32[72,256]{1,0:T(8,128)S(1)}, f32[72,256]{1,0:T(8,128)S(1)}, u32[]{:S(2)}, u32[]{:S(2)}) collective-permute-start(f32[72,256]{1,0:T(8,128)S(1)} %add.38), channel_id=1, source_target_pairs={{0,128},{128,0},{1,129},{129,1},{2,130},{130,2},{3,131},{131,3},{4... | collective-permute-start | bytes 221192 | tf_op jit(solution)/shard_map/ppermute | solution.py:485
  230.5 1.6 collective-permute-start.11
  (21 other events, 155.6 us)

commit v2 on v1

v2 whole, which is shorter than its diff:
```python
import functools
import math

import jax
import jax.numpy as jnp
from jax import lax
from jax.experimental import pallas as pl
from jax.experimental.pallas import tpu as pltpu
from jax.sharding import Mesh
from jax.sharding import PartitionSpec as P

HEAD_DIM = 64
EPS = 1e-06
SLOTS = 8
HOT_SLOT = 5
SHARD = ("x", "y", "z")
PAD = 16
BF = jnp.bfloat16
F32 = jnp.float32
VMEM = pl.BlockSpec(memory_space=pltpu.VMEM)
SMEM = pl.BlockSpec(memory_space=pltpu.SMEM)
HBM = pl.BlockSpec(memory_space=pltpu.HBM)
NT = (((1,), (1,)), ((), ()))
TN = (((0,), (0,)), ((), ()))


def dot(a, b):
    return jnp.dot(a, b, preferred_element_type=F32)


def dot_nt(a, b):
    return lax.dot_general(a, b, NT, preferred_element_type=F32)


def dot_tn(a, b):
    return lax.dot_general(a, b, TN, preferred_element_type=F32)


def iota(shape, axis):
    return lax.broadcasted_iota(jnp.int32, shape, axis)


def one_hot(mask):
    return jnp.where(mask, 1.0, 0.0).astype(BF)


def params(mib):
    return pltpu.CompilerParams(vmem_limit_bytes=mib * 1024 * 1024)


def copies_of(pairs, sems):
    copies = [pltpu.make_async_copy(a, b, sems.at[i]) for i, (a, b) in enumerate(pairs)]
    for copy in copies:
        copy.start()
    return copies


def index_kernel(
    rare_count, owners, history_ref, items_ref, request_ref, row_hbm, column_hbm, row, column, sems
):
    hot_count = owners
    users = history_ref.shape[0]
    span = row.shape[1]
    parts = [history_ref[u : u + 1, :] for u in range(users)] + [items_ref[...]]
    filled = sum(p.shape[1] for p in parts)
    ids = jnp.concatenate(parts + [jnp.full((1, span - filled), -1, jnp.int32)], axis=1)
    is_rare = ids >= hot_count
    index = ids - hot_count
    owner = jnp.where(is_rare, index // rare_count, -1)
    value = jnp.where(is_rare, index % rare_count + 1, 0).astype(F32)
    hits = iota((owners, span), 0) == owner
    before = one_hot(iota((span, span), 0) < iota((span, span), 1))
    earlier = dot(one_hot(hits), before)
    position = jnp.sum(jnp.where(hits, earlier, 0.0), axis=0, keepdims=True).astype(jnp.int32)
    places = jnp.where(
        is_rare, owner * SLOTS + position, jnp.where(ids >= 0, ids * SLOTS + HOT_SLOT, -1)
    )
    row[...] = jnp.broadcast_to(places, row.shape)
    column[...] = jnp.transpose(jnp.broadcast_to(places.astype(F32), (128, span))).astype(jnp.int32)
    copies = copies_of([(row, row_hbm), (column, column_hbm)], sems)
    order = jnp.where(hits, earlier, -1.0)
    lanes = iota(request_ref.shape, 1)
    request = jnp.zeros(request_ref.shape, F32)
    for slot in range(HOT_SLOT):
        wanted = jnp.sum(jnp.where(order == float(slot), value, 0.0), axis=1, keepdims=True)
        request = jnp.where(lanes == slot, wanted, request)
    request_ref[...] = request.astype(jnp.int32)
    for copy in copies:
        copy.wait()


def serve_kernel(asked_ref, table_hbm, served_hbm, row_hbm, table, served, row, sems):
    load = pltpu.make_async_copy(table_hbm, table, sems.at[0])
    load.start()
    slots = served.shape[0]
    sources = asked_ref.shape[0]
    asked = asked_ref[...]
    high = (asked // 2).astype(F32).astype(BF)
    low = (asked % 2).astype(F32).astype(BF)
    expand = one_hot(iota((slots, sources), 0) // SLOTS == iota((slots, sources), 1))
    wide = 2.0 * dot(expand, high) + dot(expand, low)
    mine = iota(wide.shape, 1) == iota(wide.shape, 0) % SLOTS
    index = jnp.sum(jnp.where(mine, wide, 0.0), axis=1, keepdims=True) - 1.0
    index = jnp.broadcast_to(index, wide.shape)
    row[...] = jnp.transpose(index)[0:8].astype(jnp.int32)
    keep = pltpu.make_async_copy(row, row_hbm, sems.at[1])
    keep.start()
    index = index.astype(jnp.int32)
    lanes = iota(index.shape, 1)
    rows = table.shape[0]
    picks = jnp.concatenate(
        [one_hot(index == lanes + 128 * j) for j in range(rows // 128)], axis=1
    )
    load.wait()
    known = table[...].astype(BF)
    chunk = slots // 4
    copies = []
    for c in range(4):
        at = pl.ds(c * chunk, chunk)
        served[at, :] = dot(picks[c * chunk : (c + 1) * chunk], known).astype(BF)
        copies.append(pltpu.make_async_copy(served.at[at], served_hbm.at[at], sems.at[2 + c]))
        copies[-1].start()
    keep.wait()
    for copy in copies:
        copy.wait()


def head_mask(heads, width):
    return iota((heads, width), 1) // HEAD_DIM == iota((heads, width), 0)


def spread_heads(values, mask, users):
    return jnp.concatenate(
        [jnp.where(mask, values[u : u + 1], 0.0) for u in range(users)], axis=0
    ).astype(BF)


def join_heads(full, mask, users):
    heads = mask.shape[0]
    parts = [
        jnp.sum(
            jnp.where(mask, full[u * heads : (u + 1) * heads], 0.0), axis=0, keepdims=True
        )
        for u in range(users)
    ]
    return jnp.concatenate(parts + [jnp.zeros((PAD - users, full.shape[1]), F32)], axis=0)


def forward_kernel(
    users,
    fetched_ref,
    norm_gain_ref,
    out_gain_ref,
    item_gain_ref,
    *refs,
):
    sources, refs = refs[:10], refs[10:]
    vectors_ref, kept_hbm, refs = refs[0], refs[1:8], refs[8:]
    targets, kept, (in_sems, out_sems) = refs[:10], refs[10:17], refs[17:]
    hot, column_of, pos_of, in_proj, w_query, w_key, w_value, w_out, item_w1, item_w2 = targets
    hidden_ref, normed_ref, qk_ref, weights_ref, mixed_ref, inner_ref, outer_ref = kept
    copies = copies_of(zip(sources, targets), in_sems)
    saves = [
        pltpu.make_async_copy(a, b, out_sems.at[i]) for i, (a, b) in enumerate(zip(kept, kept_hbm))
    ]
    hist, width = pos_of.shape
    heads = width // HEAD_DIM
    span = users * hist
    slots = fetched_ref.shape[0]
    copies[0].wait()
    copies[1].wait()
    column = column_of[0 : span + PAD, :]
    lanes = iota(column.shape, 1)
    picks = jnp.concatenate(
        [one_hot(column == lanes + 128 * j) for j in range(slots // 128)], axis=1
    )
    hot_picks = one_hot(column == lanes * SLOTS + HOT_SLOT)
    rows = (dot(picks, fetched_ref[...]) + dot(hot_picks, hot[...].astype(BF))).astype(BF)
    copies[2].wait()
    copies[3].wait()
    pos = pos_of[...].astype(F32)
    hidden = dot(rows[0:span], in_proj[...]) + jnp.concatenate([pos] * users, axis=0)
    hidden_ref[...] = hidden
    saves[0].start()
    scale = lax.rsqrt(jnp.mean(hidden * hidden, axis=-1, keepdims=True) + EPS)
    normed = (hidden * scale * norm_gain_ref[...]).astype(BF)
    normed_ref[...] = normed
    saves[1].start()
    last = jnp.concatenate(
        [normed[(u + 1) * hist - PAD : (u + 1) * hist].astype(F32)[PAD - 1 :] for u in range(users)]
        + [jnp.zeros((PAD - users, width), F32)],
        axis=0,
    ).astype(BF)
    mask = head_mask(heads, width)
    copies[4].wait()
    query = dot(last, w_query[...]).astype(BF).astype(F32)
    copies[5].wait()
    qk = dot_nt(spread_heads(query, mask, users), w_key[...]).astype(BF)
    qk_ref[...] = qk
    saves[2].start()
    mixes = []
    for u in range(users):
        own = normed[u * hist : (u + 1) * hist]
        scores = dot_nt(qk[u * heads : (u + 1) * heads], own) * (1.0 / math.sqrt(HEAD_DIM))
        raised = jnp.exp(scores - jnp.max(scores, axis=1, keepdims=True))
        weights = raised / jnp.sum(raised, axis=1, keepdims=True)
        weights_ref[u * heads : (u + 1) * heads, :] = weights
        mixes.append(dot(weights.astype(BF), own))
    saves[3].start()
    mixes = jnp.concatenate(mixes, axis=0).astype(BF)
    copies[6].wait()
    attended = join_heads(dot(mixes, w_value[...]), mask, users).astype(BF)
    copies[7].wait()
    hidden_last = jnp.concatenate(
        [hidden_ref[(u + 1) * hist - 1 : (u + 1) * hist, :] for u in range(users)]
        + [jnp.zeros((PAD - users, width), F32)],
        axis=0,
    )
    mixed = hidden_last + dot(attended, w_out[...])
    mixed_ref[...] = mixed
    saves[4].start()
    scale = lax.rsqrt(jnp.mean(mixed * mixed, axis=-1, keepdims=True) + EPS)
    user_vec = mixed * scale * out_gain_ref[...]
    copies[8].wait()
    inner = dot(rows[span : span + PAD], item_w1[...])
    inner_ref[...] = inner
    saves[5].start()
    copies[9].wait()
    outer = dot((inner * jax.nn.sigmoid(inner)).astype(BF), item_w2[...])
    outer_ref[...] = outer
    saves[6].start()
    scale = lax.rsqrt(jnp.mean(outer * outer, axis=-1, keepdims=True) + EPS)
    item_vec = outer * scale * item_gain_ref[...]
    both = jnp.concatenate([user_vec[0:users], item_vec[0:users]], axis=0)
    peers = vectors_ref.shape[0] // (2 * users)
    vectors_ref[...] = jnp.concatenate([both] * peers, axis=0).astype(BF)
    for save in saves:
        save.wait()


def arrange_kernel(users, vectors_ref, spread_ref):
    vectors = vectors_ref[...]
    rows, width = vectors.shape
    half = rows // 2
    out = iota((half, rows), 0)
    source = out // users * (2 * users) + out % users
    at = iota((half, rows), 1)
    user_rows = dot(one_hot(at == source), vectors).astype(BF)
    item_rows = dot(one_hot(at == source + users), vectors).astype(BF)
    for peer in range(spread_ref.shape[0] // half):
        spread_ref[peer * half : (peer + 1) * half, 0:width] = user_rows
        spread_ref[peer * half : (peer + 1) * half, width : 2 * width] = item_rows


def softmax_step(users, scale, base, parts, vectors, logits):
    rows, width = parts[0].shape
    width //= 2
    total = rows * len(parts)
    chunk = 256
    tops = [jnp.full((1, rows), -jnp.inf, F32) for _ in parts]
    for i, items in enumerate(parts):
        for c in range(0, rows, chunk):
            some = items[c : c + chunk, width:]
            for j, part in enumerate(parts):
                here = scale * dot_nt(some, part[:, :width])
                logits[i * rows + c : i * rows + c + chunk, j * rows : (j + 1) * rows] = here
                tops[j] = jnp.maximum(tops[j], jnp.max(here, axis=0, keepdims=True))
    top = jnp.concatenate(tops, axis=1)
    count = jnp.zeros((1, total), F32)
    for c in range(0, total, chunk):
        here = logits[c : c + chunk, :]
        count = count + jnp.sum(jnp.exp(here - top), axis=0, keepdims=True)
    normalizer = top + jnp.log(count)
    none = jnp.zeros((PAD - users, width), F32)
    user_vec = jnp.concatenate([vectors[0:users], none], axis=0).astype(BF)
    item_vec = jnp.concatenate([vectors[users : 2 * users], none], axis=0).astype(BF)
    lines = iota((PAD, total), 0)
    valid = lines < users
    target = iota((PAD, total), 1) == lines + base
    one = jnp.where(target, 1.0, 0.0)

    def against(vec, at):
        return scale * jnp.concatenate([dot_nt(vec, p[:, at]) for p in parts], axis=1)

    def pulled(slope, at):
        sums = [dot(slope[:, j * rows : (j + 1) * rows], p[:, at]) for j, p in enumerate(parts)]
        return (scale * sum(sums)).astype(BF).astype(F32)

    of_users, of_items = slice(0, width), slice(width, 2 * width)
    item_logits = against(item_vec, of_users)
    slope = jnp.where(valid, jnp.exp(item_logits - normalizer) - one, 0.0).astype(BF)
    d_item = pulled(slope, of_users)
    user_logits = against(user_vec, of_items)
    top = jnp.max(user_logits, axis=1, keepdims=True)
    normalizer = top + jnp.log(jnp.sum(jnp.exp(user_logits - top), axis=1, keepdims=True))
    slope = jnp.where(valid, jnp.exp(user_logits - normalizer) - one, 0.0).astype(BF)
    d_user = pulled(slope, of_items)
    each = jnp.sum(jnp.where(valid & target, normalizer - user_logits, 0.0), axis=1, keepdims=True)
    return d_user, d_item, jnp.sum(each, axis=0, keepdims=True)


def norm_backward(values, cotangent, gain):
    inverse = lax.rsqrt(jnp.mean(values * values, axis=-1, keepdims=True) + EPS)
    pulled = cotangent * gain
    along = jnp.mean(pulled * values, axis=-1, keepdims=True)
    return inverse * pulled - values * (inverse * inverse * inverse * along)


def backward_kernel(
    users,
    loss_scale,
    base_ref,
    gathered_ref,
    swapped_ref,
    norm_gain_ref,
    out_gain_ref,
    item_gain_ref,
    *refs,
):
    sources, refs = refs[:16], refs[16:]
    (outgoing_hbm, loss_ref), refs = refs[:2], refs[2:]
    targets, (outgoing, logits, d_normed, in_sems, out_sems) = refs[:16], refs[16:]
    vectors_ref, row_ref = targets[:2]
    hidden_ref, normed_ref, qk_ref, weights_ref, mixed_ref, inner_ref, outer_ref = targets[2:9]
    in_proj, w_query, w_key, w_value, w_out, item_w1, item_w2 = targets[9:]
    copies = copies_of(zip(sources, targets), in_sems)
    copies[0].wait()
    vectors = vectors_ref[0:PAD, :].astype(F32)
    d_user, d_item, loss = softmax_step(
        users, loss_scale, base_ref[0], (gathered_ref, swapped_ref), vectors, logits
    )
    loss_ref[...] = jnp.broadcast_to(loss, loss_ref.shape)
    for copy in copies[1:]:
        copy.wait()
    span, width = hidden_ref.shape
    hist = span // users
    heads = width // HEAD_DIM
    mask = head_mask(heads, width)
    d_mixed = norm_backward(mixed_ref[...], d_user, out_gain_ref[...])
    d_attended = dot_nt(d_mixed.astype(BF), w_out[...])
    d_mixes = dot_nt(spread_heads(d_attended, mask, users), w_value[...]).astype(BF)
    d_qk = []
    for u in range(users):
        own = normed_ref[u * hist : (u + 1) * hist, :]
        weights = weights_ref[u * heads : (u + 1) * heads, :]
        pulled = d_mixes[u * heads : (u + 1) * heads]
        d_weights = dot_nt(pulled, own)
        d_scores = weights * (d_weights - jnp.sum(weights * d_weights, axis=1, keepdims=True))
        d_scores = (d_scores * (1.0 / math.sqrt(HEAD_DIM))).astype(BF)
        d_normed[u * hist : (u + 1) * hist, :] = dot_tn(weights.astype(BF), pulled) + dot_tn(
            d_scores, qk_ref[u * heads : (u + 1) * heads, :]
        )
        d_qk.append(dot(d_scores, own))
    d_qk = jnp.concatenate(d_qk, axis=0).astype(BF)
    d_query = join_heads(dot(d_qk, w_key[...]), mask, users).astype(BF)
    d_last = dot_nt(d_query, w_query[...])
    for u in range(users):
        at = slice((u + 1) * hist - 1, (u + 1) * hist)
        d_normed[at, :] = d_normed[at, :] + d_last[u : u + 1]
    d_normed[...] = norm_backward(hidden_ref[...], d_normed[...], norm_gain_ref[...])
    for u in range(users):
        at = slice((u + 1) * hist - 1, (u + 1) * hist)
        d_normed[at, :] = d_normed[at, :] + d_mixed[u : u + 1]
    d_rows = dot_nt(d_normed[...].astype(BF), in_proj[...])
    d_outer = norm_backward(outer_ref[...], d_item, item_gain_ref[...])
    inner = inner_ref[...]
    gate = jax.nn.sigmoid(inner)
    d_inner = dot_nt(d_outer.astype(BF), item_w2[...]) * (gate * (1.0 + inner * (1.0 - gate)))
    d_items = dot_nt(d_inner.astype(BF), item_w1[...])
    wide = row_ref.shape[1]
    d_all = jnp.concatenate(
        [d_rows, d_items, jnp.zeros((wide - span - PAD, d_rows.shape[1]), F32)], axis=0
    ).astype(BF)
    slots = outgoing.shape[0]
    column = row_ref[0:1, :]
    chunk = slots // 4
    saves = []
    for c in range(4):
        at = pl.ds(c * chunk, chunk)
        picks = one_hot(iota((chunk, wide), 0) + c * chunk == column)
        outgoing[at, :] = dot(picks, d_all).astype(BF)
        saves.append(pltpu.make_async_copy(outgoing.at[at], outgoing_hbm.at[at], out_sems.at[c]))
        saves[-1].start()
    for save in saves:
        save.wait()


def scatter_kernel(returned_ref, row_ref, loss_ref, part_ref, hot_ref):
    rows, emb = part_ref.shape
    slots = returned_ref.shape[0]
    returned = returned_ref[...]
    picks = one_hot(iota((rows, slots), 0) == row_ref[0:1, :])
    part_ref[...] = dot(picks, returned).astype(BF)
    hot = dot(one_hot(iota((PAD, slots), 1) % SLOTS == HOT_SLOT), returned)
    hot_ref[:, 0:emb] = hot[0:1]
    hot_ref[:, emb:] = loss_ref[0:1, :]


def shards(
    history,
    item_ids,
    hot_table,
    rare_table,
    in_proj,
    pos_embed,
    norm_gain,
    w_query,
    w_key,
    w_value,
    w_out,
    out_gain,
    item_w1,
    item_w2,
    item_gain,
):
    users, hist = history.shape
    emb = hot_table.shape[1]
    rare_count = rare_table.shape[0]
    width = in_proj.shape[1]
    heads = width // HEAD_DIM
    scale = 4.0 / math.sqrt(width)
    owners = lax.axis_size(SHARD)
    towers = lax.axis_size("tower")
    near = lax.axis_size("z")
    total = users * towers * owners
    slots = owners * SLOTS
    span = users * hist
    wide = -(-(span + PAD) // 128) * 128
    swap = [(i, towers - 1 - i) for i in range(towers)]
    shape = jax.ShapeDtypeStruct
    sems = lambda n: pltpu.SemaphoreType.DMA((n,))
    like = lambda arrays: [pltpu.VMEM(a.shape, a.dtype) for a in arrays]
    exchange = functools.partial(lax.all_to_all, split_axis=0, concat_axis=0, tiled=True)

    places = (shape((8, wide), jnp.int32), shape((wide, 128), jnp.int32))
    request, row, column = pl.pallas_call(
        functools.partial(index_kernel, rare_count, owners),
        out_shape=(shape((owners, 128), jnp.int32),) + places,
        in_specs=[VMEM, VMEM],
        out_specs=(VMEM, HBM, HBM),
        scratch_shapes=like(places) + [sems(2)],
        compiler_params=params(24),
        name="index",
    )(history, item_ids.reshape(1, users))
    asked = exchange(request, SHARD)
    served_shapes = (shape((slots, emb), BF), shape((8, slots), jnp.int32))
    served, asked_row = pl.pallas_call(
        serve_kernel,
        out_shape=served_shapes,
        in_specs=[VMEM, HBM],
        out_specs=(HBM, HBM),
        scratch_shapes=like((rare_table,) + served_shapes) + [sems(6)],
        compiler_params=params(24),
        name="serve",
    )(asked, rare_table)
    fetched = exchange(served, SHARD)

    weights = (in_proj, w_query, w_key, w_value, w_out, item_w1, item_w2)
    gains = tuple(g.reshape(1, width) for g in (norm_gain, out_gain, item_gain))
    kept_shapes = (
        shape((span, width), F32),
        shape((span, width), BF),
        shape((users * heads, width), BF),
        shape((users * heads, hist), F32),
        shape((PAD, width), F32),
        shape((PAD, width), F32),
        shape((PAD, width), F32),
    )
    loads = (hot_table, column, pos_embed) + weights
    vectors, *kept = pl.pallas_call(
        functools.partial(forward_kernel, users),
        out_shape=(shape((near * 2 * users, width), BF),) + kept_shapes,
        in_specs=[VMEM] * 4 + [HBM] * len(loads),
        out_specs=(VMEM,) + (HBM,) * len(kept_shapes),
        scratch_shapes=like(loads + kept_shapes) + [sems(len(loads)), sems(len(kept_shapes))],
        compiler_params=params(40),
        name="forward",
    )(fetched, *gains, *loads)

    near_vectors = exchange(vectors, "z")
    spread = pl.pallas_call(
        functools.partial(arrange_kernel, users),
        out_shape=shape((owners * users, 2 * width), BF),
        in_specs=[VMEM],
        out_specs=VMEM,
        compiler_params=params(24),
        name="arrange",
    )(near_vectors)
    gathered = exchange(spread, ("x", "y"))
    swapped = lax.ppermute(gathered, "tower", swap)
    base = (lax.axis_index(SHARD) * users).astype(jnp.int32).reshape(1)

    loads = (vectors, row) + tuple(kept) + weights
    outgoing, loss = pl.pallas_call(
        functools.partial(backward_kernel, users, scale),
        out_shape=(shape((slots, emb), BF), shape((8, 128), F32)),
        in_specs=[SMEM] + [VMEM] * 5 + [HBM] * len(loads),
        out_specs=(HBM, VMEM),
        scratch_shapes=like(loads)
        + [
            pltpu.VMEM((slots, emb), BF),
            pltpu.VMEM((total, total), F32),
            pltpu.VMEM((span, width), F32),
            sems(len(loads)),
            sems(4),
        ],
        compiler_params=params(48),
        name="backward",
    )(base, gathered, swapped, *gains, *loads)

    returned = exchange(outgoing, SHARD)
    part, mine = pl.pallas_call(
        scatter_kernel,
        out_shape=(shape((rare_count, emb), BF), shape((1, emb + 128), F32)),
        in_specs=[VMEM, VMEM, VMEM],
        out_specs=(VMEM, VMEM),
        compiler_params=params(24),
        name="scatter",
    )(returned, asked_row, loss)
    mine = mine + lax.ppermute(mine, "tower", swap)
    rare_grad = part.astype(F32) + lax.ppermute(part, "tower", swap).astype(F32)
    sums = exchange(jnp.broadcast_to(mine, (owners, emb + 128)), SHARD)
    return (sums[:, :emb], rare_grad, jnp.sum(sums[:, emb]) / total)


def solution(mesh):
    sizes = (mesh.shape["tower"], 4, 4, mesh.shape["shard"] // 16)
    mesh = Mesh(mesh.devices.reshape(sizes), ("tower",) + SHARD)
    return jax.shard_map(
        shards,
        mesh=mesh,
        in_specs=(
            P(("tower",) + SHARD, None),
            P(("tower",) + SHARD),
            P(),
            P(SHARD, None),
            P(),
            P(),
            P(),
            P(),
            P(),
            P(),
            P(),
            P(),
            P(),
            P(),
            P(),
        ),
        out_specs=(P(), P(SHARD, None), P()),
        check_vma=False,
    )
```

time: 235 us -> 196 us (0.83)
  waiting for transfers between devices: 50.8 us -> 17.2 us
  starting transfers between devices: 44.2 us -> 14.8 us
  blocking collectives: 93.9 us -> 112 us
  Pallas kernels: 20.7 us -> 25.8 us
    ppermute x10 -> x1, waiting for transfers between devices: 29.5 us -> 1.06 us  [shards(): mine = mine + lax.ppermute(mine, 'tower', swap)]
    ppermute x10 -> x1, starting transfers between devices: 27.8 us -> 0.1 us  [shards(): mine = mine + lax.ppermute(mine, 'tower', swap)]
    all_to_all x2 -> x5, blocking collectives: 93.9 us -> 112 us  [the longest x1 26.7 us: shards(): asked = exchange(request, SHARD)]
    all_to_all x2 -> x1, starting transfers between devices: 13.7 us -> 6.13 us  [shards(): sums = exchange(jnp.broadcast_to(mine, (owners, emb + 128)), SHARD)]
    all_to_all x2 -> x1, waiting for transfers between devices: 16.9 us -> 12.2 us  [shards(): sums = exchange(jnp.broadcast_to(mine, (owners, emb + 128)), SHARD)]
    ppermute x1, starting transfers between devices: 2.28 us -> 6.49 us  [shards(): swapped = lax.ppermute(gathered, 'tower', swap)]
    pallas_call x3 -> x4, Pallas kernels: 1.75 us -> 4.38 us  [the longest x1 2.71 us: shards(): pl.pallas_call(serve_kernel, out_shape=served_shapes, in_specs=[VMEM, HBM...]
    unnamed x62 -> x61, local copies, waits for them, and re-layouts: 17.6 us -> 19.5 us
  transfers between devices with their start and end apart: 14 -> 4, of which waited for: 12 -> 3; matrix products, arithmetic and copies ran while one was open for 1% -> 1% of each run, Pallas kernels for 0% -> 0%
where the time goes in v2:
time: 196 us; the launch traced here: 195 us
  blocking collectives  112 us (57%)
  Pallas kernels  25.8 us (13%)
  local copies, waits for them, and re-layouts  20.9 us (11%)
  waiting for transfers between devices  17.2 us (9%)
  starting transfers between devices  14.8 us (8%)
  between operations  2.62 us (1%)
    all_to_all x1, blocking collectives, shards(): asked = exchange(request, SHARD)  26.7 us
    all_to_all x1, blocking collectives, shards(): gathered = exchange(spread, ('x', 'y'))  25.8 us
    all_to_all x1, blocking collectives, shards(): returned = exchange(outgoing, SHARD)  25.2 us
    all_to_all x1, blocking collectives, shards(): fetched = exchange(served, SHARD)  23.6 us
    unnamed x61, local copies, waits for them, and re-layouts  19.5 us
    pallas_call x1, Pallas kernels, shards(): pl.pallas_call(functools.partial(backward_kernel, users, scale), out_shap...  14.2 us
    all_to_all x1, waiting for transfers between devices, shards(): sums = exchange(jnp.broadcast_to(mine, (owners, emb + 128)), SHARD)  12.2 us
    all_to_all x1, blocking collectives, shards(): near_vectors = exchange(vectors, 'z')  10.8 us
  transfers between devices with their start and end apart: 4, of which 3 were waited for; matrix products, arithmetic and copies ran while one was open for 1% of the time, Pallas kernels for 0%

profile of v2, /device:TPU:1, one launch (start us, length us, event | category | flops | bytes accessed | tf_op | source)
XLA Modules:
  0.0 195.0 jit_solution(8931033383746886408)
XLA Ops:
  3.5 26.7 %all_to_all.64 = s32[128,1,128]{2,1,0:T(1,128)S(1)} all-to-all(s32[128,1,128]{2,1,0:T(1,128)S(1)} %bitcast.30), channel_id=1, replica_groups=mesh['tower'=2,'x'=4,'y'=4,'z'=8] {'x','y','z'}, dimensions={0} | all-to-all | bytes 131072 | tf_op jit(solution)/shard_map/all_to_all | solution.py:445
  30.2 1.0 copy-done.11
  31.3 2.7 %serve.1 = (bf16[1024,256]{1,0:T(8,128)(2,1)S(1)}, s32[8,1024]{1,0:T(8,128)S(1)}) custom-call(s32[128,128]{1,0:T(8,128)S(1)} %bitcast.29, f32[512,256]{1,0:T(8,128)S(1)} %copy-done.11), custom_call_target="tpu_custom_call" | custom-call | tf_op jit(solution)/shard_map/serve/pallas_call | solution.py:447
  34.0 23.6 %all_to_all.65 = bf16[128,8,256]{2,1,0:T(8,128)(2,1)S(1)} all-to-all(bf16[128,8,256]{2,1,0:T(8,128)(2,1)S(1)} %bitcast.28), channel_id=1, replica_groups=mesh['tower'=2,'x'=4,'y'=4,'z'=8] {'x','y','z'}, dimensions={0} | all-to-all | bytes 1048576 | tf_op jit(solution)/shard_map/all_to_all | solution.py:456
  57.6 1.6 copy-done
  59.2 1.6 copy-done.1
  60.8 1.6 copy-done.2
  62.4 1.6 copy-done.3
  64.0 1.6 copy-done.4
  65.6 0.9 copy-done.12
  66.5 0.9 copy-done.13
  69.4 7.2 %forward.1 = (bf16[64,1024]{1,0:T(8,128)(2,1)S(1)}, f32[256,1024]{1,0:T(8,128)S(1)}, bf16[256,1024]{1,0:T(8,128)(2,1)S(1)}, bf16[64,1024]{1,0:T(8,128)(2,1)S(1)}...) custom-call(bf16[1024,256]{1,0:T(8,128)(2,1)S(1)} %bitcast.23, ...), custom_call_target="tpu_custom_call" | custom-call | tf_op jit(solution)/shard_map/forward/pallas_call | solution.py:470
  76.7 10.8 %all_to_all.66 = bf16[8,8,1024]{2,1,0:T(8,128)(2,1)S(1)} all-to-all(bf16[8,8,1024]{2,1,0:T(8,128)(2,1)S(1)} %bitcast.25), channel_id=1, replica_groups=mesh['tower'=2,'x'=4,'y'=4,'z'=8] {'z'}, dimensions={0} | all-to-all | bytes 262144 | tf_op jit(solution)/shard_map/all_to_all | solution.py:480
  87.9 25.8 %all_to_all.67 = bf16[16,32,2048]{2,1,0:T(8,128)(2,1)S(1)} all-to-all(bf16[16,32,2048]{2,1,0:T(8,128)(2,1)S(1)} %bitcast.20), channel_id=1, replica_groups=mesh['tower'=2,'x'=4,'y'=4,'z'=8] {'x','y'}, dimensions={0} | all-to-all | bytes 4194304 | tf_op jit(solution)/shard_map/all_to_all | solution.py:489
  113.8 6.5 %collective-permute-start = (bf16[512,2048]{1,0:T(8,128)(2,1)S(1)}, bf16[512,2048]{1,0:T(8,128)(2,1)}, u32[]{:S(2)}, u32[]{:S(2)}) collective-permute-start(bf16[512,2048]{1,0:T(8,128)(2,1)S(1)} %bitcast.21), channel_id=1, source_target_pairs={{0,128},{128,0},{1,129},{129,1},{2,130},{130,2},{3,131},{131,3},{4... | collective-permute-start | bytes 6291464 | tf_op jit(solution)/shard_map/ppermute | solution.py:490
  120.3 3.9 %collective-permute-done.swapped_ref = bf16[512,2048]{1,0:T(8,128)(2,1)} collective-permute-done((bf16[512,2048]{1,0:T(8,128)(2,1)S(1)}, bf16[512,2048]{1,0:T(8,128)(2,1)}, u32[]{:S(2)}, u32[]{:S(2)}) %collective-permute-start) | collective-permute-done | bytes 2097184 | tf_op jit(solution)/shard_map/ppermute | solution.py:490
  124.2 1.2 copy-done.8
  125.4 1.0 copy-done.10
  128.8 14.2 %backward.1 = (bf16[1024,256]{1,0:T(8,128)(2,1)S(1)}, f32[8,128]{1,0:T(8,128)S(1)}) custom-call(s32[1]{0:T(128)} %bitcast.base_ref, bf16[512,2048]{1,0:T(8,128)(2,1)S(1)} %bitcast.22, bf16[512,2048]{1,0:T(8,128)(2,1)} %collective-permute-done.swapped_ref, f32[1,1024]{1,0:T(1,128)S(1)} %bitcast.32, f32[1,1024]{1,0:T(1,128)S(1)} %bitcast.34, ...), custom_call_target="tpu_custom_call" | custom-call | tf_op jit(solution)/shard_map/backward/pallas_call | solution.py:494
  143.0 25.2 %all_to_all.68 = bf16[128,8,256]{2,1,0:T(8,128)(2,1)S(1)} all-to-all(bf16[128,8,256]{2,1,0:T(8,128)(2,1)S(1)} %bitcast.27), channel_id=1, replica_groups=mesh['tower'=2,'x'=4,'y'=4,'z'=8] {'x','y','z'}, dimensions={0} | all-to-all | bytes 1048576 | tf_op jit(solution)/shard_map/all_to_all | solution.py:511
  168.7 2.1 %collective-permute-start.2 = (bf16[512,256]{1,0:T(8,128)(2,1)S(1)}, bf16[512,256]{1,0:T(8,128)(2,1)S(1)}, u32[]{:S(2)}, u32[]{:S(2)}) collective-permute-start(bf16[512,256]{1,0:T(8,128)(2,1)S(1)} %get-tuple-element.36), channel_id=1, source_target_pairs={{0,128},{128,0},{1,129},{129,1},{2,130},{130,2},{3,131},{131,3},{4... | collective-permute-start | bytes 786440 | tf_op jit(solution)/shard_map/ppermute | solution.py:521
  170.9 1.1 collective-permute-done.1
  172.7 6.1 %all-to-all-start.5 = ((f32[128,1,384]{2,1,0:T(1,128)}), f32[128,1,384]{2,1,0:T(1,128)S(1)}, u32[]{:S(2)}, u32[]{:S(2)}) async-start(f32[128,1,384]{2,1,0:T(1,128)} %broadcast_in_dim.2), calls=%async_computation.5 | async-start | bytes 393216 | tf_op jit(solution)/shard_map/all_to_all | solution.py:522
  179.7 12.2 %all-to-all-done.5 = f32[128,1,384]{2,1,0:T(1,128)S(1)} async-done(((f32[128,1,384]{2,1,0:T(1,128)}), f32[128,1,384]{2,1,0:T(1,128)S(1)}, u32[]{:S(2)}, u32[]{:S(2)}) %all-to-all-start.5) | async-done | bytes 196640 | tf_op jit(solution)/shard_map/all_to_all | solution.py:522
  (61 shorter events, 11.2 us)
Async XLA Ops:
  0.6 57.0 %copy-start.6 = (bf16[256,1024]{1,0:T(8,128)(2,1)S(1)}, bf16[256,1024]{1,0:T(8,128)(2,1)}, u32[]{:S(2)}) copy-start(bf16[256,1024]{1,0:T(8,128)(2,1)} %refs_14_.1) | copy-start | bytes 1572868
  0.6 57.0 %copy-start.5 = (bf16[256,1024]{1,0:T(8,128)(2,1)S(1)}, bf16[256,1024]{1,0:T(8,128)(2,1)}, u32[]{:S(2)}) copy-start(bf16[256,1024]{1,0:T(8,128)(2,1)} %refs_9_.3) | copy-start | bytes 1572868
  30.2 1.0 copy-start.11
  34.0 23.6 %copy-start.18 = (s32[8,1024]{1,0:T(8,128)}, s32[8,1024]{1,0:T(8,128)S(1)}, u32[]{:S(2)}) copy-start(s32[8,1024]{1,0:T(8,128)S(1)} %get-tuple-element.33.row_ref) | copy-start | bytes 98308
  57.6 1.6 copy-start
  59.2 1.6 copy-start.1
  60.8 1.6 copy-start.2
  62.4 1.6 copy-start.3
  64.0 1.6 copy-start.4
  65.6 0.9 copy-start.12
  76.7 37.1 %copy-start.7 = (f32[256,1024]{1,0:T(8,128)}, f32[256,1024]{1,0:T(8,128)S(1)}, u32[]{:S(2)}) copy-start(f32[256,1024]{1,0:T(8,128)S(1)} %get-tuple-element.25.refs_2_) | copy-start | bytes 3145732
  76.7 37.1 %copy-start.9 = (bf16[256,1024]{1,0:T(8,128)(2,1)}, bf16[256,1024]{1,0:T(8,128)(2,1)S(1)}, u32[]{:S(2)}) copy-start(bf16[256,1024]{1,0:T(8,128)(2,1)S(1)} %get-tuple-element.26.refs_3_) | copy-start | bytes 1572868
  76.7 37.0 %copy-start.14 = (f32[16,1024]{1,0:T(8,128)}, f32[16,1024]{1,0:T(8,128)S(1)}, u32[]{:S(2)}) copy-start(f32[16,1024]{1,0:T(8,128)S(1)} %get-tuple-element.31.refs_8_) | copy-start | bytes 196612
  76.7 37.0 %copy-start.16 = (f32[64,64]{1,0:T(8,128)}, f32[64,64]{1,0:T(8,128)S(1)}, u32[]{:S(2)}) copy-start(f32[64,64]{1,0:T(8,128)S(1)} %get-tuple-element.28.refs_5_) | copy-start | bytes 49156
  87.9 36.3 %copy-start.21 = (f32[1024]{0:T(1024)S(1)}, f32[1024]{0:T(1024)}, u32[]{:S(2)}) copy-start(f32[1024]{0:T(1024)} %param.21) | copy-start | bytes 12292
  87.9 36.3 %copy-start.23 = (f32[1024]{0:T(1024)S(1)}, f32[1024]{0:T(1024)}, u32[]{:S(2)}) copy-start(f32[1024]{0:T(1024)} %param.26) | copy-start | bytes 12292
  87.9 36.3 %copy-start.25 = (f32[1024]{0:T(1024)S(1)}, f32[1024]{0:T(1024)}, u32[]{:S(2)}) copy-start(f32[1024]{0:T(1024)} %param.29) | copy-start | bytes 12292
  113.8 10.4 %collective-permute-start = (bf16[512,2048]{1,0:T(8,128)(2,1)S(1)}, bf16[512,2048]{1,0:T(8,128)(2,1)}, u32[]{:S(2)}, u32[]{:S(2)}) collective-permute-start(bf16[512,2048]{1,0:T(8,128)(2,1)S(1)} %bitcast.21), channel_id=1, source_target_pairs={{0,128},{128,0},{1,129},{129,1},{2,130},{130,2},{3,131},{131,3},{4... | collective-permute-start | bytes 6291464 | tf_op jit(solution)/shard_map/ppermute | solution.py:490
  124.2 1.2 copy-start.8
  125.4 1.0 copy-start.10
  128.8 39.4 %copy-start.19 = (s32[8,1024]{1,0:T(8,128)S(1)}, s32[8,1024]{1,0:T(8,128)}, u32[]{:S(2)}) copy-start(s32[8,1024]{1,0:T(8,128)} %copy-done.18) | copy-start | bytes 98308
  168.7 10.2 %collective-permute-start.2 = (bf16[512,256]{1,0:T(8,128)(2,1)S(1)}, bf16[512,256]{1,0:T(8,128)(2,1)S(1)}, u32[]{:S(2)}, u32[]{:S(2)}) collective-permute-start(bf16[512,256]{1,0:T(8,128)(2,1)S(1)} %get-tuple-element.36), channel_id=1, source_target_pairs={{0,128},{128,0},{1,129},{129,1},{2,130},{130,2},{3,131},{131,3},{4... | collective-permute-start | bytes 786440 | tf_op jit(solution)/shard_map/ppermute | solution.py:521
  170.8 1.2 collective-permute-start.1
  172.7 19.2 %all-to-all-start.5 = ((f32[128,1,384]{2,1,0:T(1,128)}), f32[128,1,384]{2,1,0:T(1,128)S(1)}, u32[]{:S(2)}, u32[]{:S(2)}) async-start(f32[128,1,384]{2,1,0:T(1,128)} %broadcast_in_dim.2), calls=%async_computation.5 | async-start | bytes 393216 | tf_op jit(solution)/shard_map/all_to_all | solution.py:522
  (10 other events, 7.3 us)

commit v3 on v2

--- a/solution.py
+++ b/solution.py
@@ -14,6 +14,7 @@
 SLOTS = 8
 HOT_SLOT = 5
 SHARD = ("x", "y", "z")
+FULL = 62
 PAD = 16
 BF = jnp.bfloat16
 F32 = jnp.float32
@@ -56,9 +57,28 @@
 
 
 def index_kernel(
-    rare_count, owners, history_ref, items_ref, request_ref, row_hbm, column_hbm, row, column, sems
+    owners,
+    history_hbm,
+    items_hbm,
+    table_hbm,
+    request_ref,
+    known_ref,
+    row_hbm,
+    column_hbm,
+    history_ref,
+    items_ref,
+    table,
+    row,
+    column,
+    sems,
 ):
+    loads = copies_of(
+        [(history_hbm, history_ref), (items_hbm, items_ref), (table_hbm, table)], sems
+    )
+    loads[0].wait()
+    loads[1].wait()
     hot_count = owners
+    rare_count = table.shape[0]
     users = history_ref.shape[0]
     span = row.shape[1]
     parts = [history_ref[u : u + 1, :] for u in range(users)] + [items_ref[...]]
@@ -77,7 +97,12 @@
     )
     row[...] = jnp.broadcast_to(places, row.shape)
     column[...] = jnp.transpose(jnp.broadcast_to(places.astype(F32), (128, span))).astype(jnp.int32)
-    copies = copies_of([(row, row_hbm), (column, column_hbm)], sems)
+    copies = [
+        pltpu.make_async_copy(row, row_hbm, sems.at[3]),
+        pltpu.make_async_copy(column, column_hbm, sems.at[4]),
+    ]
+    for copy in copies:
+        copy.start()
     order = jnp.where(hits, earlier, -1.0)
     lanes = iota(request_ref.shape, 1)
     request = jnp.zeros(request_ref.shape, F32)
@@ -85,13 +110,13 @@
         wanted = jnp.sum(jnp.where(order == float(slot), value, 0.0), axis=1, keepdims=True)
         request = jnp.where(lanes == slot, wanted, request)
     request_ref[...] = request.astype(jnp.int32)
+    loads[2].wait()
+    known_ref[...] = table[...].astype(BF)
     for copy in copies:
         copy.wait()
 
 
-def serve_kernel(asked_ref, table_hbm, served_hbm, row_hbm, table, served, row, sems):
-    load = pltpu.make_async_copy(table_hbm, table, sems.at[0])
-    load.start()
+def serve_kernel(asked_ref, known_ref, served, row_hbm, row, sem):
     slots = served.shape[0]
     sources = asked_ref.shape[0]
     asked = asked_ref[...]
@@ -103,26 +128,16 @@
     index = jnp.sum(jnp.where(mine, wide, 0.0), axis=1, keepdims=True) - 1.0
     index = jnp.broadcast_to(index, wide.shape)
     row[...] = jnp.transpose(index)[0:8].astype(jnp.int32)
-    keep = pltpu.make_async_copy(row, row_hbm, sems.at[1])
+    keep = pltpu.make_async_copy(row, row_hbm, sem)
     keep.start()
     index = index.astype(jnp.int32)
     lanes = iota(index.shape, 1)
-    rows = table.shape[0]
+    rows = known_ref.shape[0]
     picks = jnp.concatenate(
         [one_hot(index == lanes + 128 * j) for j in range(rows // 128)], axis=1
     )
-    load.wait()
-    known = table[...].astype(BF)
-    chunk = slots // 4
-    copies = []
-    for c in range(4):
-        at = pl.ds(c * chunk, chunk)
-        served[at, :] = dot(picks[c * chunk : (c + 1) * chunk], known).astype(BF)
-        copies.append(pltpu.make_async_copy(served.at[at], served_hbm.at[at], sems.at[2 + c]))
-        copies[-1].start()
+    served[...] = dot(picks, known_ref[...]).astype(BF)
     keep.wait()
-    for copy in copies:
-        copy.wait()
 
 
 def head_mask(heads, width):
@@ -148,16 +163,13 @@
 
 def forward_kernel(
     users,
-    fetched_ref,
-    norm_gain_ref,
-    out_gain_ref,
-    item_gain_ref,
     *refs,
 ):
-    sources, refs = refs[:10], refs[10:]
+    sources, refs = refs[:14], refs[14:]
     vectors_ref, kept_hbm, refs = refs[0], refs[1:8], refs[8:]
-    targets, kept, (in_sems, out_sems) = refs[:10], refs[10:17], refs[17:]
-    hot, column_of, pos_of, in_proj, w_query, w_key, w_value, w_out, item_w1, item_w2 = targets
+    targets, kept, (in_sems, out_sems) = refs[:14], refs[14:21], refs[21:]
+    column_of, fetched_ref, hot, pos_of, norm_gain_ref, out_gain_ref, item_gain_ref = targets[:7]
+    in_proj, w_query, w_key, w_value, w_out, item_w1, item_w2 = targets[7:]
     hidden_ref, normed_ref, qk_ref, weights_ref, mixed_ref, inner_ref, outer_ref = kept
     copies = copies_of(zip(sources, targets), in_sems)
     saves = [
@@ -168,16 +180,17 @@
     span = users * hist
     slots = fetched_ref.shape[0]
     copies[0].wait()
-    copies[1].wait()
     column = column_of[0 : span + PAD, :]
     lanes = iota(column.shape, 1)
     picks = jnp.concatenate(
         [one_hot(column == lanes + 128 * j) for j in range(slots // 128)], axis=1
     )
     hot_picks = one_hot(column == lanes * SLOTS + HOT_SLOT)
+    copies[1].wait()
+    copies[2].wait()
     rows = (dot(picks, fetched_ref[...]) + dot(hot_picks, hot[...].astype(BF))).astype(BF)
-    copies[2].wait()
-    copies[3].wait()
+    for copy in copies[3:8]:
+        copy.wait()
     pos = pos_of[...].astype(F32)
     hidden = dot(rows[0:span], in_proj[...]) + jnp.concatenate([pos] * users, axis=0)
     hidden_ref[...] = hidden
@@ -192,9 +205,9 @@
         axis=0,
     ).astype(BF)
     mask = head_mask(heads, width)
-    copies[4].wait()
+    copies[8].wait()
     query = dot(last, w_query[...]).astype(BF).astype(F32)
-    copies[5].wait()
+    copies[9].wait()
     qk = dot_nt(spread_heads(query, mask, users), w_key[...]).astype(BF)
     qk_ref[...] = qk
     saves[2].start()
@@ -208,9 +221,9 @@
         mixes.append(dot(weights.astype(BF), own))
     saves[3].start()
     mixes = jnp.concatenate(mixes, axis=0).astype(BF)
-    copies[6].wait()
+    copies[10].wait()
     attended = join_heads(dot(mixes, w_value[...]), mask, users).astype(BF)
-    copies[7].wait()
+    copies[11].wait()
     hidden_last = jnp.concatenate(
         [hidden_ref[(u + 1) * hist - 1 : (u + 1) * hist, :] for u in range(users)]
         + [jnp.zeros((PAD - users, width), F32)],
@@ -221,11 +234,11 @@
     saves[4].start()
     scale = lax.rsqrt(jnp.mean(mixed * mixed, axis=-1, keepdims=True) + EPS)
     user_vec = mixed * scale * out_gain_ref[...]
-    copies[8].wait()
+    copies[12].wait()
     inner = dot(rows[span : span + PAD], item_w1[...])
     inner_ref[...] = inner
     saves[5].start()
-    copies[9].wait()
+    copies[13].wait()
     outer = dot((inner * jax.nn.sigmoid(inner)).astype(BF), item_w2[...])
     outer_ref[...] = outer
     saves[6].start()
@@ -312,17 +325,15 @@
     base_ref,
     gathered_ref,
     swapped_ref,
-    norm_gain_ref,
-    out_gain_ref,
-    item_gain_ref,
     *refs,
 ):
-    sources, refs = refs[:16], refs[16:]
+    sources, refs = refs[:19], refs[19:]
     (outgoing_hbm, loss_ref), refs = refs[:2], refs[2:]
-    targets, (outgoing, logits, d_normed, in_sems, out_sems) = refs[:16], refs[16:]
+    targets, (outgoing, logits, d_normed, in_sems, out_sems) = refs[:19], refs[19:]
     vectors_ref, row_ref = targets[:2]
-    hidden_ref, normed_ref, qk_ref, weights_ref, mixed_ref, inner_ref, outer_ref = targets[2:9]
-    in_proj, w_query, w_key, w_value, w_out, item_w1, item_w2 = targets[9:]
+    norm_gain_ref, out_gain_ref, item_gain_ref = targets[2:5]
+    hidden_ref, normed_ref, qk_ref, weights_ref, mixed_ref, inner_ref, outer_ref = targets[5:12]
+    in_proj, w_query, w_key, w_value, w_out, item_w1, item_w2 = targets[12:]
     copies = copies_of(zip(sources, targets), in_sems)
     copies[0].wait()
     vectors = vectors_ref[0:PAD, :].astype(F32)
@@ -433,26 +444,27 @@
     exchange = functools.partial(lax.all_to_all, split_axis=0, concat_axis=0, tiled=True)
 
     places = (shape((8, wide), jnp.int32), shape((wide, 128), jnp.int32))
-    request, row, column = pl.pallas_call(
-        functools.partial(index_kernel, rare_count, owners),
-        out_shape=(shape((owners, 128), jnp.int32),) + places,
-        in_specs=[VMEM, VMEM],
-        out_specs=(VMEM, HBM, HBM),
-        scratch_shapes=like(places) + [sems(2)],
-        compiler_params=params(24),
+    loads = (history, item_ids.reshape(1, users), rare_table)
+    request, known, row, column = pl.pallas_call(
+        functools.partial(index_kernel, owners),
+        out_shape=(shape((owners, 128), jnp.int32), shape((rare_count, emb), BF)) + places,
+        in_specs=[HBM] * 3,
+        out_specs=(VMEM, VMEM, HBM, HBM),
+        scratch_shapes=like(loads + places) + [sems(5)],
+        compiler_params=params(FULL - 2),
         name="index",
-    )(history, item_ids.reshape(1, users))
+    )(*loads)
     asked = exchange(request, SHARD)
     served_shapes = (shape((slots, emb), BF), shape((8, slots), jnp.int32))
     served, asked_row = pl.pallas_call(
         serve_kernel,
         out_shape=served_shapes,
-        in_specs=[VMEM, HBM],
-        out_specs=(HBM, HBM),
-        scratch_shapes=like((rare_table,) + served_shapes) + [sems(6)],
+        in_specs=[VMEM, VMEM],
+        out_specs=(VMEM, HBM),
+        scratch_shapes=like(served_shapes[1:]) + [pltpu.SemaphoreType.DMA],
         compiler_params=params(24),
         name="serve",
-    )(asked, rare_table)
+    )(asked, known)
     fetched = exchange(served, SHARD)
 
     weights = (in_proj, w_query, w_key, w_value, w_out, item_w1, item_w2)
@@ -466,16 +478,16 @@
         shape((PAD, width), F32),
         shape((PAD, width), F32),
     )
-    loads = (hot_table, column, pos_embed) + weights
+    loads = (column, fetched, hot_table, pos_embed) + gains + weights
     vectors, *kept = pl.pallas_call(
         functools.partial(forward_kernel, users),
         out_shape=(shape((near * 2 * users, width), BF),) + kept_shapes,
-        in_specs=[VMEM] * 4 + [HBM] * len(loads),
+        in_specs=[HBM] * len(loads),
         out_specs=(VMEM,) + (HBM,) * len(kept_shapes),
         scratch_shapes=like(loads + kept_shapes) + [sems(len(loads)), sems(len(kept_shapes))],
-        compiler_params=params(40),
+        compiler_params=params(FULL),
         name="forward",
-    )(fetched, *gains, *loads)
+    )(*loads)
 
     near_vectors = exchange(vectors, "z")
     spread = pl.pallas_call(
@@ -490,11 +502,11 @@
     swapped = lax.ppermute(gathered, "tower", swap)
     base = (lax.axis_index(SHARD) * users).astype(jnp.int32).reshape(1)
 
-    loads = (vectors, row) + tuple(kept) + weights
+    loads = (vectors, row) + gains + tuple(kept) + weights
     outgoing, loss = pl.pallas_call(
         functools.partial(backward_kernel, users, scale),
         out_shape=(shape((slots, emb), BF), shape((8, 128), F32)),
-        in_specs=[SMEM] + [VMEM] * 5 + [HBM] * len(loads),
+        in_specs=[SMEM, VMEM, VMEM] + [HBM] * len(loads),
         out_specs=(HBM, VMEM),
         scratch_shapes=like(loads)
         + [
@@ -504,9 +516,9 @@
             sems(len(loads)),
             sems(4),
         ],
-        compiler_params=params(48),
+        compiler_params=params(FULL - 4),
         name="backward",
-    )(base, gathered, swapped, *gains, *loads)
+    )(base, gathered, swapped, *loads)
 
     returned = exchange(outgoing, SHARD)
     part, mine = pl.pallas_call(

time: 196 us -> 182 us (0.929)
  local copies, waits for them, and re-layouts: 20.9 us -> 3.08 us
  blocking collectives: 112 us -> 115 us
    unnamed x61 -> x5, local copies, waits for them, and re-layouts: 19.5 us -> 1.65 us
where the time goes in v3:
time: 182 us; the launch traced here: 181 us
  blocking collectives  115 us (63%)
  Pallas kernels  27.1 us (15%)
  waiting for transfers between devices  17.4 us (10%)
  starting transfers between devices  14.3 us (8%)
  local copies, waits for them, and re-layouts  3.08 us (2%)
  between operations  2.48 us (1%)
    all_to_all x1, blocking collectives, shards(): asked = exchange(request, SHARD)  26.8 us
    all_to_all x1, blocking collectives, shards(): gathered = exchange(spread, ('x', 'y'))  26.7 us
    all_to_all x1, blocking collectives, shards(): returned = exchange(outgoing, SHARD)  26.1 us
    all_to_all x1, blocking collectives, shards(): fetched = exchange(served, SHARD)  24.3 us
    pallas_call x1, Pallas kernels, shards(): pl.pallas_call(functools.partial(backward_kernel, users, scale), out_shap...  14.9 us
    all_to_all x1, waiting for transfers between devices, shards(): sums = exchange(jnp.broadcast_to(mine, (owners, emb + 128)), SHARD)  12.2 us
    all_to_all x1, blocking collectives, shards(): near_vectors = exchange(vectors, 'z')  11.2 us
    pallas_call x1, Pallas kernels, shards(): pl.pallas_call(functools.partial(forward_kernel, users), out_shape=(shape...  7.76 us
  transfers between devices with their start and end apart: 4, of which 3 were waited for; matrix products, arithmetic and copies ran while one was open for 1% of the time, Pallas kernels for 0%

profile of v3, /device:TPU:1, one launch (start us, length us, event | category | flops | bytes accessed | tf_op | source)
XLA Modules:
  0.0 181.0 jit_solution(1471838568845303243)
XLA Ops:
  0.6 2.6 %index.1 = (s32[128,128]{1,0:T(8,128)}, bf16[512,256]{1,0:T(8,128)(2,1)}, s32[8,384]{1,0:T(8,128)}, s32[384,128]{1,0:T(8,128)}) custom-call(s32[4,64]{1,0:T(4,128)} %history_hbm.1, s32[1,4]{1,0:T(1,128)} %bitcast.37, f32[512,256]{1,0:T(8,128)} %table_hbm.1), custom_call_target="tpu_custom_call" | custom-call | tf_op jit(solution)/shard_map/index/pallas_call | solution.py:448
  3.2 26.8 %all_to_all.64 = s32[128,1,128]{2,1,0:T(1,128)S(1)} all-to-all(s32[128,1,128]{2,1,0:T(1,128)} %bitcast.30), channel_id=1, replica_groups=mesh['tower'=2,'x'=4,'y'=4,'z'=8] {'x','y','z'}, dimensions={0} | all-to-all | bytes 131072 | tf_op jit(solution)/shard_map/all_to_all | solution.py:457
  30.1 0.9 copy-done
  31.0 1.0 serve.1
  32.1 24.3 %all_to_all.65 = bf16[128,8,256]{2,1,0:T(8,128)(2,1)} all-to-all(bf16[128,8,256]{2,1,0:T(8,128)(2,1)S(1)} %bitcast.23), channel_id=1, replica_groups=mesh['tower'=2,'x'=4,'y'=4,'z'=8] {'x','y','z'}, dimensions={0} | all-to-all | bytes 1048576 | tf_op jit(solution)/shard_map/all_to_all | solution.py:468
  56.4 7.8 %forward.1 = (bf16[64,1024]{1,0:T(8,128)(2,1)}, f32[256,1024]{1,0:T(8,128)}, bf16[256,1024]{1,0:T(8,128)(2,1)}, bf16[64,1024]{1,0:T(8,128)(2,1)}, f32[64,64]{1,0...) custom-call(s32[384,128]{1,0:T(8,128)} %get-tuple-element.21.refs_0_, ...), custom_call_target="tpu_custom_call" | custom-call | tf_op jit(solution)/shard_map/forward/pallas_call | solution.py:482
  64.2 11.2 %all_to_all.66 = bf16[8,8,1024]{2,1,0:T(8,128)(2,1)S(1)} all-to-all(bf16[8,8,1024]{2,1,0:T(8,128)(2,1)} %bitcast.28), channel_id=1, replica_groups=mesh['tower'=2,'x'=4,'y'=4,'z'=8] {'z'}, dimensions={0} | all-to-all | bytes 262144 | tf_op jit(solution)/shard_map/all_to_all | solution.py:492
  75.4 0.3 arrange.1
  75.7 26.7 %all_to_all.67 = bf16[16,32,2048]{2,1,0:T(8,128)(2,1)} all-to-all(bf16[16,32,2048]{2,1,0:T(8,128)(2,1)S(1)} %bitcast.20), channel_id=1, replica_groups=mesh['tower'=2,'x'=4,'y'=4,'z'=8] {'x','y'}, dimensions={0} | all-to-all | bytes 4194304 | tf_op jit(solution)/shard_map/all_to_all | solution.py:501
  102.4 6.0 %collective-permute-start = (bf16[512,2048]{1,0:T(8,128)(2,1)}, bf16[512,2048]{1,0:T(8,128)(2,1)}, u32[]{:S(2)}, u32[]{:S(2)}) collective-permute-start(bf16[512,2048]{1,0:T(8,128)(2,1)} %bitcast.13.gathered_ref), channel_id=1, source_target_pairs={{0,128},{128,0},{1,129},{129,1},{2,130},{130,2},{3,131},{131,3},{4... | collective-permute-start | bytes 6291464 | tf_op jit(solution)/shard_map/ppermute | solution.py:502
  108.3 4.1 %collective-permute-done.swapped_ref = bf16[512,2048]{1,0:T(8,128)(2,1)} collective-permute-done((bf16[512,2048]{1,0:T(8,128)(2,1)}, bf16[512,2048]{1,0:T(8,128)(2,1)}, u32[]{:S(2)}, u32[]{:S(2)}) %collective-permute-start) | collective-permute-done | bytes 2097184 | tf_op jit(solution)/shard_map/ppermute | solution.py:502
  112.5 14.9 %backward.1 = (bf16[1024,256]{1,0:T(8,128)(2,1)}, f32[8,128]{1,0:T(8,128)}) custom-call(s32[1]{0:T(128)} %bitcast.base_ref, bf16[512,2048]{1,0:T(8,128)(2,1)} %bitcast.13.gathered_ref, bf16[512,2048]{1,0:T(8,128)(2,1)} %collective-permute-done.swapped_ref, bf16[64,1024]{1,0:T(8,128)(2,1)} %get-tuple-element.25.refs_0_, s32[8,384]{1,0:T(8,128)} %get-tuple-element.26.refs_1_, ...), custom_call_target="tpu_custom_call" | custom-call | tf_op jit(solution)/shard_map/backward/pallas_call | solution.py:506
  127.4 26.1 %all_to_all.68 = bf16[128,8,256]{2,1,0:T(8,128)(2,1)S(1)} all-to-all(bf16[128,8,256]{2,1,0:T(8,128)(2,1)} %bitcast.29), channel_id=1, replica_groups=mesh['tower'=2,'x'=4,'y'=4,'z'=8] {'x','y','z'}, dimensions={0} | all-to-all | bytes 1048576 | tf_op jit(solution)/shard_map/all_to_all | solution.py:523
  153.4 0.7 copy-done.1
  154.1 0.5 scatter.1
  154.6 2.1 %collective-permute-start.2 = (bf16[512,256]{1,0:T(8,128)(2,1)S(1)}, bf16[512,256]{1,0:T(8,128)(2,1)S(1)}, u32[]{:S(2)}, u32[]{:S(2)}) collective-permute-start(bf16[512,256]{1,0:T(8,128)(2,1)S(1)} %get-tuple-element.38), channel_id=1, source_target_pairs={{0,128},{128,0},{1,129},{129,1},{2,130},{130,2},{3,131},{131,3},{4... | collective-permute-start | bytes 786440 | tf_op jit(solution)/shard_map/ppermute | solution.py:533
  156.7 0.1 collective-permute-start.1
  156.8 1.1 collective-permute-done.1
  157.9 0.8 broadcast_in_dim.2
  158.7 6.2 %all-to-all-start.5 = ((f32[128,1,384]{2,1,0:T(1,128)}), f32[128,1,384]{2,1,0:T(1,128)S(1)}, u32[]{:S(2)}, u32[]{:S(2)}) async-start(f32[128,1,384]{2,1,0:T(1,128)} %broadcast_in_dim.2), calls=%async_computation.5 | async-start | bytes 393216 | tf_op jit(solution)/shard_map/all_to_all | solution.py:534
  164.9 0.8 convert_add_fusion
  165.7 12.2 %all-to-all-done.5 = f32[128,1,384]{2,1,0:T(1,128)S(1)} async-done(((f32[128,1,384]{2,1,0:T(1,128)}), f32[128,1,384]{2,1,0:T(1,128)S(1)}, u32[]{:S(2)}, u32[]{:S(2)}) %all-to-all-start.5) | async-done | bytes 196640 | tf_op jit(solution)/shard_map/all_to_all | solution.py:534
  177.9 0.6 slice_reduce_fusion
  178.5 0.7 slice.8
  (5 shorter events, 0.0 us)
Async XLA Ops:
  30.1 1.0 copy-start
  102.4 10.1 %collective-permute-start = (bf16[512,2048]{1,0:T(8,128)(2,1)}, bf16[512,2048]{1,0:T(8,128)(2,1)}, u32[]{:S(2)}, u32[]{:S(2)}) collective-permute-start(bf16[512,2048]{1,0:T(8,128)(2,1)} %bitcast.13.gathered_ref), channel_id=1, source_target_pairs={{0,128},{128,0},{1,129},{129,1},{2,130},{130,2},{3,131},{131,3},{4... | collective-permute-start | bytes 6291464 | tf_op jit(solution)/shard_map/ppermute | solution.py:502
  153.4 0.7 copy-start.1
  154.6 10.2 %collective-permute-start.2 = (bf16[512,256]{1,0:T(8,128)(2,1)S(1)}, bf16[512,256]{1,0:T(8,128)(2,1)S(1)}, u32[]{:S(2)}, u32[]{:S(2)}) collective-permute-start(bf16[512,256]{1,0:T(8,128)(2,1)S(1)} %get-tuple-element.38), channel_id=1, source_target_pairs={{0,128},{128,0},{1,129},{129,1},{2,130},{130,2},{3,131},{131,3},{4... | collective-permute-start | bytes 786440 | tf_op jit(solution)/shard_map/ppermute | solution.py:533
  156.7 1.2 collective-permute-start.1
  158.7 19.3 %all-to-all-start.5 = ((f32[128,1,384]{2,1,0:T(1,128)}), f32[128,1,384]{2,1,0:T(1,128)S(1)}, u32[]{:S(2)}, u32[]{:S(2)}) async-start(f32[128,1,384]{2,1,0:T(1,128)} %broadcast_in_dim.2), calls=%async_computation.5 | async-start | bytes 393216 | tf_op jit(solution)/shard_map/all_to_all | solution.py:534

commit v4 on v3

--- a/solution.py
+++ b/solution.py
@@ -14,7 +14,6 @@
 SLOTS = 8
 HOT_SLOT = 5
 SHARD = ("x", "y", "z")
-FULL = 62
 PAD = 16
 BF = jnp.bfloat16
 F32 = jnp.float32
@@ -63,13 +62,11 @@
     table_hbm,
     request_ref,
     known_ref,
-    row_hbm,
-    column_hbm,
+    row,
+    column,
     history_ref,
     items_ref,
     table,
-    row,
-    column,
     sems,
 ):
     loads = copies_of(
@@ -97,12 +94,6 @@
     )
     row[...] = jnp.broadcast_to(places, row.shape)
     column[...] = jnp.transpose(jnp.broadcast_to(places.astype(F32), (128, span))).astype(jnp.int32)
-    copies = [
-        pltpu.make_async_copy(row, row_hbm, sems.at[3]),
-        pltpu.make_async_copy(column, column_hbm, sems.at[4]),
-    ]
-    for copy in copies:
-        copy.start()
     order = jnp.where(hits, earlier, -1.0)
     lanes = iota(request_ref.shape, 1)
     request = jnp.zeros(request_ref.shape, F32)
@@ -112,11 +103,9 @@
     request_ref[...] = request.astype(jnp.int32)
     loads[2].wait()
     known_ref[...] = table[...].astype(BF)
-    for copy in copies:
-        copy.wait()
-
-
-def serve_kernel(asked_ref, known_ref, served, row_hbm, row, sem):
+
+
+def serve_kernel(asked_ref, known_ref, served, row):
     slots = served.shape[0]
     sources = asked_ref.shape[0]
     asked = asked_ref[...]
@@ -128,8 +117,6 @@
     index = jnp.sum(jnp.where(mine, wide, 0.0), axis=1, keepdims=True) - 1.0
     index = jnp.broadcast_to(index, wide.shape)
     row[...] = jnp.transpose(index)[0:8].astype(jnp.int32)
-    keep = pltpu.make_async_copy(row, row_hbm, sem)
-    keep.start()
     index = index.astype(jnp.int32)
     lanes = iota(index.shape, 1)
     rows = known_ref.shape[0]
@@ -137,7 +124,12 @@
         [one_hot(index == lanes + 128 * j) for j in range(rows // 128)], axis=1
     )
     served[...] = dot(picks, known_ref[...]).astype(BF)
-    keep.wait()
+
+
+def prefetch_kernel(count, after_ref, *refs):
+    copies = copies_of(zip(refs[:count], refs[count : 2 * count]), refs[2 * count])
+    for copy in copies:
+        copy.wait()
 
 
 def head_mask(heads, width):
@@ -161,56 +153,36 @@
     return jnp.concatenate(parts + [jnp.zeros((PAD - users, full.shape[1]), F32)], axis=0)
 
 
-def forward_kernel(
-    users,
-    *refs,
-):
-    sources, refs = refs[:14], refs[14:]
-    vectors_ref, kept_hbm, refs = refs[0], refs[1:8], refs[8:]
-    targets, kept, (in_sems, out_sems) = refs[:14], refs[14:21], refs[21:]
-    column_of, fetched_ref, hot, pos_of, norm_gain_ref, out_gain_ref, item_gain_ref = targets[:7]
-    in_proj, w_query, w_key, w_value, w_out, item_w1, item_w2 = targets[7:]
-    hidden_ref, normed_ref, qk_ref, weights_ref, mixed_ref, inner_ref, outer_ref = kept
-    copies = copies_of(zip(sources, targets), in_sems)
-    saves = [
-        pltpu.make_async_copy(a, b, out_sems.at[i]) for i, (a, b) in enumerate(zip(kept, kept_hbm))
-    ]
+def forward_kernel(users, *refs):
+    column_of, fetched_ref, hot, pos_of, norm_gain_ref, out_gain_ref, item_gain_ref = refs[:7]
+    in_proj, w_query, w_key, w_value, w_out, item_w1, item_w2 = refs[7:14]
+    vectors_ref, hidden_ref, normed_ref, qk_ref, weights_ref, mixed_ref, inner_ref, outer_ref = refs[14:]
     hist, width = pos_of.shape
     heads = width // HEAD_DIM
     span = users * hist
     slots = fetched_ref.shape[0]
-    copies[0].wait()
     column = column_of[0 : span + PAD, :]
     lanes = iota(column.shape, 1)
     picks = jnp.concatenate(
         [one_hot(column == lanes + 128 * j) for j in range(slots // 128)], axis=1
     )
     hot_picks = one_hot(column == lanes * SLOTS + HOT_SLOT)
-    copies[1].wait()
-    copies[2].wait()
     rows = (dot(picks, fetched_ref[...]) + dot(hot_picks, hot[...].astype(BF))).astype(BF)
-    for copy in copies[3:8]:
-        copy.wait()
     pos = pos_of[...].astype(F32)
     hidden = dot(rows[0:span], in_proj[...]) + jnp.concatenate([pos] * users, axis=0)
     hidden_ref[...] = hidden
-    saves[0].start()
     scale = lax.rsqrt(jnp.mean(hidden * hidden, axis=-1, keepdims=True) + EPS)
     normed = (hidden * scale * norm_gain_ref[...]).astype(BF)
     normed_ref[...] = normed
-    saves[1].start()
     last = jnp.concatenate(
         [normed[(u + 1) * hist - PAD : (u + 1) * hist].astype(F32)[PAD - 1 :] for u in range(users)]
         + [jnp.zeros((PAD - users, width), F32)],
         axis=0,
     ).astype(BF)
     mask = head_mask(heads, width)
-    copies[8].wait()
     query = dot(last, w_query[...]).astype(BF).astype(F32)
-    copies[9].wait()
     qk = dot_nt(spread_heads(query, mask, users), w_key[...]).astype(BF)
     qk_ref[...] = qk
-    saves[2].start()
     mixes = []
     for u in range(users):
         own = normed[u * hist : (u + 1) * hist]
@@ -219,11 +191,8 @@
         weights = raised / jnp.sum(raised, axis=1, keepdims=True)
         weights_ref[u * heads : (u + 1) * heads, :] = weights
         mixes.append(dot(weights.astype(BF), own))
-    saves[3].start()
     mixes = jnp.concatenate(mixes, axis=0).astype(BF)
-    copies[10].wait()
     attended = join_heads(dot(mixes, w_value[...]), mask, users).astype(BF)
-    copies[11].wait()
     hidden_last = jnp.concatenate(
         [hidden_ref[(u + 1) * hist - 1 : (u + 1) * hist, :] for u in range(users)]
         + [jnp.zeros((PAD - users, width), F32)],
@@ -231,24 +200,17 @@
     )
     mixed = hidden_last + dot(attended, w_out[...])
     mixed_ref[...] = mixed
-    saves[4].start()
     scale = lax.rsqrt(jnp.mean(mixed * mixed, axis=-1, keepdims=True) + EPS)
     user_vec = mixed * scale * out_gain_ref[...]
-    copies[12].wait()
     inner = dot(rows[span : span + PAD], item_w1[...])
     inner_ref[...] = inner
-    saves[5].start()
-    copies[13].wait()
     outer = dot((inner * jax.nn.sigmoid(inner)).astype(BF), item_w2[...])
     outer_ref[...] = outer
-    saves[6].start()
     scale = lax.rsqrt(jnp.mean(outer * outer, axis=-1, keepdims=True) + EPS)
     item_vec = outer * scale * item_gain_ref[...]
     both = jnp.concatenate([user_vec[0:users], item_vec[0:users]], axis=0)
     peers = vectors_ref.shape[0] // (2 * users)
     vectors_ref[...] = jnp.concatenate([both] * peers, axis=0).astype(BF)
-    for save in saves:
-        save.wait()
 
 
 def arrange_kernel(users, vectors_ref, spread_ref):
@@ -325,24 +287,19 @@
     base_ref,
     gathered_ref,
     swapped_ref,
+    vectors_ref,
+    row_ref,
     *refs,
 ):
-    sources, refs = refs[:19], refs[19:]
-    (outgoing_hbm, loss_ref), refs = refs[:2], refs[2:]
-    targets, (outgoing, logits, d_normed, in_sems, out_sems) = refs[:19], refs[19:]
-    vectors_ref, row_ref = targets[:2]
-    norm_gain_ref, out_gain_ref, item_gain_ref = targets[2:5]
-    hidden_ref, normed_ref, qk_ref, weights_ref, mixed_ref, inner_ref, outer_ref = targets[5:12]
-    in_proj, w_query, w_key, w_value, w_out, item_w1, item_w2 = targets[12:]
-    copies = copies_of(zip(sources, targets), in_sems)
-    copies[0].wait()
+    norm_gain_ref, out_gain_ref, item_gain_ref = refs[:3]
+    hidden_ref, normed_ref, qk_ref, weights_ref, mixed_ref, inner_ref, outer_ref = refs[3:10]
+    in_proj, w_query, w_key, w_value, w_out, item_w1, item_w2 = refs[10:17]
+    outgoing, loss_ref, logits, d_normed = refs[17:]
     vectors = vectors_ref[0:PAD, :].astype(F32)
     d_user, d_item, loss = softmax_step(
         users, loss_scale, base_ref[0], (gathered_ref, swapped_ref), vectors, logits
     )
     loss_ref[...] = jnp.broadcast_to(loss, loss_ref.shape)
-    for copy in copies[1:]:
-        copy.wait()
     span, width = hidden_ref.shape
     hist = span // users
     heads = width // HEAD_DIM
@@ -384,16 +341,8 @@
     ).astype(BF)
     slots = outgoing.shape[0]
     column = row_ref[0:1, :]
-    chunk = slots // 4
-    saves = []
-    for c in range(4):
-        at = pl.ds(c * chunk, chunk)
-        picks = one_hot(iota((chunk, wide), 0) + c * chunk == column)
-        outgoing[at, :] = dot(picks, d_all).astype(BF)
-        saves.append(pltpu.make_async_copy(outgoing.at[at], outgoing_hbm.at[at], out_sems.at[c]))
-        saves[-1].start()
-    for save in saves:
-        save.wait()
+    picks = one_hot(iota((slots, wide), 0) == column)
+    outgoing[...] = dot(picks, d_all).astype(BF)
 
 
 def scatter_kernel(returned_ref, row_ref, loss_ref, part_ref, hot_ref):
@@ -440,54 +389,67 @@
     swap = [(i, towers - 1 - i) for i in range(towers)]
     shape = jax.ShapeDtypeStruct
     sems = lambda n: pltpu.SemaphoreType.DMA((n,))
+    in_hbm = lambda a: pltpu.with_memory_space_constraint(a, pltpu.HBM)
+    in_vmem = lambda a: pltpu.with_memory_space_constraint(a, pltpu.VMEM)
     like = lambda arrays: [pltpu.VMEM(a.shape, a.dtype) for a in arrays]
     exchange = functools.partial(lax.all_to_all, split_axis=0, concat_axis=0, tiled=True)
 
-    places = (shape((8, wide), jnp.int32), shape((wide, 128), jnp.int32))
     loads = (history, item_ids.reshape(1, users), rare_table)
     request, known, row, column = pl.pallas_call(
         functools.partial(index_kernel, owners),
-        out_shape=(shape((owners, 128), jnp.int32), shape((rare_count, emb), BF)) + places,
+        out_shape=(
+            shape((owners, 128), jnp.int32),
+            pltpu.VMEM((rare_count, emb), BF),
+            pltpu.VMEM((8, wide), jnp.int32),
+            pltpu.VMEM((wide, 128), jnp.int32),
+        ),
         in_specs=[HBM] * 3,
-        out_specs=(VMEM, VMEM, HBM, HBM),
-        scratch_shapes=like(loads + places) + [sems(5)],
-        compiler_params=params(FULL - 2),
+        out_specs=(VMEM,) * 4,
+        scratch_shapes=like(loads) + [sems(3)],
+        compiler_params=params(24),
         name="index",
-    )(*loads)
+    )(*map(in_hbm, loads))
     asked = exchange(request, SHARD)
-    served_shapes = (shape((slots, emb), BF), shape((8, slots), jnp.int32))
     served, asked_row = pl.pallas_call(
         serve_kernel,
-        out_shape=served_shapes,
+        out_shape=(shape((slots, emb), BF), pltpu.VMEM((8, slots), jnp.int32)),
         in_specs=[VMEM, VMEM],
-        out_specs=(VMEM, HBM),
-        scratch_shapes=like(served_shapes[1:]) + [pltpu.SemaphoreType.DMA],
+        out_specs=(VMEM, VMEM),
         compiler_params=params(24),
         name="serve",
-    )(asked, known)
+    )(asked, in_vmem(known))
     fetched = exchange(served, SHARD)
 
-    weights = (in_proj, w_query, w_key, w_value, w_out, item_w1, item_w2)
     gains = tuple(g.reshape(1, width) for g in (norm_gain, out_gain, item_gain))
-    kept_shapes = (
-        shape((span, width), F32),
-        shape((span, width), BF),
-        shape((users * heads, width), BF),
-        shape((users * heads, hist), F32),
-        shape((PAD, width), F32),
-        shape((PAD, width), F32),
-        shape((PAD, width), F32),
-    )
-    loads = (column, fetched, hot_table, pos_embed) + gains + weights
+    loads = (in_proj, w_query, w_key, w_value, w_out, item_w1, item_w2, hot_table, pos_embed) + gains
+    ready = pl.pallas_call(
+        functools.partial(prefetch_kernel, len(loads)),
+        out_shape=tuple(pltpu.VMEM(a.shape, a.dtype) for a in loads),
+        in_specs=[pl.BlockSpec(memory_space=pl.ANY)] + [HBM] * len(loads),
+        out_specs=(VMEM,) * len(loads),
+        scratch_shapes=[sems(len(loads))],
+        compiler_params=params(8),
+        name="prefetch",
+    )(served, *map(in_hbm, loads))
+    weights, (hot_ready, pos_ready), gains = ready[:7], ready[7:9], ready[9:]
+
     vectors, *kept = pl.pallas_call(
         functools.partial(forward_kernel, users),
-        out_shape=(shape((near * 2 * users, width), BF),) + kept_shapes,
-        in_specs=[HBM] * len(loads),
-        out_specs=(VMEM,) + (HBM,) * len(kept_shapes),
-        scratch_shapes=like(loads + kept_shapes) + [sems(len(loads)), sems(len(kept_shapes))],
-        compiler_params=params(FULL),
+        out_shape=(
+            pltpu.VMEM((near * 2 * users, width), BF),
+            pltpu.VMEM((span, width), F32),
+            pltpu.VMEM((span, width), BF),
+            pltpu.VMEM((users * heads, width), BF),
+            pltpu.VMEM((users * heads, hist), F32),
+            pltpu.VMEM((PAD, width), F32),
+            pltpu.VMEM((PAD, width), F32),
+            pltpu.VMEM((PAD, width), F32),
+        ),
+        in_specs=[VMEM] * 14,
+        out_specs=(VMEM,) * 8,
+        compiler_params=params(24),
         name="forward",
-    )(*loads)
+    )(in_vmem(column), fetched, *map(in_vmem, (hot_ready, pos_ready, *gains, *weights)))
 
     near_vectors = exchange(vectors, "z")
     spread = pl.pallas_call(
@@ -502,23 +464,16 @@
     swapped = lax.ppermute(gathered, "tower", swap)
     base = (lax.axis_index(SHARD) * users).astype(jnp.int32).reshape(1)
 
-    loads = (vectors, row) + gains + tuple(kept) + weights
+    loads = (vectors, row) + tuple(gains) + tuple(kept) + tuple(weights)
     outgoing, loss = pl.pallas_call(
         functools.partial(backward_kernel, users, scale),
-        out_shape=(shape((slots, emb), BF), shape((8, 128), F32)),
-        in_specs=[SMEM, VMEM, VMEM] + [HBM] * len(loads),
-        out_specs=(HBM, VMEM),
-        scratch_shapes=like(loads)
-        + [
-            pltpu.VMEM((slots, emb), BF),
-            pltpu.VMEM((total, total), F32),
-            pltpu.VMEM((span, width), F32),
-            sems(len(loads)),
-            sems(4),
-        ],
-        compiler_params=params(FULL - 4),
+        out_shape=(shape((slots, emb), BF), pltpu.VMEM((8, 128), F32)),
+        in_specs=[SMEM] + [VMEM] * (2 + len(loads)),
+        out_specs=(VMEM, VMEM),
+        scratch_shapes=[pltpu.VMEM((total, total), F32), pltpu.VMEM((span, width), F32)],
+        compiler_params=params(24),
         name="backward",
-    )(base, gathered, swapped, *loads)
+    )(base, gathered, swapped, *map(in_vmem, loads))
 
     returned = exchange(outgoing, SHARD)
     part, mine = pl.pallas_call(
@@ -528,7 +483,7 @@
         out_specs=(VMEM, VMEM),
         compiler_params=params(24),
         name="scatter",
-    )(returned, asked_row, loss)
+    )(returned, in_vmem(asked_row), in_vmem(loss))
     mine = mine + lax.ppermute(mine, "tower", swap)
     rare_grad = part.astype(F32) + lax.ppermute(part, "tower", swap).astype(F32)
     sums = exchange(jnp.broadcast_to(mine, (owners, emb + 128)), SHARD)

time: 182 us -> 196 us (1.077)
  local copies, waits for them, and re-layouts: 3.08 us -> 30.1 us
  blocking collectives: 115 us -> 90.2 us
  starting transfers between devices: 14.3 us -> 21.2 us
  waiting for transfers between devices: 17.4 us -> 23.8 us
    unnamed x5 -> x65, local copies, waits for them, and re-layouts: 1.65 us -> 28.7 us
    all_to_all x1 -> x0, blocking collectives: 24.3 us -> none  [shards(): fetched = exchange(served, SHARD)]
    all_to_all x0 -> x1, starting transfers between devices: none -> 7.3 us  [shards(): fetched = exchange(served, SHARD)]
    all_to_all x0 -> x1, waiting for transfers between devices: none -> 6.38 us  [shards(): fetched = exchange(served, SHARD)]
    pallas_call x2 -> x3, Pallas kernels: 8.79 us -> 11.4 us  [the longest x1 5.37 us: shards(): pl.pallas_call(functools.partial(forward_kernel, users), out_shape=(pltpu...]
    pallas_call x1, Pallas kernels: 14.9 us -> 12.6 us  [shards(): pl.pallas_call(functools.partial(backward_kernel, users, scale), out_shap...]
  transfers between devices with their start and end apart: 4 -> 5, of which waited for: 3 -> 4; matrix products, arithmetic and copies ran while one was open for 1% -> 1% of each run, Pallas kernels for 0% -> 2%
where the time goes in v4:
time: 196 us; the launch traced here: 195 us
  blocking collectives  90.2 us (46%)
  local copies, waits for them, and re-layouts  30.1 us (15%)
  Pallas kernels  26.1 us (13%)
  waiting for transfers between devices  23.8 us (12%)
  starting transfers between devices  21.2 us (11%)
  between operations  2.57 us (1%)
    unnamed x65, local copies, waits for them, and re-layouts  28.7 us
    all_to_all x1, blocking collectives, shards(): gathered = exchange(spread, ('x', 'y'))  27.4 us
    all_to_all x1, blocking collectives, shards(): asked = exchange(request, SHARD)  26.7 us
    all_to_all x1, blocking collectives, shards(): returned = exchange(outgoing, SHARD)  25.2 us
    pallas_call x1, Pallas kernels, shards(): pl.pallas_call(functools.partial(backward_kernel, users, scale), out_shap...  12.6 us
    all_to_all x1, waiting for transfers between devices, shards(): sums = exchange(jnp.broadcast_to(mine, (owners, emb + 128)), SHARD)  12.2 us
    all_to_all x1, blocking collectives, shards(): near_vectors = exchange(vectors, 'z')  10.9 us
    all_to_all x1, starting transfers between devices, shards(): fetched = exchange(served, SHARD)  7.3 us
  transfers between devices with their start and end apart: 5, of which 4 were waited for; matrix products, arithmetic and copies ran while one was open for 1% of the time, Pallas kernels for 2%

profile of v4, /device:TPU:1, one launch (start us, length us, event | category | flops | bytes accessed | tf_op | source)
XLA Modules:
  0.0 195.4 jit_solution(11505670534161393358)
XLA Ops:
  2.5 26.7 %all_to_all.64 = s32[128,1,128]{2,1,0:T(1,128)S(1)} all-to-all(s32[128,1,128]{2,1,0:T(1,128)S(1)} %bitcast.26), channel_id=1, replica_groups=mesh['tower'=2,'x'=4,'y'=4,'z'=8] {'x','y','z'}, dimensions={0} | all-to-all | bytes 131072 | tf_op jit(solution)/shard_map/all_to_all | solution.py:412
  29.2 1.5 serve.1
  31.3 7.3 %all-to-all-start.1 = ((bf16[128,8,256]{2,1,0:T(8,128)(2,1)}), bf16[128,8,256]{2,1,0:T(8,128)(2,1)}, u32[]{:S(2)}, u32[]{:S(2)}) async-start(bf16[128,8,256]{2,1,0:T(8,128)(2,1)} %bitcast.5), calls=%async_computation.1 | async-start | bytes 1048576 | tf_op jit(solution)/shard_map/all_to_all | solution.py:421
  38.6 4.5 %prefetch.1 = (bf16[256,1024]{1,0:T(8,128)(2,1)S(1)}, bf16[1024,1024]{1,0:T(8,128)(2,1)S(1)}, bf16[1024,1024]{1,0:T(8,128)(2,1)S(1)}, bf16[1024,1024]{1,0:T(8,12...) custom-call(bf16[1024,256]{1,0:T(8,128)(2,1)} %get-tuple-element.36., ...), custom_call_target="tpu_custom_call" | custom-call | tf_op jit(solution)/shard_map/prefetch/pallas_call | solution.py:425
  47.2 1.4 copy-done.9
  49.9 6.4 %all-to-all-done.1 = bf16[128,8,256]{2,1,0:T(8,128)(2,1)} async-done(((bf16[128,8,256]{2,1,0:T(8,128)(2,1)}), bf16[128,8,256]{2,1,0:T(8,128)(2,1)}, u32[]{:S(2)}, u32[]{:S(2)}) %all-to-all-start.1) | async-done | bytes 524320 | tf_op jit(solution)/shard_map/all_to_all | solution.py:421
  56.3 1.6 copy-done.1
  57.9 1.6 copy-done.4
  59.4 1.6 copy-done.7
  61.0 1.6 copy-done.10
  64.4 5.4 %forward.1 = (bf16[64,1024]{1,0:T(8,128)(2,1)S(1)}, f32[256,1024]{1,0:T(8,128)S(1)}, bf16[256,1024]{1,0:T(8,128)(2,1)S(1)}, bf16[64,1024]{1,0:T(8,128)(2,1)S(1)}...) custom-call(s32[384,128]{1,0:T(8,128)S(1)} %get-tuple-element.33.refs_0_, ...), custom_call_target="tpu_custom_call" | custom-call | tf_op jit(solution)/shard_map/forward/pallas_call | solution.py:436
  71.2 10.9 %all_to_all.65 = bf16[8,8,1024]{2,1,0:T(8,128)(2,1)S(1)} all-to-all(bf16[8,8,1024]{2,1,0:T(8,128)(2,1)S(1)} %bitcast.22), channel_id=1, replica_groups=mesh['tower'=2,'x'=4,'y'=4,'z'=8] {'z'}, dimensions={0} | all-to-all | bytes 262144 | tf_op jit(solution)/shard_map/all_to_all | solution.py:454
  82.5 27.4 %all_to_all.66 = bf16[16,32,2048]{2,1,0:T(8,128)(2,1)} all-to-all(bf16[16,32,2048]{2,1,0:T(8,128)(2,1)S(1)} %bitcast.20), channel_id=1, replica_groups=mesh['tower'=2,'x'=4,'y'=4,'z'=8] {'x','y'}, dimensions={0} | all-to-all | bytes 4194304 | tf_op jit(solution)/shard_map/all_to_all | solution.py:463
  109.9 5.6 %collective-permute-start = (bf16[512,2048]{1,0:T(8,128)(2,1)}, bf16[512,2048]{1,0:T(8,128)(2,1)}, u32[]{:S(2)}, u32[]{:S(2)}) collective-permute-start(bf16[512,2048]{1,0:T(8,128)(2,1)} %bitcast.13.gathered_ref), channel_id=1, source_target_pairs={{0,128},{128,0},{1,129},{129,1},{2,130},{130,2},{3,131},{131,3},{4... | collective-permute-start | bytes 6291464 | tf_op jit(solution)/shard_map/ppermute | solution.py:464
  115.6 4.1 %collective-permute-done.swapped_ref = bf16[512,2048]{1,0:T(8,128)(2,1)} collective-permute-done((bf16[512,2048]{1,0:T(8,128)(2,1)}, bf16[512,2048]{1,0:T(8,128)(2,1)}, u32[]{:S(2)}, u32[]{:S(2)}) %collective-permute-start) | collective-permute-done | bytes 2097184 | tf_op jit(solution)/shard_map/ppermute | solution.py:464
  119.7 1.6 copy-done.2
  121.3 1.6 copy-done.5
  122.9 1.6 copy-done.8
  124.5 1.6 copy-done.11
  130.8 12.6 %backward.1 = (bf16[1024,256]{1,0:T(8,128)(2,1)S(1)}, f32[8,128]{1,0:T(8,128)S(1)}) custom-call(s32[1]{0:T(128)} %bitcast.base_ref, bf16[512,2048]{1,0:T(8,128)(2,1)} %bitcast.13.gathered_ref, bf16[512,2048]{1,0:T(8,128)(2,1)} %collective-permute-done.swapped_ref, bf16[64,1024]{1,0:T(8,128)(2,1)S(1)} %get-tuple-element.49.vectors_ref, ...), custom_call_target="tpu_custom_call" | custom-call | tf_op jit(solution)/shard_map/backward/pallas_call | solution.py:468
  143.4 25.2 %all_to_all.67 = bf16[128,8,256]{2,1,0:T(8,128)(2,1)S(1)} all-to-all(bf16[128,8,256]{2,1,0:T(8,128)(2,1)S(1)} %bitcast.24), channel_id=1, replica_groups=mesh['tower'=2,'x'=4,'y'=4,'z'=8] {'x','y','z'}, dimensions={0} | all-to-all | bytes 1048576 | tf_op jit(solution)/shard_map/all_to_all | solution.py:478
  169.1 2.1 %collective-permute-start.2 = (bf16[512,256]{1,0:T(8,128)(2,1)S(1)}, bf16[512,256]{1,0:T(8,128)(2,1)S(1)}, u32[]{:S(2)}, u32[]{:S(2)}) collective-permute-start(bf16[512,256]{1,0:T(8,128)(2,1)S(1)} %get-tuple-element.62), channel_id=1, source_target_pairs={{0,128},{128,0},{1,129},{129,1},{2,130},{130,2},{3,131},{131,3},{4... | collective-permute-start | bytes 786440 | tf_op jit(solution)/shard_map/ppermute | solution.py:488
  173.2 6.1 %all-to-all-start.5 = ((f32[128,1,384]{2,1,0:T(1,128)}), f32[128,1,384]{2,1,0:T(1,128)S(1)}, u32[]{:S(2)}, u32[]{:S(2)}) async-start(f32[128,1,384]{2,1,0:T(1,128)} %broadcast_in_dim.2), calls=%async_computation.5 | async-start | bytes 393216 | tf_op jit(solution)/shard_map/all_to_all | solution.py:489
  180.2 12.2 %all-to-all-done.5 = f32[128,1,384]{2,1,0:T(1,128)S(1)} async-done(((f32[128,1,384]{2,1,0:T(1,128)}), f32[128,1,384]{2,1,0:T(1,128)S(1)}, u32[]{:S(2)}, u32[]{:S(2)}) %all-to-all-start.5) | async-done | bytes 196640 | tf_op jit(solution)/shard_map/all_to_all | solution.py:489
  (67 shorter events, 20.8 us)
Async XLA Ops:
  31.3 25.0 %all-to-all-start.1 = ((bf16[128,8,256]{2,1,0:T(8,128)(2,1)}), bf16[128,8,256]{2,1,0:T(8,128)(2,1)}, u32[]{:S(2)}, u32[]{:S(2)}) async-start(bf16[128,8,256]{2,1,0:T(8,128)(2,1)} %bitcast.5), calls=%async_computation.1 | async-start | bytes 1048576 | tf_op jit(solution)/shard_map/all_to_all | solution.py:421
  43.1 1.4 copy-start
  44.5 1.3 copy-start.3
  45.8 1.4 copy-start.6
  47.2 1.4 copy-start.9
  56.3 1.6 copy-start.1
  57.9 1.6 copy-start.4
  59.4 1.6 copy-start.7
  61.0 1.6 copy-start.10
  71.2 38.7 %copy-start.12 = (f32[256,1024]{1,0:T(8,128)}, f32[256,1024]{1,0:T(8,128)S(1)}, u32[]{:S(2)}) copy-start(f32[256,1024]{1,0:T(8,128)S(1)} %get-tuple-element.51.refs_3_) | copy-start | bytes 3145732
  71.2 38.7 %copy-start.16 = (bf16[64,1024]{1,0:T(8,128)(2,1)}, bf16[64,1024]{1,0:T(8,128)(2,1)S(1)}, u32[]{:S(2)}) copy-start(bf16[64,1024]{1,0:T(8,128)(2,1)S(1)} %get-tuple-element.53.refs_5_) | copy-start | bytes 393220
  71.2 38.7 %copy-start.24 = (f32[16,1024]{1,0:T(8,128)}, f32[16,1024]{1,0:T(8,128)S(1)}, u32[]{:S(2)}) copy-start(f32[16,1024]{1,0:T(8,128)S(1)} %get-tuple-element.57.refs_9_) | copy-start | bytes 196612
  71.2 38.7 %copy-start.26 = (f32[64,64]{1,0:T(8,128)}, f32[64,64]{1,0:T(8,128)S(1)}, u32[]{:S(2)}) copy-start(f32[64,64]{1,0:T(8,128)S(1)} %get-tuple-element.54.refs_6_) | copy-start | bytes 49156
  82.5 37.2 %copy-start.23 = (f32[16,1024]{1,0:T(8,128)S(1)}, f32[16,1024]{1,0:T(8,128)}, u32[]{:S(2)}) copy-start(f32[16,1024]{1,0:T(8,128)} %copy-done.22) | copy-start | bytes 196612
  82.5 37.2 %copy-start.31 = (s32[8,384]{1,0:T(8,128)S(1)}, s32[8,384]{1,0:T(8,128)}, u32[]{:S(2)}) copy-start(s32[8,384]{1,0:T(8,128)} %copy-done.30) | copy-start | bytes 36868
  109.9 9.8 %collective-permute-start = (bf16[512,2048]{1,0:T(8,128)(2,1)}, bf16[512,2048]{1,0:T(8,128)(2,1)}, u32[]{:S(2)}, u32[]{:S(2)}) collective-permute-start(bf16[512,2048]{1,0:T(8,128)(2,1)} %bitcast.13.gathered_ref), channel_id=1, source_target_pairs={{0,128},{128,0},{1,129},{129,1},{2,130},{130,2},{3,131},{131,3},{4... | collective-permute-start | bytes 6291464 | tf_op jit(solution)/shard_map/ppermute | solution.py:464
  119.7 1.6 copy-start.2
  121.3 1.6 copy-start.5
  122.9 1.6 copy-start.8
  124.5 1.6 copy-start.11
  130.8 37.8 %copy-start.29 = (s32[8,1024]{1,0:T(8,128)S(1)}, s32[8,1024]{1,0:T(8,128)}, u32[]{:S(2)}) copy-start(s32[8,1024]{1,0:T(8,128)} %copy-done.28) | copy-start | bytes 98308
  169.1 10.2 %collective-permute-start.2 = (bf16[512,256]{1,0:T(8,128)(2,1)S(1)}, bf16[512,256]{1,0:T(8,128)(2,1)S(1)}, u32[]{:S(2)}, u32[]{:S(2)}) collective-permute-start(bf16[512,256]{1,0:T(8,128)(2,1)S(1)} %get-tuple-element.62), channel_id=1, source_target_pairs={{0,128},{128,0},{1,129},{129,1},{2,130},{130,2},{3,131},{131,3},{4... | collective-permute-start | bytes 786440 | tf_op jit(solution)/shard_map/ppermute | solution.py:488
  171.2 1.2 collective-permute-start.1
  173.2 19.2 %all-to-all-start.5 = ((f32[128,1,384]{2,1,0:T(1,128)}), f32[128,1,384]{2,1,0:T(1,128)S(1)}, u32[]{:S(2)}, u32[]{:S(2)}) async-start(f32[128,1,384]{2,1,0:T(1,128)} %broadcast_in_dim.2), calls=%async_computation.5 | async-start | bytes 393216 | tf_op jit(solution)/shard_map/all_to_all | solution.py:489
  (13 other events, 10.5 us)

commit v5 on v4

v5 whole, which is shorter than its diff:
```python
import functools
import math

import jax
import jax.numpy as jnp
from jax import lax
from jax.experimental import pallas as pl
from jax.experimental.pallas import tpu as pltpu
from jax.sharding import Mesh
from jax.sharding import PartitionSpec as P

HEAD_DIM = 64
EPS = 1e-06
SLOTS = 8
HOT_SLOT = 5
SHARD = ("x", "y", "z")
PAD = 16
BF = jnp.bfloat16
F32 = jnp.float32
VMEM = pl.BlockSpec(memory_space=pltpu.VMEM)
SMEM = pl.BlockSpec(memory_space=pltpu.SMEM)
HBM = pl.BlockSpec(memory_space=pltpu.HBM)
NT = (((1,), (1,)), ((), ()))
TN = (((0,), (0,)), ((), ()))


def dot(a, b):
    return jnp.dot(a, b, preferred_element_type=F32)


def dot_nt(a, b):
    return lax.dot_general(a, b, NT, preferred_element_type=F32)


def dot_tn(a, b):
    return lax.dot_general(a, b, TN, preferred_element_type=F32)


def iota(shape, axis):
    return lax.broadcasted_iota(jnp.int32, shape, axis)


def one_hot(mask):
    return jnp.where(mask, 1.0, 0.0).astype(BF)


def params(mib):
    return pltpu.CompilerParams(vmem_limit_bytes=mib * 1024 * 1024)


def copies_of(pairs, sems):
    copies = [pltpu.make_async_copy(a, b, sems.at[i]) for i, (a, b) in enumerate(pairs)]
    for copy in copies:
        copy.start()
    return copies


def index_kernel(
    owners,
    history_hbm,
    items_hbm,
    table_hbm,
    request_ref,
    known_ref,
    row_hbm,
    column_hbm,
    history_ref,
    items_ref,
    table,
    row,
    column,
    sems,
):
    loads = copies_of(
        [(history_hbm, history_ref), (items_hbm, items_ref), (table_hbm, table)], sems
    )
    loads[0].wait()
    loads[1].wait()
    hot_count = owners
    rare_count = table.shape[0]
    users = history_ref.shape[0]
    span = row.shape[1]
    parts = [history_ref[u : u + 1, :] for u in range(users)] + [items_ref[...]]
    filled = sum(p.shape[1] for p in parts)
    ids = jnp.concatenate(parts + [jnp.full((1, span - filled), -1, jnp.int32)], axis=1)
    is_rare = ids >= hot_count
    index = ids - hot_count
    owner = jnp.where(is_rare, index // rare_count, -1)
    value = jnp.where(is_rare, index % rare_count + 1, 0).astype(F32)
    hits = iota((owners, span), 0) == owner
    before = one_hot(iota((span, span), 0) < iota((span, span), 1))
    earlier = dot(one_hot(hits), before)
    position = jnp.sum(jnp.where(hits, earlier, 0.0), axis=0, keepdims=True).astype(jnp.int32)
    places = jnp.where(
        is_rare, owner * SLOTS + position, jnp.where(ids >= 0, ids * SLOTS + HOT_SLOT, -1)
    )
    row[...] = jnp.broadcast_to(places, row.shape)
    column[...] = jnp.transpose(jnp.broadcast_to(places.astype(F32), (128, span))).astype(jnp.int32)
    saves = copies_of([(row, row_hbm), (column, column_hbm)], sems.at[pl.ds(3, 2)])
    order = jnp.where(hits, earlier, -1.0)
    lanes = iota(request_ref.shape, 1)
    request = jnp.zeros(request_ref.shape, F32)
    for slot in range(HOT_SLOT):
        wanted = jnp.sum(jnp.where(order == float(slot), value, 0.0), axis=1, keepdims=True)
        request = jnp.where(lanes == slot, wanted, request)
    request_ref[...] = request.astype(jnp.int32)
    loads[2].wait()
    known_ref[...] = table[...].astype(BF)
    for save in saves:
        save.wait()


def serve_kernel(asked_ref, known_ref, served, row_hbm, row, sem):
    slots = served.shape[0]
    sources = asked_ref.shape[0]
    asked = asked_ref[...]
    high = (asked // 2).astype(F32).astype(BF)
    low = (asked % 2).astype(F32).astype(BF)
    expand = one_hot(iota((slots, sources), 0) // SLOTS == iota((slots, sources), 1))
    wide = 2.0 * dot(expand, high) + dot(expand, low)
    mine = iota(wide.shape, 1) == iota(wide.shape, 0) % SLOTS
    index = jnp.sum(jnp.where(mine, wide, 0.0), axis=1, keepdims=True) - 1.0
    index = jnp.broadcast_to(index, wide.shape)
    row[...] = jnp.transpose(index)[0:8].astype(jnp.int32)
    save = pltpu.make_async_copy(row, row_hbm, sem)
    save.start()
    index = index.astype(jnp.int32)
    lanes = iota(index.shape, 1)
    rows = known_ref.shape[0]
    picks = jnp.concatenate(
        [one_hot(index == lanes + 128 * j) for j in range(rows // 128)], axis=1
    )
    served[...] = dot(picks, known_ref[...]).astype(BF)
    save.wait()


def head_mask(heads, width):
    return iota((heads, width), 1) // HEAD_DIM == iota((heads, width), 0)


def spread_heads(values, mask, users):
    return jnp.concatenate(
        [jnp.where(mask, values[u : u + 1], 0.0) for u in range(users)], axis=0
    ).astype(BF)


def join_heads(full, mask, users):
    heads = mask.shape[0]
    parts = [
        jnp.sum(
            jnp.where(mask, full[u * heads : (u + 1) * heads], 0.0), axis=0, keepdims=True
        )
        for u in range(users)
    ]
    return jnp.concatenate(parts + [jnp.zeros((PAD - users, full.shape[1]), F32)], axis=0)


def look_up(column, fetched, hot):
    lanes = iota(column.shape, 1)
    slots = fetched.shape[0]
    picks = jnp.concatenate(
        [one_hot(column == lanes + 128 * j) for j in range(slots // 128)], axis=1
    )
    hot_picks = one_hot(column == lanes * SLOTS + HOT_SLOT)
    return (dot(picks, fetched[...]) + dot(hot_picks, hot[...].astype(BF))).astype(BF)


def item_forward_kernel(users, *refs):
    fetched_ref, sources, refs = refs[0], refs[1:6], refs[6:]
    vectors_ref, kept_hbm, refs = refs[0], refs[1:3], refs[3:]
    targets, kept, (in_sems, out_sems) = refs[:5], refs[5:7], refs[7:]
    column_of, hot, gain, item_w1, item_w2 = targets
    inner_ref, outer_ref = kept
    span = sources[0].shape[0]
    sources = (sources[0].at[pl.ds(span - 128, PAD)],) + tuple(sources[1:])
    copies = copies_of(zip(sources, targets), in_sems)
    copies[0].wait()
    copies[1].wait()
    rows = look_up(column_of[...], fetched_ref, hot)
    copies[2].wait()
    copies[3].wait()
    inner = dot(rows, item_w1[...])
    inner_ref[...] = inner
    gated = (inner * jax.nn.sigmoid(inner)).astype(BF)
    copies[4].wait()
    outer = dot(gated, item_w2[...])
    outer_ref[...] = outer
    saves = copies_of(zip(kept, kept_hbm), out_sems)
    scale = lax.rsqrt(jnp.mean(outer * outer, axis=-1, keepdims=True) + EPS)
    vectors = jnp.where(iota(outer.shape, 0) < users, outer * scale * gain[...], 0.0)
    peers = vectors_ref.shape[0] // 8
    vectors_ref[...] = jnp.concatenate([vectors[0:8]] * peers, axis=0).astype(BF)
    for save in saves:
        save.wait()


def user_forward_kernel(users, *refs):
    fetched_ref, sources, refs = refs[0], refs[1:11], refs[11:]
    vectors_ref, kept_hbm, refs = refs[0], refs[1:6], refs[6:]
    targets, kept, (in_sems, out_sems) = refs[:10], refs[10:15], refs[15:]
    column_of, hot, pos_of, norm_gain_ref, out_gain_ref = targets[:5]
    in_proj, w_query, w_key, w_value, w_out = targets[5:]
    hidden_ref, normed_ref, qk_ref, weights_ref, mixed_ref = kept
    copies = copies_of(zip(sources, targets), in_sems)
    saves = [
        pltpu.make_async_copy(a, b, out_sems.at[i]) for i, (a, b) in enumerate(zip(kept, kept_hbm))
    ]
    hist, width = pos_of.shape
    heads = width // HEAD_DIM
    span = users * hist
    copies[0].wait()
    copies[1].wait()
    rows = look_up(column_of[0:span, :], fetched_ref, hot)
    for copy in copies[2:6]:
        copy.wait()
    pos = pos_of[...].astype(F32)
    hidden = dot(rows, in_proj[...]) + jnp.concatenate([pos] * users, axis=0)
    hidden_ref[...] = hidden
    saves[0].start()
    scale = lax.rsqrt(jnp.mean(hidden * hidden, axis=-1, keepdims=True) + EPS)
    normed = (hidden * scale * norm_gain_ref[...]).astype(BF)
    normed_ref[...] = normed
    saves[1].start()
    last = jnp.concatenate(
        [normed[(u + 1) * hist - PAD : (u + 1) * hist].astype(F32)[PAD - 1 :] for u in range(users)]
        + [jnp.zeros((PAD - users, width), F32)],
        axis=0,
    ).astype(BF)
    mask = head_mask(heads, width)
    copies[6].wait()
    query = dot(last, w_query[...]).astype(BF).astype(F32)
    copies[7].wait()
    qk = dot_nt(spread_heads(query, mask, users), w_key[...]).astype(BF)
    qk_ref[...] = qk
    saves[2].start()
    mixes = []
    for u in range(users):
        own = normed[u * hist : (u + 1) * hist]
        scores = dot_nt(qk[u * heads : (u + 1) * heads], own) * (1.0 / math.sqrt(HEAD_DIM))
        raised = jnp.exp(scores - jnp.max(scores, axis=1, keepdims=True))
        weights = raised / jnp.sum(raised, axis=1, keepdims=True)
        weights_ref[u * heads : (u + 1) * heads, :] = weights
        mixes.append(dot(weights.astype(BF), own))
    saves[3].start()
    mixes = jnp.concatenate(mixes, axis=0).astype(BF)
    copies[8].wait()
    attended = join_heads(dot(mixes, w_value[...]), mask, users).astype(BF)
    copies[9].wait()
    hidden_last = jnp.concatenate(
        [hidden[(u + 1) * hist - 1 : (u + 1) * hist] for u in range(users)]
        + [jnp.zeros((PAD - users, width), F32)],
        axis=0,
    )
    mixed = hidden_last + dot(attended, w_out[...])
    mixed_ref[...] = mixed
    saves[4].start()
    scale = lax.rsqrt(jnp.mean(mixed * mixed, axis=-1, keepdims=True) + EPS)
    vectors_ref[...] = (mixed * scale * out_gain_ref[...]).astype(BF)
    for save in saves:
        save.wait()


def arrange_kernel(users, near, near_ref, vectors_ref, spread_ref):
    total, width = spread_ref.shape
    block = near * users + 8
    at = iota((total, near * 8), 0) % block
    source = jnp.where(at < near * users, at // users * 8 + at % users, -1)
    item_rows = dot(one_hot(iota((total, near * 8), 1) == source), near_ref[...])
    at = iota((total, PAD), 0) % block
    source = jnp.where((at >= near * users) & (at < (near + 1) * users), at - near * users, -1)
    user_rows = dot(one_hot(iota((total, PAD), 1) == source), vectors_ref[...])
    spread_ref[...] = (item_rows + user_rows).astype(BF)


def softmax_kernel(
    users, near, scale, place_ref, gathered_ref, swapped_ref, d_user_ref, d_part_ref, loss_ref
):
    rows, width = gathered_ref.shape
    items = near * users
    block = items + 8
    blocks = rows // block
    mine, plane = place_ref[0], place_ref[1]
    own, other = gathered_ref[...], swapped_ref[...]

    def source_of_users(shape):
        line = iota(shape, 0)
        return line // users * block + items + line % users

    group = (blocks * users, rows)
    at_group = iota(group, 1) == source_of_users(group)
    line = (near * 8, rows)
    at_line = (iota(line, 0) % 8 < users) & (
        iota(line, 1) == mine * block + iota(line, 0) // 8 * users + iota(line, 0) % 8
    )
    self = (PAD, rows)
    at_self = (iota(self, 0) < users) & (iota(self, 1) == mine * block + items + iota(self, 0))
    picked = dot(jnp.concatenate([one_hot(at_group), one_hot(at_line), one_hot(at_self)], axis=0), own)
    own_users = picked[0 : blocks * users].astype(BF)
    line_items = picked[blocks * users : blocks * users + near * 8].astype(BF)
    self_users = picked[blocks * users + near * 8 :].astype(BF)
    other_users = dot(one_hot(at_group), other).astype(BF)
    group_users = jnp.concatenate([own_users, other_users], axis=0)
    total = 2 * blocks * users

    valid = iota((rows, total), 0) % block < items
    first = jnp.where(valid, scale * dot_nt(own, group_users), -jnp.inf)
    second = jnp.where(valid, scale * dot_nt(other, group_users), -jnp.inf)
    top = jnp.maximum(
        jnp.max(first, axis=0, keepdims=True), jnp.max(second, axis=0, keepdims=True)
    )
    count = jnp.sum(jnp.exp(first - top), axis=0, keepdims=True) + jnp.sum(
        jnp.exp(second - top), axis=0, keepdims=True
    )
    normalizer = top + jnp.log(count)
    shape = (near * 8, total)
    which = iota(shape, 0)
    target = (which // 8 == plane) & (iota(shape, 1) == mine * users + which % 8)
    slope = jnp.exp(scale * dot_nt(line_items, group_users) - normalizer)
    slope = jnp.where(which % 8 < users, slope - jnp.where(target, 1.0, 0.0), 0.0).astype(BF)
    d_part_ref[...] = (scale * dot(slope, group_users)).astype(BF)

    shape = (PAD, rows)
    lanes = iota(shape, 1)
    real = lanes % block < items
    valid = iota(shape, 0) < users
    target = lanes == mine * block + plane * users + iota(shape, 0)
    first = jnp.where(real, scale * dot_nt(self_users, own), -jnp.inf)
    second = jnp.where(real, scale * dot_nt(self_users, other), -jnp.inf)
    top = jnp.maximum(
        jnp.max(first, axis=1, keepdims=True), jnp.max(second, axis=1, keepdims=True)
    )
    count = jnp.sum(jnp.exp(first - top), axis=1, keepdims=True) + jnp.sum(
        jnp.exp(second - top), axis=1, keepdims=True
    )
    normalizer = top + jnp.log(count)
    slope = jnp.exp(first - normalizer) - jnp.where(target, 1.0, 0.0)
    d_user = dot(jnp.where(valid, slope, 0.0).astype(BF), own)
    slope = jnp.exp(second - normalizer)
    d_user = d_user + dot(jnp.where(valid, slope, 0.0).astype(BF), other)
    d_user_ref[...] = (scale * d_user).astype(BF).astype(F32)
    each = jnp.sum(jnp.where(valid & target, normalizer - first, 0.0), axis=1, keepdims=True)
    loss_ref[...] = jnp.broadcast_to(jnp.sum(each, axis=0, keepdims=True), loss_ref.shape)


def norm_backward(values, cotangent, gain):
    inverse = lax.rsqrt(jnp.mean(values * values, axis=-1, keepdims=True) + EPS)
    pulled = cotangent * gain
    along = jnp.mean(pulled * values, axis=-1, keepdims=True)
    return inverse * pulled - values * (inverse * inverse * inverse * along)


def user_backward_kernel(users, d_user_ref, *refs):
    sources, d_rows_ref, refs = refs[:12], refs[12], refs[13:]
    targets, (d_normed, sems) = refs[:12], refs[12:]
    mixed_ref, out_gain_ref, w_out, w_value, normed_ref, weights_ref, qk_ref = targets[:7]
    w_key, w_query, hidden_ref, norm_gain_ref, in_proj = targets[7:]
    copies = copies_of(zip(sources, targets), sems)
    span, width = hidden_ref.shape
    hist = span // users
    heads = width // HEAD_DIM
    mask = head_mask(heads, width)
    for copy in copies[:3]:
        copy.wait()
    d_mixed = norm_backward(mixed_ref[...], d_user_ref[...], out_gain_ref[...])
    d_attended = dot_nt(d_mixed.astype(BF), w_out[...])
    copies[3].wait()
    d_mixes = dot_nt(spread_heads(d_attended, mask, users), w_value[...]).astype(BF)
    for copy in copies[4:7]:
        copy.wait()
    d_qk = []
    for u in range(users):
        own = normed_ref[u * hist : (u + 1) * hist, :]
        weights = weights_ref[u * heads : (u + 1) * heads, :]
        pulled = d_mixes[u * heads : (u + 1) * heads]
        d_weights = dot_nt(pulled, own)
        d_scores = weights * (d_weights - jnp.sum(weights * d_weights, axis=1, keepdims=True))
        d_scores = (d_scores * (1.0 / math.sqrt(HEAD_DIM))).astype(BF)
        d_normed[u * hist : (u + 1) * hist, :] = dot_tn(weights.astype(BF), pulled) + dot_tn(
            d_scores, qk_ref[u * heads : (u + 1) * heads, :]
        )
        d_qk.append(dot(d_scores, own))
    d_qk = jnp.concatenate(d_qk, axis=0).astype(BF)
    copies[7].wait()
    d_query = join_heads(dot(d_qk, w_key[...]), mask, users).astype(BF)
    copies[8].wait()
    d_last = dot_nt(d_query, w_query[...])
    for u in range(users):
        at = slice((u + 1) * hist - 1, (u + 1) * hist)
        d_normed[at, :] = d_normed[at, :] + d_last[u : u + 1]
    copies[9].wait()
    copies[10].wait()
    d_normed[...] = norm_backward(hidden_ref[...], d_normed[...], norm_gain_ref[...])
    for u in range(users):
        at = slice((u + 1) * hist - 1, (u + 1) * hist)
        d_normed[at, :] = d_normed[at, :] + d_mixed[u : u + 1]
    copies[11].wait()
    d_rows_ref[...] = dot_nt(d_normed[...].astype(BF), in_proj[...]).astype(BF)


def item_backward_kernel(users, parts_ref, d_rows_ref, *refs):
    sources, outgoing, refs = refs[:6], refs[6], refs[7:]
    targets, sems = refs[:6], refs[6]
    row_ref, gain, outer_ref, inner_ref, item_w2, item_w1 = targets
    copies = copies_of(zip(sources, targets), sems)
    slots = outgoing.shape[0]
    span = d_rows_ref.shape[0]
    wide = row_ref.shape[1]
    peers = parts_ref.shape[0]
    shape = (PAD, peers)
    added = (iota(shape, 1) % 8 == iota(shape, 0)) & (iota(shape, 0) < users)
    d_item = dot(one_hot(added), parts_ref[...]).astype(BF).astype(F32)
    copies[0].wait()
    picks = one_hot(iota((slots, wide), 0) == row_ref[0:1, :])
    total = dot(picks[:, 0:span], d_rows_ref[...])
    copies[1].wait()
    copies[2].wait()
    d_outer = norm_backward(outer_ref[...], d_item, gain[...])
    copies[3].wait()
    inner = inner_ref[...]
    gate = jax.nn.sigmoid(inner)
    copies[4].wait()
    d_inner = dot_nt(d_outer.astype(BF), item_w2[...]) * (gate * (1.0 + inner * (1.0 - gate)))
    copies[5].wait()
    d_items = dot_nt(d_inner.astype(BF), item_w1[...])
    d_items = jnp.concatenate(
        [d_items, jnp.zeros((wide - span - PAD, d_items.shape[1]), F32)], axis=0
    ).astype(BF)
    outgoing[...] = (total + dot(picks[:, span:], d_items)).astype(BF)


def finish_kernel(total, sums_ref, hot_ref, loss_ref):
    emb = hot_ref.shape[1]
    sums = sums_ref[...]
    hot_ref[...] = sums[:, 0:emb]
    loss_ref[...] = jnp.sum(sums[:, emb : emb + 1], axis=0, keepdims=True) / total


def scatter_kernel(returned_ref, row_ref, loss_ref, part_ref, hot_ref):
    rows, emb = part_ref.shape
    slots = returned_ref.shape[0]
    returned = returned_ref[...]
    picks = one_hot(iota((rows, slots), 0) == row_ref[0:1, :])
    part_ref[...] = dot(picks, returned).astype(BF)
    hot = dot(one_hot(iota((PAD, slots), 1) % SLOTS == HOT_SLOT), returned)
    hot_ref[:, 0:emb] = hot[0:1]
    hot_ref[:, emb:] = loss_ref[0:1, :]


def shards(
    history,
    item_ids,
    hot_table,
    rare_table,
    in_proj,
    pos_embed,
    norm_gain,
    w_query,
    w_key,
    w_value,
    w_out,
    out_gain,
    item_w1,
    item_w2,
    item_gain,
):
    users, hist = history.shape
    emb = hot_table.shape[1]
    rare_count = rare_table.shape[0]
    width = in_proj.shape[1]
    heads = width // HEAD_DIM
    scale = 4.0 / math.sqrt(width)
    owners = lax.axis_size(SHARD)
    towers = lax.axis_size("tower")
    near = lax.axis_size("z")
    total = users * towers * owners
    slots = owners * SLOTS
    span = users * hist
    wide = -(-(span + PAD) // 128) * 128
    swap = [(i, towers - 1 - i) for i in range(towers)]
    shape = jax.ShapeDtypeStruct
    sems = lambda n: pltpu.SemaphoreType.DMA((n,))
    hbm = lambda a: pltpu.HBM(a.shape, a.dtype)
    in_hbm = lambda a: pltpu.with_memory_space_constraint(a, pltpu.HBM)
    in_vmem = lambda a: pltpu.with_memory_space_constraint(a, pltpu.VMEM)
    like = lambda arrays: [pltpu.VMEM(a.shape, a.dtype) for a in arrays]
    exchange = functools.partial(lax.all_to_all, split_axis=0, concat_axis=0, tiled=True)

    places = (shape((8, wide), jnp.int32), shape((wide, 128), jnp.int32))
    loads = (history, item_ids.reshape(1, users), rare_table)
    request, known, row, column = pl.pallas_call(
        functools.partial(index_kernel, owners),
        out_shape=(
            shape((owners, 128), jnp.int32),
            pltpu.VMEM((rare_count, emb), BF),
            *map(hbm, places),
        ),
        in_specs=[HBM] * 3,
        out_specs=(VMEM, VMEM, HBM, HBM),
        scratch_shapes=like(loads + places) + [sems(5)],
        compiler_params=params(24),
        name="index",
    )(*map(in_hbm, loads))
    asked = exchange(request, SHARD)
    served, asked_row = pl.pallas_call(
        serve_kernel,
        out_shape=(shape((slots, emb), BF), pltpu.HBM((8, slots), jnp.int32)),
        in_specs=[VMEM, VMEM],
        out_specs=(VMEM, HBM),
        scratch_shapes=[pltpu.VMEM((8, slots), jnp.int32), pltpu.SemaphoreType.DMA],
        compiler_params=params(24),
        name="serve",
    )(asked, in_vmem(known))
    fetched = exchange(served, SHARD)

    norm_gain, out_gain, item_gain = (g.reshape(1, width) for g in (norm_gain, out_gain, item_gain))
    loads = (column, hot_table, item_gain, item_w1, item_w2)
    kept = (shape((PAD, width), F32), shape((PAD, width), F32))
    item_vec, inner, outer = pl.pallas_call(
        functools.partial(item_forward_kernel, users),
        out_shape=(shape((near * 8, width), BF), *map(hbm, kept)),
        in_specs=[VMEM] + [HBM] * 5,
        out_specs=(VMEM, HBM, HBM),
        scratch_shapes=[pltpu.VMEM((PAD, 128), jnp.int32)]
        + like(loads[1:] + kept)
        + [sems(5), sems(2)],
        compiler_params=params(24),
        name="item_forward",
    )(fetched, *map(in_hbm, loads))
    near_items = exchange(item_vec, "z")

    loads = (column, hot_table, pos_embed, norm_gain, out_gain)
    loads += (in_proj, w_query, w_key, w_value, w_out)
    kept = (
        shape((span, width), F32),
        shape((span, width), BF),
        shape((users * heads, width), BF),
        shape((users * heads, hist), F32),
        shape((PAD, width), F32),
    )
    user_vec, hidden, normed, qk, weights, mixed = pl.pallas_call(
        functools.partial(user_forward_kernel, users),
        out_shape=(shape((PAD, width), BF), *map(hbm, kept)),
        in_specs=[VMEM] + [HBM] * len(loads),
        out_specs=(VMEM,) + (HBM,) * len(kept),
        scratch_shapes=like(loads + kept) + [sems(len(loads)), sems(len(kept))],
        compiler_params=params(40),
        name="user_forward",
    )(fetched, *map(in_hbm, loads))

    rows = owners // near * (near * users + 8)
    spread = pl.pallas_call(
        functools.partial(arrange_kernel, users, near),
        out_shape=shape((rows, width), BF),
        in_specs=[VMEM, VMEM],
        out_specs=VMEM,
        compiler_params=params(24),
        name="arrange",
    )(near_items, user_vec)
    gathered = exchange(spread, ("x", "y"))
    swapped = lax.ppermute(gathered, "tower", swap)
    place = jnp.stack([lax.axis_index(("x", "y")), lax.axis_index("z")]).astype(jnp.int32)
    d_user, d_part, loss = pl.pallas_call(
        functools.partial(softmax_kernel, users, near, scale),
        out_shape=(shape((PAD, width), F32), shape((near * 8, width), BF), shape((8, 128), F32)),
        in_specs=[SMEM, VMEM, VMEM],
        out_specs=(VMEM, VMEM, VMEM),
        compiler_params=params(32),
        name="softmax",
    )(place, gathered, swapped)
    parts = exchange(d_part, "z")

    loads = (mixed, out_gain, w_out, w_value, normed, weights, qk)
    loads += (w_key, w_query, hidden, norm_gain, in_proj)
    d_rows = pl.pallas_call(
        functools.partial(user_backward_kernel, users),
        out_shape=shape((span, emb), BF),
        in_specs=[VMEM] + [HBM] * len(loads),
        out_specs=VMEM,
        scratch_shapes=like(loads) + [pltpu.VMEM((span, width), F32), sems(len(loads))],
        compiler_params=params(40),
        name="user_backward",
    )(d_user, *map(in_hbm, loads))
    loads = (row, item_gain, outer, inner, item_w2, item_w1)
    outgoing = pl.pallas_call(
        functools.partial(item_backward_kernel, users),
        out_shape=shape((slots, emb), BF),
        in_specs=[VMEM, VMEM] + [HBM] * len(loads),
        out_specs=VMEM,
        scratch_shapes=like(loads) + [sems(len(loads))],
        compiler_params=params(32),
        name="item_backward",
    )(parts, d_rows, *map(in_hbm, loads))

    returned = exchange(outgoing, SHARD)
    part, mine = pl.pallas_call(
        scatter_kernel,
        out_shape=(shape((rare_count, emb), BF), shape((1, emb + 128), F32)),
        in_specs=[VMEM, VMEM, VMEM],
        out_specs=(VMEM, VMEM),
        compiler_params=params(24),
        name="scatter",
    )(returned, asked_row, loss)
    mine = mine + lax.ppermute(mine, "tower", swap)
    rare_grad = part.astype(F32) + lax.ppermute(part, "tower", swap).astype(F32)
    sums = exchange(jnp.broadcast_to(mine, (owners, emb + 128)), SHARD)
    hot_total, loss_total = pl.pallas_call(
        functools.partial(finish_kernel, total),
        out_shape=(shape((owners, emb), F32), shape((1, 1), F32)),
        in_specs=[VMEM],
        out_specs=(VMEM, VMEM),
        compiler_params=params(24),
        name="finish",
    )(sums)
    return (hot_total, rare_grad, loss_total[0, 0])


def solution(mesh):
    sizes = (mesh.shape["tower"], 4, 4, mesh.shape["shard"] // 16)
    mesh = Mesh(mesh.devices.reshape(sizes), ("tower",) + SHARD)
    return jax.shard_map(
        shards,
        mesh=mesh,
        in_specs=(
            P(("tower",) + SHARD, None),
            P(("tower",) + SHARD),
            P(),
            P(SHARD, None),
            P(),
            P(),
            P(),
            P(),
            P(),
            P(),
            P(),
            P(),
            P(),
            P(),
            P(),
        ),
        out_specs=(P(), P(SHARD, None), P()),
        check_vma=False,
    )
```

time: 196 us -> 170 us (0.87)
  local copies, waits for them, and re-layouts: 30.1 us -> 0.81 us
  waiting for transfers between devices: 23.8 us -> 17.9 us
  blocking collectives: 90.2 us -> 96.1 us
  Pallas kernels: 26.1 us -> 29.3 us
  starting transfers between devices: 21.2 us -> 23.8 us
    unnamed x65 -> x3, local copies, waits for them, and re-layouts: 28.7 us -> 0.02 us
    all_to_all x1, blocking collectives: 10.9 us -> 23.6 us  [shards(): fetched = exchange(served, SHARD)]
    all_to_all x1, blocking collectives: 27.4 us -> 17.3 us  [shards(): gathered = exchange(spread, ('x', 'y'))]
    all_to_all x1 -> x2, waiting for transfers between devices: 6.38 us -> 2.05 us  [the longest x1 1.23 us: shards(): near_items = exchange(item_vec, 'z')]
    all_to_all x1, blocking collectives: 25.2 us -> 28.6 us  [shards(): returned = exchange(outgoing, SHARD)]
    pallas_call x5 -> x8, Pallas kernels: 24.3 us -> 26.9 us  [the longest x1 7.04 us: shards(): pl.pallas_call(functools.partial(user_backward_kernel, users), out_shape=...]
    all_to_all x1 -> x2, starting transfers between devices: 7.3 us -> 8.72 us  [the longest x1 5.34 us: shards(): parts = exchange(d_part, 'z')]
  transfers between devices with their start and end apart: 5 -> 6, of which waited for: 4 -> 5; matrix products, arithmetic and copies ran while one was open for 1% -> 1% of each run, Pallas kernels for 2% -> 8%
where the time goes in v5:
time: 170 us
  blocking collectives  96.1 us (57%)
  Pallas kernels  29.3 us (17%)
  starting transfers between devices  23.8 us (14%)
  waiting for transfers between devices  17.9 us (11%)
    all_to_all x1, blocking collectives, shards(): returned = exchange(outgoing, SHARD)  28.6 us
    all_to_all x1, blocking collectives, shards(): asked = exchange(request, SHARD)  26.7 us
    all_to_all x1, blocking collectives, shards(): fetched = exchange(served, SHARD)  23.6 us
    all_to_all x1, blocking collectives, shards(): gathered = exchange(spread, ('x', 'y'))  17.3 us
    all_to_all x1, waiting for transfers between devices, shards(): sums = exchange(jnp.broadcast_to(mine, (owners, emb + 128)), SHARD)  12.2 us
    pallas_call x1, Pallas kernels, shards(): pl.pallas_call(functools.partial(user_backward_kernel, users), out_shape=...  7.04 us
    pallas_call x1, Pallas kernels, shards(): pl.pallas_call(functools.partial(user_forward_kernel, users), out_shape=(...  6.6 us
    all_to_all x1, starting transfers between devices, shards(): sums = exchange(jnp.broadcast_to(mine, (owners, emb + 128)), SHARD)  6.13 us
  transfers between devices with their start and end apart: 6, of which 5 were waited for; matrix products, arithmetic and copies ran while one was open for 1% of the time, Pallas kernels for 8%

profile of v5, /device:TPU:1, one launch (start us, length us, event | category | flops | bytes accessed | tf_op | source)
XLA Modules:
  0.0 169.6 jit_solution(994085254373702910)
XLA Ops:
  0.6 1.9 %index.1 = (s32[128,128]{1,0:T(8,128)S(1)}, bf16[512,256]{1,0:T(8,128)(2,1)S(1)}, s32[8,384]{1,0:T(8,128)}, s32[384,128]{1,0:T(8,128)}) custom-call(s32[4,64]{1,0:T(4,128)} %history_hbm.1, s32[1,4]{1,0:T(1,128)} %bitcast.43, f32[512,256]{1,0:T(8,128)} %table_hbm.1), custom_call_target="tpu_custom_call" | custom-call | tf_op jit(solution)/shard_map/index/pallas_call | solution.py:490
  2.5 26.7 %all_to_all.74 = s32[128,1,128]{2,1,0:T(1,128)S(1)} all-to-all(s32[128,1,128]{2,1,0:T(1,128)S(1)} %bitcast.36), channel_id=1, replica_groups=mesh['tower'=2,'x'=4,'y'=4,'z'=8] {'x','y','z'}, dimensions={0} | all-to-all | bytes 131072 | tf_op jit(solution)/shard_map/all_to_all | solution.py:503
  29.2 1.2 serve.1
  30.5 23.6 %all_to_all.75 = bf16[128,8,256]{2,1,0:T(8,128)(2,1)S(1)} all-to-all(bf16[128,8,256]{2,1,0:T(8,128)(2,1)S(1)} %bitcast.34), channel_id=1, replica_groups=mesh['tower'=2,'x'=4,'y'=4,'z'=8] {'x','y','z'}, dimensions={0} | all-to-all | bytes 1048576 | tf_op jit(solution)/shard_map/all_to_all | solution.py:513
  54.1 3.6 %item_forward.1 = (bf16[64,1024]{1,0:T(8,128)(2,1)}, f32[16,1024]{1,0:T(8,128)}, f32[16,1024]{1,0:T(8,128)}) custom-call(bf16[1024,256]{1,0:T(8,128)(2,1)S(1)} %bitcast.27, s32[384,128]{1,0:T(8,128)} %get-tuple-element.28.refs_1_, f32[128,256]{1,0:T(8,128)} %refs_2_.4, f32[1,1024]{1,0:T(1,128)} %bitcast.41, bf16[256,1024]{1,0:T(8,128)(2,1)} %refs_5_.3, ...), custom_call_target="tpu_custom_call" | custom-call | tf_op jit(solution)/shard_map/item_forward/pallas_call | solution.py:518
  57.7 3.4 %all-to-all-start.2 = ((bf16[8,8,1024]{2,1,0:T(8,128)(2,1)}), bf16[8,8,1024]{2,1,0:T(8,128)(2,1)S(1)}, u32[]{:S(2)}, u32[]{:S(2)}) async-start(bf16[8,8,1024]{2,1,0:T(8,128)(2,1)} %bitcast.9), calls=%async_computation.2 | async-start | bytes 262144 | tf_op jit(solution)/shard_map/all_to_all | solution.py:529
  61.1 6.6 %user_forward.1 = (bf16[16,1024]{1,0:T(8,128)(2,1)S(1)}, f32[256,1024]{1,0:T(8,128)}, bf16[256,1024]{1,0:T(8,128)(2,1)}, bf16[64,1024]{1,0:T(8,128)(2,1)}, f32[64,64]{1,0:T(8,128)}, /*index=5*/f32[16,1024]{1,0:T(8,128)}) custom-call(bf16[1024,256]{1,0:T(8,128)(2,1)S(1)} %bitcast.28, s32[384,128]{1,0:T(8,128)} %get-tuple-element.28.refs_1_, ...), custom_call_target="tpu_custom_call" | custom-call | tf_op jit(solution)/shard_map/user_forward/pallas_call | solution.py:540
  67.7 1.2 all-to-all-done.2
  68.9 0.9 arrange.1
  69.9 17.3 %all_to_all.76 = bf16[16,40,1024]{2,1,0:T(8,128)(2,1)S(1)} all-to-all(bf16[16,40,1024]{2,1,0:T(8,128)(2,1)S(1)} %bitcast.26), channel_id=1, replica_groups=mesh['tower'=2,'x'=4,'y'=4,'z'=8] {'x','y'}, dimensions={0} | all-to-all | bytes 2621440 | tf_op jit(solution)/shard_map/all_to_all | solution.py:559
  87.1 6.0 %collective-permute-start = (bf16[640,1024]{1,0:T(8,128)(2,1)S(1)}, bf16[640,1024]{1,0:T(8,128)(2,1)S(1)}, u32[]{:S(2)}, u32[]{:S(2)}) collective-permute-start(bf16[640,1024]{1,0:T(8,128)(2,1)S(1)} %bitcast.24), channel_id=1, source_target_pairs={{0,128},{128,0},{1,129},{129,1},{2,130},{130,2},{3,131},{131,3},{4... | collective-permute-start | bytes 3932168 | tf_op jit(solution)/shard_map/ppermute | solution.py:560
  93.2 2.6 %collective-permute-done.swapped_ref = bf16[640,1024]{1,0:T(8,128)(2,1)S(1)} collective-permute-done((bf16[640,1024]{1,0:T(8,128)(2,1)S(1)}, bf16[640,1024]{1,0:T(8,128)(2,1)S(1)}, u32[]{:S(2)}, u32[]{:S(2)}) %collective-permute-start) | collective-permute-done | bytes 1310752 | tf_op jit(solution)/shard_map/ppermute | solution.py:560
  95.8 3.5 %softmax.1 = (f32[16,1024]{1,0:T(8,128)S(1)}, bf16[64,1024]{1,0:T(8,128)(2,1)}, f32[8,128]{1,0:T(8,128)S(1)}) custom-call(s32[2]{0:T(128)S(1)} %pad_add_fusion.place_ref, bf16[640,1024]{1,0:T(8,128)(2,1)S(1)} %bitcast.25, bf16[640,1024]{1,0:T(8,128)(2,1)S(1)} %collective-permute-done.swapped_ref), custom_call_target="tpu_custom_call" | custom-call | tf_op jit(solution)/shard_map/softmax/pallas_call | solution.py:562
  99.3 5.3 %all-to-all-start.4 = ((bf16[8,8,1024]{2,1,0:T(8,128)(2,1)}), bf16[8,8,1024]{2,1,0:T(8,128)(2,1)S(1)}, u32[]{:S(2)}, u32[]{:S(2)}) async-start(bf16[8,8,1024]{2,1,0:T(8,128)(2,1)} %bitcast.15), calls=%async_computation.4 | async-start | bytes 262144 | tf_op jit(solution)/shard_map/all_to_all | solution.py:570
  104.7 7.0 %user_backward.1.d_rows_ref = bf16[256,256]{1,0:T(8,128)(2,1)S(1)} custom-call(f32[16,1024]{1,0:T(8,128)S(1)} %get-tuple-element.32.d_user_ref, f32[16,1024]{1,0:T(8,128)} %get-tuple-element.33.refs_0_, f32[1,1024]{1,0:T(1,128)} %bitcast.40, bf16[1024,1024]{1,0:T(8,128)(2,1)} %refs_2_.5, bf16[1024,1024]{1,0:T(8,128)(2,1)} %refs_3_.3, ...), custom_call_target="tpu_custom_call" | custom-call | tf_op jit(solution)/shard_map/user_backward/pallas_call | solution.py:574
  111.7 0.8 all-to-all-done.4
  112.5 3.3 %item_backward.1 = bf16[1024,256]{1,0:T(8,128)(2,1)S(1)} custom-call(bf16[64,1024]{1,0:T(8,128)(2,1)S(1)} %bitcast.32, bf16[256,256]{1,0:T(8,128)(2,1)S(1)} %user_backward.1.d_rows_ref, s32[8,384]{1,0:T(8,128)} %get-tuple-element.38.refs_0_, f32[1,1024]{1,0:T(1,128)} %bitcast.42, f32[16,1024]{1,0:T(8,128)} %get-tuple-element.39.refs_2_, ...), custom_call_target="tpu_custom_call" | custom-call | tf_op jit(solution)/shard_map/item_backward/pallas_call | solution.py:584
  115.9 28.6 %all_to_all.77 = bf16[128,8,256]{2,1,0:T(8,128)(2,1)S(1)} all-to-all(bf16[128,8,256]{2,1,0:T(8,128)(2,1)S(1)} %bitcast.29), channel_id=1, replica_groups=mesh['tower'=2,'x'=4,'y'=4,'z'=8] {'x','y','z'}, dimensions={0} | all-to-all | bytes 1048576 | tf_op jit(solution)/shard_map/all_to_all | solution.py:594
  145.0 2.8 %collective-permute-start.2 = (bf16[512,256]{1,0:T(8,128)(2,1)S(1)}, bf16[512,256]{1,0:T(8,128)(2,1)S(1)}, u32[]{:S(2)}, u32[]{:S(2)}) collective-permute-start(bf16[512,256]{1,0:T(8,128)(2,1)S(1)} %get-tuple-element.45), channel_id=1, source_target_pairs={{0,128},{128,0},{1,129},{129,1},{2,130},{130,2},{3,131},{131,3},{4... | collective-permute-start | bytes 786440 | tf_op jit(solution)/shard_map/ppermute | solution.py:604
  147.9 1.1 collective-permute-done.1
  148.9 0.8 broadcast_in_dim.2
  149.7 6.1 %all-to-all-start.6 = ((f32[128,1,384]{2,1,0:T(1,128)}), f32[128,1,384]{2,1,0:T(1,128)S(1)}, u32[]{:S(2)}, u32[]{:S(2)}) async-start(f32[128,1,384]{2,1,0:T(1,128)} %broadcast_in_dim.2), calls=%async_computation.6 | async-start | bytes 393216 | tf_op jit(solution)/shard_map/all_to_all | solution.py:605
  155.9 0.8 convert_add_fusion
  156.7 12.2 %all-to-all-done.6 = f32[128,1,384]{2,1,0:T(1,128)S(1)} async-done(((f32[128,1,384]{2,1,0:T(1,128)}), f32[128,1,384]{2,1,0:T(1,128)S(1)}, u32[]{:S(2)}, u32[]{:S(2)}) %all-to-all-start.6) | async-done | bytes 196640 | tf_op jit(solution)/shard_map/all_to_all | solution.py:605
  (9 shorter events, 1.4 us)
Async XLA Ops:
  57.7 11.2 %all-to-all-start.2 = ((bf16[8,8,1024]{2,1,0:T(8,128)(2,1)}), bf16[8,8,1024]{2,1,0:T(8,128)(2,1)S(1)}, u32[]{:S(2)}, u32[]{:S(2)}) async-start(bf16[8,8,1024]{2,1,0:T(8,128)(2,1)} %bitcast.9), calls=%async_computation.2 | async-start | bytes 262144 | tf_op jit(solution)/shard_map/all_to_all | solution.py:529
  87.1 8.7 %collective-permute-start = (bf16[640,1024]{1,0:T(8,128)(2,1)S(1)}, bf16[640,1024]{1,0:T(8,128)(2,1)S(1)}, u32[]{:S(2)}, u32[]{:S(2)}) collective-permute-start(bf16[640,1024]{1,0:T(8,128)(2,1)S(1)} %bitcast.24), channel_id=1, source_target_pairs={{0,128},{128,0},{1,129},{129,1},{2,130},{130,2},{3,131},{131,3},{4... | collective-permute-start | bytes 3932168 | tf_op jit(solution)/shard_map/ppermute | solution.py:560
  99.3 13.2 %all-to-all-start.4 = ((bf16[8,8,1024]{2,1,0:T(8,128)(2,1)}), bf16[8,8,1024]{2,1,0:T(8,128)(2,1)S(1)}, u32[]{:S(2)}, u32[]{:S(2)}) async-start(bf16[8,8,1024]{2,1,0:T(8,128)(2,1)} %bitcast.15), calls=%async_computation.4 | async-start | bytes 262144 | tf_op jit(solution)/shard_map/all_to_all | solution.py:570
  112.5 31.9 %copy-start = (s32[8,1024]{1,0:T(8,128)S(1)}, s32[8,1024]{1,0:T(8,128)}, u32[]{:S(2)}) copy-start(s32[8,1024]{1,0:T(8,128)} %get-tuple-element.41.row_ref) | copy-start | bytes 98308
  145.0 10.9 %collective-permute-start.2 = (bf16[512,256]{1,0:T(8,128)(2,1)S(1)}, bf16[512,256]{1,0:T(8,128)(2,1)S(1)}, u32[]{:S(2)}, u32[]{:S(2)}) collective-permute-start(bf16[512,256]{1,0:T(8,128)(2,1)S(1)} %get-tuple-element.45), channel_id=1, source_target_pairs={{0,128},{128,0},{1,129},{129,1},{2,130},{130,2},{3,131},{131,3},{4... | collective-permute-start | bytes 786440 | tf_op jit(solution)/shard_map/ppermute | solution.py:604
  147.8 1.2 collective-permute-start.1
  149.7 19.2 %all-to-all-start.6 = ((f32[128,1,384]{2,1,0:T(1,128)}), f32[128,1,384]{2,1,0:T(1,128)S(1)}, u32[]{:S(2)}, u32[]{:S(2)}) async-start(f32[128,1,384]{2,1,0:T(1,128)} %broadcast_in_dim.2), calls=%async_computation.6 | async-start | bytes 393216 | tf_op jit(solution)/shard_map/all_to_all | solution.py:605

commit v6 on v5

--- a/solution.py
+++ b/solution.py
@@ -134,6 +134,12 @@
     save.wait()
 
 
+def prefetch_kernel(count, after_ref, *refs):
+    copies = copies_of(zip(refs[:count], refs[count : 2 * count]), refs[2 * count])
+    for copy in copies:
+        copy.wait()
+
+
 def head_mask(heads, width):
     return iota((heads, width), 1) // HEAD_DIM == iota((heads, width), 0)
 
@@ -166,23 +172,21 @@
 
 
 def item_forward_kernel(users, *refs):
-    fetched_ref, sources, refs = refs[0], refs[1:6], refs[6:]
+    fetched_ref, column_ref, hot_ref, item_w2, refs = *refs[:4], refs[4:]
+    sources, refs = refs[:4], refs[4:]
     vectors_ref, kept_hbm, refs = refs[0], refs[1:3], refs[3:]
-    targets, kept, (in_sems, out_sems) = refs[:5], refs[5:7], refs[7:]
-    column_of, hot, gain, item_w1, item_w2 = targets
+    ahead, refs = refs[:2], refs[2:]
+    targets, kept, (in_sems, out_sems) = refs[:2], refs[2:4], refs[4:]
+    item_w1, gain = targets
     inner_ref, outer_ref = kept
-    span = sources[0].shape[0]
-    sources = (sources[0].at[pl.ds(span - 128, PAD)],) + tuple(sources[1:])
-    copies = copies_of(zip(sources, targets), in_sems)
+    copies = copies_of(zip(sources, tuple(targets) + tuple(ahead)), in_sems)
+    span = column_ref.shape[0] - 128
+    rows = look_up(column_ref[span : span + PAD, :], fetched_ref, hot_ref)
     copies[0].wait()
     copies[1].wait()
-    rows = look_up(column_of[...], fetched_ref, hot)
-    copies[2].wait()
-    copies[3].wait()
     inner = dot(rows, item_w1[...])
     inner_ref[...] = inner
     gated = (inner * jax.nn.sigmoid(inner)).astype(BF)
-    copies[4].wait()
     outer = dot(gated, item_w2[...])
     outer_ref[...] = outer
     saves = copies_of(zip(kept, kept_hbm), out_sems)
@@ -190,16 +194,16 @@
     vectors = jnp.where(iota(outer.shape, 0) < users, outer * scale * gain[...], 0.0)
     peers = vectors_ref.shape[0] // 8
     vectors_ref[...] = jnp.concatenate([vectors[0:8]] * peers, axis=0).astype(BF)
-    for save in saves:
-        save.wait()
+    for copy in copies[2:] + saves:
+        copy.wait()
 
 
 def user_forward_kernel(users, *refs):
-    fetched_ref, sources, refs = refs[0], refs[1:11], refs[11:]
+    fetched_ref, column_ref, hot_ref, in_proj, pos_of, refs = *refs[:5], refs[5:]
+    sources, refs = refs[:6], refs[6:]
     vectors_ref, kept_hbm, refs = refs[0], refs[1:6], refs[6:]
-    targets, kept, (in_sems, out_sems) = refs[:10], refs[10:15], refs[15:]
-    column_of, hot, pos_of, norm_gain_ref, out_gain_ref = targets[:5]
-    in_proj, w_query, w_key, w_value, w_out = targets[5:]
+    targets, kept, (in_sems, out_sems) = refs[:6], refs[6:11], refs[11:]
+    norm_gain_ref, w_query, w_key, w_value, w_out, out_gain_ref = targets
     hidden_ref, normed_ref, qk_ref, weights_ref, mixed_ref = kept
     copies = copies_of(zip(sources, targets), in_sems)
     saves = [
@@ -208,13 +212,10 @@
     hist, width = pos_of.shape
     heads = width // HEAD_DIM
     span = users * hist
-    copies[0].wait()
-    copies[1].wait()
-    rows = look_up(column_of[0:span, :], fetched_ref, hot)
-    for copy in copies[2:6]:
-        copy.wait()
+    rows = look_up(column_ref[0:span, :], fetched_ref, hot_ref)
     pos = pos_of[...].astype(F32)
     hidden = dot(rows, in_proj[...]) + jnp.concatenate([pos] * users, axis=0)
+    copies[0].wait()
     hidden_ref[...] = hidden
     saves[0].start()
     scale = lax.rsqrt(jnp.mean(hidden * hidden, axis=-1, keepdims=True) + EPS)
@@ -227,9 +228,9 @@
         axis=0,
     ).astype(BF)
     mask = head_mask(heads, width)
-    copies[6].wait()
+    copies[1].wait()
     query = dot(last, w_query[...]).astype(BF).astype(F32)
-    copies[7].wait()
+    copies[2].wait()
     qk = dot_nt(spread_heads(query, mask, users), w_key[...]).astype(BF)
     qk_ref[...] = qk
     saves[2].start()
@@ -243,9 +244,10 @@
         mixes.append(dot(weights.astype(BF), own))
     saves[3].start()
     mixes = jnp.concatenate(mixes, axis=0).astype(BF)
-    copies[8].wait()
+    copies[3].wait()
     attended = join_heads(dot(mixes, w_value[...]), mask, users).astype(BF)
-    copies[9].wait()
+    copies[4].wait()
+    copies[5].wait()
     hidden_last = jnp.concatenate(
         [hidden[(u + 1) * hist - 1 : (u + 1) * hist] for u in range(users)]
         + [jnp.zeros((PAD - users, width), F32)],
@@ -263,18 +265,24 @@
 def arrange_kernel(users, near, near_ref, vectors_ref, spread_ref):
     total, width = spread_ref.shape
     block = near * users + 8
-    at = iota((total, near * 8), 0) % block
+    pair = 2 * block
+    at = iota((pair, near * 8), 0) % block
     source = jnp.where(at < near * users, at // users * 8 + at % users, -1)
-    item_rows = dot(one_hot(iota((total, near * 8), 1) == source), near_ref[...])
-    at = iota((total, PAD), 0) % block
+    item_rows = dot(one_hot(iota((pair, near * 8), 1) == source), near_ref[...])
+    at = iota((pair, PAD), 0) % block
     source = jnp.where((at >= near * users) & (at < (near + 1) * users), at - near * users, -1)
-    user_rows = dot(one_hot(iota((total, PAD), 1) == source), vectors_ref[...])
-    spread_ref[...] = (item_rows + user_rows).astype(BF)
+    user_rows = dot(one_hot(iota((pair, PAD), 1) == source), vectors_ref[...])
+    rows = (item_rows + user_rows).astype(BF)
+    for i in range(total // pair):
+        spread_ref[i * pair : (i + 1) * pair, :] = rows
 
 
 def softmax_kernel(
-    users, near, scale, place_ref, gathered_ref, swapped_ref, d_user_ref, d_part_ref, loss_ref
+    users, near, scale, place_ref, gathered_ref, swapped_ref, *refs
 ):
+    ahead, refs = refs[:3], refs[3:]
+    d_user_ref, d_part_ref, loss_ref, refs = *refs[:3], refs[3:]
+    copies = copies_of(zip(ahead, refs[:3]), refs[3])
     rows, width = gathered_ref.shape
     items = near * users
     block = items + 8
@@ -340,6 +348,8 @@
     d_user_ref[...] = (scale * d_user).astype(BF).astype(F32)
     each = jnp.sum(jnp.where(valid & target, normalizer - first, 0.0), axis=1, keepdims=True)
     loss_ref[...] = jnp.broadcast_to(jnp.sum(each, axis=0, keepdims=True), loss_ref.shape)
+    for copy in copies:
+        copy.wait()
 
 
 def norm_backward(values, cotangent, gain):
@@ -349,23 +359,22 @@
     return inverse * pulled - values * (inverse * inverse * inverse * along)
 
 
-def user_backward_kernel(users, d_user_ref, *refs):
-    sources, d_rows_ref, refs = refs[:12], refs[12], refs[13:]
-    targets, (d_normed, sems) = refs[:12], refs[12:]
-    mixed_ref, out_gain_ref, w_out, w_value, normed_ref, weights_ref, qk_ref = targets[:7]
-    w_key, w_query, hidden_ref, norm_gain_ref, in_proj = targets[7:]
-    copies = copies_of(zip(sources, targets), sems)
+def user_backward_kernel(users, d_user_ref, mixed_ref, out_gain_ref, w_out, *refs):
+    sources, refs = refs[:15], refs[15:]
+    d_rows_ref, ahead, refs = refs[0], refs[1:7], refs[7:]
+    targets, (d_normed, sems) = refs[:9], refs[9:]
+    w_value, normed_ref, weights_ref, qk_ref, w_key, w_query = targets[:6]
+    hidden_ref, norm_gain_ref, in_proj = targets[6:]
+    copies = copies_of(zip(sources, tuple(targets) + tuple(ahead)), sems)
     span, width = hidden_ref.shape
     hist = span // users
     heads = width // HEAD_DIM
     mask = head_mask(heads, width)
-    for copy in copies[:3]:
-        copy.wait()
     d_mixed = norm_backward(mixed_ref[...], d_user_ref[...], out_gain_ref[...])
     d_attended = dot_nt(d_mixed.astype(BF), w_out[...])
-    copies[3].wait()
+    copies[0].wait()
     d_mixes = dot_nt(spread_heads(d_attended, mask, users), w_value[...]).astype(BF)
-    for copy in copies[4:7]:
+    for copy in copies[1:4]:
         copy.wait()
     d_qk = []
     for u in range(users):
@@ -380,28 +389,27 @@
         )
         d_qk.append(dot(d_scores, own))
     d_qk = jnp.concatenate(d_qk, axis=0).astype(BF)
-    copies[7].wait()
+    copies[4].wait()
     d_query = join_heads(dot(d_qk, w_key[...]), mask, users).astype(BF)
-    copies[8].wait()
+    copies[5].wait()
     d_last = dot_nt(d_query, w_query[...])
     for u in range(users):
         at = slice((u + 1) * hist - 1, (u + 1) * hist)
         d_normed[at, :] = d_normed[at, :] + d_last[u : u + 1]
-    copies[9].wait()
-    copies[10].wait()
+    copies[6].wait()
+    copies[7].wait()
     d_normed[...] = norm_backward(hidden_ref[...], d_normed[...], norm_gain_ref[...])
     for u in range(users):
         at = slice((u + 1) * hist - 1, (u + 1) * hist)
         d_normed[at, :] = d_normed[at, :] + d_mixed[u : u + 1]
-    copies[11].wait()
+    copies[8].wait()
     d_rows_ref[...] = dot_nt(d_normed[...].astype(BF), in_proj[...]).astype(BF)
+    for copy in copies[9:]:
+        copy.wait()
 
 
 def item_backward_kernel(users, parts_ref, d_rows_ref, *refs):
-    sources, outgoing, refs = refs[:6], refs[6], refs[7:]
-    targets, sems = refs[:6], refs[6]
-    row_ref, gain, outer_ref, inner_ref, item_w2, item_w1 = targets
-    copies = copies_of(zip(sources, targets), sems)
+    row_ref, gain, outer_ref, inner_ref, item_w2, item_w1, outgoing = refs
     slots = outgoing.shape[0]
     span = d_rows_ref.shape[0]
     wide = row_ref.shape[1]
@@ -409,18 +417,12 @@
     shape = (PAD, peers)
     added = (iota(shape, 1) % 8 == iota(shape, 0)) & (iota(shape, 0) < users)
     d_item = dot(one_hot(added), parts_ref[...]).astype(BF).astype(F32)
-    copies[0].wait()
     picks = one_hot(iota((slots, wide), 0) == row_ref[0:1, :])
     total = dot(picks[:, 0:span], d_rows_ref[...])
-    copies[1].wait()
-    copies[2].wait()
     d_outer = norm_backward(outer_ref[...], d_item, gain[...])
-    copies[3].wait()
     inner = inner_ref[...]
     gate = jax.nn.sigmoid(inner)
-    copies[4].wait()
     d_inner = dot_nt(d_outer.astype(BF), item_w2[...]) * (gate * (1.0 + inner * (1.0 - gate)))
-    copies[5].wait()
     d_items = dot_nt(d_inner.astype(BF), item_w1[...])
     d_items = jnp.concatenate(
         [d_items, jnp.zeros((wide - span - PAD, d_items.shape[1]), F32)], axis=0
@@ -428,9 +430,9 @@
     outgoing[...] = (total + dot(picks[:, span:], d_items)).astype(BF)
 
 
-def finish_kernel(total, sums_ref, hot_ref, loss_ref):
+def finish_kernel(total, sums_ref, other_ref, hot_ref, loss_ref):
     emb = hot_ref.shape[1]
-    sums = sums_ref[...]
+    sums = sums_ref[...] + other_ref[...]
     hot_ref[...] = sums[:, 0:emb]
     loss_ref[...] = jnp.sum(sums[:, emb : emb + 1], axis=0, keepdims=True) / total
 
@@ -442,8 +444,8 @@
     picks = one_hot(iota((rows, slots), 0) == row_ref[0:1, :])
     part_ref[...] = dot(picks, returned).astype(BF)
     hot = dot(one_hot(iota((PAD, slots), 1) % SLOTS == HOT_SLOT), returned)
-    hot_ref[:, 0:emb] = hot[0:1]
-    hot_ref[:, emb:] = loss_ref[0:1, :]
+    hot_ref[:, 0:emb] = jnp.broadcast_to(hot[0:1], (hot_ref.shape[0], emb))
+    hot_ref[:, emb:] = jnp.broadcast_to(loss_ref[0:1, :], (hot_ref.shape[0], 128))
 
 
 def shards(
@@ -479,6 +481,7 @@
     swap = [(i, towers - 1 - i) for i in range(towers)]
     shape = jax.ShapeDtypeStruct
     sems = lambda n: pltpu.SemaphoreType.DMA((n,))
+    vmem = lambda a: pltpu.VMEM(a.shape, a.dtype)
     hbm = lambda a: pltpu.HBM(a.shape, a.dtype)
     in_hbm = lambda a: pltpu.with_memory_space_constraint(a, pltpu.HBM)
     in_vmem = lambda a: pltpu.with_memory_space_constraint(a, pltpu.VMEM)
@@ -513,23 +516,36 @@
     fetched = exchange(served, SHARD)
 
     norm_gain, out_gain, item_gain = (g.reshape(1, width) for g in (norm_gain, out_gain, item_gain))
-    loads = (column, hot_table, item_gain, item_w1, item_w2)
+    loads = (column, hot_table, item_w2)
+    column_ready, hot_ready, item_w2_ready = pl.pallas_call(
+        functools.partial(prefetch_kernel, len(loads)),
+        out_shape=tuple(map(vmem, loads)),
+        in_specs=[pl.BlockSpec(memory_space=pl.ANY)] + [HBM] * len(loads),
+        out_specs=(VMEM,) * len(loads),
+        scratch_shapes=[sems(len(loads))],
+        compiler_params=params(24),
+        name="prefetch",
+    )(served, *map(in_hbm, loads))
+
+    loads = (item_w1, item_gain)
+    ahead = (in_proj, pos_embed)
     kept = (shape((PAD, width), F32), shape((PAD, width), F32))
-    item_vec, inner, outer = pl.pallas_call(
+    item_vec, inner, outer, in_proj_ready, pos_ready = pl.pallas_call(
         functools.partial(item_forward_kernel, users),
-        out_shape=(shape((near * 8, width), BF), *map(hbm, kept)),
-        in_specs=[VMEM] + [HBM] * 5,
-        out_specs=(VMEM, HBM, HBM),
-        scratch_shapes=[pltpu.VMEM((PAD, 128), jnp.int32)]
-        + like(loads[1:] + kept)
-        + [sems(5), sems(2)],
+        out_shape=(shape((near * 8, width), BF), *map(hbm, kept), *map(vmem, ahead)),
+        in_specs=[VMEM] * 4 + [HBM] * 4,
+        out_specs=(VMEM, HBM, HBM, VMEM, VMEM),
+        scratch_shapes=like(loads + kept) + [sems(4), sems(2)],
         compiler_params=params(24),
         name="item_forward",
-    )(fetched, *map(in_hbm, loads))
+    )(
+        fetched,
+        *map(in_vmem, (column_ready, hot_ready, item_w2_ready)),
+        *map(in_hbm, loads + ahead),
+    )
     near_items = exchange(item_vec, "z")
 
-    loads = (column, hot_table, pos_embed, norm_gain, out_gain)
-    loads += (in_proj, w_query, w_key, w_value, w_out)
+    loads = (norm_gain, w_query, w_key, w_value, w_out, out_gain)
     kept = (
         shape((span, width), F32),
         shape((span, width), BF),
@@ -540,12 +556,16 @@
     user_vec, hidden, normed, qk, weights, mixed = pl.pallas_call(
         functools.partial(user_forward_kernel, users),
         out_shape=(shape((PAD, width), BF), *map(hbm, kept)),
-        in_specs=[VMEM] + [HBM] * len(loads),
+        in_specs=[VMEM] * 5 + [HBM] * len(loads),
         out_specs=(VMEM,) + (HBM,) * len(kept),
         scratch_shapes=like(loads + kept) + [sems(len(loads)), sems(len(kept))],
         compiler_params=params(40),
         name="user_forward",
-    )(fetched, *map(in_hbm, loads))
+    )(
+        fetched,
+        *map(in_vmem, (column_ready, hot_ready, in_proj_ready, pos_ready)),
+        *map(in_hbm, loads),
+    )
 
     rows = owners // near * (near * users + 8)
     spread = pl.pallas_call(
@@ -559,58 +579,63 @@
     gathered = exchange(spread, ("x", "y"))
     swapped = lax.ppermute(gathered, "tower", swap)
     place = jnp.stack([lax.axis_index(("x", "y")), lax.axis_index("z")]).astype(jnp.int32)
-    d_user, d_part, loss = pl.pallas_call(
+    ahead = (mixed, out_gain, w_out)
+    d_user, d_part, loss, *ready = pl.pallas_call(
         functools.partial(softmax_kernel, users, near, scale),
-        out_shape=(shape((PAD, width), F32), shape((near * 8, width), BF), shape((8, 128), F32)),
-        in_specs=[SMEM, VMEM, VMEM],
-        out_specs=(VMEM, VMEM, VMEM),
+        out_shape=(
+            shape((PAD, width), F32),
+            shape((near * 8, width), BF),
+            shape((8, 128), F32),
+            *map(vmem, ahead),
+        ),
+        in_specs=[SMEM, VMEM, VMEM] + [HBM] * 3,
+        out_specs=(VMEM,) * 6,
+        scratch_shapes=[sems(3)],
         compiler_params=params(32),
         name="softmax",
-    )(place, gathered, swapped)
+    )(place, gathered, swapped, *map(in_hbm, ahead))
     parts = exchange(d_part, "z")
 
-    loads = (mixed, out_gain, w_out, w_value, normed, weights, qk)
-    loads += (w_key, w_query, hidden, norm_gain, in_proj)
-    d_rows = pl.pallas_call(
+    loads = (w_value, normed, weights, qk, w_key, w_query, hidden, norm_gain, in_proj)
+    ahead = (row, item_gain, outer, inner, item_w2, item_w1)
+    d_rows, *item_ready = pl.pallas_call(
         functools.partial(user_backward_kernel, users),
-        out_shape=shape((span, emb), BF),
-        in_specs=[VMEM] + [HBM] * len(loads),
-        out_specs=VMEM,
-        scratch_shapes=like(loads) + [pltpu.VMEM((span, width), F32), sems(len(loads))],
+        out_shape=(shape((span, emb), BF), *map(vmem, ahead)),
+        in_specs=[VMEM] * 4 + [HBM] * 15,
+        out_specs=(VMEM,) * 7,
+        scratch_shapes=like(loads) + [pltpu.VMEM((span, width), F32), sems(15)],
         compiler_params=params(40),
         name="user_backward",
-    )(d_user, *map(in_hbm, loads))
-    loads = (row, item_gain, outer, inner, item_w2, item_w1)
+    )(d_user, *map(in_vmem, ready), *map(in_hbm, loads + ahead))
     outgoing = pl.pallas_call(
         functools.partial(item_backward_kernel, users),
         out_shape=shape((slots, emb), BF),
-        in_specs=[VMEM, VMEM] + [HBM] * len(loads),
+        in_specs=[VMEM] * 8,
         out_specs=VMEM,
-        scratch_shapes=like(loads) + [sems(len(loads))],
         compiler_params=params(32),
         name="item_backward",
-    )(parts, d_rows, *map(in_hbm, loads))
+    )(parts, d_rows, *map(in_vmem, item_ready))
 
     returned = exchange(outgoing, SHARD)
     part, mine = pl.pallas_call(
         scatter_kernel,
-        out_shape=(shape((rare_count, emb), BF), shape((1, emb + 128), F32)),
+        out_shape=(shape((rare_count, emb), BF), shape((owners, emb + 128), F32)),
         in_specs=[VMEM, VMEM, VMEM],
         out_specs=(VMEM, VMEM),
         compiler_params=params(24),
         name="scatter",
     )(returned, asked_row, loss)
-    mine = mine + lax.ppermute(mine, "tower", swap)
     rare_grad = part.astype(F32) + lax.ppermute(part, "tower", swap).astype(F32)
-    sums = exchange(jnp.broadcast_to(mine, (owners, emb + 128)), SHARD)
+    sums = exchange(mine, SHARD)
+    other_sums = lax.ppermute(sums, "tower", swap)
     hot_total, loss_total = pl.pallas_call(
         functools.partial(finish_kernel, total),
         out_shape=(shape((owners, emb), F32), shape((1, 1), F32)),
-        in_specs=[VMEM],
+        in_specs=[VMEM, VMEM],
         out_specs=(VMEM, VMEM),
         compiler_params=params(24),
         name="finish",
-    )(sums)
+    )(sums, other_sums)
     return (hot_total, rare_grad, loss_total[0, 0])
 
 

time: 170 us -> 173 us (1.018)
  blocking collectives: 96.1 us -> 73.3 us
  waiting for transfers between devices: 17.9 us -> 29.1 us
  starting transfers between devices: 23.8 us -> 34.2 us
  local copies, waits for them, and re-layouts: 0.81 us -> 6.01 us
    all_to_all x1 -> x0, blocking collectives: 23.6 us -> none  [shards(): fetched = exchange(served, SHARD)]
    all_to_all x1 -> x2, waiting for transfers between devices: 12.2 us -> 26 us  [the longest x1 16.3 us: shards(): fetched = exchange(served, SHARD)]
    all_to_all x1 -> x2, starting transfers between devices: 6.13 us -> 12.7 us  [the longest x1 6.5 us: shards(): sums = exchange(mine, SHARD)]
    unnamed x3 -> x13, local copies, waits for them, and re-layouts: 0.02 us -> 5.13 us
    ppermute x1, starting transfers between devices: 0.1 us -> 3.31 us  [shards(): other_sums = lax.ppermute(sums, 'tower', swap)]
    pallas_call x0 -> x1, Pallas kernels: none -> 1.81 us  [shards(): pl.pallas_call(functools.partial(prefetch_kernel, len(loads)), out_shape=...]
    pallas_call x1, Pallas kernels: 3.34 us -> 1.6 us  [shards(): pl.pallas_call(functools.partial(item_backward_kernel, users), out_shape=...]
  transfers between devices with their start and end apart: 6 -> 7, of which waited for: 5 -> 6; matrix products, arithmetic and copies ran while one was open for 1% -> 1% of each run, Pallas kernels for 8% -> 9%
where the time goes in v6:
time: 173 us
  blocking collectives  73.3 us (42%)
  starting transfers between devices  34.2 us (20%)
  waiting for transfers between devices  29.1 us (17%)
  Pallas kernels  28.3 us (16%)
  local copies, waits for them, and re-layouts  6.01 us (3%)
    all_to_all x1, blocking collectives, shards(): returned = exchange(outgoing, SHARD)  29.3 us
    all_to_all x1, blocking collectives, shards(): asked = exchange(request, SHARD)  26.7 us
    all_to_all x1, blocking collectives, shards(): gathered = exchange(spread, ('x', 'y'))  17.3 us
    all_to_all x1, waiting for transfers between devices, shards(): fetched = exchange(served, SHARD)  16.3 us
    all_to_all x1, waiting for transfers between devices, shards(): sums = exchange(mine, SHARD)  9.67 us
    pallas_call x1, Pallas kernels, shards(): pl.pallas_call(functools.partial(user_forward_kernel, users), out_shape=(...  6.7 us
    all_to_all x1, starting transfers between devices, shards(): sums = exchange(mine, SHARD)  6.5 us
    all_to_all x1, starting transfers between devices, shards(): parts = exchange(d_part, 'z')  6.35 us
  transfers between devices with their start and end apart: 7, of which 6 were waited for; matrix products, arithmetic and copies ran while one was open for 1% of the time, Pallas kernels for 9%

profile of v6, /device:TPU:1, one launch (start us, length us, event | category | flops | bytes accessed | tf_op | source)
XLA Modules:
  0.0 172.6 jit_solution(220917335050888645)
XLA Ops:
  0.6 1.9 %index.1 = (s32[128,128]{1,0:T(8,128)S(1)}, bf16[512,256]{1,0:T(8,128)(2,1)S(1)}, s32[8,384]{1,0:T(8,128)}, s32[384,128]{1,0:T(8,128)}) custom-call(s32[4,64]{1,0:T(4,128)} %history_hbm.1, s32[1,4]{1,0:T(1,128)} %bitcast.46, f32[512,256]{1,0:T(8,128)} %table_hbm.1), custom_call_target="tpu_custom_call" | custom-call | tf_op jit(solution)/shard_map/index/pallas_call | solution.py:493
  2.5 26.7 %all_to_all.77 = s32[128,1,128]{2,1,0:T(1,128)S(1)} all-to-all(s32[128,1,128]{2,1,0:T(1,128)S(1)} %bitcast.39), channel_id=1, replica_groups=mesh['tower'=2,'x'=4,'y'=4,'z'=8] {'x','y','z'}, dimensions={0} | all-to-all | bytes 131072 | tf_op jit(solution)/shard_map/all_to_all | solution.py:506
  29.2 2.0 %serve.1 = (bf16[1024,256]{1,0:T(8,128)(2,1)}, s32[8,1024]{1,0:T(8,128)}) custom-call(s32[128,128]{1,0:T(8,128)S(1)} %bitcast.36, bf16[512,256]{1,0:T(8,128)(2,1)S(1)} %get-tuple-element.41.known_ref), custom_call_target="tpu_custom_call" | custom-call | tf_op jit(solution)/shard_map/serve/pallas_call | solution.py:507
  31.3 6.2 %all-to-all-start.1 = ((bf16[128,8,256]{2,1,0:T(8,128)(2,1)}), bf16[128,8,256]{2,1,0:T(8,128)(2,1)S(1)}, u32[]{:S(2)}, u32[]{:S(2)}) async-start(bf16[128,8,256]{2,1,0:T(8,128)(2,1)} %bitcast.6), calls=%async_computation.1 | async-start | bytes 1048576 | tf_op jit(solution)/shard_map/all_to_all | solution.py:516
  37.5 1.8 %prefetch.1 = (s32[384,128]{1,0:T(8,128)S(1)}, f32[128,256]{1,0:T(8,128)S(1)}, bf16[1024,1024]{1,0:T(8,128)(2,1)S(1)}) custom-call(bf16[1024,256]{1,0:T(8,128)(2,1)} %get-tuple-element.42.after_ref, s32[384,128]{1,0:T(8,128)} %get-tuple-element.43.refs_0_, f32[128,256]{1,0:T(8,128)} %refs_1_.1, bf16[1024,1024]{1,0:T(8,128)(2,1)} %refs_13_.1), custom_call_target="tpu_custom_call" | custom-call | tf_op jit(solution)/shard_map/prefetch/pallas_call | solution.py:520
  39.3 16.3 %all-to-all-done.1 = bf16[128,8,256]{2,1,0:T(8,128)(2,1)S(1)} async-done(((bf16[128,8,256]{2,1,0:T(8,128)(2,1)}), bf16[128,8,256]{2,1,0:T(8,128)(2,1)S(1)}, u32[]{:S(2)}, u32[]{:S(2)}) %all-to-all-start.1) | async-done | bytes 524320 | tf_op jit(solution)/shard_map/all_to_all | solution.py:516
  55.6 2.2 %item_forward.1 = (bf16[64,1024]{1,0:T(8,128)(2,1)S(1)}, f32[16,1024]{1,0:T(8,128)}, f32[16,1024]{1,0:T(8,128)}, bf16[256,1024]{1,0:T(8,128)(2,1)S(1)}, bf16[64,1024]{1,0:T(8,128)(2,1)S(1)}) custom-call(bf16[1024,256]{1,0:T(8,128)(2,1)S(1)} %bitcast.28, s32[384,128]{1,0:T(8,128)S(1)} %get-tuple-element.44.refs_1_, f32[128,256]{1,0:T(8,128)S(1)} %get-tuple-element.45.refs_2_, ...), custom_call_target="tpu_custom_call" | custom-call | tf_op jit(solution)/shard_map/item_forward/pallas_call | solution.py:533
  59.1 3.4 %all-to-all-start.2 = ((bf16[8,8,1024]{2,1,0:T(8,128)(2,1)}), bf16[8,8,1024]{2,1,0:T(8,128)(2,1)S(1)}, u32[]{:S(2)}, u32[]{:S(2)}) async-start(bf16[8,8,1024]{2,1,0:T(8,128)(2,1)} %bitcast.38), calls=%async_computation.2 | async-start | bytes 262144 | tf_op jit(solution)/shard_map/all_to_all | solution.py:546
  62.5 0.9 copy-done.3
  63.4 6.7 %user_forward.1 = (bf16[16,1024]{1,0:T(8,128)(2,1)S(1)}, f32[256,1024]{1,0:T(8,128)}, bf16[256,1024]{1,0:T(8,128)(2,1)}, bf16[64,1024]{1,0:T(8,128)(2,1)}, f32[64,64]{1,0:T(8,128)}, /*index=5*/f32[16,1024]{1,0:T(8,128)}) custom-call(bf16[1024,256]{1,0:T(8,128)(2,1)S(1)} %bitcast.29, s32[384,128]{1,0:T(8,128)S(1)} %get-tuple-element.44.refs_1_, ...), custom_call_target="tpu_custom_call" | custom-call | tf_op jit(solution)/shard_map/user_forward/pallas_call | solution.py:556
  70.7 17.3 %all_to_all.78 = bf16[16,40,1024]{2,1,0:T(8,128)(2,1)S(1)} all-to-all(bf16[16,40,1024]{2,1,0:T(8,128)(2,1)S(1)} %bitcast.25), channel_id=1, replica_groups=mesh['tower'=2,'x'=4,'y'=4,'z'=8] {'x','y'}, dimensions={0} | all-to-all | bytes 2621440 | tf_op jit(solution)/shard_map/all_to_all | solution.py:579
  87.9 6.0 %collective-permute-start = (bf16[640,1024]{1,0:T(8,128)(2,1)S(1)}, bf16[640,1024]{1,0:T(8,128)(2,1)S(1)}, u32[]{:S(2)}, u32[]{:S(2)}) collective-permute-start(bf16[640,1024]{1,0:T(8,128)(2,1)S(1)} %bitcast.26), channel_id=1, source_target_pairs={{0,128},{128,0},{1,129},{129,1},{2,130},{130,2},{3,131},{131,3},{4... | collective-permute-start | bytes 3932168 | tf_op jit(solution)/shard_map/ppermute | solution.py:580
  94.0 2.6 %collective-permute-done.swapped_ref = bf16[640,1024]{1,0:T(8,128)(2,1)S(1)} collective-permute-done((bf16[640,1024]{1,0:T(8,128)(2,1)S(1)}, bf16[640,1024]{1,0:T(8,128)(2,1)S(1)}, u32[]{:S(2)}, u32[]{:S(2)}) %collective-permute-start) | collective-permute-done | bytes 1310752 | tf_op jit(solution)/shard_map/ppermute | solution.py:580
  96.6 4.4 %softmax.1 = (f32[16,1024]{1,0:T(8,128)S(1)}, bf16[64,1024]{1,0:T(8,128)(2,1)}, f32[8,128]{1,0:T(8,128)S(1)}, f32[16,1024]{1,0:T(8,128)S(1)}, f32[1,1024]{1,0:T(1,128)S(1)}, /*index=5*/bf16[1024,1024]{1,0:T(8,128)(2,1)S(1)}) custom-call(s32[2]{0:T(128)S(1)} %pad_add_fusion.place_ref, bf16[640,1024]{1,0:T(8,128)(2,1)S(1)} %bitcast.27, ...), custom_call_target="tpu_custom_call" | custom-call | tf_op jit(solution)/shard_map/softmax/pallas_call | solution.py:583
  101.0 1.3 copy-done
  102.3 6.4 %all-to-all-start.4 = ((bf16[8,8,1024]{2,1,0:T(8,128)(2,1)}), bf16[8,8,1024]{2,1,0:T(8,128)(2,1)S(1)}, u32[]{:S(2)}, u32[]{:S(2)}) async-start(bf16[8,8,1024]{2,1,0:T(8,128)(2,1)} %bitcast.15), calls=%async_computation.4 | async-start | bytes 262144 | tf_op jit(solution)/shard_map/all_to_all | solution.py:597
  108.7 1.6 copy-done.1
  110.3 6.2 %user_backward.1 = (bf16[256,256]{1,0:T(8,128)(2,1)S(1)}, s32[8,384]{1,0:T(8,128)S(1)}, f32[1,1024]{1,0:T(1,128)S(1)}, f32[16,1024]{1,0:T(8,128)S(1)}, f32[16,10...) custom-call(f32[16,1024]{1,0:T(8,128)S(1)} %get-tuple-element.53.d_user_ref, ...), custom_call_target="tpu_custom_call" | custom-call | tf_op jit(solution)/shard_map/user_backward/pallas_call | solution.py:601
  116.6 1.6 item_backward.1
  118.2 29.3 %all_to_all.79 = bf16[128,8,256]{2,1,0:T(8,128)(2,1)S(1)} all-to-all(bf16[128,8,256]{2,1,0:T(8,128)(2,1)S(1)} %bitcast.30), channel_id=1, replica_groups=mesh['tower'=2,'x'=4,'y'=4,'z'=8] {'x','y','z'}, dimensions={0} | all-to-all | bytes 1048576 | tf_op jit(solution)/shard_map/all_to_all | solution.py:619
  148.9 6.5 %all-to-all-start.6 = ((f32[128,1,384]{2,1,0:T(1,128)}), f32[128,1,384]{2,1,0:T(1,128)S(1)}, u32[]{:S(2)}, u32[]{:S(2)}) async-start(f32[128,1,384]{2,1,0:T(1,128)} %copy.19), calls=%async_computation.6 | async-start | bytes 393216 | tf_op jit(solution)/shard_map/all_to_all | solution.py:629
  155.4 2.5 %collective-permute-start.2 = (bf16[512,256]{1,0:T(8,128)(2,1)S(1)}, bf16[512,256]{1,0:T(8,128)(2,1)S(1)}, u32[]{:S(2)}, u32[]{:S(2)}) collective-permute-start(bf16[512,256]{1,0:T(8,128)(2,1)S(1)} %get-tuple-element.75), channel_id=1, source_target_pairs={{0,128},{128,0},{1,129},{129,1},{2,130},{130,2},{3,131},{131,3},{4... | collective-permute-start | bytes 786440 | tf_op jit(solution)/shard_map/ppermute | solution.py:628
  157.9 9.7 %all-to-all-done.6 = f32[128,1,384]{2,1,0:T(1,128)S(1)} async-done(((f32[128,1,384]{2,1,0:T(1,128)}), f32[128,1,384]{2,1,0:T(1,128)S(1)}, u32[]{:S(2)}, u32[]{:S(2)}) %all-to-all-start.6) | async-done | bytes 196640 | tf_op jit(solution)/shard_map/all_to_all | solution.py:629
  167.6 3.3 %collective-permute-start.1 = (f32[128,384]{1,0:T(8,128)S(1)}, f32[128,384]{1,0:T(8,128)S(1)}, u32[]{:S(2)}, u32[]{:S(2)}) collective-permute-start(f32[128,384]{1,0:T(8,128)S(1)} %bitcast.32), channel_id=1, source_target_pairs={{0,128},{128,0},{1,129},{129,1},{2,130},{130,2},{3,131},{131,3},{4... | collective-permute-start | bytes 589832 | tf_op jit(solution)/shard_map/ppermute | solution.py:630
  (20 shorter events, 5.1 us)
Async XLA Ops:
  31.3 24.3 %all-to-all-start.1 = ((bf16[128,8,256]{2,1,0:T(8,128)(2,1)}), bf16[128,8,256]{2,1,0:T(8,128)(2,1)S(1)}, u32[]{:S(2)}, u32[]{:S(2)}) async-start(bf16[128,8,256]{2,1,0:T(8,128)(2,1)} %bitcast.6), calls=%async_computation.1 | async-start | bytes 1048576 | tf_op jit(solution)/shard_map/all_to_all | solution.py:516
  57.8 0.7 copy-start.2
  58.5 0.7 copy-start.4
  59.1 11.2 %all-to-all-start.2 = ((bf16[8,8,1024]{2,1,0:T(8,128)(2,1)}), bf16[8,8,1024]{2,1,0:T(8,128)(2,1)S(1)}, u32[]{:S(2)}, u32[]{:S(2)}) async-start(bf16[8,8,1024]{2,1,0:T(8,128)(2,1)} %bitcast.38), calls=%async_computation.2 | async-start | bytes 262144 | tf_op jit(solution)/shard_map/all_to_all | solution.py:546
  62.5 0.9 copy-start.3
  87.9 8.7 %collective-permute-start = (bf16[640,1024]{1,0:T(8,128)(2,1)S(1)}, bf16[640,1024]{1,0:T(8,128)(2,1)S(1)}, u32[]{:S(2)}, u32[]{:S(2)}) collective-permute-start(bf16[640,1024]{1,0:T(8,128)(2,1)S(1)} %bitcast.26), channel_id=1, source_target_pairs={{0,128},{128,0},{1,129},{129,1},{2,130},{130,2},{3,131},{131,3},{4... | collective-permute-start | bytes 3932168 | tf_op jit(solution)/shard_map/ppermute | solution.py:580
  101.0 1.3 copy-start
  102.3 14.3 %all-to-all-start.4 = ((bf16[8,8,1024]{2,1,0:T(8,128)(2,1)}), bf16[8,8,1024]{2,1,0:T(8,128)(2,1)S(1)}, u32[]{:S(2)}, u32[]{:S(2)}) async-start(bf16[8,8,1024]{2,1,0:T(8,128)(2,1)} %bitcast.15), calls=%async_computation.4 | async-start | bytes 262144 | tf_op jit(solution)/shard_map/all_to_all | solution.py:597
  108.7 1.6 copy-start.1
  116.6 30.9 %copy-start.5 = (s32[8,1024]{1,0:T(8,128)S(1)}, s32[8,1024]{1,0:T(8,128)}, u32[]{:S(2)}) copy-start(s32[8,1024]{1,0:T(8,128)} %get-tuple-element.71.row_ref) | copy-start | bytes 98308
  148.9 18.6 %all-to-all-start.6 = ((f32[128,1,384]{2,1,0:T(1,128)}), f32[128,1,384]{2,1,0:T(1,128)S(1)}, u32[]{:S(2)}, u32[]{:S(2)}) async-start(f32[128,1,384]{2,1,0:T(1,128)} %copy.19), calls=%async_computation.6 | async-start | bytes 393216 | tf_op jit(solution)/shard_map/all_to_all | solution.py:629
  155.4 15.4 %collective-permute-start.2 = (bf16[512,256]{1,0:T(8,128)(2,1)S(1)}, bf16[512,256]{1,0:T(8,128)(2,1)S(1)}, u32[]{:S(2)}, u32[]{:S(2)}) collective-permute-start(bf16[512,256]{1,0:T(8,128)(2,1)S(1)} %get-tuple-element.75), channel_id=1, source_target_pairs={{0,128},{128,0},{1,129},{129,1},{2,130},{130,2},{3,131},{131,3},{4... | collective-permute-start | bytes 786440 | tf_op jit(solution)/shard_map/ppermute | solution.py:628
  167.6 4.4 %collective-permute-start.1 = (f32[128,384]{1,0:T(8,128)S(1)}, f32[128,384]{1,0:T(8,128)S(1)}, u32[]{:S(2)}, u32[]{:S(2)}) collective-permute-start(f32[128,384]{1,0:T(8,128)S(1)} %bitcast.32), channel_id=1, source_target_pairs={{0,128},{128,0},{1,129},{129,1},{2,130},{130,2},{3,131},{131,3},{4... | collective-permute-start | bytes 589832 | tf_op jit(solution)/shard_map/ppermute | solution.py:630

commit v7 on v5

--- a/solution.py
+++ b/solution.py
@@ -233,16 +233,14 @@
     qk = dot_nt(spread_heads(query, mask, users), w_key[...]).astype(BF)
     qk_ref[...] = qk
     saves[2].start()
-    mixes = []
-    for u in range(users):
-        own = normed[u * hist : (u + 1) * hist]
-        scores = dot_nt(qk[u * heads : (u + 1) * heads], own) * (1.0 / math.sqrt(HEAD_DIM))
-        raised = jnp.exp(scores - jnp.max(scores, axis=1, keepdims=True))
-        weights = raised / jnp.sum(raised, axis=1, keepdims=True)
-        weights_ref[u * heads : (u + 1) * heads, :] = weights
-        mixes.append(dot(weights.astype(BF), own))
+    shape = (users * heads, span)
+    own = iota(shape, 0) // heads == iota(shape, 1) // hist
+    scores = jnp.where(own, dot_nt(qk, normed) * (1.0 / math.sqrt(HEAD_DIM)), -jnp.inf)
+    raised = jnp.exp(scores - jnp.max(scores, axis=1, keepdims=True))
+    weights = raised / jnp.sum(raised, axis=1, keepdims=True)
+    weights_ref[...] = weights
     saves[3].start()
-    mixes = jnp.concatenate(mixes, axis=0).astype(BF)
+    mixes = dot(weights.astype(BF), normed).astype(BF)
     copies[8].wait()
     attended = join_heads(dot(mixes, w_value[...]), mask, users).astype(BF)
     copies[9].wait()
@@ -263,17 +261,20 @@
 def arrange_kernel(users, near, near_ref, vectors_ref, spread_ref):
     total, width = spread_ref.shape
     block = near * users + 8
-    at = iota((total, near * 8), 0) % block
+    pair = 2 * block
+    at = iota((pair, near * 8), 0) % block
     source = jnp.where(at < near * users, at // users * 8 + at % users, -1)
-    item_rows = dot(one_hot(iota((total, near * 8), 1) == source), near_ref[...])
-    at = iota((total, PAD), 0) % block
+    item_rows = dot(one_hot(iota((pair, near * 8), 1) == source), near_ref[...])
+    at = iota((pair, PAD), 0) % block
     source = jnp.where((at >= near * users) & (at < (near + 1) * users), at - near * users, -1)
-    user_rows = dot(one_hot(iota((total, PAD), 1) == source), vectors_ref[...])
-    spread_ref[...] = (item_rows + user_rows).astype(BF)
+    user_rows = dot(one_hot(iota((pair, PAD), 1) == source), vectors_ref[...])
+    rows = (item_rows + user_rows).astype(BF)
+    for i in range(total // pair):
+        spread_ref[i * pair : (i + 1) * pair, :] = rows
 
 
 def softmax_kernel(
-    users, near, scale, place_ref, gathered_ref, swapped_ref, d_user_ref, d_part_ref, loss_ref
+    users, near, scale, place_ref, gathered_ref, swapped_ref, d_user_ref, d_part_ref, loss_ref, raised_ref
 ):
     rows, width = gathered_ref.shape
     items = near * users
@@ -281,65 +282,48 @@
     blocks = rows // block
     mine, plane = place_ref[0], place_ref[1]
     own, other = gathered_ref[...], swapped_ref[...]
-
-    def source_of_users(shape):
-        line = iota(shape, 0)
-        return line // users * block + items + line % users
-
-    group = (blocks * users, rows)
-    at_group = iota(group, 1) == source_of_users(group)
-    line = (near * 8, rows)
-    at_line = (iota(line, 0) % 8 < users) & (
-        iota(line, 1) == mine * block + iota(line, 0) // 8 * users + iota(line, 0) % 8
-    )
-    self = (PAD, rows)
-    at_self = (iota(self, 0) < users) & (iota(self, 1) == mine * block + items + iota(self, 0))
-    picked = dot(jnp.concatenate([one_hot(at_group), one_hot(at_line), one_hot(at_self)], axis=0), own)
-    own_users = picked[0 : blocks * users].astype(BF)
-    line_items = picked[blocks * users : blocks * users + near * 8].astype(BF)
-    self_users = picked[blocks * users + near * 8 :].astype(BF)
-    other_users = dot(one_hot(at_group), other).astype(BF)
-    group_users = jnp.concatenate([own_users, other_users], axis=0)
+    shape = (blocks * users, rows)
+    line = iota(shape, 0)
+    picks = one_hot(iota(shape, 1) == line // users * block + items + line % users)
+    group_users = jnp.concatenate([dot(picks, own), dot(picks, other)], axis=0).astype(BF)
     total = 2 * blocks * users
 
-    valid = iota((rows, total), 0) % block < items
+    shape = (rows, total)
+    line = iota(shape, 0)
+    valid = line % block < items
     first = jnp.where(valid, scale * dot_nt(own, group_users), -jnp.inf)
     second = jnp.where(valid, scale * dot_nt(other, group_users), -jnp.inf)
     top = jnp.maximum(
         jnp.max(first, axis=0, keepdims=True), jnp.max(second, axis=0, keepdims=True)
     )
-    count = jnp.sum(jnp.exp(first - top), axis=0, keepdims=True) + jnp.sum(
-        jnp.exp(second - top), axis=0, keepdims=True
-    )
-    normalizer = top + jnp.log(count)
-    shape = (near * 8, total)
-    which = iota(shape, 0)
-    target = (which // 8 == plane) & (iota(shape, 1) == mine * users + which % 8)
-    slope = jnp.exp(scale * dot_nt(line_items, group_users) - normalizer)
-    slope = jnp.where(which % 8 < users, slope - jnp.where(target, 1.0, 0.0), 0.0).astype(BF)
-    d_part_ref[...] = (scale * dot(slope, group_users)).astype(BF)
-
-    shape = (PAD, rows)
-    lanes = iota(shape, 1)
-    real = lanes % block < items
-    valid = iota(shape, 0) < users
-    target = lanes == mine * block + plane * users + iota(shape, 0)
-    first = jnp.where(real, scale * dot_nt(self_users, own), -jnp.inf)
-    second = jnp.where(real, scale * dot_nt(self_users, other), -jnp.inf)
-    top = jnp.maximum(
-        jnp.max(first, axis=1, keepdims=True), jnp.max(second, axis=1, keepdims=True)
-    )
-    count = jnp.sum(jnp.exp(first - top), axis=1, keepdims=True) + jnp.sum(
-        jnp.exp(second - top), axis=1, keepdims=True
-    )
-    normalizer = top + jnp.log(count)
-    slope = jnp.exp(first - normalizer) - jnp.where(target, 1.0, 0.0)
-    d_user = dot(jnp.where(valid, slope, 0.0).astype(BF), own)
-    slope = jnp.exp(second - normalizer)
-    d_user = d_user + dot(jnp.where(valid, slope, 0.0).astype(BF), other)
+    raised = jnp.exp(first - top)
+    raised_ref[...] = raised
+    other_raised = jnp.exp(second - top)
+    count = jnp.sum(raised, axis=0, keepdims=True) + jnp.sum(other_raised, axis=0, keepdims=True)
+    share = 1.0 / count
+
+    line = (items, total)
+    target = (iota(line, 0) // users == plane) & (
+        iota(line, 1) == mine * users + iota(line, 0) % users
+    )
+    near_raised = raised_ref[pl.ds(pl.multiple_of(mine * block, 8), items), :]
+    slope = (near_raised * share - jnp.where(target, 1.0, 0.0)).astype(BF)
+    apart = (near * 8, items)
+    at = iota(apart, 0)
+    apart = one_hot((at % 8 < users) & (iota(apart, 1) == at // 8 * users + at % 8))
+    d_part_ref[...] = (scale * dot(dot(apart, slope).astype(BF), group_users)).astype(BF)
+
+    who = iota(shape, 1) - mine * users
+    target = (who >= 0) & (who < users) & (iota(shape, 0) == mine * block + plane * users + who)
+    slope = (raised * share - jnp.where(target, 1.0, 0.0)).astype(BF)
+    other_slope = (other_raised * share).astype(BF)
+    self = (PAD, total)
+    self = one_hot((iota(self, 0) < users) & (iota(self, 1) == mine * users + iota(self, 0)))
+    d_user = dot(dot_nt(self, slope).astype(BF), own)
+    d_user = d_user + dot(dot_nt(self, other_slope).astype(BF), other)
     d_user_ref[...] = (scale * d_user).astype(BF).astype(F32)
-    each = jnp.sum(jnp.where(valid & target, normalizer - first, 0.0), axis=1, keepdims=True)
-    loss_ref[...] = jnp.broadcast_to(jnp.sum(each, axis=0, keepdims=True), loss_ref.shape)
+    each = jnp.sum(jnp.where(target, top + jnp.log(count) - first, 0.0), axis=0, keepdims=True)
+    loss_ref[...] = jnp.broadcast_to(jnp.sum(each, axis=1, keepdims=True), loss_ref.shape)
 
 
 def norm_backward(values, cotangent, gain):
@@ -350,11 +334,12 @@
 
 
 def user_backward_kernel(users, d_user_ref, *refs):
-    sources, d_rows_ref, refs = refs[:12], refs[12], refs[13:]
+    sources, refs = refs[:18], refs[18:]
+    d_rows_ref, ahead, refs = refs[0], refs[1:7], refs[7:]
     targets, (d_normed, sems) = refs[:12], refs[12:]
     mixed_ref, out_gain_ref, w_out, w_value, normed_ref, weights_ref, qk_ref = targets[:7]
     w_key, w_query, hidden_ref, norm_gain_ref, in_proj = targets[7:]
-    copies = copies_of(zip(sources, targets), sems)
+    copies = copies_of(zip(sources, tuple(targets) + tuple(ahead)), sems)
     span, width = hidden_ref.shape
     hist = span // users
     heads = width // HEAD_DIM
@@ -367,19 +352,18 @@
     d_mixes = dot_nt(spread_heads(d_attended, mask, users), w_value[...]).astype(BF)
     for copy in copies[4:7]:
         copy.wait()
-    d_qk = []
-    for u in range(users):
-        own = normed_ref[u * hist : (u + 1) * hist, :]
-        weights = weights_ref[u * heads : (u + 1) * heads, :]
-        pulled = d_mixes[u * heads : (u + 1) * heads]
-        d_weights = dot_nt(pulled, own)
-        d_scores = weights * (d_weights - jnp.sum(weights * d_weights, axis=1, keepdims=True))
-        d_scores = (d_scores * (1.0 / math.sqrt(HEAD_DIM))).astype(BF)
-        d_normed[u * hist : (u + 1) * hist, :] = dot_tn(weights.astype(BF), pulled) + dot_tn(
-            d_scores, qk_ref[u * heads : (u + 1) * heads, :]
-        )
-        d_qk.append(dot(d_scores, own))
-    d_qk = jnp.concatenate(d_qk, axis=0).astype(BF)
+    normed = normed_ref[...]
+    weights = weights_ref[...]
+    shape = weights.shape
+    own = iota(shape, 0) // heads == iota(shape, 1) // hist
+    d_weights = jnp.where(own, dot_nt(d_mixes, normed), 0.0)
+    d_scores = weights * (d_weights - jnp.sum(weights * d_weights, axis=1, keepdims=True))
+    d_scores = (d_scores * (1.0 / math.sqrt(HEAD_DIM))).astype(BF)
+    d_normed[...] = dot_tn(
+        jnp.concatenate([weights.astype(BF), d_scores], axis=0),
+        jnp.concatenate([d_mixes, qk_ref[...]], axis=0),
+    )
+    d_qk = dot(d_scores, normed).astype(BF)
     copies[7].wait()
     d_query = join_heads(dot(d_qk, w_key[...]), mask, users).astype(BF)
     copies[8].wait()
@@ -395,13 +379,12 @@
         d_normed[at, :] = d_normed[at, :] + d_mixed[u : u + 1]
     copies[11].wait()
     d_rows_ref[...] = dot_nt(d_normed[...].astype(BF), in_proj[...]).astype(BF)
+    for copy in copies[12:]:
+        copy.wait()
 
 
 def item_backward_kernel(users, parts_ref, d_rows_ref, *refs):
-    sources, outgoing, refs = refs[:6], refs[6], refs[7:]
-    targets, sems = refs[:6], refs[6]
-    row_ref, gain, outer_ref, inner_ref, item_w2, item_w1 = targets
-    copies = copies_of(zip(sources, targets), sems)
+    row_ref, gain, outer_ref, inner_ref, item_w2, item_w1, outgoing = refs
     slots = outgoing.shape[0]
     span = d_rows_ref.shape[0]
     wide = row_ref.shape[1]
@@ -409,18 +392,12 @@
     shape = (PAD, peers)
     added = (iota(shape, 1) % 8 == iota(shape, 0)) & (iota(shape, 0) < users)
     d_item = dot(one_hot(added), parts_ref[...]).astype(BF).astype(F32)
-    copies[0].wait()
     picks = one_hot(iota((slots, wide), 0) == row_ref[0:1, :])
     total = dot(picks[:, 0:span], d_rows_ref[...])
-    copies[1].wait()
-    copies[2].wait()
     d_outer = norm_backward(outer_ref[...], d_item, gain[...])
-    copies[3].wait()
     inner = inner_ref[...]
     gate = jax.nn.sigmoid(inner)
-    copies[4].wait()
     d_inner = dot_nt(d_outer.astype(BF), item_w2[...]) * (gate * (1.0 + inner * (1.0 - gate)))
-    copies[5].wait()
     d_items = dot_nt(d_inner.astype(BF), item_w1[...])
     d_items = jnp.concatenate(
         [d_items, jnp.zeros((wide - span - PAD, d_items.shape[1]), F32)], axis=0
@@ -428,9 +405,9 @@
     outgoing[...] = (total + dot(picks[:, span:], d_items)).astype(BF)
 
 
-def finish_kernel(total, sums_ref, hot_ref, loss_ref):
+def finish_kernel(total, sums_ref, other_ref, hot_ref, loss_ref):
     emb = hot_ref.shape[1]
-    sums = sums_ref[...]
+    sums = sums_ref[:, 0, :] + other_ref[:, 0, :]
     hot_ref[...] = sums[:, 0:emb]
     loss_ref[...] = jnp.sum(sums[:, emb : emb + 1], axis=0, keepdims=True) / total
 
@@ -442,8 +419,8 @@
     picks = one_hot(iota((rows, slots), 0) == row_ref[0:1, :])
     part_ref[...] = dot(picks, returned).astype(BF)
     hot = dot(one_hot(iota((PAD, slots), 1) % SLOTS == HOT_SLOT), returned)
-    hot_ref[:, 0:emb] = hot[0:1]
-    hot_ref[:, emb:] = loss_ref[0:1, :]
+    line = jnp.concatenate([hot[0:1], loss_ref[0:1, :]], axis=1)
+    hot_ref[...] = jnp.broadcast_to(line[None], hot_ref.shape)
 
 
 def shards(
@@ -479,6 +456,7 @@
     swap = [(i, towers - 1 - i) for i in range(towers)]
     shape = jax.ShapeDtypeStruct
     sems = lambda n: pltpu.SemaphoreType.DMA((n,))
+    vmem = lambda a: pltpu.VMEM(a.shape, a.dtype)
     hbm = lambda a: pltpu.HBM(a.shape, a.dtype)
     in_hbm = lambda a: pltpu.with_memory_space_constraint(a, pltpu.HBM)
     in_vmem = lambda a: pltpu.with_memory_space_constraint(a, pltpu.VMEM)
@@ -534,7 +512,7 @@
         shape((span, width), F32),
         shape((span, width), BF),
         shape((users * heads, width), BF),
-        shape((users * heads, hist), F32),
+        shape((users * heads, span), F32),
         shape((PAD, width), F32),
     )
     user_vec, hidden, normed, qk, weights, mixed = pl.pallas_call(
@@ -564,6 +542,7 @@
         out_shape=(shape((PAD, width), F32), shape((near * 8, width), BF), shape((8, 128), F32)),
         in_specs=[SMEM, VMEM, VMEM],
         out_specs=(VMEM, VMEM, VMEM),
+        scratch_shapes=[pltpu.VMEM((rows, 2 * owners // near * users), F32)],
         compiler_params=params(32),
         name="softmax",
     )(place, gathered, swapped)
@@ -571,46 +550,45 @@
 
     loads = (mixed, out_gain, w_out, w_value, normed, weights, qk)
     loads += (w_key, w_query, hidden, norm_gain, in_proj)
-    d_rows = pl.pallas_call(
+    ahead = (row, item_gain, outer, inner, item_w2, item_w1)
+    d_rows, *item_ready = pl.pallas_call(
         functools.partial(user_backward_kernel, users),
-        out_shape=shape((span, emb), BF),
-        in_specs=[VMEM] + [HBM] * len(loads),
-        out_specs=VMEM,
-        scratch_shapes=like(loads) + [pltpu.VMEM((span, width), F32), sems(len(loads))],
+        out_shape=(shape((span, emb), BF), *map(vmem, ahead)),
+        in_specs=[VMEM] + [HBM] * 18,
+        out_specs=(VMEM,) * 7,
+        scratch_shapes=like(loads) + [pltpu.VMEM((span, width), F32), sems(18)],
         compiler_params=params(40),
         name="user_backward",
-    )(d_user, *map(in_hbm, loads))
-    loads = (row, item_gain, outer, inner, item_w2, item_w1)
+    )(d_user, *map(in_hbm, loads + ahead))
     outgoing = pl.pallas_call(
         functools.partial(item_backward_kernel, users),
         out_shape=shape((slots, emb), BF),
-        in_specs=[VMEM, VMEM] + [HBM] * len(loads),
+        in_specs=[VMEM] * 8,
         out_specs=VMEM,
-        scratch_shapes=like(loads) + [sems(len(loads))],
         compiler_params=params(32),
         name="item_backward",
-    )(parts, d_rows, *map(in_hbm, loads))
+    )(parts, d_rows, *map(in_vmem, item_ready))
 
     returned = exchange(outgoing, SHARD)
     part, mine = pl.pallas_call(
         scatter_kernel,
-        out_shape=(shape((rare_count, emb), BF), shape((1, emb + 128), F32)),
+        out_shape=(shape((rare_count, emb), BF), shape((owners, 1, emb + 128), F32)),
         in_specs=[VMEM, VMEM, VMEM],
         out_specs=(VMEM, VMEM),
         compiler_params=params(24),
         name="scatter",
     )(returned, asked_row, loss)
-    mine = mine + lax.ppermute(mine, "tower", swap)
     rare_grad = part.astype(F32) + lax.ppermute(part, "tower", swap).astype(F32)
-    sums = exchange(jnp.broadcast_to(mine, (owners, emb + 128)), SHARD)
+    sums = exchange(mine, SHARD)
+    other_sums = lax.ppermute(sums, "tower", swap)
     hot_total, loss_total = pl.pallas_call(
         functools.partial(finish_kernel, total),
         out_shape=(shape((owners, emb), F32), shape((1, 1), F32)),
-        in_specs=[VMEM],
+        in_specs=[VMEM, VMEM],
         out_specs=(VMEM, VMEM),
         compiler_params=params(24),
         name="finish",
-    )(sums)
+    )(sums, other_sums)
     return (hot_total, rare_grad, loss_total[0, 0])
 
 

time: 170 us -> 165 us (0.971)
  Pallas kernels: 29.3 us -> 25.6 us
  starting transfers between devices: 23.8 us -> 26.1 us
  waiting for transfers between devices: 17.9 us -> 16.1 us
    ppermute x1, starting transfers between devices: 0.1 us -> 3.22 us  [shards(): other_sums = lax.ppermute(sums, 'tower', swap)]
    all_to_all x1, waiting for transfers between devices: 12.2 us -> 9.66 us  [shards(): sums = exchange(mine, SHARD)]
    pallas_call x1, Pallas kernels: 3.34 us -> 1.6 us  [shards(): pl.pallas_call(functools.partial(item_backward_kernel, users), out_shape=...]
  transfers between devices with their start and end apart: 6 -> 6, of which waited for: 5 -> 5; matrix products, arithmetic and copies ran while one was open for 1% -> 1% of each run, Pallas kernels for 8% -> 7%
where the time goes in v7:
time: 165 us
  blocking collectives  95.4 us (58%)
  starting transfers between devices  26.1 us (16%)
  Pallas kernels  25.6 us (16%)
  waiting for transfers between devices  16.1 us (10%)
    all_to_all x1, blocking collectives, shards(): returned = exchange(outgoing, SHARD)  27.9 us
    all_to_all x1, blocking collectives, shards(): asked = exchange(request, SHARD)  26.7 us
    all_to_all x1, blocking collectives, shards(): fetched = exchange(served, SHARD)  23.6 us
    all_to_all x1, blocking collectives, shards(): gathered = exchange(spread, ('x', 'y'))  17.2 us
    all_to_all x1, waiting for transfers between devices, shards(): sums = exchange(mine, SHARD)  9.66 us
    all_to_all x1, starting transfers between devices, shards(): sums = exchange(mine, SHARD)  6.5 us
    pallas_call x1, Pallas kernels, shards(): pl.pallas_call(functools.partial(user_backward_kernel, users), out_shape=...  6.34 us
    ppermute x1, starting transfers between devices, shards(): swapped = lax.ppermute(gathered, 'tower', swap)  6.04 us
  transfers between devices with their start and end apart: 6, of which 5 were waited for; matrix products, arithmetic and copies ran while one was open for 1% of the time, Pallas kernels for 7%

profile of v7, /device:TPU:1, one launch (start us, length us, event | category | flops | bytes accessed | tf_op | source)
XLA Modules:
  0.0 164.8 jit_solution(1887376416436541735)
XLA Ops:
  0.6 1.9 %index.1 = (s32[128,128]{1,0:T(8,128)S(1)}, bf16[512,256]{1,0:T(8,128)(2,1)S(1)}, s32[8,384]{1,0:T(8,128)}, s32[384,128]{1,0:T(8,128)}) custom-call(s32[4,64]{1,0:T(4,128)} %history_hbm.1, s32[1,4]{1,0:T(1,128)} %bitcast.39, f32[512,256]{1,0:T(8,128)} %table_hbm.1), custom_call_target="tpu_custom_call" | custom-call | tf_op jit(solution)/shard_map/index/pallas_call | solution.py:468
  2.5 26.7 %all_to_all.71 = s32[128,1,128]{2,1,0:T(1,128)S(1)} all-to-all(s32[128,1,128]{2,1,0:T(1,128)S(1)} %bitcast.32), channel_id=1, replica_groups=mesh['tower'=2,'x'=4,'y'=4,'z'=8] {'x','y','z'}, dimensions={0} | all-to-all | bytes 131072 | tf_op jit(solution)/shard_map/all_to_all | solution.py:481
  29.2 1.2 serve.1
  30.5 23.6 %all_to_all.72 = bf16[128,8,256]{2,1,0:T(8,128)(2,1)S(1)} all-to-all(bf16[128,8,256]{2,1,0:T(8,128)(2,1)S(1)} %bitcast.30), channel_id=1, replica_groups=mesh['tower'=2,'x'=4,'y'=4,'z'=8] {'x','y','z'}, dimensions={0} | all-to-all | bytes 1048576 | tf_op jit(solution)/shard_map/all_to_all | solution.py:491
  54.1 3.6 %item_forward.1 = (bf16[64,1024]{1,0:T(8,128)(2,1)}, f32[16,1024]{1,0:T(8,128)}, f32[16,1024]{1,0:T(8,128)}) custom-call(bf16[1024,256]{1,0:T(8,128)(2,1)S(1)} %bitcast.24, s32[384,128]{1,0:T(8,128)} %get-tuple-element.35.refs_1_, f32[128,256]{1,0:T(8,128)} %refs_2_.4, f32[1,1024]{1,0:T(1,128)} %bitcast.33, bf16[256,1024]{1,0:T(8,128)(2,1)} %refs_17_.1, ...), custom_call_target="tpu_custom_call" | custom-call | tf_op jit(solution)/shard_map/item_forward/pallas_call | solution.py:496
  57.7 3.4 %all-to-all-start.2 = ((bf16[8,8,1024]{2,1,0:T(8,128)(2,1)}), bf16[8,8,1024]{2,1,0:T(8,128)(2,1)S(1)}, u32[]{:S(2)}, u32[]{:S(2)}) async-start(bf16[8,8,1024]{2,1,0:T(8,128)(2,1)} %bitcast.9), calls=%async_computation.2 | async-start | bytes 262144 | tf_op jit(solution)/shard_map/all_to_all | solution.py:507
  61.1 5.7 %user_forward.1 = (bf16[16,1024]{1,0:T(8,128)(2,1)S(1)}, f32[256,1024]{1,0:T(8,128)}, bf16[256,1024]{1,0:T(8,128)(2,1)}, bf16[64,1024]{1,0:T(8,128)(2,1)}, f32[64,256]{1,0:T(8,128)}, /*index=5*/f32[16,1024]{1,0:T(8,128)}) custom-call(bf16[1024,256]{1,0:T(8,128)(2,1)S(1)} %bitcast.25, s32[384,128]{1,0:T(8,128)} %get-tuple-element.35.refs_1_, ...), custom_call_target="tpu_custom_call" | custom-call | tf_op jit(solution)/shard_map/user_forward/pallas_call | solution.py:518
  66.8 2.1 %all-to-all-done.2 = bf16[8,8,1024]{2,1,0:T(8,128)(2,1)S(1)} async-done(((bf16[8,8,1024]{2,1,0:T(8,128)(2,1)}), bf16[8,8,1024]{2,1,0:T(8,128)(2,1)S(1)}, u32[]{:S(2)}, u32[]{:S(2)}) %all-to-all-start.2) | async-done | bytes 131104 | tf_op jit(solution)/shard_map/all_to_all | solution.py:507
  69.2 17.2 %all_to_all.73 = bf16[16,40,1024]{2,1,0:T(8,128)(2,1)S(1)} all-to-all(bf16[16,40,1024]{2,1,0:T(8,128)(2,1)S(1)} %bitcast.23), channel_id=1, replica_groups=mesh['tower'=2,'x'=4,'y'=4,'z'=8] {'x','y'}, dimensions={0} | all-to-all | bytes 2621440 | tf_op jit(solution)/shard_map/all_to_all | solution.py:537
  86.5 6.0 %collective-permute-start = (bf16[640,1024]{1,0:T(8,128)(2,1)S(1)}, bf16[640,1024]{1,0:T(8,128)(2,1)S(1)}, u32[]{:S(2)}, u32[]{:S(2)}) collective-permute-start(bf16[640,1024]{1,0:T(8,128)(2,1)S(1)} %bitcast.21), channel_id=1, source_target_pairs={{0,128},{128,0},{1,129},{129,1},{2,130},{130,2},{3,131},{131,3},{4... | collective-permute-start | bytes 3932168 | tf_op jit(solution)/shard_map/ppermute | solution.py:538
  92.6 2.6 %collective-permute-done.swapped_ref = bf16[640,1024]{1,0:T(8,128)(2,1)S(1)} collective-permute-done((bf16[640,1024]{1,0:T(8,128)(2,1)S(1)}, bf16[640,1024]{1,0:T(8,128)(2,1)S(1)}, u32[]{:S(2)}, u32[]{:S(2)}) %collective-permute-start) | collective-permute-done | bytes 1310752 | tf_op jit(solution)/shard_map/ppermute | solution.py:538
  95.2 3.0 %softmax.1 = (f32[16,1024]{1,0:T(8,128)S(1)}, bf16[64,1024]{1,0:T(8,128)(2,1)}, f32[8,128]{1,0:T(8,128)S(1)}) custom-call(s32[2]{0:T(128)S(1)} %pad_add_fusion.place_ref, bf16[640,1024]{1,0:T(8,128)(2,1)S(1)} %bitcast.22, bf16[640,1024]{1,0:T(8,128)(2,1)S(1)} %collective-permute-done.swapped_ref), custom_call_target="tpu_custom_call" | custom-call | tf_op jit(solution)/shard_map/softmax/pallas_call | solution.py:540
  98.1 4.4 %all-to-all-start.4 = ((bf16[8,8,1024]{2,1,0:T(8,128)(2,1)}), bf16[8,8,1024]{2,1,0:T(8,128)(2,1)S(1)}, u32[]{:S(2)}, u32[]{:S(2)}) async-start(bf16[8,8,1024]{2,1,0:T(8,128)(2,1)} %bitcast.15), calls=%async_computation.4 | async-start | bytes 262144 | tf_op jit(solution)/shard_map/all_to_all | solution.py:549
  102.6 6.3 %user_backward.1 = (bf16[256,256]{1,0:T(8,128)(2,1)S(1)}, s32[8,384]{1,0:T(8,128)S(1)}, f32[1,1024]{1,0:T(1,128)S(1)}, f32[16,1024]{1,0:T(8,128)S(1)}, f32[16,10...) custom-call(f32[16,1024]{1,0:T(8,128)S(1)} %get-tuple-element.39.d_user_ref, ...), custom_call_target="tpu_custom_call" | custom-call | tf_op jit(solution)/shard_map/user_backward/pallas_call | solution.py:554
  108.9 1.5 all-to-all-done.4
  110.5 1.6 item_backward.1
  112.1 27.9 %all_to_all.74 = bf16[128,8,256]{2,1,0:T(8,128)(2,1)S(1)} all-to-all(bf16[128,8,256]{2,1,0:T(8,128)(2,1)S(1)} %bitcast.26), channel_id=1, replica_groups=mesh['tower'=2,'x'=4,'y'=4,'z'=8] {'x','y','z'}, dimensions={0} | all-to-all | bytes 1048576 | tf_op jit(solution)/shard_map/all_to_all | solution.py:572
  140.0 1.2 scatter.1
  141.2 6.5 %all-to-all-start.6 = ((f32[128,1,384]{2,1,0:T(1,128)}), f32[128,1,384]{2,1,0:T(1,128)S(1)}, u32[]{:S(2)}, u32[]{:S(2)}) async-start(f32[128,1,384]{2,1,0:T(1,128)} %get-tuple-element.57), calls=%async_computation.6 | async-start | bytes 393216 | tf_op jit(solution)/shard_map/all_to_all | solution.py:582
  147.7 2.5 %collective-permute-start.2 = (bf16[512,256]{1,0:T(8,128)(2,1)S(1)}, bf16[512,256]{1,0:T(8,128)(2,1)S(1)}, u32[]{:S(2)}, u32[]{:S(2)}) collective-permute-start(bf16[512,256]{1,0:T(8,128)(2,1)S(1)} %get-tuple-element.59), channel_id=1, source_target_pairs={{0,128},{128,0},{1,129},{129,1},{2,130},{130,2},{3,131},{131,3},{4... | collective-permute-start | bytes 786440 | tf_op jit(solution)/shard_map/ppermute | solution.py:581
  150.1 9.7 %all-to-all-done.6.sums_ref = f32[128,1,384]{2,1,0:T(1,128)S(1)} async-done(((f32[128,1,384]{2,1,0:T(1,128)}), f32[128,1,384]{2,1,0:T(1,128)S(1)}, u32[]{:S(2)}, u32[]{:S(2)}) %all-to-all-start.6) | async-done | bytes 196640 | tf_op jit(solution)/shard_map/all_to_all | solution.py:582
  159.8 3.2 %collective-permute-start.1 = (f32[128,1,384]{2,1,0:T(1,128)S(1)}, f32[128,1,384]{2,1,0:T(1,128)S(1)}, u32[]{:S(2)}, u32[]{:S(2)}) collective-permute-start(f32[128,1,384]{2,1,0:T(1,128)S(1)} %all-to-all-done.6.sums_ref), channel_id=1, source_target_pairs={{0,128},{128,0},{1,129},{129,1},{2,130},{130,2},{3,131},{131,3},{4... | collective-permute-start | bytes 589832 | tf_op jit(solution)/shard_map/ppermute | solution.py:583
  163.0 0.8 convert_add_fusion
  164.1 0.7 finish.1
  (6 shorter events, 0.6 us)
Async XLA Ops:
  57.7 11.2 %all-to-all-start.2 = ((bf16[8,8,1024]{2,1,0:T(8,128)(2,1)}), bf16[8,8,1024]{2,1,0:T(8,128)(2,1)S(1)}, u32[]{:S(2)}, u32[]{:S(2)}) async-start(bf16[8,8,1024]{2,1,0:T(8,128)(2,1)} %bitcast.9), calls=%async_computation.2 | async-start | bytes 262144 | tf_op jit(solution)/shard_map/all_to_all | solution.py:507
  86.5 8.7 %collective-permute-start = (bf16[640,1024]{1,0:T(8,128)(2,1)S(1)}, bf16[640,1024]{1,0:T(8,128)(2,1)S(1)}, u32[]{:S(2)}, u32[]{:S(2)}) collective-permute-start(bf16[640,1024]{1,0:T(8,128)(2,1)S(1)} %bitcast.21), channel_id=1, source_target_pairs={{0,128},{128,0},{1,129},{129,1},{2,130},{130,2},{3,131},{131,3},{4... | collective-permute-start | bytes 3932168 | tf_op jit(solution)/shard_map/ppermute | solution.py:538
  98.1 12.3 %all-to-all-start.4 = ((bf16[8,8,1024]{2,1,0:T(8,128)(2,1)}), bf16[8,8,1024]{2,1,0:T(8,128)(2,1)S(1)}, u32[]{:S(2)}, u32[]{:S(2)}) async-start(bf16[8,8,1024]{2,1,0:T(8,128)(2,1)} %bitcast.15), calls=%async_computation.4 | async-start | bytes 262144 | tf_op jit(solution)/shard_map/all_to_all | solution.py:549
  110.5 29.5 %copy-start = (s32[8,1024]{1,0:T(8,128)S(1)}, s32[8,1024]{1,0:T(8,128)}, u32[]{:S(2)}) copy-start(s32[8,1024]{1,0:T(8,128)} %get-tuple-element.55.row_ref) | copy-start | bytes 98308
  141.2 18.6 %all-to-all-start.6 = ((f32[128,1,384]{2,1,0:T(1,128)}), f32[128,1,384]{2,1,0:T(1,128)S(1)}, u32[]{:S(2)}, u32[]{:S(2)}) async-start(f32[128,1,384]{2,1,0:T(1,128)} %get-tuple-element.57), calls=%async_computation.6 | async-start | bytes 393216 | tf_op jit(solution)/shard_map/all_to_all | solution.py:582
  147.7 15.3 %collective-permute-start.2 = (bf16[512,256]{1,0:T(8,128)(2,1)S(1)}, bf16[512,256]{1,0:T(8,128)(2,1)S(1)}, u32[]{:S(2)}, u32[]{:S(2)}) collective-permute-start(bf16[512,256]{1,0:T(8,128)(2,1)S(1)} %get-tuple-element.59), channel_id=1, source_target_pairs={{0,128},{128,0},{1,129},{129,1},{2,130},{130,2},{3,131},{131,3},{4... | collective-permute-start | bytes 786440 | tf_op jit(solution)/shard_map/ppermute | solution.py:581
  159.8 4.3 %collective-permute-start.1 = (f32[128,1,384]{2,1,0:T(1,128)S(1)}, f32[128,1,384]{2,1,0:T(1,128)S(1)}, u32[]{:S(2)}, u32[]{:S(2)}) collective-permute-start(f32[128,1,384]{2,1,0:T(1,128)S(1)} %all-to-all-done.6.sums_ref), channel_id=1, source_target_pairs={{0,128},{128,0},{1,129},{129,1},{2,130},{130,2},{3,131},{131,3},{4... | collective-permute-start | bytes 589832 | tf_op jit(solution)/shard_map/ppermute | solution.py:583

commit v8 on v7

--- a/solution.py
+++ b/solution.py
@@ -13,7 +13,10 @@
 EPS = 1e-06
 SLOTS = 8
 HOT_SLOT = 5
-SHARD = ("x", "y", "z")
+HOT_CODE = 4096
+GROUP = ("x", "y", "zh")
+LINE = ("zh", "zl")
+SHARD = GROUP + ("zl",)
 PAD = 16
 BF = jnp.bfloat16
 F32 = jnp.float32
@@ -92,7 +95,7 @@
     earlier = dot(one_hot(hits), before)
     position = jnp.sum(jnp.where(hits, earlier, 0.0), axis=0, keepdims=True).astype(jnp.int32)
     places = jnp.where(
-        is_rare, owner * SLOTS + position, jnp.where(ids >= 0, ids * SLOTS + HOT_SLOT, -1)
+        is_rare, owner * SLOTS + position, jnp.where(ids >= 0, ids + HOT_CODE, -1)
     )
     row[...] = jnp.broadcast_to(places, row.shape)
     column[...] = jnp.transpose(jnp.broadcast_to(places.astype(F32), (128, span))).astype(jnp.int32)
@@ -110,7 +113,13 @@
         save.wait()
 
 
-def serve_kernel(asked_ref, known_ref, served, row_hbm, row, sem):
+def serve_kernel(
+    asked_ref, known_ref, hot_hbm, column_hbm, served, hot_ref, column_ref, row_hbm, hot, row, sems
+):
+    span = column_hbm.shape[0] - 128
+    loads = copies_of(
+        [(hot_hbm, hot), (column_hbm.at[pl.ds(span, PAD)], column_ref)], sems
+    )
     slots = served.shape[0]
     sources = asked_ref.shape[0]
     asked = asked_ref[...]
@@ -122,7 +131,7 @@
     index = jnp.sum(jnp.where(mine, wide, 0.0), axis=1, keepdims=True) - 1.0
     index = jnp.broadcast_to(index, wide.shape)
     row[...] = jnp.transpose(index)[0:8].astype(jnp.int32)
-    save = pltpu.make_async_copy(row, row_hbm, sem)
+    save = pltpu.make_async_copy(row, row_hbm, sems.at[2])
     save.start()
     index = index.astype(jnp.int32)
     lanes = iota(index.shape, 1)
@@ -131,6 +140,9 @@
         [one_hot(index == lanes + 128 * j) for j in range(rows // 128)], axis=1
     )
     served[...] = dot(picks, known_ref[...]).astype(BF)
+    for load in loads:
+        load.wait()
+    hot_ref[...] = hot[...].astype(BF)
     save.wait()
 
 
@@ -161,37 +173,31 @@
     picks = jnp.concatenate(
         [one_hot(column == lanes + 128 * j) for j in range(slots // 128)], axis=1
     )
-    hot_picks = one_hot(column == lanes * SLOTS + HOT_SLOT)
+    hot_picks = one_hot(column == lanes + HOT_CODE)
     return (dot(picks, fetched[...]) + dot(hot_picks, hot[...].astype(BF))).astype(BF)
 
 
-def item_forward_kernel(users, *refs):
-    fetched_ref, sources, refs = refs[0], refs[1:6], refs[6:]
-    vectors_ref, kept_hbm, refs = refs[0], refs[1:3], refs[3:]
-    targets, kept, (in_sems, out_sems) = refs[:5], refs[5:7], refs[7:]
-    column_of, hot, gain, item_w1, item_w2 = targets
-    inner_ref, outer_ref = kept
-    span = sources[0].shape[0]
-    sources = (sources[0].at[pl.ds(span - 128, PAD)],) + tuple(sources[1:])
-    copies = copies_of(zip(sources, targets), in_sems)
+def item_forward_kernel(users, fetched_ref, hot_ref, column_ref, *refs):
+    sources, refs = refs[:3], refs[3:]
+    vectors_ref, inner_hbm, refs = refs[0], refs[1], refs[2:]
+    targets, (inner_ref, sems) = refs[:3], refs[3:]
+    item_w1, item_w2, gain = targets
+    copies = copies_of(zip(sources, targets), sems)
+    rows = look_up(column_ref[...], fetched_ref, hot_ref)
     copies[0].wait()
-    copies[1].wait()
-    rows = look_up(column_of[...], fetched_ref, hot)
-    copies[2].wait()
-    copies[3].wait()
     inner = dot(rows, item_w1[...])
     inner_ref[...] = inner
+    save = pltpu.make_async_copy(inner_ref, inner_hbm, sems.at[3])
+    save.start()
     gated = (inner * jax.nn.sigmoid(inner)).astype(BF)
-    copies[4].wait()
+    copies[1].wait()
+    copies[2].wait()
     outer = dot(gated, item_w2[...])
-    outer_ref[...] = outer
-    saves = copies_of(zip(kept, kept_hbm), out_sems)
     scale = lax.rsqrt(jnp.mean(outer * outer, axis=-1, keepdims=True) + EPS)
     vectors = jnp.where(iota(outer.shape, 0) < users, outer * scale * gain[...], 0.0)
     peers = vectors_ref.shape[0] // 8
     vectors_ref[...] = jnp.concatenate([vectors[0:8]] * peers, axis=0).astype(BF)
-    for save in saves:
-        save.wait()
+    save.wait()
 
 
 def user_forward_kernel(users, *refs):
@@ -274,7 +280,7 @@
 
 
 def softmax_kernel(
-    users, near, scale, place_ref, gathered_ref, swapped_ref, d_user_ref, d_part_ref, loss_ref, raised_ref
+    users, near, scale, place_ref, gathered_ref, swapped_ref, d_user_ref, d_part_ref, raised_ref
 ):
     rows, width = gathered_ref.shape
     items = near * users
@@ -311,7 +317,7 @@
     apart = (near * 8, items)
     at = iota(apart, 0)
     apart = one_hot((at % 8 < users) & (iota(apart, 1) == at // 8 * users + at % 8))
-    d_part_ref[...] = (scale * dot(dot(apart, slope).astype(BF), group_users)).astype(BF)
+    d_part = scale * dot(dot(apart, slope).astype(BF), group_users)
 
     who = iota(shape, 1) - mine * users
     target = (who >= 0) & (who < users) & (iota(shape, 0) == mine * block + plane * users + who)
@@ -323,7 +329,14 @@
     d_user = d_user + dot(dot_nt(self, other_slope).astype(BF), other)
     d_user_ref[...] = (scale * d_user).astype(BF).astype(F32)
     each = jnp.sum(jnp.where(target, top + jnp.log(count) - first, 0.0), axis=0, keepdims=True)
-    loss_ref[...] = jnp.broadcast_to(jnp.sum(each, axis=1, keepdims=True), loss_ref.shape)
+    loss = jnp.sum(each, axis=1, keepdims=True)
+    high = loss.astype(BF).astype(F32)
+    middle = (loss - high).astype(BF).astype(F32)
+    low = loss - high - middle
+    shape = d_part.shape
+    lanes = iota(shape, 1)
+    loss = jnp.where(lanes == 0, high, jnp.where(lanes == 1, middle, jnp.where(lanes == 2, low, 0.0)))
+    d_part_ref[...] = jnp.where(iota(shape, 0) % 8 == users, loss, d_part).astype(BF)
 
 
 def norm_backward(values, cotangent, gain):
@@ -334,8 +347,8 @@
 
 
 def user_backward_kernel(users, d_user_ref, *refs):
-    sources, refs = refs[:18], refs[18:]
-    d_rows_ref, ahead, refs = refs[0], refs[1:7], refs[7:]
+    sources, refs = refs[:17], refs[17:]
+    d_rows_ref, ahead, outer_ref, refs = refs[0], refs[1:6], refs[6], refs[7:]
     targets, (d_normed, sems) = refs[:12], refs[12:]
     mixed_ref, out_gain_ref, w_out, w_value, normed_ref, weights_ref, qk_ref = targets[:7]
     w_key, w_query, hidden_ref, norm_gain_ref, in_proj = targets[7:]
@@ -381,18 +394,27 @@
     d_rows_ref[...] = dot_nt(d_normed[...].astype(BF), in_proj[...]).astype(BF)
     for copy in copies[12:]:
         copy.wait()
+    inner = ahead[2][...]
+    outer_ref[...] = dot((inner * jax.nn.sigmoid(inner)).astype(BF), ahead[3][...])
 
 
 def item_backward_kernel(users, parts_ref, d_rows_ref, *refs):
-    row_ref, gain, outer_ref, inner_ref, item_w2, item_w1, outgoing = refs
+    row_ref, gain, inner_ref, item_w2, item_w1, outer_ref, outgoing, loss_ref = refs
     slots = outgoing.shape[0]
     span = d_rows_ref.shape[0]
     wide = row_ref.shape[1]
     peers = parts_ref.shape[0]
     shape = (PAD, peers)
-    added = (iota(shape, 1) % 8 == iota(shape, 0)) & (iota(shape, 0) < users)
-    d_item = dot(one_hot(added), parts_ref[...]).astype(BF).astype(F32)
-    picks = one_hot(iota((slots, wide), 0) == row_ref[0:1, :])
+    sums = dot(one_hot(iota(shape, 1) % 8 == iota(shape, 0)), parts_ref[...])
+    shape = (1, 128)
+    loss = jnp.where(iota(shape, 1) < 3, sums[users : users + 1, 0:128], 0.0)
+    loss_ref[...] = jnp.broadcast_to(jnp.sum(loss, axis=1, keepdims=True), loss_ref.shape)
+    d_item = jnp.where(iota(sums.shape, 0) < users, sums, 0.0).astype(BF).astype(F32)
+    line = iota((slots, 1), 0)
+    slot = line % SLOTS
+    hot = HOT_CODE + line // (2 * SLOTS) + (slot - HOT_SLOT) * (slots // (2 * SLOTS))
+    code = jnp.where(slot < HOT_SLOT, line, jnp.where(slot < HOT_SLOT + 2, hot, -2))
+    picks = one_hot(code == row_ref[0:1, :])
     total = dot(picks[:, 0:span], d_rows_ref[...])
     d_outer = norm_backward(outer_ref[...], d_item, gain[...])
     inner = inner_ref[...]
@@ -405,22 +427,33 @@
     outgoing[...] = (total + dot(picks[:, span:], d_items)).astype(BF)
 
 
-def finish_kernel(total, sums_ref, other_ref, hot_ref, loss_ref):
-    emb = hot_ref.shape[1]
-    sums = sums_ref[:, 0, :] + other_ref[:, 0, :]
-    hot_ref[...] = sums[:, 0:emb]
-    loss_ref[...] = jnp.sum(sums[:, emb : emb + 1], axis=0, keepdims=True) / total
-
-
-def scatter_kernel(returned_ref, row_ref, loss_ref, part_ref, hot_ref):
+def scatter_kernel(returned_ref, row_ref, loss_ref, part_ref, sums_ref):
     rows, emb = part_ref.shape
     slots = returned_ref.shape[0]
     returned = returned_ref[...]
     picks = one_hot(iota((rows, slots), 0) == row_ref[0:1, :])
     part_ref[...] = dot(picks, returned).astype(BF)
-    hot = dot(one_hot(iota((PAD, slots), 1) % SLOTS == HOT_SLOT), returned)
-    line = jnp.concatenate([hot[0:1], loss_ref[0:1, :]], axis=1)
-    hot_ref[...] = jnp.broadcast_to(line[None], hot_ref.shape)
+    shape = (PAD, slots)
+    hot = dot(one_hot((iota(shape, 0) < 2) & (iota(shape, 1) % SLOTS == iota(shape, 0) + HOT_SLOT)), returned)
+    halves = [hot[i : i + 1, j : j + 128] for i in range(2) for j in range(0, emb, 128)]
+    block = jnp.concatenate(halves + [loss_ref[0 : 8 - len(halves), :]], axis=0)
+    sums_ref[...] = jnp.concatenate([block] * (sums_ref.shape[0] // 8), axis=0)
+
+
+def finish_kernel(count, sums_ref, other_ref, hot_ref, loss_ref):
+    emb = hot_ref.shape[1]
+    groups = sums_ref.shape[0] // 8
+
+    def of_row(row):
+        at = pl.ds(row, groups, stride=8)
+        return sums_ref[at, :] + other_ref[at, :]
+
+    row = 0
+    for i in range(2):
+        for j in range(0, emb, 128):
+            hot_ref[i * groups : (i + 1) * groups, j : j + 128] = of_row(row)
+            row += 1
+    loss_ref[...] = jnp.sum(of_row(row)[:, 0:1], axis=0, keepdims=True) / count
 
 
 def shards(
@@ -448,7 +481,7 @@
     scale = 4.0 / math.sqrt(width)
     owners = lax.axis_size(SHARD)
     towers = lax.axis_size("tower")
-    near = lax.axis_size("z")
+    near = lax.axis_size(LINE)
     total = users * towers * owners
     slots = owners * SLOTS
     span = users * hist
@@ -479,32 +512,38 @@
         name="index",
     )(*map(in_hbm, loads))
     asked = exchange(request, SHARD)
-    served, asked_row = pl.pallas_call(
+    served, hot_ready, item_column, asked_row = pl.pallas_call(
         serve_kernel,
-        out_shape=(shape((slots, emb), BF), pltpu.HBM((8, slots), jnp.int32)),
-        in_specs=[VMEM, VMEM],
-        out_specs=(VMEM, HBM),
-        scratch_shapes=[pltpu.VMEM((8, slots), jnp.int32), pltpu.SemaphoreType.DMA],
+        out_shape=(
+            shape((slots, emb), BF),
+            pltpu.VMEM(hot_table.shape, BF),
+            pltpu.VMEM((PAD, 128), jnp.int32),
+            pltpu.HBM((8, slots), jnp.int32),
+        ),
+        in_specs=[VMEM, VMEM, HBM, HBM],
+        out_specs=(VMEM, VMEM, VMEM, HBM),
+        scratch_shapes=[
+            pltpu.VMEM(hot_table.shape, F32),
+            pltpu.VMEM((8, slots), jnp.int32),
+            sems(3),
+        ],
         compiler_params=params(24),
         name="serve",
-    )(asked, in_vmem(known))
+    )(asked, in_vmem(known), in_hbm(hot_table), in_hbm(column))
     fetched = exchange(served, SHARD)
 
     norm_gain, out_gain, item_gain = (g.reshape(1, width) for g in (norm_gain, out_gain, item_gain))
-    loads = (column, hot_table, item_gain, item_w1, item_w2)
-    kept = (shape((PAD, width), F32), shape((PAD, width), F32))
-    item_vec, inner, outer = pl.pallas_call(
+    loads = (item_w1, item_w2, item_gain)
+    item_vec, inner = pl.pallas_call(
         functools.partial(item_forward_kernel, users),
-        out_shape=(shape((near * 8, width), BF), *map(hbm, kept)),
-        in_specs=[VMEM] + [HBM] * 5,
-        out_specs=(VMEM, HBM, HBM),
-        scratch_shapes=[pltpu.VMEM((PAD, 128), jnp.int32)]
-        + like(loads[1:] + kept)
-        + [sems(5), sems(2)],
+        out_shape=(shape((near * 8, width), BF), pltpu.HBM((PAD, width), F32)),
+        in_specs=[VMEM] * 3 + [HBM] * 3,
+        out_specs=(VMEM, HBM),
+        scratch_shapes=like(loads) + [pltpu.VMEM((PAD, width), F32), sems(4)],
         compiler_params=params(24),
         name="item_forward",
-    )(fetched, *map(in_hbm, loads))
-    near_items = exchange(item_vec, "z")
+    )(fetched, in_vmem(hot_ready), in_vmem(item_column), *map(in_hbm, loads))
+    near_items = exchange(item_vec, LINE)
 
     loads = (column, hot_table, pos_embed, norm_gain, out_gain)
     loads += (in_proj, w_query, w_key, w_value, w_out)
@@ -536,35 +575,35 @@
     )(near_items, user_vec)
     gathered = exchange(spread, ("x", "y"))
     swapped = lax.ppermute(gathered, "tower", swap)
-    place = jnp.stack([lax.axis_index(("x", "y")), lax.axis_index("z")]).astype(jnp.int32)
-    d_user, d_part, loss = pl.pallas_call(
+    place = jnp.stack([lax.axis_index(("x", "y")), lax.axis_index(LINE)]).astype(jnp.int32)
+    d_user, d_part = pl.pallas_call(
         functools.partial(softmax_kernel, users, near, scale),
-        out_shape=(shape((PAD, width), F32), shape((near * 8, width), BF), shape((8, 128), F32)),
+        out_shape=(shape((PAD, width), F32), shape((near * 8, width), BF)),
         in_specs=[SMEM, VMEM, VMEM],
-        out_specs=(VMEM, VMEM, VMEM),
+        out_specs=(VMEM, VMEM),
         scratch_shapes=[pltpu.VMEM((rows, 2 * owners // near * users), F32)],
         compiler_params=params(32),
         name="softmax",
     )(place, gathered, swapped)
-    parts = exchange(d_part, "z")
+    parts = exchange(d_part, LINE)
 
     loads = (mixed, out_gain, w_out, w_value, normed, weights, qk)
     loads += (w_key, w_query, hidden, norm_gain, in_proj)
-    ahead = (row, item_gain, outer, inner, item_w2, item_w1)
+    ahead = (row, item_gain, inner, item_w2, item_w1)
     d_rows, *item_ready = pl.pallas_call(
         functools.partial(user_backward_kernel, users),
-        out_shape=(shape((span, emb), BF), *map(vmem, ahead)),
-        in_specs=[VMEM] + [HBM] * 18,
+        out_shape=(shape((span, emb), BF), *map(vmem, ahead), pltpu.VMEM((PAD, width), F32)),
+        in_specs=[VMEM] + [HBM] * 17,
         out_specs=(VMEM,) * 7,
-        scratch_shapes=like(loads) + [pltpu.VMEM((span, width), F32), sems(18)],
+        scratch_shapes=like(loads) + [pltpu.VMEM((span, width), F32), sems(17)],
         compiler_params=params(40),
         name="user_backward",
     )(d_user, *map(in_hbm, loads + ahead))
-    outgoing = pl.pallas_call(
+    outgoing, loss = pl.pallas_call(
         functools.partial(item_backward_kernel, users),
-        out_shape=shape((slots, emb), BF),
+        out_shape=(shape((slots, emb), BF), shape((8, 128), F32)),
         in_specs=[VMEM] * 8,
-        out_specs=VMEM,
+        out_specs=(VMEM, VMEM),
         compiler_params=params(32),
         name="item_backward",
     )(parts, d_rows, *map(in_vmem, item_ready))
@@ -572,17 +611,17 @@
     returned = exchange(outgoing, SHARD)
     part, mine = pl.pallas_call(
         scatter_kernel,
-        out_shape=(shape((rare_count, emb), BF), shape((owners, 1, emb + 128), F32)),
+        out_shape=(shape((rare_count, emb), BF), shape((owners // 2 * 8, 128), F32)),
         in_specs=[VMEM, VMEM, VMEM],
         out_specs=(VMEM, VMEM),
         compiler_params=params(24),
         name="scatter",
     )(returned, asked_row, loss)
     rare_grad = part.astype(F32) + lax.ppermute(part, "tower", swap).astype(F32)
-    sums = exchange(mine, SHARD)
+    sums = exchange(mine, GROUP)
     other_sums = lax.ppermute(sums, "tower", swap)
     hot_total, loss_total = pl.pallas_call(
-        functools.partial(finish_kernel, total),
+        functools.partial(finish_kernel, total * (near // 2)),
         out_shape=(shape((owners, emb), F32), shape((1, 1), F32)),
         in_specs=[VMEM, VMEM],
         out_specs=(VMEM, VMEM),
@@ -593,7 +632,7 @@
 
 
 def solution(mesh):
-    sizes = (mesh.shape["tower"], 4, 4, mesh.shape["shard"] // 16)
+    sizes = (mesh.shape["tower"], 4, 4, mesh.shape["shard"] // 32, 2)
     mesh = Mesh(mesh.devices.reshape(sizes), ("tower",) + SHARD)
     return jax.shard_map(
         shards,

time: 165 us -> 165 us (level)
  transfers between devices with their start and end apart: 6 -> 6, of which waited for: 5 -> 5; matrix products, arithmetic and copies ran while one was open for 1% -> 1% of each run, Pallas kernels for 7% -> 8%
where the time goes in v8:
time: 165 us; the launch traced here: 164 us
  blocking collectives  95.8 us (58%)
  Pallas kernels  25.4 us (15%)
  starting transfers between devices  24.9 us (15%)
  waiting for transfers between devices  16.6 us (10%)
    all_to_all x1, blocking collectives, shards(): returned = exchange(outgoing, SHARD)  28.3 us
    all_to_all x1, blocking collectives, shards(): asked = exchange(request, SHARD)  26.7 us
    all_to_all x1, blocking collectives, shards(): fetched = exchange(served, SHARD)  23.6 us
    all_to_all x1, blocking collectives, shards(): gathered = exchange(spread, ('x', 'y'))  17.2 us
    all_to_all x1, waiting for transfers between devices, shards(): sums = exchange(mine, GROUP)  10.4 us
    pallas_call x1, Pallas kernels, shards(): pl.pallas_call(functools.partial(user_backward_kernel, users), out_shape=...  6.73 us
    ppermute x1, starting transfers between devices, shards(): swapped = lax.ppermute(gathered, 'tower', swap)  6.03 us
    pallas_call x1, Pallas kernels, shards(): pl.pallas_call(functools.partial(user_forward_kernel, users), out_shape=(...  5.74 us
  transfers between devices with their start and end apart: 6, of which 5 were waited for; matrix products, arithmetic and copies ran while one was open for 1% of the time, Pallas kernels for 8%

profile of v8, /device:TPU:1, one launch (start us, length us, event | category | flops | bytes accessed | tf_op | source)
XLA Modules:
  0.0 164.4 jit_solution(6640967006557259767)
XLA Ops:
  0.6 1.9 %index.1 = (s32[128,128]{1,0:T(8,128)S(1)}, bf16[512,256]{1,0:T(8,128)(2,1)S(1)}, s32[8,384]{1,0:T(8,128)}, s32[384,128]{1,0:T(8,128)}) custom-call(s32[4,64]{1,0:T(4,128)} %history_hbm.1, s32[1,4]{1,0:T(1,128)} %bitcast.43, f32[512,256]{1,0:T(8,128)} %table_hbm.1), custom_call_target="tpu_custom_call" | custom-call | tf_op jit(solution)/shard_map/index/pallas_call | solution.py:501
  2.5 26.7 %all_to_all.77 = s32[128,1,128]{2,1,0:T(1,128)S(1)} all-to-all(s32[128,1,128]{2,1,0:T(1,128)S(1)} %bitcast.36), channel_id=1, replica_groups=mesh['tower'=2,'x'=4,'y'=4,'zh'=4,'zl'=2] {'x','y','zh','zl'}, dimensions={0} | all-to-all | bytes 131072 | tf_op jit(solution)/shard_map/all_to_all | solution.py:514
  29.2 1.3 serve.1
  30.5 23.6 %all_to_all.78 = bf16[128,8,256]{2,1,0:T(8,128)(2,1)S(1)} all-to-all(bf16[128,8,256]{2,1,0:T(8,128)(2,1)S(1)} %bitcast.34), channel_id=1, replica_groups=mesh['tower'=2,'x'=4,'y'=4,'zh'=4,'zl'=2] {'x','y','zh','zl'}, dimensions={0} | all-to-all | bytes 1048576 | tf_op jit(solution)/shard_map/all_to_all | solution.py:533
  54.1 3.0 %item_forward.1 = (bf16[64,1024]{1,0:T(8,128)(2,1)}, f32[16,1024]{1,0:T(8,128)}) custom-call(bf16[1024,256]{1,0:T(8,128)(2,1)S(1)} %bitcast.26, bf16[128,256]{1,0:T(8,128)(2,1)S(1)} %get-tuple-element.38.hot_ref, s32[16,128]{1,0:T(8,128)S(1)} %get-tuple-element.39.column_ref, bf16[256,1024]{1,0:T(8,128)(2,1)} %refs_16_.1, bf16[1024,1024]{1,0:T(8,128)(2,1)} %refs_15_.1, ...), custom_call_target="tpu_custom_call" | custom-call | tf_op jit(solution)/shard_map/item_forward/pallas_call | solution.py:537
  57.1 3.4 %all-to-all-start.2 = ((bf16[8,8,1024]{2,1,0:T(8,128)(2,1)}), bf16[8,8,1024]{2,1,0:T(8,128)(2,1)S(1)}, u32[]{:S(2)}, u32[]{:S(2)}) async-start(bf16[8,8,1024]{2,1,0:T(8,128)(2,1)} %bitcast.9), calls=%async_computation.2 | async-start | bytes 262144 | tf_op jit(solution)/shard_map/all_to_all | solution.py:546
  60.5 5.7 %user_forward.1 = (bf16[16,1024]{1,0:T(8,128)(2,1)S(1)}, f32[256,1024]{1,0:T(8,128)}, bf16[256,1024]{1,0:T(8,128)(2,1)}, bf16[64,1024]{1,0:T(8,128)(2,1)}, f32[64,256]{1,0:T(8,128)}, /*index=5*/f32[16,1024]{1,0:T(8,128)}) custom-call(bf16[1024,256]{1,0:T(8,128)(2,1)S(1)} %bitcast.27, s32[384,128]{1,0:T(8,128)} %get-tuple-element.36.column_hbm.refs_1_, ...), custom_call_target="tpu_custom_call" | custom-call | tf_op jit(solution)/shard_map/user_forward/pallas_call | solution.py:557
  66.3 2.1 %all-to-all-done.2 = bf16[8,8,1024]{2,1,0:T(8,128)(2,1)S(1)} async-done(((bf16[8,8,1024]{2,1,0:T(8,128)(2,1)}), bf16[8,8,1024]{2,1,0:T(8,128)(2,1)S(1)}, u32[]{:S(2)}, u32[]{:S(2)}) %all-to-all-start.2) | async-done | bytes 131104 | tf_op jit(solution)/shard_map/all_to_all | solution.py:546
  68.7 17.2 %all_to_all.79 = bf16[16,40,1024]{2,1,0:T(8,128)(2,1)S(1)} all-to-all(bf16[16,40,1024]{2,1,0:T(8,128)(2,1)S(1)} %bitcast.25), channel_id=1, replica_groups=mesh['tower'=2,'x'=4,'y'=4,'zh'=4,'zl'=2] {'x','y'}, dimensions={0} | all-to-all | bytes 2621440 | tf_op jit(solution)/shard_map/all_to_all | solution.py:576
  85.9 6.0 %collective-permute-start = (bf16[640,1024]{1,0:T(8,128)(2,1)S(1)}, bf16[640,1024]{1,0:T(8,128)(2,1)S(1)}, u32[]{:S(2)}, u32[]{:S(2)}) collective-permute-start(bf16[640,1024]{1,0:T(8,128)(2,1)S(1)} %bitcast.23), channel_id=1, source_target_pairs={{0,128},{128,0},{1,129},{129,1},{2,130},{130,2},{3,131},{131,3},{4... | collective-permute-start | bytes 3932168 | tf_op jit(solution)/shard_map/ppermute | solution.py:577
  92.0 2.6 %collective-permute-done.swapped_ref = bf16[640,1024]{1,0:T(8,128)(2,1)S(1)} collective-permute-done((bf16[640,1024]{1,0:T(8,128)(2,1)S(1)}, bf16[640,1024]{1,0:T(8,128)(2,1)S(1)}, u32[]{:S(2)}, u32[]{:S(2)}) %collective-permute-start) | collective-permute-done | bytes 1310752 | tf_op jit(solution)/shard_map/ppermute | solution.py:577
  94.6 3.0 %softmax.1 = (f32[16,1024]{1,0:T(8,128)S(1)}, bf16[64,1024]{1,0:T(8,128)(2,1)}) custom-call(s32[2]{0:T(128)S(1)} %pad_add_fusion.place_ref, bf16[640,1024]{1,0:T(8,128)(2,1)S(1)} %bitcast.24, bf16[640,1024]{1,0:T(8,128)(2,1)S(1)} %collective-permute-done.swapped_ref), custom_call_target="tpu_custom_call" | custom-call | tf_op jit(solution)/shard_map/softmax/pallas_call | solution.py:579
  97.6 4.5 %all-to-all-start.4 = ((bf16[8,8,1024]{2,1,0:T(8,128)(2,1)}), bf16[8,8,1024]{2,1,0:T(8,128)(2,1)S(1)}, u32[]{:S(2)}, u32[]{:S(2)}) async-start(bf16[8,8,1024]{2,1,0:T(8,128)(2,1)} %bitcast.15), calls=%async_computation.4 | async-start | bytes 262144 | tf_op jit(solution)/shard_map/all_to_all | solution.py:588
  102.1 6.7 %user_backward.1 = (bf16[256,256]{1,0:T(8,128)(2,1)S(1)}, s32[8,384]{1,0:T(8,128)S(1)}, f32[1,1024]{1,0:T(1,128)S(1)}, f32[16,1024]{1,0:T(8,128)S(1)}, bf16[1024...) custom-call(f32[16,1024]{1,0:T(8,128)S(1)} %get-tuple-element.43.d_user_ref, ...), custom_call_target="tpu_custom_call" | custom-call | tf_op jit(solution)/shard_map/user_backward/pallas_call | solution.py:593
  108.8 1.1 all-to-all-done.4
  109.9 1.6 item_backward.1
  111.6 28.3 %all_to_all.80 = bf16[128,8,256]{2,1,0:T(8,128)(2,1)S(1)} all-to-all(bf16[128,8,256]{2,1,0:T(8,128)(2,1)S(1)} %bitcast.33), channel_id=1, replica_groups=mesh['tower'=2,'x'=4,'y'=4,'zh'=4,'zl'=2] {'x','y','zh','zl'}, dimensions={0} | all-to-all | bytes 1048576 | tf_op jit(solution)/shard_map/all_to_all | solution.py:611
  139.8 1.2 scatter.1
  141.0 5.3 %all-to-all-start.6 = ((f32[64,8,128]{2,1,0:T(8,128)}), f32[64,8,128]{2,1,0:T(8,128)S(1)}, u32[]{:S(2)}, u32[]{:S(2)}) async-start(f32[64,8,128]{2,1,0:T(8,128)} %bitcast.19), calls=%async_computation.6 | async-start | bytes 524288 | tf_op jit(solution)/shard_map/all_to_all | solution.py:621
  146.3 2.1 %collective-permute-start.2 = (bf16[512,256]{1,0:T(8,128)(2,1)S(1)}, bf16[512,256]{1,0:T(8,128)(2,1)S(1)}, u32[]{:S(2)}, u32[]{:S(2)}) collective-permute-start(bf16[512,256]{1,0:T(8,128)(2,1)S(1)} %get-tuple-element.63), channel_id=1, source_target_pairs={{0,128},{128,0},{1,129},{129,1},{2,130},{130,2},{3,131},{131,3},{4... | collective-permute-start | bytes 786440 | tf_op jit(solution)/shard_map/ppermute | solution.py:620
  148.5 10.4 %all-to-all-done.6 = f32[64,8,128]{2,1,0:T(8,128)S(1)} async-done(((f32[64,8,128]{2,1,0:T(8,128)}), f32[64,8,128]{2,1,0:T(8,128)S(1)}, u32[]{:S(2)}, u32[]{:S(2)}) %all-to-all-start.6) | async-done | bytes 262176 | tf_op jit(solution)/shard_map/all_to_all | solution.py:621
  158.9 3.6 %collective-permute-start.1 = (f32[512,128]{1,0:T(8,128)S(1)}, f32[512,128]{1,0:T(8,128)S(1)}, u32[]{:S(2)}, u32[]{:S(2)}) collective-permute-start(f32[512,128]{1,0:T(8,128)S(1)} %bitcast.29), channel_id=1, source_target_pairs={{0,128},{128,0},{1,129},{129,1},{2,130},{130,2},{3,131},{131,3},{4... | collective-permute-start | bytes 786440 | tf_op jit(solution)/shard_map/ppermute | solution.py:622
  162.5 0.8 convert_add_fusion
  163.7 0.7 finish.1
  (6 shorter events, 0.7 us)
Async XLA Ops:
  57.1 11.2 %all-to-all-start.2 = ((bf16[8,8,1024]{2,1,0:T(8,128)(2,1)}), bf16[8,8,1024]{2,1,0:T(8,128)(2,1)S(1)}, u32[]{:S(2)}, u32[]{:S(2)}) async-start(bf16[8,8,1024]{2,1,0:T(8,128)(2,1)} %bitcast.9), calls=%async_computation.2 | async-start | bytes 262144 | tf_op jit(solution)/shard_map/all_to_all | solution.py:546
  85.9 8.7 %collective-permute-start = (bf16[640,1024]{1,0:T(8,128)(2,1)S(1)}, bf16[640,1024]{1,0:T(8,128)(2,1)S(1)}, u32[]{:S(2)}, u32[]{:S(2)}) collective-permute-start(bf16[640,1024]{1,0:T(8,128)(2,1)S(1)} %bitcast.23), channel_id=1, source_target_pairs={{0,128},{128,0},{1,129},{129,1},{2,130},{130,2},{3,131},{131,3},{4... | collective-permute-start | bytes 3932168 | tf_op jit(solution)/shard_map/ppermute | solution.py:577
  97.6 12.4 %all-to-all-start.4 = ((bf16[8,8,1024]{2,1,0:T(8,128)(2,1)}), bf16[8,8,1024]{2,1,0:T(8,128)(2,1)S(1)}, u32[]{:S(2)}, u32[]{:S(2)}) async-start(bf16[8,8,1024]{2,1,0:T(8,128)(2,1)} %bitcast.15), calls=%async_computation.4 | async-start | bytes 262144 | tf_op jit(solution)/shard_map/all_to_all | solution.py:588
  108.8 31.0 %copy-start = (s32[8,1024]{1,0:T(8,128)S(1)}, s32[8,1024]{1,0:T(8,128)}, u32[]{:S(2)}) copy-start(s32[8,1024]{1,0:T(8,128)} %get-tuple-element.59.row_ref) | copy-start | bytes 98308
  141.0 17.9 %all-to-all-start.6 = ((f32[64,8,128]{2,1,0:T(8,128)}), f32[64,8,128]{2,1,0:T(8,128)S(1)}, u32[]{:S(2)}, u32[]{:S(2)}) async-start(f32[64,8,128]{2,1,0:T(8,128)} %bitcast.19), calls=%async_computation.6 | async-start | bytes 524288 | tf_op jit(solution)/shard_map/all_to_all | solution.py:621
  146.3 16.2 %collective-permute-start.2 = (bf16[512,256]{1,0:T(8,128)(2,1)S(1)}, bf16[512,256]{1,0:T(8,128)(2,1)S(1)}, u32[]{:S(2)}, u32[]{:S(2)}) collective-permute-start(bf16[512,256]{1,0:T(8,128)(2,1)S(1)} %get-tuple-element.63), channel_id=1, source_target_pairs={{0,128},{128,0},{1,129},{129,1},{2,130},{130,2},{3,131},{131,3},{4... | collective-permute-start | bytes 786440 | tf_op jit(solution)/shard_map/ppermute | solution.py:620
  158.9 4.8 %collective-permute-start.1 = (f32[512,128]{1,0:T(8,128)S(1)}, f32[512,128]{1,0:T(8,128)S(1)}, u32[]{:S(2)}, u32[]{:S(2)}) collective-permute-start(f32[512,128]{1,0:T(8,128)S(1)} %bitcast.29), channel_id=1, source_target_pairs={{0,128},{128,0},{1,129},{129,1},{2,130},{130,2},{3,131},{131,3},{4... | collective-permute-start | bytes 786440 | tf_op jit(solution)/shard_map/ppermute | solution.py:622

commit v9 on v8

--- a/solution.py
+++ b/solution.py
@@ -13,6 +13,7 @@
 EPS = 1e-06
 SLOTS = 8
 HOT_SLOT = 5
+PIECES = 4
 HOT_CODE = 4096
 GROUP = ("x", "y", "zh")
 LINE = ("zh", "zl")
@@ -352,18 +353,34 @@
     targets, (d_normed, sems) = refs[:12], refs[12:]
     mixed_ref, out_gain_ref, w_out, w_value, normed_ref, weights_ref, qk_ref = targets[:7]
     w_key, w_query, hidden_ref, norm_gain_ref, in_proj = targets[7:]
-    copies = copies_of(zip(sources, tuple(targets) + tuple(ahead)), sems)
+    pairs = []
+    for source, target in zip(sources, tuple(targets) + tuple(ahead)):
+        pieces = PIECES if target is w_out or target is w_value else 1
+        size = target.shape[0] // pieces
+        for piece in range(pieces):
+            at = pl.ds(piece * size, size)
+            pairs.append((source.at[at], target.at[at]) if pieces > 1 else (source, target))
+    copies = copies_of(pairs, sems)
+    parts, copies = copies[2 : 2 + 2 * PIECES], copies[:2] + copies[2 + 2 * PIECES :]
+
+    def times(values, weights, arrivals):
+        size = weights.shape[0] // PIECES
+        columns = []
+        for piece, arrival in enumerate(arrivals):
+            arrival.wait()
+            columns.append(dot_nt(values, weights[piece * size : (piece + 1) * size, :]))
+        return jnp.concatenate(columns, axis=1)
+
     span, width = hidden_ref.shape
     hist = span // users
     heads = width // HEAD_DIM
     mask = head_mask(heads, width)
-    for copy in copies[:3]:
+    for copy in copies[:2]:
         copy.wait()
     d_mixed = norm_backward(mixed_ref[...], d_user_ref[...], out_gain_ref[...])
-    d_attended = dot_nt(d_mixed.astype(BF), w_out[...])
-    copies[3].wait()
-    d_mixes = dot_nt(spread_heads(d_attended, mask, users), w_value[...]).astype(BF)
-    for copy in copies[4:7]:
+    d_attended = times(d_mixed.astype(BF), w_out, parts[:PIECES])
+    d_mixes = times(spread_heads(d_attended, mask, users), w_value, parts[PIECES:]).astype(BF)
+    for copy in copies[2:5]:
         copy.wait()
     normed = normed_ref[...]
     weights = weights_ref[...]
@@ -377,22 +394,22 @@
         jnp.concatenate([d_mixes, qk_ref[...]], axis=0),
     )
     d_qk = dot(d_scores, normed).astype(BF)
-    copies[7].wait()
+    copies[5].wait()
     d_query = join_heads(dot(d_qk, w_key[...]), mask, users).astype(BF)
-    copies[8].wait()
+    copies[6].wait()
     d_last = dot_nt(d_query, w_query[...])
     for u in range(users):
         at = slice((u + 1) * hist - 1, (u + 1) * hist)
         d_normed[at, :] = d_normed[at, :] + d_last[u : u + 1]
-    copies[9].wait()
-    copies[10].wait()
+    copies[7].wait()
+    copies[8].wait()
     d_normed[...] = norm_backward(hidden_ref[...], d_normed[...], norm_gain_ref[...])
     for u in range(users):
         at = slice((u + 1) * hist - 1, (u + 1) * hist)
         d_normed[at, :] = d_normed[at, :] + d_mixed[u : u + 1]
-    copies[11].wait()
+    copies[9].wait()
     d_rows_ref[...] = dot_nt(d_normed[...].astype(BF), in_proj[...]).astype(BF)
-    for copy in copies[12:]:
+    for copy in copies[10:]:
         copy.wait()
     inner = ahead[2][...]
     outer_ref[...] = dot((inner * jax.nn.sigmoid(inner)).astype(BF), ahead[3][...])
@@ -595,7 +612,7 @@
         out_shape=(shape((span, emb), BF), *map(vmem, ahead), pltpu.VMEM((PAD, width), F32)),
         in_specs=[VMEM] + [HBM] * 17,
         out_specs=(VMEM,) * 7,
-        scratch_shapes=like(loads) + [pltpu.VMEM((span, width), F32), sems(17)],
+        scratch_shapes=like(loads) + [pltpu.VMEM((span, width), F32), sems(15 + 2 * PIECES)],
         compiler_params=params(40),
         name="user_backward",
     )(d_user, *map(in_hbm, loads + ahead))
@@ -617,8 +634,8 @@
         compiler_params=params(24),
         name="scatter",
     )(returned, asked_row, loss)
+    sums, part = lax.optimization_barrier((exchange(mine, GROUP), part))
     rare_grad = part.astype(F32) + lax.ppermute(part, "tower", swap).astype(F32)
-    sums = exchange(mine, GROUP)
     other_sums = lax.ppermute(sums, "tower", swap)
     hot_total, loss_total = pl.pallas_call(
         functools.partial(finish_kernel, total * (near // 2)),

time: 165 us -> 166 us (level)
  blocking collectives: 95.8 us -> 115 us
  waiting for transfers between devices: 16.6 us -> 5.84 us
  starting transfers between devices: 24.9 us -> 17.5 us
    all_to_all x0 -> x1, blocking collectives: none -> 17.6 us  [shards(): sums, part = lax.optimization_barrier((exchange(mine, GROUP), part))]
    all_to_all x1 -> x0, waiting for transfers between devices: 10.4 us -> none  [shards(): sums = exchange(mine, GROUP)]
    all_to_all x1 -> x0, starting transfers between devices: 5.28 us -> none  [shards(): sums = exchange(mine, GROUP)]
    ppermute x1, starting transfers between devices: 2.13 us -> 0.01 us  [shards(): rare_grad = part.astype(F32) + lax.ppermute(part, 'tower', swap).astype(F32)]
  transfers between devices with their start and end apart: 6 -> 5, of which waited for: 5 -> 3; matrix products, arithmetic and copies ran while one was open for 1% -> 0% of each run, Pallas kernels for 8% -> 9%
where the time goes in v9:
time: 166 us
  blocking collectives  115 us (69%)
  Pallas kernels  25.9 us (16%)
  starting transfers between devices  17.5 us (11%)
  waiting for transfers between devices  5.84 us (4%)
    all_to_all x1, blocking collectives, shards(): returned = exchange(outgoing, SHARD)  29.4 us
    all_to_all x1, blocking collectives, shards(): asked = exchange(request, SHARD)  26.7 us
    all_to_all x1, blocking collectives, shards(): fetched = exchange(served, SHARD)  23.6 us
    all_to_all x1, blocking collectives, shards(): sums, part = lax.optimization_barrier((exchange(mine, GROUP), part))  17.6 us
    all_to_all x1, blocking collectives, shards(): gathered = exchange(spread, ('x', 'y'))  17.3 us
    pallas_call x1, Pallas kernels, shards(): pl.pallas_call(functools.partial(user_backward_kernel, users), out_shape=...  7.94 us
    ppermute x1, starting transfers between devices, shards(): swapped = lax.ppermute(gathered, 'tower', swap)  6.03 us
    pallas_call x1, Pallas kernels, shards(): pl.pallas_call(functools.partial(user_forward_kernel, users), out_shape=(...  5.74 us
  transfers between devices with their start and end apart: 5, of which 3 were waited for; matrix products, arithmetic and copies ran while one was open for 0% of the time, Pallas kernels for 9%

profile of v9, /device:TPU:1, one launch (start us, length us, event | category | flops | bytes accessed | tf_op | source)
XLA Modules:
  0.0 165.6 jit_solution(861804585663947578)
XLA Ops:
  0.6 1.9 %index.1 = (s32[128,128]{1,0:T(8,128)S(1)}, bf16[512,256]{1,0:T(8,128)(2,1)S(1)}, s32[8,384]{1,0:T(8,128)}, s32[384,128]{1,0:T(8,128)}) custom-call(s32[4,64]{1,0:T(4,128)} %history_hbm.1, s32[1,4]{1,0:T(1,128)} %bitcast.44, f32[512,256]{1,0:T(8,128)} %table_hbm.1), custom_call_target="tpu_custom_call" | custom-call | tf_op jit(solution)/shard_map/index/pallas_call | solution.py:518
  2.5 26.7 %all_to_all.78 = s32[128,1,128]{2,1,0:T(1,128)S(1)} all-to-all(s32[128,1,128]{2,1,0:T(1,128)S(1)} %bitcast.37), channel_id=1, replica_groups=mesh['tower'=2,'x'=4,'y'=4,'zh'=4,'zl'=2] {'x','y','zh','zl'}, dimensions={0} | all-to-all | bytes 131072 | tf_op jit(solution)/shard_map/all_to_all | solution.py:531
  29.2 1.3 serve.1
  30.5 23.6 %all_to_all.79 = bf16[128,8,256]{2,1,0:T(8,128)(2,1)S(1)} all-to-all(bf16[128,8,256]{2,1,0:T(8,128)(2,1)S(1)} %bitcast.34), channel_id=1, replica_groups=mesh['tower'=2,'x'=4,'y'=4,'zh'=4,'zl'=2] {'x','y','zh','zl'}, dimensions={0} | all-to-all | bytes 1048576 | tf_op jit(solution)/shard_map/all_to_all | solution.py:550
  54.1 3.0 %item_forward.1 = (bf16[64,1024]{1,0:T(8,128)(2,1)}, f32[16,1024]{1,0:T(8,128)}) custom-call(bf16[1024,256]{1,0:T(8,128)(2,1)S(1)} %bitcast.26, bf16[128,256]{1,0:T(8,128)(2,1)S(1)} %get-tuple-element.40.hot_ref, s32[16,128]{1,0:T(8,128)S(1)} %get-tuple-element.41.column_ref, bf16[256,1024]{1,0:T(8,128)(2,1)} %refs_16_.1, bf16[1024,1024]{1,0:T(8,128)(2,1)} %refs_15_.1, ...), custom_call_target="tpu_custom_call" | custom-call | tf_op jit(solution)/shard_map/item_forward/pallas_call | solution.py:554
  57.1 3.4 %all-to-all-start.2 = ((bf16[8,8,1024]{2,1,0:T(8,128)(2,1)}), bf16[8,8,1024]{2,1,0:T(8,128)(2,1)S(1)}, u32[]{:S(2)}, u32[]{:S(2)}) async-start(bf16[8,8,1024]{2,1,0:T(8,128)(2,1)} %bitcast.9), calls=%async_computation.2 | async-start | bytes 262144 | tf_op jit(solution)/shard_map/all_to_all | solution.py:563
  60.5 5.7 %user_forward.1 = (bf16[16,1024]{1,0:T(8,128)(2,1)S(1)}, f32[256,1024]{1,0:T(8,128)}, bf16[256,1024]{1,0:T(8,128)(2,1)}, bf16[64,1024]{1,0:T(8,128)(2,1)}, f32[64,256]{1,0:T(8,128)}, /*index=5*/f32[16,1024]{1,0:T(8,128)}) custom-call(bf16[1024,256]{1,0:T(8,128)(2,1)S(1)} %bitcast.27, s32[384,128]{1,0:T(8,128)} %get-tuple-element.38.column_hbm.refs_1_, ...), custom_call_target="tpu_custom_call" | custom-call | tf_op jit(solution)/shard_map/user_forward/pallas_call | solution.py:574
  66.3 2.1 %all-to-all-done.2 = bf16[8,8,1024]{2,1,0:T(8,128)(2,1)S(1)} async-done(((bf16[8,8,1024]{2,1,0:T(8,128)(2,1)}), bf16[8,8,1024]{2,1,0:T(8,128)(2,1)S(1)}, u32[]{:S(2)}, u32[]{:S(2)}) %all-to-all-start.2) | async-done | bytes 131104 | tf_op jit(solution)/shard_map/all_to_all | solution.py:563
  68.4 0.3 arrange.1
  68.7 17.3 %all_to_all.80 = bf16[16,40,1024]{2,1,0:T(8,128)(2,1)S(1)} all-to-all(bf16[16,40,1024]{2,1,0:T(8,128)(2,1)S(1)} %bitcast.25), channel_id=1, replica_groups=mesh['tower'=2,'x'=4,'y'=4,'zh'=4,'zl'=2] {'x','y'}, dimensions={0} | all-to-all | bytes 2621440 | tf_op jit(solution)/shard_map/all_to_all | solution.py:593
  85.9 6.0 %collective-permute-start = (bf16[640,1024]{1,0:T(8,128)(2,1)S(1)}, bf16[640,1024]{1,0:T(8,128)(2,1)S(1)}, u32[]{:S(2)}, u32[]{:S(2)}) collective-permute-start(bf16[640,1024]{1,0:T(8,128)(2,1)S(1)} %bitcast.23), channel_id=1, source_target_pairs={{0,128},{128,0},{1,129},{129,1},{2,130},{130,2},{3,131},{131,3},{4... | collective-permute-start | bytes 3932168 | tf_op jit(solution)/shard_map/ppermute | solution.py:594
  92.0 0.1 pad_add_fusion.place_ref
  92.0 2.6 %collective-permute-done.swapped_ref = bf16[640,1024]{1,0:T(8,128)(2,1)S(1)} collective-permute-done((bf16[640,1024]{1,0:T(8,128)(2,1)S(1)}, bf16[640,1024]{1,0:T(8,128)(2,1)S(1)}, u32[]{:S(2)}, u32[]{:S(2)}) %collective-permute-start) | collective-permute-done | bytes 1310752 | tf_op jit(solution)/shard_map/ppermute | solution.py:594
  94.6 3.0 %softmax.1 = (f32[16,1024]{1,0:T(8,128)S(1)}, bf16[64,1024]{1,0:T(8,128)(2,1)}) custom-call(s32[2]{0:T(128)S(1)} %pad_add_fusion.place_ref, bf16[640,1024]{1,0:T(8,128)(2,1)S(1)} %bitcast.24, bf16[640,1024]{1,0:T(8,128)(2,1)S(1)} %collective-permute-done.swapped_ref), custom_call_target="tpu_custom_call" | custom-call | tf_op jit(solution)/shard_map/softmax/pallas_call | solution.py:596
  97.6 4.5 %all-to-all-start.4 = ((bf16[8,8,1024]{2,1,0:T(8,128)(2,1)}), bf16[8,8,1024]{2,1,0:T(8,128)(2,1)S(1)}, u32[]{:S(2)}, u32[]{:S(2)}) async-start(bf16[8,8,1024]{2,1,0:T(8,128)(2,1)} %bitcast.15), calls=%async_computation.4 | async-start | bytes 262144 | tf_op jit(solution)/shard_map/all_to_all | solution.py:605
  102.0 7.9 %user_backward.1 = (bf16[256,256]{1,0:T(8,128)(2,1)S(1)}, s32[8,384]{1,0:T(8,128)S(1)}, f32[1,1024]{1,0:T(1,128)S(1)}, f32[16,1024]{1,0:T(8,128)S(1)}, bf16[1024...) custom-call(f32[16,1024]{1,0:T(8,128)S(1)} %get-tuple-element.45.d_user_ref, ...), custom_call_target="tpu_custom_call" | custom-call | tf_op jit(solution)/shard_map/user_backward/pallas_call | solution.py:610
  110.0 1.6 item_backward.1
  111.6 29.4 %all_to_all.81 = bf16[128,8,256]{2,1,0:T(8,128)(2,1)S(1)} all-to-all(bf16[128,8,256]{2,1,0:T(8,128)(2,1)S(1)} %bitcast.33), channel_id=1, replica_groups=mesh['tower'=2,'x'=4,'y'=4,'zh'=4,'zl'=2] {'x','y','zh','zl'}, dimensions={0} | all-to-all | bytes 1048576 | tf_op jit(solution)/shard_map/all_to_all | solution.py:628
  141.0 0.5 scatter.1
  141.6 17.6 %all_to_all.82 = f32[64,8,128]{2,1,0:T(8,128)S(1)} all-to-all(f32[64,8,128]{2,1,0:T(8,128)S(1)} %bitcast.36), channel_id=1, replica_groups=mesh['tower'=2,'x'=4,'y'=4,'zh'=4,'zl'=2] {'x','y','zh'}, dimensions={0} | all-to-all | bytes 524288 | tf_op jit(solution)/shard_map/all_to_all | solution.py:637
  159.2 3.6 %collective-permute-start.1 = (f32[512,128]{1,0:T(8,128)S(1)}, f32[512,128]{1,0:T(8,128)S(1)}, u32[]{:S(2)}, u32[]{:S(2)}) collective-permute-start(f32[512,128]{1,0:T(8,128)S(1)} %bitcast.29), channel_id=1, source_target_pairs={{0,128},{128,0},{1,129},{129,1},{2,130},{130,2},{3,131},{131,3},{4... | collective-permute-start | bytes 786440 | tf_op jit(solution)/shard_map/ppermute | solution.py:639
  162.8 1.2 collective-permute-done.1.other_ref
  164.0 0.7 finish.1
  164.7 0.9 convert_add_fusion
  (5 shorter events, 0.0 us)
Async XLA Ops:
  57.1 11.2 %all-to-all-start.2 = ((bf16[8,8,1024]{2,1,0:T(8,128)(2,1)}), bf16[8,8,1024]{2,1,0:T(8,128)(2,1)S(1)}, u32[]{:S(2)}, u32[]{:S(2)}) async-start(bf16[8,8,1024]{2,1,0:T(8,128)(2,1)} %bitcast.9), calls=%async_computation.2 | async-start | bytes 262144 | tf_op jit(solution)/shard_map/all_to_all | solution.py:563
  85.9 8.7 %collective-permute-start = (bf16[640,1024]{1,0:T(8,128)(2,1)S(1)}, bf16[640,1024]{1,0:T(8,128)(2,1)S(1)}, u32[]{:S(2)}, u32[]{:S(2)}) collective-permute-start(bf16[640,1024]{1,0:T(8,128)(2,1)S(1)} %bitcast.23), channel_id=1, source_target_pairs={{0,128},{128,0},{1,129},{129,1},{2,130},{130,2},{3,131},{131,3},{4... | collective-permute-start | bytes 3932168 | tf_op jit(solution)/shard_map/ppermute | solution.py:594
  97.6 12.4 %all-to-all-start.4 = ((bf16[8,8,1024]{2,1,0:T(8,128)(2,1)}), bf16[8,8,1024]{2,1,0:T(8,128)(2,1)S(1)}, u32[]{:S(2)}, u32[]{:S(2)}) async-start(bf16[8,8,1024]{2,1,0:T(8,128)(2,1)} %bitcast.15), calls=%async_computation.4 | async-start | bytes 262144 | tf_op jit(solution)/shard_map/all_to_all | solution.py:605
  110.0 31.0 %copy-start = (s32[8,1024]{1,0:T(8,128)S(1)}, s32[8,1024]{1,0:T(8,128)}, u32[]{:S(2)}) copy-start(s32[8,1024]{1,0:T(8,128)} %get-tuple-element.61.row_ref) | copy-start | bytes 98308
  159.2 4.8 %collective-permute-start.1 = (f32[512,128]{1,0:T(8,128)S(1)}, f32[512,128]{1,0:T(8,128)S(1)}, u32[]{:S(2)}, u32[]{:S(2)}) collective-permute-start(f32[512,128]{1,0:T(8,128)S(1)} %bitcast.29), channel_id=1, source_target_pairs={{0,128},{128,0},{1,129},{129,1},{2,130},{130,2},{3,131},{131,3},{4... | collective-permute-start | bytes 786440 | tf_op jit(solution)/shard_map/ppermute | solution.py:639
  162.8 1.9 %collective-permute-start.2 = (bf16[512,256]{1,0:T(8,128)(2,1)S(1)}, bf16[512,256]{1,0:T(8,128)(2,1)S(1)}, u32[]{:S(2)}, u32[]{:S(2)}) collective-permute-start(bf16[512,256]{1,0:T(8,128)(2,1)S(1)} %get-tuple-element.67), channel_id=1, source_target_pairs={{0,128},{128,0},{1,129},{129,1},{2,130},{130,2},{3,131},{131,3},{4... | collective-permute-start | bytes 786440 | tf_op jit(solution)/shard_map/ppermute | solution.py:638

commit v10 on v8

--- a/solution.py
+++ b/solution.py
@@ -12,11 +12,11 @@
 HEAD_DIM = 64
 EPS = 1e-06
 SLOTS = 8
-HOT_SLOT = 5
+USED = 5
 HOT_CODE = 4096
-GROUP = ("x", "y", "zh")
 LINE = ("zh", "zl")
-SHARD = GROUP + ("zl",)
+SHARD = ("x", "y") + LINE
+GROUP = ("x", "y", "zl")
 PAD = 16
 BF = jnp.bfloat16
 F32 = jnp.float32
@@ -103,7 +103,7 @@
     order = jnp.where(hits, earlier, -1.0)
     lanes = iota(request_ref.shape, 1)
     request = jnp.zeros(request_ref.shape, F32)
-    for slot in range(HOT_SLOT):
+    for slot in range(USED):
         wanted = jnp.sum(jnp.where(order == float(slot), value, 0.0), axis=1, keepdims=True)
         request = jnp.where(lanes == slot, wanted, request)
     request_ref[...] = request.astype(jnp.int32)
@@ -410,12 +410,17 @@
     loss = jnp.where(iota(shape, 1) < 3, sums[users : users + 1, 0:128], 0.0)
     loss_ref[...] = jnp.broadcast_to(jnp.sum(loss, axis=1, keepdims=True), loss_ref.shape)
     d_item = jnp.where(iota(sums.shape, 0) < users, sums, 0.0).astype(BF).astype(F32)
-    line = iota((slots, 1), 0)
-    slot = line % SLOTS
-    hot = HOT_CODE + line // (2 * SLOTS) + (slot - HOT_SLOT) * (slots // (2 * SLOTS))
-    code = jnp.where(slot < HOT_SLOT, line, jnp.where(slot < HOT_SLOT + 2, hot, -2))
-    picks = one_hot(code == row_ref[0:1, :])
+    emb = d_rows_ref.shape[1]
+    picks = one_hot(iota((slots, wide), 0) == row_ref[0:1, :])
     total = dot(picks[:, 0:span], d_rows_ref[...])
+    hot_count = slots // SLOTS
+    hot_picks = one_hot(iota((hot_count, wide), 0) + HOT_CODE == row_ref[0:1, :])
+    hot = dot(hot_picks[:, 0:span], d_rows_ref[...])
+    shape = (slots, hot_count)
+    line = iota(shape, 0)
+    owner = line // SLOTS
+    held = owner // 8 * 2 + owner % 2 + line % SLOTS // 2 * (hot_count // 4)
+    held = one_hot(iota(shape, 1) == held)
     d_outer = norm_backward(outer_ref[...], d_item, gain[...])
     inner = inner_ref[...]
     gate = jax.nn.sigmoid(inner)
@@ -424,36 +429,38 @@
     d_items = jnp.concatenate(
         [d_items, jnp.zeros((wide - span - PAD, d_items.shape[1]), F32)], axis=0
     ).astype(BF)
-    outgoing[...] = (total + dot(picks[:, span:], d_items)).astype(BF)
+    outgoing[:, 0:emb] = (total + dot(picks[:, span:], d_items)).astype(BF)
+    hot = (hot + dot(hot_picks[:, span:], d_items)).astype(BF)
+    hot = dot(held, hot)
+    half = emb // 2
+    odd = iota((slots, half), 0) % 2 == 1
+    outgoing[:, emb:] = jnp.where(odd, hot[:, half:], hot[:, 0:half]).astype(BF)
 
 
 def scatter_kernel(returned_ref, row_ref, loss_ref, part_ref, sums_ref):
     rows, emb = part_ref.shape
     slots = returned_ref.shape[0]
-    returned = returned_ref[...]
     picks = one_hot(iota((rows, slots), 0) == row_ref[0:1, :])
-    part_ref[...] = dot(picks, returned).astype(BF)
+    part_ref[...] = dot(picks, returned_ref[:, 0:emb]).astype(BF)
     shape = (PAD, slots)
-    hot = dot(one_hot((iota(shape, 0) < 2) & (iota(shape, 1) % SLOTS == iota(shape, 0) + HOT_SLOT)), returned)
-    halves = [hot[i : i + 1, j : j + 128] for i in range(2) for j in range(0, emb, 128)]
-    block = jnp.concatenate(halves + [loss_ref[0 : 8 - len(halves), :]], axis=0)
-    sums_ref[...] = jnp.concatenate([block] * (sums_ref.shape[0] // 8), axis=0)
+    hot = dot(one_hot(iota(shape, 1) % SLOTS == iota(shape, 0)), returned_ref[:, emb:])
+    block = jnp.concatenate([hot[0:SLOTS], loss_ref[...]], axis=0)
+    sums_ref[...] = jnp.concatenate([block] * (sums_ref.shape[0] // PAD), axis=0)
 
 
 def finish_kernel(count, sums_ref, other_ref, hot_ref, loss_ref):
     emb = hot_ref.shape[1]
-    groups = sums_ref.shape[0] // 8
+    groups = sums_ref.shape[0] // PAD
 
     def of_row(row):
-        at = pl.ds(row, groups, stride=8)
+        at = pl.ds(row, groups, stride=PAD)
         return sums_ref[at, :] + other_ref[at, :]
 
-    row = 0
-    for i in range(2):
-        for j in range(0, emb, 128):
-            hot_ref[i * groups : (i + 1) * groups, j : j + 128] = of_row(row)
-            row += 1
-    loss_ref[...] = jnp.sum(of_row(row)[:, 0:1], axis=0, keepdims=True) / count
+    for row in range(SLOTS):
+        at = row // 2 * groups
+        half = row % 2 * (emb // 2)
+        hot_ref[at : at + groups, half : half + emb // 2] = of_row(row)
+    loss_ref[...] = jnp.sum(of_row(SLOTS)[:, 0:1], axis=0, keepdims=True) / count
 
 
 def shards(
@@ -601,7 +608,7 @@
     )(d_user, *map(in_hbm, loads + ahead))
     outgoing, loss = pl.pallas_call(
         functools.partial(item_backward_kernel, users),
-        out_shape=(shape((slots, emb), BF), shape((8, 128), F32)),
+        out_shape=(shape((slots, emb + 128), BF), shape((8, 128), F32)),
         in_specs=[VMEM] * 8,
         out_specs=(VMEM, VMEM),
         compiler_params=params(32),
@@ -611,7 +618,7 @@
     returned = exchange(outgoing, SHARD)
     part, mine = pl.pallas_call(
         scatter_kernel,
-        out_shape=(shape((rare_count, emb), BF), shape((owners // 2 * 8, 128), F32)),
+        out_shape=(shape((rare_count, emb), BF), shape((owners // 4 * PAD, 128), F32)),
         in_specs=[VMEM, VMEM, VMEM],
         out_specs=(VMEM, VMEM),
         compiler_params=params(24),
@@ -621,7 +628,7 @@
     sums = exchange(mine, GROUP)
     other_sums = lax.ppermute(sums, "tower", swap)
     hot_total, loss_total = pl.pallas_call(
-        functools.partial(finish_kernel, total * (near // 2)),
+        functools.partial(finish_kernel, total * 2),
         out_shape=(shape((owners, emb), F32), shape((1, 1), F32)),
         in_specs=[VMEM, VMEM],
         out_specs=(VMEM, VMEM),

time: 165 us -> 166 us (level)
  waiting for transfers between devices: 16.6 us -> 11.3 us
  blocking collectives: 95.8 us -> 101 us
    all_to_all x1, waiting for transfers between devices: 10.4 us -> 5.15 us  [shards(): sums = exchange(mine, GROUP)]
    all_to_all x1, blocking collectives: 28.3 us -> 33.5 us  [shards(): returned = exchange(outgoing, SHARD)]
where the time goes in v10:
time: 166 us; the launch traced here: 165 us
  blocking collectives  101 us (61%)
  Pallas kernels  26 us (16%)
  starting transfers between devices  25.1 us (15%)
  waiting for transfers between devices  11.3 us (7%)
    all_to_all x1, blocking collectives, shards(): returned = exchange(outgoing, SHARD)  33.5 us
    all_to_all x1, blocking collectives, shards(): asked = exchange(request, SHARD)  26.7 us
    all_to_all x1, blocking collectives, shards(): fetched = exchange(served, SHARD)  23.6 us
    all_to_all x1, blocking collectives, shards(): gathered = exchange(spread, ('x', 'y'))  17.2 us
    pallas_call x1, Pallas kernels, shards(): pl.pallas_call(functools.partial(user_backward_kernel, users), out_shape=...  6.73 us
    ppermute x1, starting transfers between devices, shards(): swapped = lax.ppermute(gathered, 'tower', swap)  6.03 us
    pallas_call x1, Pallas kernels, shards(): pl.pallas_call(functools.partial(user_forward_kernel, users), out_shape=(...  5.74 us
    all_to_all x1, waiting for transfers between devices, shards(): sums = exchange(mine, GROUP)  5.15 us
  transfers between devices with their start and end apart: 6, of which 5 were waited for; matrix products, arithmetic and copies ran while one was open for 1% of the time, Pallas kernels for 8%

profile of v10, /device:TPU:1, one launch (start us, length us, event | category | flops | bytes accessed | tf_op | source)
XLA Modules:
  0.0 165.2 jit_solution(16506284329669331032)
XLA Ops:
  0.6 1.9 %index.1 = (s32[128,128]{1,0:T(8,128)S(1)}, bf16[512,256]{1,0:T(8,128)(2,1)S(1)}, s32[8,384]{1,0:T(8,128)}, s32[384,128]{1,0:T(8,128)}) custom-call(s32[4,64]{1,0:T(4,128)} %history_hbm.1, s32[1,4]{1,0:T(1,128)} %bitcast.43, f32[512,256]{1,0:T(8,128)} %table_hbm.1), custom_call_target="tpu_custom_call" | custom-call | tf_op jit(solution)/shard_map/index/pallas_call | solution.py:508
  2.5 26.7 %all_to_all.77 = s32[128,1,128]{2,1,0:T(1,128)S(1)} all-to-all(s32[128,1,128]{2,1,0:T(1,128)S(1)} %bitcast.36), channel_id=1, replica_groups=mesh['tower'=2,'x'=4,'y'=4,'zh'=4,'zl'=2] {'x','y','zh','zl'}, dimensions={0} | all-to-all | bytes 131072 | tf_op jit(solution)/shard_map/all_to_all | solution.py:521
  29.2 1.3 serve.1
  30.5 23.6 %all_to_all.78 = bf16[128,8,256]{2,1,0:T(8,128)(2,1)S(1)} all-to-all(bf16[128,8,256]{2,1,0:T(8,128)(2,1)S(1)} %bitcast.34), channel_id=1, replica_groups=mesh['tower'=2,'x'=4,'y'=4,'zh'=4,'zl'=2] {'x','y','zh','zl'}, dimensions={0} | all-to-all | bytes 1048576 | tf_op jit(solution)/shard_map/all_to_all | solution.py:540
  54.1 3.0 %item_forward.1 = (bf16[64,1024]{1,0:T(8,128)(2,1)}, f32[16,1024]{1,0:T(8,128)}) custom-call(bf16[1024,256]{1,0:T(8,128)(2,1)S(1)} %bitcast.26, bf16[128,256]{1,0:T(8,128)(2,1)S(1)} %get-tuple-element.38.hot_ref, s32[16,128]{1,0:T(8,128)S(1)} %get-tuple-element.39.column_ref, bf16[256,1024]{1,0:T(8,128)(2,1)} %refs_16_.1, bf16[1024,1024]{1,0:T(8,128)(2,1)} %refs_15_.1, ...), custom_call_target="tpu_custom_call" | custom-call | tf_op jit(solution)/shard_map/item_forward/pallas_call | solution.py:544
  57.1 3.4 %all-to-all-start.2 = ((bf16[8,8,1024]{2,1,0:T(8,128)(2,1)}), bf16[8,8,1024]{2,1,0:T(8,128)(2,1)S(1)}, u32[]{:S(2)}, u32[]{:S(2)}) async-start(bf16[8,8,1024]{2,1,0:T(8,128)(2,1)} %bitcast.9), calls=%async_computation.2 | async-start | bytes 262144 | tf_op jit(solution)/shard_map/all_to_all | solution.py:553
  60.5 5.7 %user_forward.1 = (bf16[16,1024]{1,0:T(8,128)(2,1)S(1)}, f32[256,1024]{1,0:T(8,128)}, bf16[256,1024]{1,0:T(8,128)(2,1)}, bf16[64,1024]{1,0:T(8,128)(2,1)}, f32[64,256]{1,0:T(8,128)}, /*index=5*/f32[16,1024]{1,0:T(8,128)}) custom-call(bf16[1024,256]{1,0:T(8,128)(2,1)S(1)} %bitcast.27, s32[384,128]{1,0:T(8,128)} %get-tuple-element.36.column_hbm.refs_1_, ...), custom_call_target="tpu_custom_call" | custom-call | tf_op jit(solution)/shard_map/user_forward/pallas_call | solution.py:564
  66.3 2.1 %all-to-all-done.2 = bf16[8,8,1024]{2,1,0:T(8,128)(2,1)S(1)} async-done(((bf16[8,8,1024]{2,1,0:T(8,128)(2,1)}), bf16[8,8,1024]{2,1,0:T(8,128)(2,1)S(1)}, u32[]{:S(2)}, u32[]{:S(2)}) %all-to-all-start.2) | async-done | bytes 131104 | tf_op jit(solution)/shard_map/all_to_all | solution.py:553
  68.7 17.2 %all_to_all.79 = bf16[16,40,1024]{2,1,0:T(8,128)(2,1)S(1)} all-to-all(bf16[16,40,1024]{2,1,0:T(8,128)(2,1)S(1)} %bitcast.25), channel_id=1, replica_groups=mesh['tower'=2,'x'=4,'y'=4,'zh'=4,'zl'=2] {'x','y'}, dimensions={0} | all-to-all | bytes 2621440 | tf_op jit(solution)/shard_map/all_to_all | solution.py:583
  85.9 6.0 %collective-permute-start = (bf16[640,1024]{1,0:T(8,128)(2,1)S(1)}, bf16[640,1024]{1,0:T(8,128)(2,1)S(1)}, u32[]{:S(2)}, u32[]{:S(2)}) collective-permute-start(bf16[640,1024]{1,0:T(8,128)(2,1)S(1)} %bitcast.23), channel_id=1, source_target_pairs={{0,128},{128,0},{1,129},{129,1},{2,130},{130,2},{3,131},{131,3},{4... | collective-permute-start | bytes 3932168 | tf_op jit(solution)/shard_map/ppermute | solution.py:584
  92.0 2.6 %collective-permute-done.swapped_ref = bf16[640,1024]{1,0:T(8,128)(2,1)S(1)} collective-permute-done((bf16[640,1024]{1,0:T(8,128)(2,1)S(1)}, bf16[640,1024]{1,0:T(8,128)(2,1)S(1)}, u32[]{:S(2)}, u32[]{:S(2)}) %collective-permute-start) | collective-permute-done | bytes 1310752 | tf_op jit(solution)/shard_map/ppermute | solution.py:584
  94.6 3.0 %softmax.1 = (f32[16,1024]{1,0:T(8,128)S(1)}, bf16[64,1024]{1,0:T(8,128)(2,1)}) custom-call(s32[2]{0:T(128)S(1)} %pad_add_fusion.place_ref, bf16[640,1024]{1,0:T(8,128)(2,1)S(1)} %bitcast.24, bf16[640,1024]{1,0:T(8,128)(2,1)S(1)} %collective-permute-done.swapped_ref), custom_call_target="tpu_custom_call" | custom-call | tf_op jit(solution)/shard_map/softmax/pallas_call | solution.py:586
  97.6 4.5 %all-to-all-start.4 = ((bf16[8,8,1024]{2,1,0:T(8,128)(2,1)}), bf16[8,8,1024]{2,1,0:T(8,128)(2,1)S(1)}, u32[]{:S(2)}, u32[]{:S(2)}) async-start(bf16[8,8,1024]{2,1,0:T(8,128)(2,1)} %bitcast.15), calls=%async_computation.4 | async-start | bytes 262144 | tf_op jit(solution)/shard_map/all_to_all | solution.py:595
  102.1 6.7 %user_backward.1 = (bf16[256,256]{1,0:T(8,128)(2,1)S(1)}, s32[8,384]{1,0:T(8,128)S(1)}, f32[1,1024]{1,0:T(1,128)S(1)}, f32[16,1024]{1,0:T(8,128)S(1)}, bf16[1024...) custom-call(f32[16,1024]{1,0:T(8,128)S(1)} %get-tuple-element.43.d_user_ref, ...), custom_call_target="tpu_custom_call" | custom-call | tf_op jit(solution)/shard_map/user_backward/pallas_call | solution.py:600
  108.8 1.1 all-to-all-done.4
  109.9 2.2 %item_backward.1 = (bf16[1024,384]{1,0:T(8,128)(2,1)S(1)}, f32[8,128]{1,0:T(8,128)S(1)}) custom-call(bf16[64,1024]{1,0:T(8,128)(2,1)S(1)} %bitcast.32, bf16[256,256]{1,0:T(8,128)(2,1)S(1)} %get-tuple-element.51.d_rows_ref, s32[8,384]{1,0:T(8,128)S(1)} %get-tuple-element.52.refs_0_, f32[1,1024]{1,0:T(1,128)S(1)} %get-tuple-element.53.refs_1_, ...), custom_call_target="tpu_custom_call" | custom-call | tf_op jit(solution)/shard_map/item_backward/pallas_call | solution.py:609
  112.2 33.5 %all_to_all.80 = bf16[128,8,384]{2,1,0:T(8,128)(2,1)S(1)} all-to-all(bf16[128,8,384]{2,1,0:T(8,128)(2,1)S(1)} %bitcast.31), channel_id=1, replica_groups=mesh['tower'=2,'x'=4,'y'=4,'zh'=4,'zl'=2] {'x','y','zh','zl'}, dimensions={0} | all-to-all | bytes 1572864 | tf_op jit(solution)/shard_map/all_to_all | solution.py:618
  145.7 1.2 scatter.1
  146.9 3.9 %all-to-all-start.6 = ((f32[32,16,128]{2,1,0:T(8,128)}), f32[32,16,128]{2,1,0:T(8,128)S(1)}, u32[]{:S(2)}, u32[]{:S(2)}) async-start(f32[32,16,128]{2,1,0:T(8,128)} %bitcast.19), calls=%async_computation.6 | async-start | bytes 524288 | tf_op jit(solution)/shard_map/all_to_all | solution.py:628
  150.7 3.1 %collective-permute-start.2 = (bf16[512,256]{1,0:T(8,128)(2,1)S(1)}, bf16[512,256]{1,0:T(8,128)(2,1)S(1)}, u32[]{:S(2)}, u32[]{:S(2)}) collective-permute-start(bf16[512,256]{1,0:T(8,128)(2,1)S(1)} %get-tuple-element.63), channel_id=1, source_target_pairs={{0,128},{128,0},{1,129},{129,1},{2,130},{130,2},{3,131},{131,3},{4... | collective-permute-start | bytes 786440 | tf_op jit(solution)/shard_map/ppermute | solution.py:627
  153.9 5.1 %all-to-all-done.6 = f32[32,16,128]{2,1,0:T(8,128)S(1)} async-done(((f32[32,16,128]{2,1,0:T(8,128)}), f32[32,16,128]{2,1,0:T(8,128)S(1)}, u32[]{:S(2)}, u32[]{:S(2)}) %all-to-all-start.6) | async-done | bytes 262176 | tf_op jit(solution)/shard_map/all_to_all | solution.py:628
  159.0 4.2 %collective-permute-start.1 = (f32[512,128]{1,0:T(8,128)S(1)}, f32[512,128]{1,0:T(8,128)S(1)}, u32[]{:S(2)}, u32[]{:S(2)}) collective-permute-start(f32[512,128]{1,0:T(8,128)S(1)} %bitcast.29), channel_id=1, source_target_pairs={{0,128},{128,0},{1,129},{129,1},{2,130},{130,2},{3,131},{131,3},{4... | collective-permute-start | bytes 786440 | tf_op jit(solution)/shard_map/ppermute | solution.py:629
  163.2 0.8 convert_add_fusion
  164.4 0.7 finish.1
  (6 shorter events, 0.7 us)
Async XLA Ops:
  57.1 11.2 %all-to-all-start.2 = ((bf16[8,8,1024]{2,1,0:T(8,128)(2,1)}), bf16[8,8,1024]{2,1,0:T(8,128)(2,1)S(1)}, u32[]{:S(2)}, u32[]{:S(2)}) async-start(bf16[8,8,1024]{2,1,0:T(8,128)(2,1)} %bitcast.9), calls=%async_computation.2 | async-start | bytes 262144 | tf_op jit(solution)/shard_map/all_to_all | solution.py:553
  85.9 8.7 %collective-permute-start = (bf16[640,1024]{1,0:T(8,128)(2,1)S(1)}, bf16[640,1024]{1,0:T(8,128)(2,1)S(1)}, u32[]{:S(2)}, u32[]{:S(2)}) collective-permute-start(bf16[640,1024]{1,0:T(8,128)(2,1)S(1)} %bitcast.23), channel_id=1, source_target_pairs={{0,128},{128,0},{1,129},{129,1},{2,130},{130,2},{3,131},{131,3},{4... | collective-permute-start | bytes 3932168 | tf_op jit(solution)/shard_map/ppermute | solution.py:584
  97.6 12.4 %all-to-all-start.4 = ((bf16[8,8,1024]{2,1,0:T(8,128)(2,1)}), bf16[8,8,1024]{2,1,0:T(8,128)(2,1)S(1)}, u32[]{:S(2)}, u32[]{:S(2)}) async-start(bf16[8,8,1024]{2,1,0:T(8,128)(2,1)} %bitcast.15), calls=%async_computation.4 | async-start | bytes 262144 | tf_op jit(solution)/shard_map/all_to_all | solution.py:595
  109.9 35.8 %copy-start = (s32[8,1024]{1,0:T(8,128)S(1)}, s32[8,1024]{1,0:T(8,128)}, u32[]{:S(2)}) copy-start(s32[8,1024]{1,0:T(8,128)} %get-tuple-element.59.row_ref) | copy-start | bytes 98308
  146.9 12.2 %all-to-all-start.6 = ((f32[32,16,128]{2,1,0:T(8,128)}), f32[32,16,128]{2,1,0:T(8,128)S(1)}, u32[]{:S(2)}, u32[]{:S(2)}) async-start(f32[32,16,128]{2,1,0:T(8,128)} %bitcast.19), calls=%async_computation.6 | async-start | bytes 524288 | tf_op jit(solution)/shard_map/all_to_all | solution.py:628
  150.7 12.5 %collective-permute-start.2 = (bf16[512,256]{1,0:T(8,128)(2,1)S(1)}, bf16[512,256]{1,0:T(8,128)(2,1)S(1)}, u32[]{:S(2)}, u32[]{:S(2)}) collective-permute-start(bf16[512,256]{1,0:T(8,128)(2,1)S(1)} %get-tuple-element.63), channel_id=1, source_target_pairs={{0,128},{128,0},{1,129},{129,1},{2,130},{130,2},{3,131},{131,3},{4... | collective-permute-start | bytes 786440 | tf_op jit(solution)/shard_map/ppermute | solution.py:627
  159.0 5.4 %collective-permute-start.1 = (f32[512,128]{1,0:T(8,128)S(1)}, f32[512,128]{1,0:T(8,128)S(1)}, u32[]{:S(2)}, u32[]{:S(2)}) collective-permute-start(f32[512,128]{1,0:T(8,128)S(1)} %bitcast.29), channel_id=1, source_target_pairs={{0,128},{128,0},{1,129},{129,1},{2,130},{130,2},{3,131},{131,3},{4... | collective-permute-start | bytes 786440 | tf_op jit(solution)/shard_map/ppermute | solution.py:629

commit v11 on v8

--- a/solution.py
+++ b/solution.py
@@ -14,9 +14,9 @@
 SLOTS = 8
 HOT_SLOT = 5
 HOT_CODE = 4096
-GROUP = ("x", "y", "zh")
 LINE = ("zh", "zl")
-SHARD = GROUP + ("zl",)
+SHARD = ("x", "y") + LINE
+GROUP = ("x", "y", "zl")
 PAD = 16
 BF = jnp.bfloat16
 F32 = jnp.float32
@@ -398,10 +398,10 @@
     outer_ref[...] = dot((inner * jax.nn.sigmoid(inner)).astype(BF), ahead[3][...])
 
 
-def item_backward_kernel(users, parts_ref, d_rows_ref, *refs):
-    row_ref, gain, inner_ref, item_w2, item_w1, outer_ref, outgoing, loss_ref = refs
-    slots = outgoing.shape[0]
-    span = d_rows_ref.shape[0]
+def item_backward_kernel(users, core_ref, parts_ref, d_rows_ref, *refs):
+    row_ref, gain, inner_ref, item_w2, item_w1, outer_ref, refs = *refs[:6], refs[6:]
+    d_all_ref, send_ref, keep_ref, loss_ref = refs
+    span, emb = d_rows_ref.shape
     wide = row_ref.shape[1]
     peers = parts_ref.shape[0]
     shape = (PAD, peers)
@@ -410,21 +410,40 @@
     loss = jnp.where(iota(shape, 1) < 3, sums[users : users + 1, 0:128], 0.0)
     loss_ref[...] = jnp.broadcast_to(jnp.sum(loss, axis=1, keepdims=True), loss_ref.shape)
     d_item = jnp.where(iota(sums.shape, 0) < users, sums, 0.0).astype(BF).astype(F32)
-    line = iota((slots, 1), 0)
-    slot = line % SLOTS
-    hot = HOT_CODE + line // (2 * SLOTS) + (slot - HOT_SLOT) * (slots // (2 * SLOTS))
-    code = jnp.where(slot < HOT_SLOT, line, jnp.where(slot < HOT_SLOT + 2, hot, -2))
-    picks = one_hot(code == row_ref[0:1, :])
-    total = dot(picks[:, 0:span], d_rows_ref[...])
+    d_all_ref[0:span, :] = d_rows_ref[...]
+    half = keep_ref.shape[0]
+    first = HOT_CODE + core_ref[0] * half
+    picks = one_hot(iota((half, wide), 0) + first == row_ref[0:1, :])
+    keep = dot(picks[:, 0:span], d_rows_ref[...])
+    first = HOT_CODE + (1 - core_ref[0]) * half
+    other_picks = one_hot(iota((half, wide), 0) + first == row_ref[0:1, :])
+    send = dot(other_picks[:, 0:span], d_rows_ref[...])
     d_outer = norm_backward(outer_ref[...], d_item, gain[...])
     inner = inner_ref[...]
     gate = jax.nn.sigmoid(inner)
     d_inner = dot_nt(d_outer.astype(BF), item_w2[...]) * (gate * (1.0 + inner * (1.0 - gate)))
     d_items = dot_nt(d_inner.astype(BF), item_w1[...])
-    d_items = jnp.concatenate(
-        [d_items, jnp.zeros((wide - span - PAD, d_items.shape[1]), F32)], axis=0
-    ).astype(BF)
-    outgoing[...] = (total + dot(picks[:, span:], d_items)).astype(BF)
+    d_items = jnp.concatenate([d_items, jnp.zeros((wide - span - PAD, emb), F32)], axis=0).astype(BF)
+    d_all_ref[span:, :] = d_items
+    keep_ref[...] = keep + dot(picks[:, span:], d_items)
+    send_ref[...] = send + dot(other_picks[:, span:], d_items)
+
+
+def rare_kernel(d_all_ref, row_ref, rare_ref):
+    shape = (rare_ref.shape[0], row_ref.shape[1])
+    rare_ref[...] = dot(one_hot(iota(shape, 0) == row_ref[0:1, :]), d_all_ref[...]).astype(BF)
+
+
+def outgoing_kernel(rare_ref, keep_ref, got_ref, outgoing_ref):
+    half = keep_ref.shape[0]
+    slots = rare_ref.shape[0]
+    shape = (slots, half)
+    line = iota(shape, 0)
+    owner, slot = line // SLOTS, line % SLOTS - HOT_SLOT
+    held = owner // 8 * 2 + owner % 2 + slot * (half // 2)
+    held = one_hot((slot >= 0) & (slot < 2) & (iota(shape, 1) == held))
+    hot = dot(held, (keep_ref[...] + got_ref[...]).astype(BF))
+    outgoing_ref[...] = (rare_ref[...].astype(F32) + hot).astype(BF)
 
 
 def scatter_kernel(returned_ref, row_ref, loss_ref, part_ref, sums_ref):
@@ -440,20 +459,19 @@
     sums_ref[...] = jnp.concatenate([block] * (sums_ref.shape[0] // 8), axis=0)
 
 
-def finish_kernel(count, sums_ref, other_ref, hot_ref, loss_ref):
-    emb = hot_ref.shape[1]
+def finish_kernel(count, core_ref, sums_ref, other_ref, hot_ref, loss_ref):
+    rows, emb = hot_ref.shape
     groups = sums_ref.shape[0] // 8
-
-    def of_row(row):
-        at = pl.ds(row, groups, stride=8)
-        return sums_ref[at, :] + other_ref[at, :]
-
-    row = 0
-    for i in range(2):
-        for j in range(0, emb, 128):
-            hot_ref[i * groups : (i + 1) * groups, j : j + 128] = of_row(row)
-            row += 1
-    loss_ref[...] = jnp.sum(of_row(row)[:, 0:1], axis=0, keepdims=True) / count
+    for core, ref in ((core_ref[0], sums_ref), (1 - core_ref[0], other_ref)):
+        row = 0
+        for i in range(2):
+            at = pl.ds(pl.multiple_of(core * (rows // 2) + i * groups, groups), groups)
+            for j in range(0, emb, 128):
+                hot_ref[at, j : j + 128] = ref[pl.ds(row, groups, stride=8), :]
+                row += 1
+    at = pl.ds(row, groups, stride=8)
+    losses = sums_ref[at, :] + other_ref[at, :]
+    loss_ref[...] = jnp.sum(losses[:, 0:1], axis=0, keepdims=True) / count
 
 
 def shards(
@@ -599,19 +617,43 @@
         compiler_params=params(40),
         name="user_backward",
     )(d_user, *map(in_hbm, loads + ahead))
-    outgoing, loss = pl.pallas_call(
+    core = lax.axis_index("tower").astype(jnp.int32).reshape(1)
+    row_ready = item_ready[0]
+    d_all, send, keep, loss = pl.pallas_call(
         functools.partial(item_backward_kernel, users),
-        out_shape=(shape((slots, emb), BF), shape((8, 128), F32)),
-        in_specs=[VMEM] * 8,
-        out_specs=(VMEM, VMEM),
+        out_shape=(
+            shape((wide, emb), BF),
+            shape((owners // 2, emb), F32),
+            shape((owners // 2, emb), F32),
+            shape((8, 128), F32),
+        ),
+        in_specs=[SMEM] + [VMEM] * 8,
+        out_specs=(VMEM,) * 4,
         compiler_params=params(32),
         name="item_backward",
-    )(parts, d_rows, *map(in_vmem, item_ready))
+    )(core, parts, d_rows, *map(in_vmem, item_ready))
+    got = lax.ppermute(send, "tower", swap)
+    rare = pl.pallas_call(
+        rare_kernel,
+        out_shape=shape((slots, emb), BF),
+        in_specs=[VMEM, VMEM],
+        out_specs=VMEM,
+        compiler_params=params(32),
+        name="rare",
+    )(d_all, in_vmem(row_ready))
+    outgoing = pl.pallas_call(
+        outgoing_kernel,
+        out_shape=shape((slots, emb), BF),
+        in_specs=[VMEM] * 3,
+        out_specs=VMEM,
+        compiler_params=params(32),
+        name="outgoing",
+    )(rare, keep, got)
 
     returned = exchange(outgoing, SHARD)
     part, mine = pl.pallas_call(
         scatter_kernel,
-        out_shape=(shape((rare_count, emb), BF), shape((owners // 2 * 8, 128), F32)),
+        out_shape=(shape((rare_count, emb), BF), shape((owners // 4 * 8, 128), F32)),
         in_specs=[VMEM, VMEM, VMEM],
         out_specs=(VMEM, VMEM),
         compiler_params=params(24),
@@ -621,13 +663,13 @@
     sums = exchange(mine, GROUP)
     other_sums = lax.ppermute(sums, "tower", swap)
     hot_total, loss_total = pl.pallas_call(
-        functools.partial(finish_kernel, total * (near // 2)),
+        functools.partial(finish_kernel, total * 2),
         out_shape=(shape((owners, emb), F32), shape((1, 1), F32)),
-        in_specs=[VMEM, VMEM],
+        in_specs=[SMEM, VMEM, VMEM],
         out_specs=(VMEM, VMEM),
         compiler_params=params(24),
         name="finish",
-    )(sums, other_sums)
+    )(core, sums, other_sums)
     return (hot_total, rare_grad, loss_total[0, 0])
 
 

time: 165 us -> 159 us (0.964)
  blocking collectives: 95.8 us -> 106 us
  waiting for transfers between devices: 16.6 us -> 6.43 us
  starting transfers between devices: 24.9 us -> 19.4 us
    all_to_all x0 -> x1, blocking collectives: none -> 11 us  [shards(): sums = exchange(mine, GROUP)]
    all_to_all x1 -> x0, waiting for transfers between devices: 10.4 us -> none  [shards(): sums = exchange(mine, GROUP)]
    all_to_all x1 -> x0, starting transfers between devices: 5.28 us -> none  [shards(): sums = exchange(mine, GROUP)]
    ppermute x1, starting transfers between devices: 3.62 us -> 0.89 us  [shards(): other_sums = lax.ppermute(sums, 'tower', swap)]
    ppermute x0 -> x1, starting transfers between devices: none -> 2.24 us  [shards(): got = lax.ppermute(send, 'tower', swap)]
where the time goes in v11:
time: 159 us
  blocking collectives  106 us (67%)
  Pallas kernels  25.2 us (16%)
  starting transfers between devices  19.4 us (12%)
  waiting for transfers between devices  6.43 us (4%)
    all_to_all x1, blocking collectives, shards(): returned = exchange(outgoing, SHARD)  27.4 us
    all_to_all x1, blocking collectives, shards(): asked = exchange(request, SHARD)  26.7 us
    all_to_all x1, blocking collectives, shards(): fetched = exchange(served, SHARD)  23.6 us
    all_to_all x1, blocking collectives, shards(): gathered = exchange(spread, ('x', 'y'))  17.2 us
    all_to_all x1, blocking collectives, shards(): sums = exchange(mine, GROUP)  11 us
    pallas_call x1, Pallas kernels, shards(): pl.pallas_call(functools.partial(user_backward_kernel, users), out_shape=...  6.73 us
    ppermute x1, starting transfers between devices, shards(): swapped = lax.ppermute(gathered, 'tower', swap)  6.04 us
    pallas_call x1, Pallas kernels, shards(): pl.pallas_call(functools.partial(user_forward_kernel, users), out_shape=(...  5.74 us
  transfers between devices with their start and end apart: 6, of which 5 were waited for; matrix products, arithmetic and copies ran while one was open for 1% of the time, Pallas kernels for 8%

profile of v11, /device:TPU:1, one launch (start us, length us, event | category | flops | bytes accessed | tf_op | source)
XLA Modules:
  0.0 158.7 jit_solution(2759523476950900523)
XLA Ops:
  0.6 1.9 %index.1 = (s32[128,128]{1,0:T(8,128)S(1)}, bf16[512,256]{1,0:T(8,128)(2,1)S(1)}, s32[8,384]{1,0:T(8,128)}, s32[384,128]{1,0:T(8,128)}) custom-call(s32[4,64]{1,0:T(4,128)} %history_hbm.1, s32[1,4]{1,0:T(1,128)} %bitcast.45, f32[512,256]{1,0:T(8,128)} %table_hbm.1), custom_call_target="tpu_custom_call" | custom-call | tf_op jit(solution)/shard_map/index/pallas_call | solution.py:519
  2.5 26.7 %all_to_all.77 = s32[128,1,128]{2,1,0:T(1,128)S(1)} all-to-all(s32[128,1,128]{2,1,0:T(1,128)S(1)} %bitcast.38), channel_id=1, replica_groups=mesh['tower'=2,'x'=4,'y'=4,'zh'=4,'zl'=2] {'x','y','zh','zl'}, dimensions={0} | all-to-all | bytes 131072 | tf_op jit(solution)/shard_map/all_to_all | solution.py:532
  29.2 1.3 serve.1
  30.5 23.6 %all_to_all.78 = bf16[128,8,256]{2,1,0:T(8,128)(2,1)S(1)} all-to-all(bf16[128,8,256]{2,1,0:T(8,128)(2,1)S(1)} %bitcast.33), channel_id=1, replica_groups=mesh['tower'=2,'x'=4,'y'=4,'zh'=4,'zl'=2] {'x','y','zh','zl'}, dimensions={0} | all-to-all | bytes 1048576 | tf_op jit(solution)/shard_map/all_to_all | solution.py:551
  54.1 3.0 %item_forward.1 = (bf16[64,1024]{1,0:T(8,128)(2,1)}, f32[16,1024]{1,0:T(8,128)}) custom-call(bf16[1024,256]{1,0:T(8,128)(2,1)S(1)} %bitcast.27, bf16[128,256]{1,0:T(8,128)(2,1)S(1)} %get-tuple-element.40.hot_ref, s32[16,128]{1,0:T(8,128)S(1)} %get-tuple-element.41.column_ref, bf16[256,1024]{1,0:T(8,128)(2,1)} %refs_16_.1, bf16[1024,1024]{1,0:T(8,128)(2,1)} %refs_15_.1, ...), custom_call_target="tpu_custom_call" | custom-call | tf_op jit(solution)/shard_map/item_forward/pallas_call | solution.py:555
  57.1 3.4 %all-to-all-start.2 = ((bf16[8,8,1024]{2,1,0:T(8,128)(2,1)}), bf16[8,8,1024]{2,1,0:T(8,128)(2,1)S(1)}, u32[]{:S(2)}, u32[]{:S(2)}) async-start(bf16[8,8,1024]{2,1,0:T(8,128)(2,1)} %bitcast.10), calls=%async_computation.2 | async-start | bytes 262144 | tf_op jit(solution)/shard_map/all_to_all | solution.py:564
  60.5 5.7 %user_forward.1 = (bf16[16,1024]{1,0:T(8,128)(2,1)S(1)}, f32[256,1024]{1,0:T(8,128)}, bf16[256,1024]{1,0:T(8,128)(2,1)}, bf16[64,1024]{1,0:T(8,128)(2,1)}, f32[64,256]{1,0:T(8,128)}, /*index=5*/f32[16,1024]{1,0:T(8,128)}) custom-call(bf16[1024,256]{1,0:T(8,128)(2,1)S(1)} %bitcast.28, s32[384,128]{1,0:T(8,128)} %get-tuple-element.38.column_hbm.refs_1_, ...), custom_call_target="tpu_custom_call" | custom-call | tf_op jit(solution)/shard_map/user_forward/pallas_call | solution.py:575
  66.3 2.1 %all-to-all-done.2 = bf16[8,8,1024]{2,1,0:T(8,128)(2,1)S(1)} async-done(((bf16[8,8,1024]{2,1,0:T(8,128)(2,1)}), bf16[8,8,1024]{2,1,0:T(8,128)(2,1)S(1)}, u32[]{:S(2)}, u32[]{:S(2)}) %all-to-all-start.2) | async-done | bytes 131104 | tf_op jit(solution)/shard_map/all_to_all | solution.py:564
  68.7 17.2 %all_to_all.79 = bf16[16,40,1024]{2,1,0:T(8,128)(2,1)S(1)} all-to-all(bf16[16,40,1024]{2,1,0:T(8,128)(2,1)S(1)} %bitcast.26), channel_id=1, replica_groups=mesh['tower'=2,'x'=4,'y'=4,'zh'=4,'zl'=2] {'x','y'}, dimensions={0} | all-to-all | bytes 2621440 | tf_op jit(solution)/shard_map/all_to_all | solution.py:594
  85.9 6.0 %collective-permute-start = (bf16[640,1024]{1,0:T(8,128)(2,1)S(1)}, bf16[640,1024]{1,0:T(8,128)(2,1)S(1)}, u32[]{:S(2)}, u32[]{:S(2)}) collective-permute-start(bf16[640,1024]{1,0:T(8,128)(2,1)S(1)} %bitcast.24), channel_id=1, source_target_pairs={{0,128},{128,0},{1,129},{129,1},{2,130},{130,2},{3,131},{131,3},{4... | collective-permute-start | bytes 3932168 | tf_op jit(solution)/shard_map/ppermute | solution.py:595
  92.0 2.6 %collective-permute-done.swapped_ref = bf16[640,1024]{1,0:T(8,128)(2,1)S(1)} collective-permute-done((bf16[640,1024]{1,0:T(8,128)(2,1)S(1)}, bf16[640,1024]{1,0:T(8,128)(2,1)S(1)}, u32[]{:S(2)}, u32[]{:S(2)}) %collective-permute-start) | collective-permute-done | bytes 1310752 | tf_op jit(solution)/shard_map/ppermute | solution.py:595
  94.6 3.0 %softmax.1 = (f32[16,1024]{1,0:T(8,128)S(1)}, bf16[64,1024]{1,0:T(8,128)(2,1)}) custom-call(s32[2]{0:T(128)S(1)} %pad_add_fusion.place_ref, bf16[640,1024]{1,0:T(8,128)(2,1)S(1)} %bitcast.25, bf16[640,1024]{1,0:T(8,128)(2,1)S(1)} %collective-permute-done.swapped_ref), custom_call_target="tpu_custom_call" | custom-call | tf_op jit(solution)/shard_map/softmax/pallas_call | solution.py:597
  97.6 4.5 %all-to-all-start.4 = ((bf16[8,8,1024]{2,1,0:T(8,128)(2,1)}), bf16[8,8,1024]{2,1,0:T(8,128)(2,1)S(1)}, u32[]{:S(2)}, u32[]{:S(2)}) async-start(bf16[8,8,1024]{2,1,0:T(8,128)(2,1)} %bitcast.16), calls=%async_computation.4 | async-start | bytes 262144 | tf_op jit(solution)/shard_map/all_to_all | solution.py:606
  102.0 6.7 %user_backward.1 = (bf16[256,256]{1,0:T(8,128)(2,1)S(1)}, s32[8,384]{1,0:T(8,128)S(1)}, f32[1,1024]{1,0:T(1,128)S(1)}, f32[16,1024]{1,0:T(8,128)S(1)}, bf16[1024...) custom-call(f32[16,1024]{1,0:T(8,128)S(1)} %get-tuple-element.45.d_user_ref, ...), custom_call_target="tpu_custom_call" | custom-call | tf_op jit(solution)/shard_map/user_backward/pallas_call | solution.py:611
  108.8 1.1 all-to-all-done.4
  109.9 1.2 item_backward.1
  111.2 2.2 %collective-permute-start.1 = (f32[64,256]{1,0:T(8,128)S(1)}, f32[64,256]{1,0:T(8,128)S(1)}, u32[]{:S(2)}, u32[]{:S(2)}) collective-permute-start(f32[64,256]{1,0:T(8,128)S(1)} %get-tuple-element.62), channel_id=1, source_target_pairs={{0,128},{128,0},{1,129},{129,1},{2,130},{130,2},{3,131},{131,3},{4... | collective-permute-start | bytes 196616 | tf_op jit(solution)/shard_map/ppermute | solution.py:635
  114.7 27.4 %all_to_all.80 = bf16[128,8,256]{2,1,0:T(8,128)(2,1)S(1)} all-to-all(bf16[128,8,256]{2,1,0:T(8,128)(2,1)S(1)} %bitcast.30), channel_id=1, replica_groups=mesh['tower'=2,'x'=4,'y'=4,'zh'=4,'zl'=2] {'x','y','zh','zl'}, dimensions={0} | all-to-all | bytes 1048576 | tf_op jit(solution)/shard_map/all_to_all | solution.py:653
  142.2 0.5 scatter.1
  142.7 2.4 %collective-permute-start.3 = (bf16[512,256]{1,0:T(8,128)(2,1)S(1)}, bf16[512,256]{1,0:T(8,128)(2,1)S(1)}, u32[]{:S(2)}, u32[]{:S(2)}) collective-permute-start(bf16[512,256]{1,0:T(8,128)(2,1)S(1)} %get-tuple-element.67), channel_id=1, source_target_pairs={{0,128},{128,0},{1,129},{129,1},{2,130},{130,2},{3,131},{131,3},{4... | collective-permute-start | bytes 786440 | tf_op jit(solution)/shard_map/ppermute | solution.py:662
  145.1 11.0 %all_to_all.81 = f32[32,8,128]{2,1,0:T(8,128)S(1)} all-to-all(f32[32,8,128]{2,1,0:T(8,128)S(1)} %bitcast.37), channel_id=1, replica_groups=mesh['tower'=2,'x'=4,'y'=4,'zh'=4,'zl'=2] {'x','y','zl'}, dimensions={0} | all-to-all | bytes 262144 | tf_op jit(solution)/shard_map/all_to_all | solution.py:663
  156.1 0.9 collective-permute-start.2
  157.0 0.8 convert_add_fusion
  158.0 0.7 finish.1
  (9 shorter events, 1.8 us)
Async XLA Ops:
  57.1 11.2 %all-to-all-start.2 = ((bf16[8,8,1024]{2,1,0:T(8,128)(2,1)}), bf16[8,8,1024]{2,1,0:T(8,128)(2,1)S(1)}, u32[]{:S(2)}, u32[]{:S(2)}) async-start(bf16[8,8,1024]{2,1,0:T(8,128)(2,1)} %bitcast.10), calls=%async_computation.2 | async-start | bytes 262144 | tf_op jit(solution)/shard_map/all_to_all | solution.py:564
  85.9 8.7 %collective-permute-start = (bf16[640,1024]{1,0:T(8,128)(2,1)S(1)}, bf16[640,1024]{1,0:T(8,128)(2,1)S(1)}, u32[]{:S(2)}, u32[]{:S(2)}) collective-permute-start(bf16[640,1024]{1,0:T(8,128)(2,1)S(1)} %bitcast.24), channel_id=1, source_target_pairs={{0,128},{128,0},{1,129},{129,1},{2,130},{130,2},{3,131},{131,3},{4... | collective-permute-start | bytes 3932168 | tf_op jit(solution)/shard_map/ppermute | solution.py:595
  97.6 12.3 %all-to-all-start.4 = ((bf16[8,8,1024]{2,1,0:T(8,128)(2,1)}), bf16[8,8,1024]{2,1,0:T(8,128)(2,1)S(1)}, u32[]{:S(2)}, u32[]{:S(2)}) async-start(bf16[8,8,1024]{2,1,0:T(8,128)(2,1)} %bitcast.16), calls=%async_computation.4 | async-start | bytes 262144 | tf_op jit(solution)/shard_map/all_to_all | solution.py:606
  111.2 31.0 %copy-start = (s32[8,1024]{1,0:T(8,128)S(1)}, s32[8,1024]{1,0:T(8,128)}, u32[]{:S(2)}) copy-start(s32[8,1024]{1,0:T(8,128)} %get-tuple-element.63.row_ref) | copy-start | bytes 98308
  111.2 3.1 %collective-permute-start.1 = (f32[64,256]{1,0:T(8,128)S(1)}, f32[64,256]{1,0:T(8,128)S(1)}, u32[]{:S(2)}, u32[]{:S(2)}) collective-permute-start(f32[64,256]{1,0:T(8,128)S(1)} %get-tuple-element.62), channel_id=1, source_target_pairs={{0,128},{128,0},{1,129},{129,1},{2,130},{130,2},{3,131},{131,3},{4... | collective-permute-start | bytes 196616 | tf_op jit(solution)/shard_map/ppermute | solution.py:635
  142.7 14.3 %collective-permute-start.3 = (bf16[512,256]{1,0:T(8,128)(2,1)S(1)}, bf16[512,256]{1,0:T(8,128)(2,1)S(1)}, u32[]{:S(2)}, u32[]{:S(2)}) collective-permute-start(bf16[512,256]{1,0:T(8,128)(2,1)S(1)} %get-tuple-element.67), channel_id=1, source_target_pairs={{0,128},{128,0},{1,129},{129,1},{2,130},{130,2},{3,131},{131,3},{4... | collective-permute-start | bytes 786440 | tf_op jit(solution)/shard_map/ppermute | solution.py:662
  156.1 1.9 %collective-permute-start.2 = (f32[256,128]{1,0:T(8,128)S(1)}, f32[256,128]{1,0:T(8,128)S(1)}, u32[]{:S(2)}, u32[]{:S(2)}) collective-permute-start(f32[256,128]{1,0:T(8,128)S(1)} %bitcast.34), channel_id=1, source_target_pairs={{0,128},{128,0},{1,129},{129,1},{2,130},{130,2},{3,131},{131,3},{4... | collective-permute-start | bytes 393224 | tf_op jit(solution)/shard_map/ppermute | solution.py:664

commit v12 on v11

--- a/solution.py
+++ b/solution.py
@@ -65,13 +65,11 @@
     table_hbm,
     request_ref,
     known_ref,
-    row_hbm,
-    column_hbm,
+    row,
+    column,
     history_ref,
     items_ref,
     table,
-    row,
-    column,
     sems,
 ):
     loads = copies_of(
@@ -99,7 +97,6 @@
     )
     row[...] = jnp.broadcast_to(places, row.shape)
     column[...] = jnp.transpose(jnp.broadcast_to(places.astype(F32), (128, span))).astype(jnp.int32)
-    saves = copies_of([(row, row_hbm), (column, column_hbm)], sems.at[pl.ds(3, 2)])
     order = jnp.where(hits, earlier, -1.0)
     lanes = iota(request_ref.shape, 1)
     request = jnp.zeros(request_ref.shape, F32)
@@ -109,17 +106,27 @@
     request_ref[...] = request.astype(jnp.int32)
     loads[2].wait()
     known_ref[...] = table[...].astype(BF)
-    for save in saves:
-        save.wait()
 
 
 def serve_kernel(
-    asked_ref, known_ref, hot_hbm, column_hbm, served, hot_ref, column_ref, row_hbm, hot, row, sems
+    asked_ref,
+    known_ref,
+    row_ref,
+    column_ref,
+    hot_hbm,
+    served,
+    hot_ref,
+    item_column_ref,
+    asked_row_hbm,
+    row_hbm,
+    column_hbm,
+    hot,
+    row,
+    sems,
 ):
-    span = column_hbm.shape[0] - 128
-    loads = copies_of(
-        [(hot_hbm, hot), (column_hbm.at[pl.ds(span, PAD)], column_ref)], sems
-    )
+    copies = copies_of([(hot_hbm, hot), (row_ref, row_hbm), (column_ref, column_hbm)], sems)
+    span = column_ref.shape[0] - 128
+    item_column_ref[...] = column_ref[span : span + PAD, :]
     slots = served.shape[0]
     sources = asked_ref.shape[0]
     asked = asked_ref[...]
@@ -131,7 +138,7 @@
     index = jnp.sum(jnp.where(mine, wide, 0.0), axis=1, keepdims=True) - 1.0
     index = jnp.broadcast_to(index, wide.shape)
     row[...] = jnp.transpose(index)[0:8].astype(jnp.int32)
-    save = pltpu.make_async_copy(row, row_hbm, sems.at[2])
+    save = pltpu.make_async_copy(row, asked_row_hbm, sems.at[3])
     save.start()
     index = index.astype(jnp.int32)
     lanes = iota(index.shape, 1)
@@ -140,10 +147,10 @@
         [one_hot(index == lanes + 128 * j) for j in range(rows // 128)], axis=1
     )
     served[...] = dot(picks, known_ref[...]).astype(BF)
-    for load in loads:
-        load.wait()
+    copies[0].wait()
     hot_ref[...] = hot[...].astype(BF)
-    save.wait()
+    for copy in copies[1:] + [save]:
+        copy.wait()
 
 
 def head_mask(heads, width):
@@ -178,39 +185,39 @@
 
 
 def item_forward_kernel(users, fetched_ref, hot_ref, column_ref, *refs):
-    sources, refs = refs[:3], refs[3:]
-    vectors_ref, inner_hbm, refs = refs[0], refs[1], refs[2:]
-    targets, (inner_ref, sems) = refs[:3], refs[3:]
+    sources, (vectors_ref, inner_ref, outer_ref), refs = refs[:3], refs[3:6], refs[6:]
+    targets, sems = refs[:3], refs[3]
     item_w1, item_w2, gain = targets
     copies = copies_of(zip(sources, targets), sems)
     rows = look_up(column_ref[...], fetched_ref, hot_ref)
     copies[0].wait()
     inner = dot(rows, item_w1[...])
     inner_ref[...] = inner
-    save = pltpu.make_async_copy(inner_ref, inner_hbm, sems.at[3])
-    save.start()
     gated = (inner * jax.nn.sigmoid(inner)).astype(BF)
     copies[1].wait()
     copies[2].wait()
     outer = dot(gated, item_w2[...])
+    outer_ref[...] = outer
     scale = lax.rsqrt(jnp.mean(outer * outer, axis=-1, keepdims=True) + EPS)
     vectors = jnp.where(iota(outer.shape, 0) < users, outer * scale * gain[...], 0.0)
     peers = vectors_ref.shape[0] // 8
     vectors_ref[...] = jnp.concatenate([vectors[0:8]] * peers, axis=0).astype(BF)
-    save.wait()
 
 
 def user_forward_kernel(users, *refs):
-    fetched_ref, sources, refs = refs[0], refs[1:11], refs[11:]
-    vectors_ref, kept_hbm, refs = refs[0], refs[1:6], refs[6:]
+    fetched_ref, item_kept, sources, refs = refs[0], refs[1:3], refs[3:13], refs[13:]
+    vectors_ref, kept_hbm, item_kept_hbm, refs = refs[0], refs[1:6], refs[6:8], refs[8:]
     targets, kept, (in_sems, out_sems) = refs[:10], refs[10:15], refs[15:]
     column_of, hot, pos_of, norm_gain_ref, out_gain_ref = targets[:5]
     in_proj, w_query, w_key, w_value, w_out = targets[5:]
     hidden_ref, normed_ref, qk_ref, weights_ref, mixed_ref = kept
     copies = copies_of(zip(sources, targets), in_sems)
     saves = [
-        pltpu.make_async_copy(a, b, out_sems.at[i]) for i, (a, b) in enumerate(zip(kept, kept_hbm))
+        pltpu.make_async_copy(a, b, out_sems.at[i])
+        for i, (a, b) in enumerate(zip(kept + item_kept, kept_hbm + item_kept_hbm))
     ]
+    saves[5].start()
+    saves[6].start()
     hist, width = pos_of.shape
     heads = width // HEAD_DIM
     span = users * hist
@@ -347,8 +354,8 @@
 
 
 def user_backward_kernel(users, d_user_ref, *refs):
-    sources, refs = refs[:17], refs[17:]
-    d_rows_ref, ahead, outer_ref, refs = refs[0], refs[1:6], refs[6], refs[7:]
+    sources, refs = refs[:18], refs[18:]
+    d_rows_ref, ahead, refs = refs[0], refs[1:7], refs[7:]
     targets, (d_normed, sems) = refs[:12], refs[12:]
     mixed_ref, out_gain_ref, w_out, w_value, normed_ref, weights_ref, qk_ref = targets[:7]
     w_key, w_query, hidden_ref, norm_gain_ref, in_proj = targets[7:]
@@ -394,8 +401,6 @@
     d_rows_ref[...] = dot_nt(d_normed[...].astype(BF), in_proj[...]).astype(BF)
     for copy in copies[12:]:
         copy.wait()
-    inner = ahead[2][...]
-    outer_ref[...] = dot((inner * jax.nn.sigmoid(inner)).astype(BF), ahead[3][...])
 
 
 def item_backward_kernel(users, core_ref, parts_ref, d_rows_ref, *refs):
@@ -521,43 +526,45 @@
         out_shape=(
             shape((owners, 128), jnp.int32),
             pltpu.VMEM((rare_count, emb), BF),
-            *map(hbm, places),
+            *map(vmem, places),
         ),
         in_specs=[HBM] * 3,
-        out_specs=(VMEM, VMEM, HBM, HBM),
-        scratch_shapes=like(loads + places) + [sems(5)],
+        out_specs=(VMEM,) * 4,
+        scratch_shapes=like(loads) + [sems(3)],
         compiler_params=params(24),
         name="index",
     )(*map(in_hbm, loads))
     asked = exchange(request, SHARD)
-    served, hot_ready, item_column, asked_row = pl.pallas_call(
+    served, hot_ready, item_column, asked_row, row, column = pl.pallas_call(
         serve_kernel,
         out_shape=(
             shape((slots, emb), BF),
             pltpu.VMEM(hot_table.shape, BF),
             pltpu.VMEM((PAD, 128), jnp.int32),
             pltpu.HBM((8, slots), jnp.int32),
+            *map(hbm, places),
         ),
-        in_specs=[VMEM, VMEM, HBM, HBM],
-        out_specs=(VMEM, VMEM, VMEM, HBM),
+        in_specs=[VMEM] * 4 + [HBM],
+        out_specs=(VMEM, VMEM, VMEM, HBM, HBM, HBM),
         scratch_shapes=[
             pltpu.VMEM(hot_table.shape, F32),
             pltpu.VMEM((8, slots), jnp.int32),
-            sems(3),
+            sems(4),
         ],
         compiler_params=params(24),
         name="serve",
-    )(asked, in_vmem(known), in_hbm(hot_table), in_hbm(column))
+    )(asked, *map(in_vmem, (known, row, column)), in_hbm(hot_table))
     fetched = exchange(served, SHARD)
 
     norm_gain, out_gain, item_gain = (g.reshape(1, width) for g in (norm_gain, out_gain, item_gain))
     loads = (item_w1, item_w2, item_gain)
-    item_vec, inner = pl.pallas_call(
+    item_kept = (shape((PAD, width), F32), shape((PAD, width), F32))
+    item_vec, inner, outer = pl.pallas_call(
         functools.partial(item_forward_kernel, users),
-        out_shape=(shape((near * 8, width), BF), pltpu.HBM((PAD, width), F32)),
+        out_shape=(shape((near * 8, width), BF), *map(vmem, item_kept)),
         in_specs=[VMEM] * 3 + [HBM] * 3,
-        out_specs=(VMEM, HBM),
-        scratch_shapes=like(loads) + [pltpu.VMEM((PAD, width), F32), sems(4)],
+        out_specs=(VMEM,) * 3,
+        scratch_shapes=like(loads) + [sems(3)],
         compiler_params=params(24),
         name="item_forward",
     )(fetched, in_vmem(hot_ready), in_vmem(item_column), *map(in_hbm, loads))
@@ -572,15 +579,15 @@
         shape((users * heads, span), F32),
         shape((PAD, width), F32),
     )
-    user_vec, hidden, normed, qk, weights, mixed = pl.pallas_call(
+    user_vec, hidden, normed, qk, weights, mixed, inner, outer = pl.pallas_call(
         functools.partial(user_forward_kernel, users),
-        out_shape=(shape((PAD, width), BF), *map(hbm, kept)),
-        in_specs=[VMEM] + [HBM] * len(loads),
-        out_specs=(VMEM,) + (HBM,) * len(kept),
-        scratch_shapes=like(loads + kept) + [sems(len(loads)), sems(len(kept))],
+        out_shape=(shape((PAD, width), BF), *map(hbm, kept + item_kept)),
+        in_specs=[VMEM] * 3 + [HBM] * len(loads),
+        out_specs=(VMEM,) + (HBM,) * (len(kept) + 2),
+        scratch_shapes=like(loads + kept) + [sems(len(loads)), sems(len(kept) + 2)],
         compiler_params=params(40),
         name="user_forward",
-    )(fetched, *map(in_hbm, loads))
+    )(fetched, in_vmem(inner), in_vmem(outer), *map(in_hbm, loads))
 
     rows = owners // near * (near * users + 8)
     spread = pl.pallas_call(
@@ -607,13 +614,13 @@
 
     loads = (mixed, out_gain, w_out, w_value, normed, weights, qk)
     loads += (w_key, w_query, hidden, norm_gain, in_proj)
-    ahead = (row, item_gain, inner, item_w2, item_w1)
+    ahead = (row, item_gain, inner, item_w2, item_w1, outer)
     d_rows, *item_ready = pl.pallas_call(
         functools.partial(user_backward_kernel, users),
-        out_shape=(shape((span, emb), BF), *map(vmem, ahead), pltpu.VMEM((PAD, width), F32)),
-        in_specs=[VMEM] + [HBM] * 17,
+        out_shape=(shape((span, emb), BF), *map(vmem, ahead)),
+        in_specs=[VMEM] + [HBM] * 18,
         out_specs=(VMEM,) * 7,
-        scratch_shapes=like(loads) + [pltpu.VMEM((span, width), F32), sems(17)],
+        scratch_shapes=like(loads) + [pltpu.VMEM((span, width), F32), sems(18)],
         compiler_params=params(40),
         name="user_backward",
     )(d_user, *map(in_hbm, loads + ahead))

time: 159 us -> 158 us (level)
  no operation moved by 1% of the time
where the time goes in v12:
time: 158 us
  blocking collectives  106 us (67%)
  Pallas kernels  24.3 us (15%)
  starting transfers between devices  19.5 us (12%)
  waiting for transfers between devices  6.75 us (4%)
    all_to_all x1, blocking collectives, shards(): returned = exchange(outgoing, SHARD)  27.1 us
    all_to_all x1, blocking collectives, shards(): asked = exchange(request, SHARD)  26.7 us
    all_to_all x1, blocking collectives, shards(): fetched = exchange(served, SHARD)  23.6 us
    all_to_all x1, blocking collectives, shards(): gathered = exchange(spread, ('x', 'y'))  17.2 us
    all_to_all x1, blocking collectives, shards(): sums = exchange(mine, GROUP)  11 us
    pallas_call x1, Pallas kernels, shards(): pl.pallas_call(functools.partial(user_backward_kernel, users), out_shape=...  6.34 us
    ppermute x1, starting transfers between devices, shards(): swapped = lax.ppermute(gathered, 'tower', swap)  6.04 us
    pallas_call x1, Pallas kernels, shards(): pl.pallas_call(functools.partial(user_forward_kernel, users), out_shape=(...  5.8 us
  transfers between devices with their start and end apart: 6, of which 5 were waited for; matrix products, arithmetic and copies ran while one was open for 1% of the time, Pallas kernels for 8%

profile of v12, /device:TPU:1, one launch (start us, length us, event | category | flops | bytes accessed | tf_op | source)
XLA Modules:
  0.0 157.8 jit_solution(3007350299067610387)
XLA Ops:
  0.6 1.3 index.1
  1.9 26.7 %all_to_all.77 = s32[128,1,128]{2,1,0:T(1,128)S(1)} all-to-all(s32[128,1,128]{2,1,0:T(1,128)S(1)} %bitcast.38), channel_id=1, replica_groups=mesh['tower'=2,'x'=4,'y'=4,'zh'=4,'zl'=2] {'x','y','zh','zl'}, dimensions={0} | all-to-all | bytes 131072 | tf_op jit(solution)/shard_map/all_to_all | solution.py:537
  28.6 1.4 serve.1
  30.0 23.6 %all_to_all.78 = bf16[128,8,256]{2,1,0:T(8,128)(2,1)S(1)} all-to-all(bf16[128,8,256]{2,1,0:T(8,128)(2,1)S(1)} %bitcast.33), channel_id=1, replica_groups=mesh['tower'=2,'x'=4,'y'=4,'zh'=4,'zl'=2] {'x','y','zh','zl'}, dimensions={0} | all-to-all | bytes 1048576 | tf_op jit(solution)/shard_map/all_to_all | solution.py:557
  53.6 3.0 %item_forward.1 = (bf16[64,1024]{1,0:T(8,128)(2,1)}, f32[16,1024]{1,0:T(8,128)S(1)}, f32[16,1024]{1,0:T(8,128)S(1)}) custom-call(bf16[1024,256]{1,0:T(8,128)(2,1)S(1)} %bitcast.27, bf16[128,256]{1,0:T(8,128)(2,1)S(1)} %get-tuple-element.46.hot_ref, s32[16,128]{1,0:T(8,128)S(1)} %get-tuple-element.47.column_ref, bf16[256,1024]{1,0:T(8,128)(2,1)} %refs_16_.1, ...), custom_call_target="tpu_custom_call" | custom-call | tf_op jit(solution)/shard_map/item_forward/pallas_call | solution.py:562
  56.6 3.4 %all-to-all-start.2 = ((bf16[8,8,1024]{2,1,0:T(8,128)(2,1)}), bf16[8,8,1024]{2,1,0:T(8,128)(2,1)S(1)}, u32[]{:S(2)}, u32[]{:S(2)}) async-start(bf16[8,8,1024]{2,1,0:T(8,128)(2,1)} %bitcast.10), calls=%async_computation.2 | async-start | bytes 262144 | tf_op jit(solution)/shard_map/all_to_all | solution.py:571
  60.0 5.8 %user_forward.1 = (bf16[16,1024]{1,0:T(8,128)(2,1)S(1)}, f32[256,1024]{1,0:T(8,128)}, bf16[256,1024]{1,0:T(8,128)(2,1)}, bf16[64,1024]{1,0:T(8,128)(2,1)}, f32[6...) custom-call(bf16[1024,256]{1,0:T(8,128)(2,1)S(1)} %bitcast.28, ...), custom_call_target="tpu_custom_call" | custom-call | tf_op jit(solution)/shard_map/user_forward/pallas_call | solution.py:582
  65.8 2.0 %all-to-all-done.2 = bf16[8,8,1024]{2,1,0:T(8,128)(2,1)S(1)} async-done(((bf16[8,8,1024]{2,1,0:T(8,128)(2,1)}), bf16[8,8,1024]{2,1,0:T(8,128)(2,1)S(1)}, u32[]{:S(2)}, u32[]{:S(2)}) %all-to-all-start.2) | async-done | bytes 131104 | tf_op jit(solution)/shard_map/all_to_all | solution.py:571
  68.1 17.2 %all_to_all.79 = bf16[16,40,1024]{2,1,0:T(8,128)(2,1)S(1)} all-to-all(bf16[16,40,1024]{2,1,0:T(8,128)(2,1)S(1)} %bitcast.26), channel_id=1, replica_groups=mesh['tower'=2,'x'=4,'y'=4,'zh'=4,'zl'=2] {'x','y'}, dimensions={0} | all-to-all | bytes 2621440 | tf_op jit(solution)/shard_map/all_to_all | solution.py:601
  85.4 6.0 %collective-permute-start = (bf16[640,1024]{1,0:T(8,128)(2,1)S(1)}, bf16[640,1024]{1,0:T(8,128)(2,1)S(1)}, u32[]{:S(2)}, u32[]{:S(2)}) collective-permute-start(bf16[640,1024]{1,0:T(8,128)(2,1)S(1)} %bitcast.24), channel_id=1, source_target_pairs={{0,128},{128,0},{1,129},{129,1},{2,130},{130,2},{3,131},{131,3},{4... | collective-permute-start | bytes 3932168 | tf_op jit(solution)/shard_map/ppermute | solution.py:602
  91.5 2.6 %collective-permute-done.swapped_ref = bf16[640,1024]{1,0:T(8,128)(2,1)S(1)} collective-permute-done((bf16[640,1024]{1,0:T(8,128)(2,1)S(1)}, bf16[640,1024]{1,0:T(8,128)(2,1)S(1)}, u32[]{:S(2)}, u32[]{:S(2)}) %collective-permute-start) | collective-permute-done | bytes 1310752 | tf_op jit(solution)/shard_map/ppermute | solution.py:602
  94.1 3.0 %softmax.1 = (f32[16,1024]{1,0:T(8,128)S(1)}, bf16[64,1024]{1,0:T(8,128)(2,1)}) custom-call(s32[2]{0:T(128)S(1)} %pad_add_fusion.place_ref, bf16[640,1024]{1,0:T(8,128)(2,1)S(1)} %bitcast.25, bf16[640,1024]{1,0:T(8,128)(2,1)S(1)} %collective-permute-done.swapped_ref), custom_call_target="tpu_custom_call" | custom-call | tf_op jit(solution)/shard_map/softmax/pallas_call | solution.py:604
  97.0 4.5 %all-to-all-start.4 = ((bf16[8,8,1024]{2,1,0:T(8,128)(2,1)}), bf16[8,8,1024]{2,1,0:T(8,128)(2,1)S(1)}, u32[]{:S(2)}, u32[]{:S(2)}) async-start(bf16[8,8,1024]{2,1,0:T(8,128)(2,1)} %bitcast.16), calls=%async_computation.4 | async-start | bytes 262144 | tf_op jit(solution)/shard_map/all_to_all | solution.py:613
  101.6 6.3 %user_backward.1 = (bf16[256,256]{1,0:T(8,128)(2,1)S(1)}, s32[8,384]{1,0:T(8,128)S(1)}, f32[1,1024]{1,0:T(1,128)S(1)}, f32[16,1024]{1,0:T(8,128)S(1)}, bf16[1024...) custom-call(f32[16,1024]{1,0:T(8,128)S(1)} %get-tuple-element.54.d_user_ref, ...), custom_call_target="tpu_custom_call" | custom-call | tf_op jit(solution)/shard_map/user_backward/pallas_call | solution.py:618
  107.9 1.5 all-to-all-done.4
  109.4 1.2 item_backward.1
  110.7 2.2 %collective-permute-start.1 = (f32[64,256]{1,0:T(8,128)S(1)}, f32[64,256]{1,0:T(8,128)S(1)}, u32[]{:S(2)}, u32[]{:S(2)}) collective-permute-start(f32[64,256]{1,0:T(8,128)S(1)} %get-tuple-element.72), channel_id=1, source_target_pairs={{0,128},{128,0},{1,129},{129,1},{2,130},{130,2},{3,131},{131,3},{4... | collective-permute-start | bytes 196616 | tf_op jit(solution)/shard_map/ppermute | solution.py:642
  114.3 27.1 %all_to_all.80 = bf16[128,8,256]{2,1,0:T(8,128)(2,1)S(1)} all-to-all(bf16[128,8,256]{2,1,0:T(8,128)(2,1)S(1)} %bitcast.30), channel_id=1, replica_groups=mesh['tower'=2,'x'=4,'y'=4,'zh'=4,'zl'=2] {'x','y','zh','zl'}, dimensions={0} | all-to-all | bytes 1048576 | tf_op jit(solution)/shard_map/all_to_all | solution.py:660
  141.3 0.5 scatter.1
  141.8 2.4 %collective-permute-start.3 = (bf16[512,256]{1,0:T(8,128)(2,1)S(1)}, bf16[512,256]{1,0:T(8,128)(2,1)S(1)}, u32[]{:S(2)}, u32[]{:S(2)}) collective-permute-start(bf16[512,256]{1,0:T(8,128)(2,1)S(1)} %get-tuple-element.77), channel_id=1, source_target_pairs={{0,128},{128,0},{1,129},{129,1},{2,130},{130,2},{3,131},{131,3},{4... | collective-permute-start | bytes 786440 | tf_op jit(solution)/shard_map/ppermute | solution.py:669
  144.2 11.0 %all_to_all.81 = f32[32,8,128]{2,1,0:T(8,128)S(1)} all-to-all(f32[32,8,128]{2,1,0:T(8,128)S(1)} %bitcast.37), channel_id=1, replica_groups=mesh['tower'=2,'x'=4,'y'=4,'zh'=4,'zl'=2] {'x','y','zl'}, dimensions={0} | all-to-all | bytes 262144 | tf_op jit(solution)/shard_map/all_to_all | solution.py:670
  155.3 0.9 collective-permute-start.2
  156.2 0.8 convert_add_fusion
  157.1 0.7 finish.1
  (9 shorter events, 1.8 us)
Async XLA Ops:
  56.6 11.2 %all-to-all-start.2 = ((bf16[8,8,1024]{2,1,0:T(8,128)(2,1)}), bf16[8,8,1024]{2,1,0:T(8,128)(2,1)S(1)}, u32[]{:S(2)}, u32[]{:S(2)}) async-start(bf16[8,8,1024]{2,1,0:T(8,128)(2,1)} %bitcast.10), calls=%async_computation.2 | async-start | bytes 262144 | tf_op jit(solution)/shard_map/all_to_all | solution.py:571
  85.4 8.7 %collective-permute-start = (bf16[640,1024]{1,0:T(8,128)(2,1)S(1)}, bf16[640,1024]{1,0:T(8,128)(2,1)S(1)}, u32[]{:S(2)}, u32[]{:S(2)}) collective-permute-start(bf16[640,1024]{1,0:T(8,128)(2,1)S(1)} %bitcast.24), channel_id=1, source_target_pairs={{0,128},{128,0},{1,129},{129,1},{2,130},{130,2},{3,131},{131,3},{4... | collective-permute-start | bytes 3932168 | tf_op jit(solution)/shard_map/ppermute | solution.py:602
  97.0 12.4 %all-to-all-start.4 = ((bf16[8,8,1024]{2,1,0:T(8,128)(2,1)}), bf16[8,8,1024]{2,1,0:T(8,128)(2,1)S(1)}, u32[]{:S(2)}, u32[]{:S(2)}) async-start(bf16[8,8,1024]{2,1,0:T(8,128)(2,1)} %bitcast.16), calls=%async_computation.4 | async-start | bytes 262144 | tf_op jit(solution)/shard_map/all_to_all | solution.py:613
  110.7 30.6 %copy-start = (s32[8,1024]{1,0:T(8,128)S(1)}, s32[8,1024]{1,0:T(8,128)}, u32[]{:S(2)}) copy-start(s32[8,1024]{1,0:T(8,128)} %get-tuple-element.73.row_ref) | copy-start | bytes 98308
  110.7 3.1 %collective-permute-start.1 = (f32[64,256]{1,0:T(8,128)S(1)}, f32[64,256]{1,0:T(8,128)S(1)}, u32[]{:S(2)}, u32[]{:S(2)}) collective-permute-start(f32[64,256]{1,0:T(8,128)S(1)} %get-tuple-element.72), channel_id=1, source_target_pairs={{0,128},{128,0},{1,129},{129,1},{2,130},{130,2},{3,131},{131,3},{4... | collective-permute-start | bytes 196616 | tf_op jit(solution)/shard_map/ppermute | solution.py:642
  141.8 14.3 %collective-permute-start.3 = (bf16[512,256]{1,0:T(8,128)(2,1)S(1)}, bf16[512,256]{1,0:T(8,128)(2,1)S(1)}, u32[]{:S(2)}, u32[]{:S(2)}) collective-permute-start(bf16[512,256]{1,0:T(8,128)(2,1)S(1)} %get-tuple-element.77), channel_id=1, source_target_pairs={{0,128},{128,0},{1,129},{129,1},{2,130},{130,2},{3,131},{131,3},{4... | collective-permute-start | bytes 786440 | tf_op jit(solution)/shard_map/ppermute | solution.py:669
  155.3 1.9 %collective-permute-start.2 = (f32[256,128]{1,0:T(8,128)S(1)}, f32[256,128]{1,0:T(8,128)S(1)}, u32[]{:S(2)}, u32[]{:S(2)}) collective-permute-start(f32[256,128]{1,0:T(8,128)S(1)} %bitcast.34), channel_id=1, source_target_pairs={{0,128},{128,0},{1,129},{129,1},{2,130},{130,2},{3,131},{131,3},{4... | collective-permute-start | bytes 393224 | tf_op jit(solution)/shard_map/ppermute | solution.py:671

commit v13 on v12

--- a/solution.py
+++ b/solution.py
@@ -184,18 +184,28 @@
     return (dot(picks, fetched[...]) + dot(hot_picks, hot[...].astype(BF))).astype(BF)
 
 
-def item_forward_kernel(users, fetched_ref, hot_ref, column_ref, *refs):
-    sources, (vectors_ref, inner_ref, outer_ref), refs = refs[:3], refs[3:6], refs[6:]
-    targets, sems = refs[:3], refs[3]
-    item_w1, item_w2, gain = targets
-    copies = copies_of(zip(sources, targets), sems)
+def item_forward_kernel(
+    users,
+    fetched_ref,
+    hot_ref,
+    column_ref,
+    item_w2,
+    item_w1_hbm,
+    gain_hbm,
+    vectors_ref,
+    inner_ref,
+    outer_ref,
+    item_w1,
+    gain,
+    sems,
+):
+    loads = copies_of([(item_w1_hbm, item_w1), (gain_hbm, gain)], sems)
     rows = look_up(column_ref[...], fetched_ref, hot_ref)
-    copies[0].wait()
+    loads[0].wait()
     inner = dot(rows, item_w1[...])
     inner_ref[...] = inner
     gated = (inner * jax.nn.sigmoid(inner)).astype(BF)
-    copies[1].wait()
-    copies[2].wait()
+    loads[1].wait()
     outer = dot(gated, item_w2[...])
     outer_ref[...] = outer
     scale = lax.rsqrt(jnp.mean(outer * outer, axis=-1, keepdims=True) + EPS)
@@ -353,24 +363,24 @@
     return inverse * pulled - values * (inverse * inverse * inverse * along)
 
 
-def user_backward_kernel(users, d_user_ref, *refs):
-    sources, refs = refs[:18], refs[18:]
+def user_backward_kernel(users, d_user_ref, w_out, *refs):
+    sources, refs = refs[:17], refs[17:]
     d_rows_ref, ahead, refs = refs[0], refs[1:7], refs[7:]
-    targets, (d_normed, sems) = refs[:12], refs[12:]
-    mixed_ref, out_gain_ref, w_out, w_value, normed_ref, weights_ref, qk_ref = targets[:7]
-    w_key, w_query, hidden_ref, norm_gain_ref, in_proj = targets[7:]
+    targets, (d_normed, sems) = refs[:11], refs[11:]
+    mixed_ref, out_gain_ref, w_value, normed_ref, weights_ref, qk_ref = targets[:6]
+    w_key, w_query, hidden_ref, norm_gain_ref, in_proj = targets[6:]
     copies = copies_of(zip(sources, tuple(targets) + tuple(ahead)), sems)
     span, width = hidden_ref.shape
     hist = span // users
     heads = width // HEAD_DIM
     mask = head_mask(heads, width)
-    for copy in copies[:3]:
+    for copy in copies[:2]:
         copy.wait()
     d_mixed = norm_backward(mixed_ref[...], d_user_ref[...], out_gain_ref[...])
     d_attended = dot_nt(d_mixed.astype(BF), w_out[...])
-    copies[3].wait()
+    copies[2].wait()
     d_mixes = dot_nt(spread_heads(d_attended, mask, users), w_value[...]).astype(BF)
-    for copy in copies[4:7]:
+    for copy in copies[3:6]:
         copy.wait()
     normed = normed_ref[...]
     weights = weights_ref[...]
@@ -384,22 +394,22 @@
         jnp.concatenate([d_mixes, qk_ref[...]], axis=0),
     )
     d_qk = dot(d_scores, normed).astype(BF)
+    copies[6].wait()
+    d_query = join_heads(dot(d_qk, w_key[...]), mask, users).astype(BF)
     copies[7].wait()
-    d_query = join_heads(dot(d_qk, w_key[...]), mask, users).astype(BF)
-    copies[8].wait()
     d_last = dot_nt(d_query, w_query[...])
     for u in range(users):
         at = slice((u + 1) * hist - 1, (u + 1) * hist)
         d_normed[at, :] = d_normed[at, :] + d_last[u : u + 1]
+    copies[8].wait()
     copies[9].wait()
-    copies[10].wait()
     d_normed[...] = norm_backward(hidden_ref[...], d_normed[...], norm_gain_ref[...])
     for u in range(users):
         at = slice((u + 1) * hist - 1, (u + 1) * hist)
         d_normed[at, :] = d_normed[at, :] + d_mixed[u : u + 1]
-    copies[11].wait()
+    copies[10].wait()
     d_rows_ref[...] = dot_nt(d_normed[...].astype(BF), in_proj[...]).astype(BF)
-    for copy in copies[12:]:
+    for copy in copies[11:]:
         copy.wait()
 
 
@@ -557,17 +567,20 @@
     fetched = exchange(served, SHARD)
 
     norm_gain, out_gain, item_gain = (g.reshape(1, width) for g in (norm_gain, out_gain, item_gain))
-    loads = (item_w1, item_w2, item_gain)
     item_kept = (shape((PAD, width), F32), shape((PAD, width), F32))
     item_vec, inner, outer = pl.pallas_call(
         functools.partial(item_forward_kernel, users),
         out_shape=(shape((near * 8, width), BF), *map(vmem, item_kept)),
-        in_specs=[VMEM] * 3 + [HBM] * 3,
+        in_specs=[VMEM] * 4 + [HBM] * 2,
         out_specs=(VMEM,) * 3,
-        scratch_shapes=like(loads) + [sems(3)],
+        scratch_shapes=like((item_w1, item_gain)) + [sems(2)],
         compiler_params=params(24),
         name="item_forward",
-    )(fetched, in_vmem(hot_ready), in_vmem(item_column), *map(in_hbm, loads))
+    )(
+        fetched,
+        *map(in_vmem, (hot_ready, item_column, item_w2)),
+        *map(in_hbm, (item_w1, item_gain)),
+    )
     near_items = exchange(item_vec, LINE)
 
     loads = (column, hot_table, pos_embed, norm_gain, out_gain)
@@ -612,18 +625,18 @@
     )(place, gathered, swapped)
     parts = exchange(d_part, LINE)
 
-    loads = (mixed, out_gain, w_out, w_value, normed, weights, qk)
+    loads = (mixed, out_gain, w_value, normed, weights, qk)
     loads += (w_key, w_query, hidden, norm_gain, in_proj)
     ahead = (row, item_gain, inner, item_w2, item_w1, outer)
     d_rows, *item_ready = pl.pallas_call(
         functools.partial(user_backward_kernel, users),
         out_shape=(shape((span, emb), BF), *map(vmem, ahead)),
-        in_specs=[VMEM] + [HBM] * 18,
+        in_specs=[VMEM] * 2 + [HBM] * 17,
         out_specs=(VMEM,) * 7,
-        scratch_shapes=like(loads) + [pltpu.VMEM((span, width), F32), sems(18)],
+        scratch_shapes=like(loads) + [pltpu.VMEM((span, width), F32), sems(17)],
         compiler_params=params(40),
         name="user_backward",
-    )(d_user, *map(in_hbm, loads + ahead))
+    )(d_user, in_vmem(w_out), *map(in_hbm, loads + ahead))
     core = lax.axis_index("tower").astype(jnp.int32).reshape(1)
     row_ready = item_ready[0]
     d_all, send, keep, loss = pl.pallas_call(

time: 158 us -> 161 us (1.019)
  local copies, waits for them, and re-layouts: 0.01 us -> 2.93 us
    unnamed x2 -> x10, local copies, waits for them, and re-layouts: 0.01 us -> 2.93 us
  transfers between devices with their start and end apart: 6 -> 6, of which waited for: 5 -> 5; matrix products, arithmetic and copies ran while one was open for 1% -> 1% of each run, Pallas kernels for 8% -> 7%
where the time goes in v13:
time: 161 us
  blocking collectives  106 us (66%)
  Pallas kernels  23.9 us (15%)
  starting transfers between devices  19.4 us (12%)
  waiting for transfers between devices  6.37 us (4%)
  local copies, waits for them, and re-layouts  2.93 us (2%)
    all_to_all x1, blocking collectives, shards(): returned = exchange(outgoing, SHARD)  27.6 us
    all_to_all x1, blocking collectives, shards(): asked = exchange(request, SHARD)  26.7 us
    all_to_all x1, blocking collectives, shards(): fetched = exchange(served, SHARD)  23.6 us
    all_to_all x1, blocking collectives, shards(): gathered = exchange(spread, ('x', 'y'))  17.2 us
    all_to_all x1, blocking collectives, shards(): sums = exchange(mine, GROUP)  11 us
    ppermute x1, starting transfers between devices, shards(): swapped = lax.ppermute(gathered, 'tower', swap)  6.04 us
    pallas_call x1, Pallas kernels, shards(): pl.pallas_call(functools.partial(user_forward_kernel, users), out_shape=(...  5.8 us
    pallas_call x1, Pallas kernels, shards(): pl.pallas_call(functools.partial(user_backward_kernel, users), out_shape=...  5.54 us
  transfers between devices with their start and end apart: 6, of which 5 were waited for; matrix products, arithmetic and copies ran while one was open for 1% of the time, Pallas kernels for 7%

profile of v13, /device:TPU:1, one launch (start us, length us, event | category | flops | bytes accessed | tf_op | source)
XLA Modules:
  0.0 160.5 jit_solution(7185935381687587017)
XLA Ops:
  0.6 1.4 index.1
  2.1 26.7 %all_to_all.77 = s32[128,1,128]{2,1,0:T(1,128)S(1)} all-to-all(s32[128,1,128]{2,1,0:T(1,128)S(1)} %bitcast.38), channel_id=1, replica_groups=mesh['tower'=2,'x'=4,'y'=4,'zh'=4,'zl'=2] {'x','y','zh','zl'}, dimensions={0} | all-to-all | bytes 131072 | tf_op jit(solution)/shard_map/all_to_all | solution.py:547
  28.8 1.3 serve.1
  30.1 23.6 %all_to_all.78 = bf16[128,8,256]{2,1,0:T(8,128)(2,1)S(1)} all-to-all(bf16[128,8,256]{2,1,0:T(8,128)(2,1)S(1)} %bitcast.33), channel_id=1, replica_groups=mesh['tower'=2,'x'=4,'y'=4,'zh'=4,'zl'=2] {'x','y','zh','zl'}, dimensions={0} | all-to-all | bytes 1048576 | tf_op jit(solution)/shard_map/all_to_all | solution.py:567
  53.7 2.5 %item_forward.1 = (bf16[64,1024]{1,0:T(8,128)(2,1)}, f32[16,1024]{1,0:T(8,128)S(1)}, f32[16,1024]{1,0:T(8,128)S(1)}) custom-call(bf16[1024,256]{1,0:T(8,128)(2,1)S(1)} %bitcast.27, bf16[128,256]{1,0:T(8,128)(2,1)S(1)} %get-tuple-element.46.hot_ref, s32[16,128]{1,0:T(8,128)S(1)} %get-tuple-element.47.column_ref, bf16[1024,1024]{1,0:T(8,128)(2,1)S(1)} %copy-done, ...), custom_call_target="tpu_custom_call" | custom-call | tf_op jit(solution)/shard_map/item_forward/pallas_call | solution.py:571
  56.2 3.4 %all-to-all-start.2 = ((bf16[8,8,1024]{2,1,0:T(8,128)(2,1)}), bf16[8,8,1024]{2,1,0:T(8,128)(2,1)S(1)}, u32[]{:S(2)}, u32[]{:S(2)}) async-start(bf16[8,8,1024]{2,1,0:T(8,128)(2,1)} %bitcast.10), calls=%async_computation.2 | async-start | bytes 262144 | tf_op jit(solution)/shard_map/all_to_all | solution.py:584
  59.6 5.8 %user_forward.1 = (bf16[16,1024]{1,0:T(8,128)(2,1)S(1)}, f32[256,1024]{1,0:T(8,128)}, bf16[256,1024]{1,0:T(8,128)(2,1)}, bf16[64,1024]{1,0:T(8,128)(2,1)}, f32[6...) custom-call(bf16[1024,256]{1,0:T(8,128)(2,1)S(1)} %bitcast.28, ...), custom_call_target="tpu_custom_call" | custom-call | tf_op jit(solution)/shard_map/user_forward/pallas_call | solution.py:595
  65.4 2.0 %all-to-all-done.2 = bf16[8,8,1024]{2,1,0:T(8,128)(2,1)S(1)} async-done(((bf16[8,8,1024]{2,1,0:T(8,128)(2,1)}), bf16[8,8,1024]{2,1,0:T(8,128)(2,1)S(1)}, u32[]{:S(2)}, u32[]{:S(2)}) %all-to-all-start.2) | async-done | bytes 131104 | tf_op jit(solution)/shard_map/all_to_all | solution.py:584
  67.8 17.2 %all_to_all.79 = bf16[16,40,1024]{2,1,0:T(8,128)(2,1)S(1)} all-to-all(bf16[16,40,1024]{2,1,0:T(8,128)(2,1)S(1)} %bitcast.26), channel_id=1, replica_groups=mesh['tower'=2,'x'=4,'y'=4,'zh'=4,'zl'=2] {'x','y'}, dimensions={0} | all-to-all | bytes 2621440 | tf_op jit(solution)/shard_map/all_to_all | solution.py:614
  85.0 6.0 %collective-permute-start = (bf16[640,1024]{1,0:T(8,128)(2,1)S(1)}, bf16[640,1024]{1,0:T(8,128)(2,1)}, u32[]{:S(2)}, u32[]{:S(2)}) collective-permute-start(bf16[640,1024]{1,0:T(8,128)(2,1)S(1)} %bitcast.24), channel_id=1, source_target_pairs={{0,128},{128,0},{1,129},{129,1},{2,130},{130,2},{3,131},{131,3},{4... | collective-permute-start | bytes 3932168 | tf_op jit(solution)/shard_map/ppermute | solution.py:615
  91.1 2.7 %collective-permute-done.swapped_ref = bf16[640,1024]{1,0:T(8,128)(2,1)} collective-permute-done((bf16[640,1024]{1,0:T(8,128)(2,1)S(1)}, bf16[640,1024]{1,0:T(8,128)(2,1)}, u32[]{:S(2)}, u32[]{:S(2)}) %collective-permute-start) | collective-permute-done | bytes 1310752 | tf_op jit(solution)/shard_map/ppermute | solution.py:615
  93.9 3.7 %softmax.1 = (f32[16,1024]{1,0:T(8,128)S(1)}, bf16[64,1024]{1,0:T(8,128)(2,1)}) custom-call(s32[2]{0:T(128)S(1)} %pad_add_fusion.place_ref, bf16[640,1024]{1,0:T(8,128)(2,1)S(1)} %bitcast.25, bf16[640,1024]{1,0:T(8,128)(2,1)} %collective-permute-done.swapped_ref), custom_call_target="tpu_custom_call" | custom-call | tf_op jit(solution)/shard_map/softmax/pallas_call | solution.py:617
  97.6 4.5 %all-to-all-start.4 = ((bf16[8,8,1024]{2,1,0:T(8,128)(2,1)}), bf16[8,8,1024]{2,1,0:T(8,128)(2,1)S(1)}, u32[]{:S(2)}, u32[]{:S(2)}) async-start(bf16[8,8,1024]{2,1,0:T(8,128)(2,1)} %bitcast.16), calls=%async_computation.4 | async-start | bytes 262144 | tf_op jit(solution)/shard_map/all_to_all | solution.py:626
  102.1 5.5 %user_backward.1 = (bf16[256,256]{1,0:T(8,128)(2,1)S(1)}, s32[8,384]{1,0:T(8,128)S(1)}, f32[1,1024]{1,0:T(1,128)S(1)}, f32[16,1024]{1,0:T(8,128)S(1)}, bf16[1024...) custom-call(f32[16,1024]{1,0:T(8,128)S(1)} %get-tuple-element.54.d_user_ref, ...), custom_call_target="tpu_custom_call" | custom-call | tf_op jit(solution)/shard_map/user_backward/pallas_call | solution.py:631
  107.7 1.3 copy-done.2
  109.0 1.0 all-to-all-done.4
  110.0 1.6 copy-done.3
  111.6 1.2 item_backward.1
  112.9 2.2 %collective-permute-start.1 = (f32[64,256]{1,0:T(8,128)S(1)}, f32[64,256]{1,0:T(8,128)S(1)}, u32[]{:S(2)}, u32[]{:S(2)}) collective-permute-start(f32[64,256]{1,0:T(8,128)S(1)} %get-tuple-element.72), channel_id=1, source_target_pairs={{0,128},{128,0},{1,129},{129,1},{2,130},{130,2},{3,131},{131,3},{4... | collective-permute-start | bytes 196616 | tf_op jit(solution)/shard_map/ppermute | solution.py:655
  116.4 27.6 %all_to_all.80 = bf16[128,8,256]{2,1,0:T(8,128)(2,1)S(1)} all-to-all(bf16[128,8,256]{2,1,0:T(8,128)(2,1)S(1)} %bitcast.30), channel_id=1, replica_groups=mesh['tower'=2,'x'=4,'y'=4,'zh'=4,'zl'=2] {'x','y','zh','zl'}, dimensions={0} | all-to-all | bytes 1048576 | tf_op jit(solution)/shard_map/all_to_all | solution.py:673
  144.5 2.4 %collective-permute-start.3 = (bf16[512,256]{1,0:T(8,128)(2,1)S(1)}, bf16[512,256]{1,0:T(8,128)(2,1)S(1)}, u32[]{:S(2)}, u32[]{:S(2)}) collective-permute-start(bf16[512,256]{1,0:T(8,128)(2,1)S(1)} %get-tuple-element.77), channel_id=1, source_target_pairs={{0,128},{128,0},{1,129},{129,1},{2,130},{130,2},{3,131},{131,3},{4... | collective-permute-start | bytes 786440 | tf_op jit(solution)/shard_map/ppermute | solution.py:682
  146.9 11.0 %all_to_all.81 = f32[32,8,128]{2,1,0:T(8,128)S(1)} all-to-all(f32[32,8,128]{2,1,0:T(8,128)S(1)} %bitcast.37), channel_id=1, replica_groups=mesh['tower'=2,'x'=4,'y'=4,'zh'=4,'zl'=2] {'x','y','zl'}, dimensions={0} | all-to-all | bytes 262144 | tf_op jit(solution)/shard_map/all_to_all | solution.py:683
  157.9 0.9 collective-permute-start.2
  158.8 0.8 convert_add_fusion
  (17 shorter events, 3.0 us)
Async XLA Ops:
  0.6 53.1 %copy-start = (bf16[1024,1024]{1,0:T(8,128)(2,1)S(1)}, bf16[1024,1024]{1,0:T(8,128)(2,1)}, u32[]{:S(2)}) copy-start(bf16[1024,1024]{1,0:T(8,128)(2,1)} %refs_14_.1) | copy-start | bytes 6291460
  56.2 11.2 %all-to-all-start.2 = ((bf16[8,8,1024]{2,1,0:T(8,128)(2,1)}), bf16[8,8,1024]{2,1,0:T(8,128)(2,1)S(1)}, u32[]{:S(2)}, u32[]{:S(2)}) async-start(bf16[8,8,1024]{2,1,0:T(8,128)(2,1)} %bitcast.10), calls=%async_computation.2 | async-start | bytes 262144 | tf_op jit(solution)/shard_map/all_to_all | solution.py:584
  85.0 17.1 %copy-start.1 = (bf16[1024,1024]{1,0:T(8,128)(2,1)S(1)}, bf16[1024,1024]{1,0:T(8,128)(2,1)}, u32[]{:S(2)}) copy-start(bf16[1024,1024]{1,0:T(8,128)(2,1)} %w_out.1) | copy-start | bytes 6291460
  85.0 8.8 %collective-permute-start = (bf16[640,1024]{1,0:T(8,128)(2,1)S(1)}, bf16[640,1024]{1,0:T(8,128)(2,1)}, u32[]{:S(2)}, u32[]{:S(2)}) collective-permute-start(bf16[640,1024]{1,0:T(8,128)(2,1)S(1)} %bitcast.24), channel_id=1, source_target_pairs={{0,128},{128,0},{1,129},{129,1},{2,130},{130,2},{3,131},{131,3},{4... | collective-permute-start | bytes 3932168 | tf_op jit(solution)/shard_map/ppermute | solution.py:615
  97.6 12.4 %all-to-all-start.4 = ((bf16[8,8,1024]{2,1,0:T(8,128)(2,1)}), bf16[8,8,1024]{2,1,0:T(8,128)(2,1)S(1)}, u32[]{:S(2)}, u32[]{:S(2)}) async-start(bf16[8,8,1024]{2,1,0:T(8,128)(2,1)} %bitcast.16), calls=%async_computation.4 | async-start | bytes 262144 | tf_op jit(solution)/shard_map/all_to_all | solution.py:626
  107.7 1.3 copy-start.2
  110.0 1.6 copy-start.3
  112.9 31.1 %copy-start.4 = (s32[8,1024]{1,0:T(8,128)S(1)}, s32[8,1024]{1,0:T(8,128)}, u32[]{:S(2)}) copy-start(s32[8,1024]{1,0:T(8,128)} %get-tuple-element.73.row_ref) | copy-start | bytes 98308
  112.9 3.1 %collective-permute-start.1 = (f32[64,256]{1,0:T(8,128)S(1)}, f32[64,256]{1,0:T(8,128)S(1)}, u32[]{:S(2)}, u32[]{:S(2)}) collective-permute-start(f32[64,256]{1,0:T(8,128)S(1)} %get-tuple-element.72), channel_id=1, source_target_pairs={{0,128},{128,0},{1,129},{129,1},{2,130},{130,2},{3,131},{131,3},{4... | collective-permute-start | bytes 196616 | tf_op jit(solution)/shard_map/ppermute | solution.py:655
  144.5 14.3 %collective-permute-start.3 = (bf16[512,256]{1,0:T(8,128)(2,1)S(1)}, bf16[512,256]{1,0:T(8,128)(2,1)S(1)}, u32[]{:S(2)}, u32[]{:S(2)}) collective-permute-start(bf16[512,256]{1,0:T(8,128)(2,1)S(1)} %get-tuple-element.77), channel_id=1, source_target_pairs={{0,128},{128,0},{1,129},{129,1},{2,130},{130,2},{3,131},{131,3},{4... | collective-permute-start | bytes 786440 | tf_op jit(solution)/shard_map/ppermute | solution.py:682
  157.9 1.9 %collective-permute-start.2 = (f32[256,128]{1,0:T(8,128)S(1)}, f32[256,128]{1,0:T(8,128)S(1)}, u32[]{:S(2)}, u32[]{:S(2)}) collective-permute-start(f32[256,128]{1,0:T(8,128)S(1)} %bitcast.34), channel_id=1, source_target_pairs={{0,128},{128,0},{1,129},{129,1},{2,130},{130,2},{3,131},{131,3},{4... | collective-permute-start | bytes 393224 | tf_op jit(solution)/shard_map/ppermute | solution.py:684

commit v14 on v13

--- a/solution.py
+++ b/solution.py
@@ -282,40 +282,47 @@
 
 
 def arrange_kernel(users, near, near_ref, vectors_ref, spread_ref):
-    total, width = spread_ref.shape
-    block = near * users + 8
-    pair = 2 * block
-    at = iota((pair, near * 8), 0) % block
-    source = jnp.where(at < near * users, at // users * 8 + at % users, -1)
-    item_rows = dot(one_hot(iota((pair, near * 8), 1) == source), near_ref[...])
-    at = iota((pair, PAD), 0) % block
-    source = jnp.where((at >= near * users) & (at < (near + 1) * users), at - near * users, -1)
-    user_rows = dot(one_hot(iota((pair, PAD), 1) == source), vectors_ref[...])
-    rows = (item_rows + user_rows).astype(BF)
-    for i in range(total // pair):
-        spread_ref[i * pair : (i + 1) * pair, :] = rows
+    width = near_ref.shape[1]
+    block = near * users
+    part = spread_ref.shape[1] - width
+    shape = (block, near * 8)
+    at = iota(shape, 0)
+    source = at // users * 8 + at % users
+    items = dot(one_hot(iota(shape, 1) == source), near_ref[...])
+    shape = (block, PAD)
+    at = iota(shape, 0)
+    mine = jnp.zeros((block, part), F32)
+    for c in range(near):
+        picks = one_hot((at % near == c) & (iota(shape, 1) == at // near))
+        mine = mine + dot(picks, vectors_ref[:, c * part : (c + 1) * part])
+    rows = jnp.concatenate([items, mine], axis=1).astype(BF)
+    for i in range(spread_ref.shape[0] // block):
+        spread_ref[i * block : (i + 1) * block, :] = rows
 
 
 def softmax_kernel(
     users, near, scale, place_ref, gathered_ref, swapped_ref, d_user_ref, d_part_ref, raised_ref
 ):
-    rows, width = gathered_ref.shape
+    rows = gathered_ref.shape[0]
+    width = d_user_ref.shape[1]
     items = near * users
-    block = items + 8
-    blocks = rows // block
+    group = rows // near
     mine, plane = place_ref[0], place_ref[1]
-    own, other = gathered_ref[...], swapped_ref[...]
-    shape = (blocks * users, rows)
+    own, other = gathered_ref[:, 0:width], swapped_ref[:, 0:width]
+    shape = (rows, rows)
     line = iota(shape, 0)
-    picks = one_hot(iota(shape, 1) == line // users * block + items + line % users)
-    group_users = jnp.concatenate([dot(picks, own), dot(picks, other)], axis=0).astype(BF)
-    total = 2 * blocks * users
+    picks = one_hot(iota(shape, 1) == line % group * near + line // group)
+
+    def users_of(ref):
+        parts = dot(picks, ref[:, width:])
+        return jnp.concatenate([parts[c * group : (c + 1) * group] for c in range(near)], axis=1)
+
+    group_users = jnp.concatenate([users_of(gathered_ref), users_of(swapped_ref)], axis=0).astype(BF)
+    total = 2 * group
 
     shape = (rows, total)
-    line = iota(shape, 0)
-    valid = line % block < items
-    first = jnp.where(valid, scale * dot_nt(own, group_users), -jnp.inf)
-    second = jnp.where(valid, scale * dot_nt(other, group_users), -jnp.inf)
+    first = scale * dot_nt(own, group_users)
+    second = scale * dot_nt(other, group_users)
     top = jnp.maximum(
         jnp.max(first, axis=0, keepdims=True), jnp.max(second, axis=0, keepdims=True)
     )
@@ -329,7 +336,7 @@
     target = (iota(line, 0) // users == plane) & (
         iota(line, 1) == mine * users + iota(line, 0) % users
     )
-    near_raised = raised_ref[pl.ds(pl.multiple_of(mine * block, 8), items), :]
+    near_raised = raised_ref[pl.ds(pl.multiple_of(mine * items, 8), items), :]
     slope = (near_raised * share - jnp.where(target, 1.0, 0.0)).astype(BF)
     apart = (near * 8, items)
     at = iota(apart, 0)
@@ -337,7 +344,7 @@
     d_part = scale * dot(dot(apart, slope).astype(BF), group_users)
 
     who = iota(shape, 1) - mine * users
-    target = (who >= 0) & (who < users) & (iota(shape, 0) == mine * block + plane * users + who)
+    target = (who >= 0) & (who < users) & (iota(shape, 0) == mine * items + plane * users + who)
     slope = (raised * share - jnp.where(target, 1.0, 0.0)).astype(BF)
     other_slope = (other_raised * share).astype(BF)
     self = (PAD, total)
@@ -363,24 +370,24 @@
     return inverse * pulled - values * (inverse * inverse * inverse * along)
 
 
-def user_backward_kernel(users, d_user_ref, w_out, *refs):
-    sources, refs = refs[:17], refs[17:]
+def user_backward_kernel(users, d_user_ref, *refs):
+    sources, refs = refs[:18], refs[18:]
     d_rows_ref, ahead, refs = refs[0], refs[1:7], refs[7:]
-    targets, (d_normed, sems) = refs[:11], refs[11:]
-    mixed_ref, out_gain_ref, w_value, normed_ref, weights_ref, qk_ref = targets[:6]
-    w_key, w_query, hidden_ref, norm_gain_ref, in_proj = targets[6:]
+    targets, (d_normed, sems) = refs[:12], refs[12:]
+    mixed_ref, out_gain_ref, w_out, w_value, normed_ref, weights_ref, qk_ref = targets[:7]
+    w_key, w_query, hidden_ref, norm_gain_ref, in_proj = targets[7:]
     copies = copies_of(zip(sources, tuple(targets) + tuple(ahead)), sems)
     span, width = hidden_ref.shape
     hist = span // users
     heads = width // HEAD_DIM
     mask = head_mask(heads, width)
-    for copy in copies[:2]:
+    for copy in copies[:3]:
         copy.wait()
     d_mixed = norm_backward(mixed_ref[...], d_user_ref[...], out_gain_ref[...])
     d_attended = dot_nt(d_mixed.astype(BF), w_out[...])
-    copies[2].wait()
+    copies[3].wait()
     d_mixes = dot_nt(spread_heads(d_attended, mask, users), w_value[...]).astype(BF)
-    for copy in copies[3:6]:
+    for copy in copies[4:7]:
         copy.wait()
     normed = normed_ref[...]
     weights = weights_ref[...]
@@ -394,22 +401,22 @@
         jnp.concatenate([d_mixes, qk_ref[...]], axis=0),
     )
     d_qk = dot(d_scores, normed).astype(BF)
-    copies[6].wait()
+    copies[7].wait()
     d_query = join_heads(dot(d_qk, w_key[...]), mask, users).astype(BF)
-    copies[7].wait()
+    copies[8].wait()
     d_last = dot_nt(d_query, w_query[...])
     for u in range(users):
         at = slice((u + 1) * hist - 1, (u + 1) * hist)
         d_normed[at, :] = d_normed[at, :] + d_last[u : u + 1]
-    copies[8].wait()
     copies[9].wait()
+    copies[10].wait()
     d_normed[...] = norm_backward(hidden_ref[...], d_normed[...], norm_gain_ref[...])
     for u in range(users):
         at = slice((u + 1) * hist - 1, (u + 1) * hist)
         d_normed[at, :] = d_normed[at, :] + d_mixed[u : u + 1]
-    copies[10].wait()
+    copies[11].wait()
     d_rows_ref[...] = dot_nt(d_normed[...].astype(BF), in_proj[...]).astype(BF)
-    for copy in copies[11:]:
+    for copy in copies[12:]:
         copy.wait()
 
 
@@ -602,10 +609,10 @@
         name="user_forward",
     )(fetched, in_vmem(inner), in_vmem(outer), *map(in_hbm, loads))
 
-    rows = owners // near * (near * users + 8)
+    rows = owners * users
     spread = pl.pallas_call(
         functools.partial(arrange_kernel, users, near),
-        out_shape=shape((rows, width), BF),
+        out_shape=shape((rows, width + width // near), BF),
         in_specs=[VMEM, VMEM],
         out_specs=VMEM,
         compiler_params=params(24),
@@ -625,18 +632,18 @@
     )(place, gathered, swapped)
     parts = exchange(d_part, LINE)
 
-    loads = (mixed, out_gain, w_value, normed, weights, qk)
+    loads = (mixed, out_gain, w_out, w_value, normed, weights, qk)
     loads += (w_key, w_query, hidden, norm_gain, in_proj)
     ahead = (row, item_gain, inner, item_w2, item_w1, outer)
     d_rows, *item_ready = pl.pallas_call(
         functools.partial(user_backward_kernel, users),
         out_shape=(shape((span, emb), BF), *map(vmem, ahead)),
-        in_specs=[VMEM] * 2 + [HBM] * 17,
+        in_specs=[VMEM] + [HBM] * 18,
         out_specs=(VMEM,) * 7,
-        scratch_shapes=like(loads) + [pltpu.VMEM((span, width), F32), sems(17)],
+        scratch_shapes=like(loads) + [pltpu.VMEM((span, width), F32), sems(18)],
         compiler_params=params(40),
         name="user_backward",
-    )(d_user, in_vmem(w_out), *map(in_hbm, loads + ahead))
+    )(d_user, *map(in_hbm, loads + ahead))
     core = lax.axis_index("tower").astype(jnp.int32).reshape(1)
     row_ready = item_ready[0]
     d_all, send, keep, loss = pl.pallas_call(

time: 161 us -> 156 us (0.969)
  local copies, waits for them, and re-layouts: 2.93 us -> 0.01 us
    unnamed x10 -> x4, local copies, waits for them, and re-layouts: 2.93 us -> 0.01 us
  transfers between devices with their start and end apart: 6 -> 6, of which waited for: 5 -> 5; matrix products, arithmetic and copies ran while one was open for 1% -> 1% of each run, Pallas kernels for 7% -> 8%
where the time goes in v14:
time: 156 us
  blocking collectives  105 us (67%)
  Pallas kernels  23.6 us (15%)
  starting transfers between devices  19.1 us (12%)
  waiting for transfers between devices  6.57 us (4%)
    all_to_all x1, blocking collectives, shards(): returned = exchange(outgoing, SHARD)  27 us
    all_to_all x1, blocking collectives, shards(): asked = exchange(request, SHARD)  26.7 us
    all_to_all x1, blocking collectives, shards(): fetched = exchange(served, SHARD)  23.6 us
    all_to_all x1, blocking collectives, shards(): gathered = exchange(spread, ('x', 'y'))  16.2 us
    all_to_all x1, blocking collectives, shards(): sums = exchange(mine, GROUP)  11 us
    pallas_call x1, Pallas kernels, shards(): pl.pallas_call(functools.partial(user_backward_kernel, users), out_shape=...  6.34 us
    pallas_call x1, Pallas kernels, shards(): pl.pallas_call(functools.partial(user_forward_kernel, users), out_shape=(...  5.81 us
    ppermute x1, starting transfers between devices, shards(): swapped = lax.ppermute(gathered, 'tower', swap)  5.71 us
  transfers between devices with their start and end apart: 6, of which 5 were waited for; matrix products, arithmetic and copies ran while one was open for 1% of the time, Pallas kernels for 8%

profile of v14, /device:TPU:1, one launch (start us, length us, event | category | flops | bytes accessed | tf_op | source)
XLA Modules:
  0.0 155.5 jit_solution(12600739136362617718)
XLA Ops:
  0.6 1.4 index.1
  2.1 26.7 %all_to_all.77 = s32[128,1,128]{2,1,0:T(1,128)S(1)} all-to-all(s32[128,1,128]{2,1,0:T(1,128)S(1)} %bitcast.38), channel_id=1, replica_groups=mesh['tower'=2,'x'=4,'y'=4,'zh'=4,'zl'=2] {'x','y','zh','zl'}, dimensions={0} | all-to-all | bytes 131072 | tf_op jit(solution)/shard_map/all_to_all | solution.py:554
  28.8 1.4 serve.1
  30.1 23.6 %all_to_all.78 = bf16[128,8,256]{2,1,0:T(8,128)(2,1)S(1)} all-to-all(bf16[128,8,256]{2,1,0:T(8,128)(2,1)S(1)} %bitcast.32), channel_id=1, replica_groups=mesh['tower'=2,'x'=4,'y'=4,'zh'=4,'zl'=2] {'x','y','zh','zl'}, dimensions={0} | all-to-all | bytes 1048576 | tf_op jit(solution)/shard_map/all_to_all | solution.py:574
  53.7 2.5 %item_forward.1 = (bf16[64,1024]{1,0:T(8,128)(2,1)}, f32[16,1024]{1,0:T(8,128)S(1)}, f32[16,1024]{1,0:T(8,128)S(1)}) custom-call(bf16[1024,256]{1,0:T(8,128)(2,1)S(1)} %bitcast.24, bf16[128,256]{1,0:T(8,128)(2,1)S(1)} %get-tuple-element.46.hot_ref, s32[16,128]{1,0:T(8,128)S(1)} %get-tuple-element.47.column_ref, bf16[1024,1024]{1,0:T(8,128)(2,1)S(1)} %copy-done, ...), custom_call_target="tpu_custom_call" | custom-call | tf_op jit(solution)/shard_map/item_forward/pallas_call | solution.py:578
  56.3 3.4 %all-to-all-start.2 = ((bf16[8,8,1024]{2,1,0:T(8,128)(2,1)}), bf16[8,8,1024]{2,1,0:T(8,128)(2,1)S(1)}, u32[]{:S(2)}, u32[]{:S(2)}) async-start(bf16[8,8,1024]{2,1,0:T(8,128)(2,1)} %bitcast.10), calls=%async_computation.2 | async-start | bytes 262144 | tf_op jit(solution)/shard_map/all_to_all | solution.py:591
  59.7 5.8 %user_forward.1 = (bf16[16,1024]{1,0:T(8,128)(2,1)S(1)}, f32[256,1024]{1,0:T(8,128)}, bf16[256,1024]{1,0:T(8,128)(2,1)}, bf16[64,1024]{1,0:T(8,128)(2,1)}, f32[6...) custom-call(bf16[1024,256]{1,0:T(8,128)(2,1)S(1)} %bitcast.25, ...), custom_call_target="tpu_custom_call" | custom-call | tf_op jit(solution)/shard_map/user_forward/pallas_call | solution.py:602
  65.5 2.0 %all-to-all-done.2 = bf16[8,8,1024]{2,1,0:T(8,128)(2,1)S(1)} async-done(((bf16[8,8,1024]{2,1,0:T(8,128)(2,1)}), bf16[8,8,1024]{2,1,0:T(8,128)(2,1)S(1)}, u32[]{:S(2)}, u32[]{:S(2)}) %all-to-all-start.2) | async-done | bytes 131104 | tf_op jit(solution)/shard_map/all_to_all | solution.py:591
  67.7 16.2 %all_to_all.79 = bf16[16,32,1152]{2,1,0:T(8,128)(2,1)S(1)} all-to-all(bf16[16,32,1152]{2,1,0:T(8,128)(2,1)S(1)} %bitcast.28), channel_id=1, replica_groups=mesh['tower'=2,'x'=4,'y'=4,'zh'=4,'zl'=2] {'x','y'}, dimensions={0} | all-to-all | bytes 2359296 | tf_op jit(solution)/shard_map/all_to_all | solution.py:621
  83.9 5.7 %collective-permute-start = (bf16[512,1152]{1,0:T(8,128)(2,1)S(1)}, bf16[512,1152]{1,0:T(8,128)(2,1)S(1)}, u32[]{:S(2)}, u32[]{:S(2)}) collective-permute-start(bf16[512,1152]{1,0:T(8,128)(2,1)S(1)} %bitcast.26), channel_id=1, source_target_pairs={{0,128},{128,0},{1,129},{129,1},{2,130},{130,2},{3,131},{131,3},{4... | collective-permute-start | bytes 3538952 | tf_op jit(solution)/shard_map/ppermute | solution.py:622
  89.7 2.4 %collective-permute-done.swapped_ref = bf16[512,1152]{1,0:T(8,128)(2,1)S(1)} collective-permute-done((bf16[512,1152]{1,0:T(8,128)(2,1)S(1)}, bf16[512,1152]{1,0:T(8,128)(2,1)S(1)}, u32[]{:S(2)}, u32[]{:S(2)}) %collective-permute-start) | collective-permute-done | bytes 1179680 | tf_op jit(solution)/shard_map/ppermute | solution.py:622
  92.1 2.7 %softmax.1 = (f32[16,1024]{1,0:T(8,128)S(1)}, bf16[64,1024]{1,0:T(8,128)(2,1)}) custom-call(s32[2]{0:T(128)S(1)} %pad_add_fusion.place_ref, bf16[512,1152]{1,0:T(8,128)(2,1)S(1)} %bitcast.27, bf16[512,1152]{1,0:T(8,128)(2,1)S(1)} %collective-permute-done.swapped_ref), custom_call_target="tpu_custom_call" | custom-call | tf_op jit(solution)/shard_map/softmax/pallas_call | solution.py:624
  94.8 4.5 %all-to-all-start.4 = ((bf16[8,8,1024]{2,1,0:T(8,128)(2,1)}), bf16[8,8,1024]{2,1,0:T(8,128)(2,1)S(1)}, u32[]{:S(2)}, u32[]{:S(2)}) async-start(bf16[8,8,1024]{2,1,0:T(8,128)(2,1)} %bitcast.16), calls=%async_computation.4 | async-start | bytes 262144 | tf_op jit(solution)/shard_map/all_to_all | solution.py:633
  99.3 6.3 %user_backward.1 = (bf16[256,256]{1,0:T(8,128)(2,1)S(1)}, s32[8,384]{1,0:T(8,128)S(1)}, f32[1,1024]{1,0:T(1,128)S(1)}, f32[16,1024]{1,0:T(8,128)S(1)}, bf16[1024...) custom-call(f32[16,1024]{1,0:T(8,128)S(1)} %get-tuple-element.54.d_user_ref, ...), custom_call_target="tpu_custom_call" | custom-call | tf_op jit(solution)/shard_map/user_backward/pallas_call | solution.py:638
  105.6 1.5 all-to-all-done.4
  107.2 1.2 item_backward.1
  108.5 2.2 %collective-permute-start.1 = (f32[64,256]{1,0:T(8,128)S(1)}, f32[64,256]{1,0:T(8,128)S(1)}, u32[]{:S(2)}, u32[]{:S(2)}) collective-permute-start(f32[64,256]{1,0:T(8,128)S(1)} %get-tuple-element.72), channel_id=1, source_target_pairs={{0,128},{128,0},{1,129},{129,1},{2,130},{130,2},{3,131},{131,3},{4... | collective-permute-start | bytes 196616 | tf_op jit(solution)/shard_map/ppermute | solution.py:662
  112.0 27.0 %all_to_all.80 = bf16[128,8,256]{2,1,0:T(8,128)(2,1)S(1)} all-to-all(bf16[128,8,256]{2,1,0:T(8,128)(2,1)S(1)} %bitcast.30), channel_id=1, replica_groups=mesh['tower'=2,'x'=4,'y'=4,'zh'=4,'zl'=2] {'x','y','zh','zl'}, dimensions={0} | all-to-all | bytes 1048576 | tf_op jit(solution)/shard_map/all_to_all | solution.py:680
  139.0 0.5 scatter.1
  139.5 2.4 %collective-permute-start.3 = (bf16[512,256]{1,0:T(8,128)(2,1)S(1)}, bf16[512,256]{1,0:T(8,128)(2,1)S(1)}, u32[]{:S(2)}, u32[]{:S(2)}) collective-permute-start(bf16[512,256]{1,0:T(8,128)(2,1)S(1)} %get-tuple-element.77), channel_id=1, source_target_pairs={{0,128},{128,0},{1,129},{129,1},{2,130},{130,2},{3,131},{131,3},{4... | collective-permute-start | bytes 786440 | tf_op jit(solution)/shard_map/ppermute | solution.py:689
  141.9 11.0 %all_to_all.81 = f32[32,8,128]{2,1,0:T(8,128)S(1)} all-to-all(f32[32,8,128]{2,1,0:T(8,128)S(1)} %bitcast.37), channel_id=1, replica_groups=mesh['tower'=2,'x'=4,'y'=4,'zh'=4,'zl'=2] {'x','y','zl'}, dimensions={0} | all-to-all | bytes 262144 | tf_op jit(solution)/shard_map/all_to_all | solution.py:690
  153.0 0.9 collective-permute-start.2
  153.9 0.8 convert_add_fusion
  154.9 0.7 finish.1
  (11 shorter events, 1.8 us)
Async XLA Ops:
  0.6 53.1 %copy-start = (bf16[1024,1024]{1,0:T(8,128)(2,1)S(1)}, bf16[1024,1024]{1,0:T(8,128)(2,1)}, u32[]{:S(2)}) copy-start(bf16[1024,1024]{1,0:T(8,128)(2,1)} %refs_15_.1) | copy-start | bytes 6291460
  56.3 11.2 %all-to-all-start.2 = ((bf16[8,8,1024]{2,1,0:T(8,128)(2,1)}), bf16[8,8,1024]{2,1,0:T(8,128)(2,1)S(1)}, u32[]{:S(2)}, u32[]{:S(2)}) async-start(bf16[8,8,1024]{2,1,0:T(8,128)(2,1)} %bitcast.10), calls=%async_computation.2 | async-start | bytes 262144 | tf_op jit(solution)/shard_map/all_to_all | solution.py:591
  83.9 8.2 %collective-permute-start = (bf16[512,1152]{1,0:T(8,128)(2,1)S(1)}, bf16[512,1152]{1,0:T(8,128)(2,1)S(1)}, u32[]{:S(2)}, u32[]{:S(2)}) collective-permute-start(bf16[512,1152]{1,0:T(8,128)(2,1)S(1)} %bitcast.26), channel_id=1, source_target_pairs={{0,128},{128,0},{1,129},{129,1},{2,130},{130,2},{3,131},{131,3},{4... | collective-permute-start | bytes 3538952 | tf_op jit(solution)/shard_map/ppermute | solution.py:622
  94.8 12.4 %all-to-all-start.4 = ((bf16[8,8,1024]{2,1,0:T(8,128)(2,1)}), bf16[8,8,1024]{2,1,0:T(8,128)(2,1)S(1)}, u32[]{:S(2)}, u32[]{:S(2)}) async-start(bf16[8,8,1024]{2,1,0:T(8,128)(2,1)} %bitcast.16), calls=%async_computation.4 | async-start | bytes 262144 | tf_op jit(solution)/shard_map/all_to_all | solution.py:633
  108.4 30.6 %copy-start.1 = (s32[8,1024]{1,0:T(8,128)S(1)}, s32[8,1024]{1,0:T(8,128)}, u32[]{:S(2)}) copy-start(s32[8,1024]{1,0:T(8,128)} %get-tuple-element.73.row_ref) | copy-start | bytes 98308
  108.5 3.1 %collective-permute-start.1 = (f32[64,256]{1,0:T(8,128)S(1)}, f32[64,256]{1,0:T(8,128)S(1)}, u32[]{:S(2)}, u32[]{:S(2)}) collective-permute-start(f32[64,256]{1,0:T(8,128)S(1)} %get-tuple-element.72), channel_id=1, source_target_pairs={{0,128},{128,0},{1,129},{129,1},{2,130},{130,2},{3,131},{131,3},{4... | collective-permute-start | bytes 196616 | tf_op jit(solution)/shard_map/ppermute | solution.py:662
  139.5 14.3 %collective-permute-start.3 = (bf16[512,256]{1,0:T(8,128)(2,1)S(1)}, bf16[512,256]{1,0:T(8,128)(2,1)S(1)}, u32[]{:S(2)}, u32[]{:S(2)}) collective-permute-start(bf16[512,256]{1,0:T(8,128)(2,1)S(1)} %get-tuple-element.77), channel_id=1, source_target_pairs={{0,128},{128,0},{1,129},{129,1},{2,130},{130,2},{3,131},{131,3},{4... | collective-permute-start | bytes 786440 | tf_op jit(solution)/shard_map/ppermute | solution.py:689
  153.0 1.9 %collective-permute-start.2 = (f32[256,128]{1,0:T(8,128)S(1)}, f32[256,128]{1,0:T(8,128)S(1)}, u32[]{:S(2)}, u32[]{:S(2)}) collective-permute-start(f32[256,128]{1,0:T(8,128)S(1)} %bitcast.33), channel_id=1, source_target_pairs={{0,128},{128,0},{1,129},{129,1},{2,130},{130,2},{3,131},{131,3},{4... | collective-permute-start | bytes 393224 | tf_op jit(solution)/shard_map/ppermute | solution.py:691

commit v15 on v14

--- a/solution.py
+++ b/solution.py
@@ -373,9 +373,9 @@
 def user_backward_kernel(users, d_user_ref, *refs):
     sources, refs = refs[:18], refs[18:]
     d_rows_ref, ahead, refs = refs[0], refs[1:7], refs[7:]
-    targets, (d_normed, sems) = refs[:12], refs[12:]
+    targets, sems = refs[:12], refs[12]
     mixed_ref, out_gain_ref, w_out, w_value, normed_ref, weights_ref, qk_ref = targets[:7]
-    w_key, w_query, hidden_ref, norm_gain_ref, in_proj = targets[7:]
+    hidden_ref, norm_gain_ref, in_proj, w_key, w_query = targets[7:]
     copies = copies_of(zip(sources, tuple(targets) + tuple(ahead)), sems)
     span, width = hidden_ref.shape
     hist = span // users
@@ -396,26 +396,29 @@
     d_weights = jnp.where(own, dot_nt(d_mixes, normed), 0.0)
     d_scores = weights * (d_weights - jnp.sum(weights * d_weights, axis=1, keepdims=True))
     d_scores = (d_scores * (1.0 / math.sqrt(HEAD_DIM))).astype(BF)
-    d_normed[...] = dot_tn(
+    d_normed = dot_tn(
         jnp.concatenate([weights.astype(BF), d_scores], axis=0),
         jnp.concatenate([d_mixes, qk_ref[...]], axis=0),
     )
     d_qk = dot(d_scores, normed).astype(BF)
-    copies[7].wait()
+    for copy in copies[7:11]:
+        copy.wait()
+    hidden, gain = hidden_ref[...], norm_gain_ref[...]
+    d_rows = dot_nt(norm_backward(hidden, d_normed, gain).astype(BF), in_proj[...])
     d_query = join_heads(dot(d_qk, w_key[...]), mask, users).astype(BF)
-    copies[8].wait()
+    copies[11].wait()
     d_last = dot_nt(d_query, w_query[...])
-    for u in range(users):
-        at = slice((u + 1) * hist - 1, (u + 1) * hist)
-        d_normed[at, :] = d_normed[at, :] + d_last[u : u + 1]
-    copies[9].wait()
-    copies[10].wait()
-    d_normed[...] = norm_backward(hidden_ref[...], d_normed[...], norm_gain_ref[...])
-    for u in range(users):
-        at = slice((u + 1) * hist - 1, (u + 1) * hist)
-        d_normed[at, :] = d_normed[at, :] + d_mixed[u : u + 1]
-    copies[11].wait()
-    d_rows_ref[...] = dot_nt(d_normed[...].astype(BF), in_proj[...]).astype(BF)
+    last = jnp.concatenate(
+        [hidden[(u + 1) * hist - 1 : (u + 1) * hist] for u in range(users)]
+        + [jnp.zeros((PAD - users, width), F32)],
+        axis=0,
+    )
+    d_last = norm_backward(last, d_last, gain) + d_mixed
+    d_last = dot_nt(d_last.astype(BF), in_proj[...]).astype(BF)
+    shape = (span, PAD)
+    at = iota(shape, 1)
+    place = one_hot((at < users) & (iota(shape, 0) == (at + 1) * hist - 1))
+    d_rows_ref[...] = (d_rows + dot(place, d_last)).astype(BF)
     for copy in copies[12:]:
         copy.wait()
 
@@ -633,14 +636,14 @@
     parts = exchange(d_part, LINE)
 
     loads = (mixed, out_gain, w_out, w_value, normed, weights, qk)
-    loads += (w_key, w_query, hidden, norm_gain, in_proj)
+    loads += (hidden, norm_gain, in_proj, w_key, w_query)
     ahead = (row, item_gain, inner, item_w2, item_w1, outer)
     d_rows, *item_ready = pl.pallas_call(
         functools.partial(user_backward_kernel, users),
         out_shape=(shape((span, emb), BF), *map(vmem, ahead)),
         in_specs=[VMEM] + [HBM] * 18,
         out_specs=(VMEM,) * 7,
-        scratch_shapes=like(loads) + [pltpu.VMEM((span, width), F32), sems(18)],
+        scratch_shapes=like(loads) + [sems(18)],
         compiler_params=params(40),
         name="user_backward",
     )(d_user, *map(in_hbm, loads + ahead))

time: 156 us -> 156 us (level)
  no operation moved by 1% of the time
where the time goes in v15:
time: 156 us
  blocking collectives  105 us (67%)
  Pallas kernels  23.8 us (15%)
  starting transfers between devices  19.1 us (12%)
  waiting for transfers between devices  6.4 us (4%)
    all_to_all x1, blocking collectives, shards(): returned = exchange(outgoing, SHARD)  27.2 us
    all_to_all x1, blocking collectives, shards(): asked = exchange(request, SHARD)  26.7 us
    all_to_all x1, blocking collectives, shards(): fetched = exchange(served, SHARD)  23.6 us
    all_to_all x1, blocking collectives, shards(): gathered = exchange(spread, ('x', 'y'))  16.2 us
    all_to_all x1, blocking collectives, shards(): sums = exchange(mine, GROUP)  11 us
    pallas_call x1, Pallas kernels, shards(): pl.pallas_call(functools.partial(user_backward_kernel, users), out_shape=...  6.51 us
    pallas_call x1, Pallas kernels, shards(): pl.pallas_call(functools.partial(user_forward_kernel, users), out_shape=(...  5.81 us
    ppermute x1, starting transfers between devices, shards(): swapped = lax.ppermute(gathered, 'tower', swap)  5.71 us
  transfers between devices with their start and end apart: 6, of which 5 were waited for; matrix products, arithmetic and copies ran while one was open for 1% of the time, Pallas kernels for 8%

profile of v15, /device:TPU:1, one launch (start us, length us, event | category | flops | bytes accessed | tf_op | source)
XLA Modules:
  0.0 155.7 jit_solution(4058105495434538522)
XLA Ops:
  0.6 1.4 index.1
  2.1 26.7 %all_to_all.77 = s32[128,1,128]{2,1,0:T(1,128)S(1)} all-to-all(s32[128,1,128]{2,1,0:T(1,128)S(1)} %bitcast.38), channel_id=1, replica_groups=mesh['tower'=2,'x'=4,'y'=4,'zh'=4,'zl'=2] {'x','y','zh','zl'}, dimensions={0} | all-to-all | bytes 131072 | tf_op jit(solution)/shard_map/all_to_all | solution.py:557
  28.8 1.4 serve.1
  30.1 23.6 %all_to_all.78 = bf16[128,8,256]{2,1,0:T(8,128)(2,1)S(1)} all-to-all(bf16[128,8,256]{2,1,0:T(8,128)(2,1)S(1)} %bitcast.32), channel_id=1, replica_groups=mesh['tower'=2,'x'=4,'y'=4,'zh'=4,'zl'=2] {'x','y','zh','zl'}, dimensions={0} | all-to-all | bytes 1048576 | tf_op jit(solution)/shard_map/all_to_all | solution.py:577
  53.7 2.5 %item_forward.1 = (bf16[64,1024]{1,0:T(8,128)(2,1)}, f32[16,1024]{1,0:T(8,128)S(1)}, f32[16,1024]{1,0:T(8,128)S(1)}) custom-call(bf16[1024,256]{1,0:T(8,128)(2,1)S(1)} %bitcast.24, bf16[128,256]{1,0:T(8,128)(2,1)S(1)} %get-tuple-element.46.hot_ref, s32[16,128]{1,0:T(8,128)S(1)} %get-tuple-element.47.column_ref, bf16[1024,1024]{1,0:T(8,128)(2,1)S(1)} %copy-done, ...), custom_call_target="tpu_custom_call" | custom-call | tf_op jit(solution)/shard_map/item_forward/pallas_call | solution.py:581
  56.3 3.4 %all-to-all-start.2 = ((bf16[8,8,1024]{2,1,0:T(8,128)(2,1)}), bf16[8,8,1024]{2,1,0:T(8,128)(2,1)S(1)}, u32[]{:S(2)}, u32[]{:S(2)}) async-start(bf16[8,8,1024]{2,1,0:T(8,128)(2,1)} %bitcast.10), calls=%async_computation.2 | async-start | bytes 262144 | tf_op jit(solution)/shard_map/all_to_all | solution.py:594
  59.7 5.8 %user_forward.1 = (bf16[16,1024]{1,0:T(8,128)(2,1)S(1)}, f32[256,1024]{1,0:T(8,128)}, bf16[256,1024]{1,0:T(8,128)(2,1)}, bf16[64,1024]{1,0:T(8,128)(2,1)}, f32[6...) custom-call(bf16[1024,256]{1,0:T(8,128)(2,1)S(1)} %bitcast.25, ...), custom_call_target="tpu_custom_call" | custom-call | tf_op jit(solution)/shard_map/user_forward/pallas_call | solution.py:605
  65.5 2.0 %all-to-all-done.2 = bf16[8,8,1024]{2,1,0:T(8,128)(2,1)S(1)} async-done(((bf16[8,8,1024]{2,1,0:T(8,128)(2,1)}), bf16[8,8,1024]{2,1,0:T(8,128)(2,1)S(1)}, u32[]{:S(2)}, u32[]{:S(2)}) %all-to-all-start.2) | async-done | bytes 131104 | tf_op jit(solution)/shard_map/all_to_all | solution.py:594
  67.7 16.2 %all_to_all.79 = bf16[16,32,1152]{2,1,0:T(8,128)(2,1)S(1)} all-to-all(bf16[16,32,1152]{2,1,0:T(8,128)(2,1)S(1)} %bitcast.28), channel_id=1, replica_groups=mesh['tower'=2,'x'=4,'y'=4,'zh'=4,'zl'=2] {'x','y'}, dimensions={0} | all-to-all | bytes 2359296 | tf_op jit(solution)/shard_map/all_to_all | solution.py:624
  83.9 5.7 %collective-permute-start = (bf16[512,1152]{1,0:T(8,128)(2,1)S(1)}, bf16[512,1152]{1,0:T(8,128)(2,1)S(1)}, u32[]{:S(2)}, u32[]{:S(2)}) collective-permute-start(bf16[512,1152]{1,0:T(8,128)(2,1)S(1)} %bitcast.26), channel_id=1, source_target_pairs={{0,128},{128,0},{1,129},{129,1},{2,130},{130,2},{3,131},{131,3},{4... | collective-permute-start | bytes 3538952 | tf_op jit(solution)/shard_map/ppermute | solution.py:625
  89.7 2.4 %collective-permute-done.swapped_ref = bf16[512,1152]{1,0:T(8,128)(2,1)S(1)} collective-permute-done((bf16[512,1152]{1,0:T(8,128)(2,1)S(1)}, bf16[512,1152]{1,0:T(8,128)(2,1)S(1)}, u32[]{:S(2)}, u32[]{:S(2)}) %collective-permute-start) | collective-permute-done | bytes 1179680 | tf_op jit(solution)/shard_map/ppermute | solution.py:625
  92.1 2.7 %softmax.1 = (f32[16,1024]{1,0:T(8,128)S(1)}, bf16[64,1024]{1,0:T(8,128)(2,1)}) custom-call(s32[2]{0:T(128)S(1)} %pad_add_fusion.place_ref, bf16[512,1152]{1,0:T(8,128)(2,1)S(1)} %bitcast.27, bf16[512,1152]{1,0:T(8,128)(2,1)S(1)} %collective-permute-done.swapped_ref), custom_call_target="tpu_custom_call" | custom-call | tf_op jit(solution)/shard_map/softmax/pallas_call | solution.py:627
  94.8 4.5 %all-to-all-start.4 = ((bf16[8,8,1024]{2,1,0:T(8,128)(2,1)}), bf16[8,8,1024]{2,1,0:T(8,128)(2,1)S(1)}, u32[]{:S(2)}, u32[]{:S(2)}) async-start(bf16[8,8,1024]{2,1,0:T(8,128)(2,1)} %bitcast.16), calls=%async_computation.4 | async-start | bytes 262144 | tf_op jit(solution)/shard_map/all_to_all | solution.py:636
  99.3 6.5 %user_backward.1 = (bf16[256,256]{1,0:T(8,128)(2,1)S(1)}, s32[8,384]{1,0:T(8,128)S(1)}, f32[1,1024]{1,0:T(1,128)S(1)}, f32[16,1024]{1,0:T(8,128)S(1)}, bf16[1024...) custom-call(f32[16,1024]{1,0:T(8,128)S(1)} %get-tuple-element.54.d_user_ref, ...), custom_call_target="tpu_custom_call" | custom-call | tf_op jit(solution)/shard_map/user_backward/pallas_call | solution.py:641
  105.8 1.4 all-to-all-done.4
  107.2 1.2 item_backward.1
  108.5 2.2 %collective-permute-start.1 = (f32[64,256]{1,0:T(8,128)S(1)}, f32[64,256]{1,0:T(8,128)S(1)}, u32[]{:S(2)}, u32[]{:S(2)}) collective-permute-start(f32[64,256]{1,0:T(8,128)S(1)} %get-tuple-element.72), channel_id=1, source_target_pairs={{0,128},{128,0},{1,129},{129,1},{2,130},{130,2},{3,131},{131,3},{4... | collective-permute-start | bytes 196616 | tf_op jit(solution)/shard_map/ppermute | solution.py:665
  112.0 27.2 %all_to_all.80 = bf16[128,8,256]{2,1,0:T(8,128)(2,1)S(1)} all-to-all(bf16[128,8,256]{2,1,0:T(8,128)(2,1)S(1)} %bitcast.30), channel_id=1, replica_groups=mesh['tower'=2,'x'=4,'y'=4,'zh'=4,'zl'=2] {'x','y','zh','zl'}, dimensions={0} | all-to-all | bytes 1048576 | tf_op jit(solution)/shard_map/all_to_all | solution.py:683
  139.2 0.5 scatter.1
  139.7 2.4 %collective-permute-start.3 = (bf16[512,256]{1,0:T(8,128)(2,1)S(1)}, bf16[512,256]{1,0:T(8,128)(2,1)S(1)}, u32[]{:S(2)}, u32[]{:S(2)}) collective-permute-start(bf16[512,256]{1,0:T(8,128)(2,1)S(1)} %get-tuple-element.77), channel_id=1, source_target_pairs={{0,128},{128,0},{1,129},{129,1},{2,130},{130,2},{3,131},{131,3},{4... | collective-permute-start | bytes 786440 | tf_op jit(solution)/shard_map/ppermute | solution.py:692
  142.1 11.0 %all_to_all.81 = f32[32,8,128]{2,1,0:T(8,128)S(1)} all-to-all(f32[32,8,128]{2,1,0:T(8,128)S(1)} %bitcast.37), channel_id=1, replica_groups=mesh['tower'=2,'x'=4,'y'=4,'zh'=4,'zl'=2] {'x','y','zl'}, dimensions={0} | all-to-all | bytes 262144 | tf_op jit(solution)/shard_map/all_to_all | solution.py:693
  153.1 0.9 collective-permute-start.2
  154.0 0.8 convert_add_fusion
  155.0 0.7 finish.1
  (11 shorter events, 1.8 us)
Async XLA Ops:
  0.6 53.1 %copy-start = (bf16[1024,1024]{1,0:T(8,128)(2,1)S(1)}, bf16[1024,1024]{1,0:T(8,128)(2,1)}, u32[]{:S(2)}) copy-start(bf16[1024,1024]{1,0:T(8,128)(2,1)} %refs_15_.1) | copy-start | bytes 6291460
  56.3 11.2 %all-to-all-start.2 = ((bf16[8,8,1024]{2,1,0:T(8,128)(2,1)}), bf16[8,8,1024]{2,1,0:T(8,128)(2,1)S(1)}, u32[]{:S(2)}, u32[]{:S(2)}) async-start(bf16[8,8,1024]{2,1,0:T(8,128)(2,1)} %bitcast.10), calls=%async_computation.2 | async-start | bytes 262144 | tf_op jit(solution)/shard_map/all_to_all | solution.py:594
  83.9 8.2 %collective-permute-start = (bf16[512,1152]{1,0:T(8,128)(2,1)S(1)}, bf16[512,1152]{1,0:T(8,128)(2,1)S(1)}, u32[]{:S(2)}, u32[]{:S(2)}) collective-permute-start(bf16[512,1152]{1,0:T(8,128)(2,1)S(1)} %bitcast.26), channel_id=1, source_target_pairs={{0,128},{128,0},{1,129},{129,1},{2,130},{130,2},{3,131},{131,3},{4... | collective-permute-start | bytes 3538952 | tf_op jit(solution)/shard_map/ppermute | solution.py:625
  94.8 12.4 %all-to-all-start.4 = ((bf16[8,8,1024]{2,1,0:T(8,128)(2,1)}), bf16[8,8,1024]{2,1,0:T(8,128)(2,1)S(1)}, u32[]{:S(2)}, u32[]{:S(2)}) async-start(bf16[8,8,1024]{2,1,0:T(8,128)(2,1)} %bitcast.16), calls=%async_computation.4 | async-start | bytes 262144 | tf_op jit(solution)/shard_map/all_to_all | solution.py:636
  108.4 30.8 %copy-start.1 = (s32[8,1024]{1,0:T(8,128)S(1)}, s32[8,1024]{1,0:T(8,128)}, u32[]{:S(2)}) copy-start(s32[8,1024]{1,0:T(8,128)} %get-tuple-element.73.row_ref) | copy-start | bytes 98308
  108.5 3.1 %collective-permute-start.1 = (f32[64,256]{1,0:T(8,128)S(1)}, f32[64,256]{1,0:T(8,128)S(1)}, u32[]{:S(2)}, u32[]{:S(2)}) collective-permute-start(f32[64,256]{1,0:T(8,128)S(1)} %get-tuple-element.72), channel_id=1, source_target_pairs={{0,128},{128,0},{1,129},{129,1},{2,130},{130,2},{3,131},{131,3},{4... | collective-permute-start | bytes 196616 | tf_op jit(solution)/shard_map/ppermute | solution.py:665
  139.7 14.3 %collective-permute-start.3 = (bf16[512,256]{1,0:T(8,128)(2,1)S(1)}, bf16[512,256]{1,0:T(8,128)(2,1)S(1)}, u32[]{:S(2)}, u32[]{:S(2)}) collective-permute-start(bf16[512,256]{1,0:T(8,128)(2,1)S(1)} %get-tuple-element.77), channel_id=1, source_target_pairs={{0,128},{128,0},{1,129},{129,1},{2,130},{130,2},{3,131},{131,3},{4... | collective-permute-start | bytes 786440 | tf_op jit(solution)/shard_map/ppermute | solution.py:692
  153.1 1.9 %collective-permute-start.2 = (f32[256,128]{1,0:T(8,128)S(1)}, f32[256,128]{1,0:T(8,128)S(1)}, u32[]{:S(2)}, u32[]{:S(2)}) collective-permute-start(f32[256,128]{1,0:T(8,128)S(1)} %bitcast.33), channel_id=1, source_target_pairs={{0,128},{128,0},{1,129},{129,1},{2,130},{130,2},{3,131},{131,3},{4... | collective-permute-start | bytes 393224 | tf_op jit(solution)/shard_map/ppermute | solution.py:694

commit v16 on v14

--- a/solution.py
+++ b/solution.py
@@ -300,8 +300,30 @@
         spread_ref[i * block : (i + 1) * block, :] = rows
 
 
+def users_of(near, width, ref):
+    rows = ref.shape[0]
+    group = rows // near
+    line = iota((rows, rows), 0)
+    picks = one_hot(iota((rows, rows), 1) == line % group * near + line // group)
+    parts = dot(picks, ref[:, width:])
+    return jnp.concatenate([parts[c * group : (c + 1) * group] for c in range(near)], axis=1).astype(BF)
+
+
+def own_users_kernel(near, gathered_ref, own_ref):
+    own_ref[...] = users_of(near, own_ref.shape[1], gathered_ref)
+
+
 def softmax_kernel(
-    users, near, scale, place_ref, gathered_ref, swapped_ref, d_user_ref, d_part_ref, raised_ref
+    users,
+    near,
+    scale,
+    place_ref,
+    gathered_ref,
+    own_users_ref,
+    swapped_ref,
+    d_user_ref,
+    d_part_ref,
+    raised_ref,
 ):
     rows = gathered_ref.shape[0]
     width = d_user_ref.shape[1]
@@ -309,15 +331,8 @@
     group = rows // near
     mine, plane = place_ref[0], place_ref[1]
     own, other = gathered_ref[:, 0:width], swapped_ref[:, 0:width]
-    shape = (rows, rows)
-    line = iota(shape, 0)
-    picks = one_hot(iota(shape, 1) == line % group * near + line // group)
-
-    def users_of(ref):
-        parts = dot(picks, ref[:, width:])
-        return jnp.concatenate([parts[c * group : (c + 1) * group] for c in range(near)], axis=1)
-
-    group_users = jnp.concatenate([users_of(gathered_ref), users_of(swapped_ref)], axis=0).astype(BF)
+    other_users = users_of(near, width, swapped_ref)
+    group_users = jnp.concatenate([own_users_ref[...], other_users], axis=0)
     total = 2 * group
 
     shape = (rows, total)
@@ -620,16 +635,24 @@
     )(near_items, user_vec)
     gathered = exchange(spread, ("x", "y"))
     swapped = lax.ppermute(gathered, "tower", swap)
+    own_users = pl.pallas_call(
+        functools.partial(own_users_kernel, near),
+        out_shape=shape((rows // near, width), BF),
+        in_specs=[VMEM],
+        out_specs=VMEM,
+        compiler_params=params(24),
+        name="own_users",
+    )(gathered)
     place = jnp.stack([lax.axis_index(("x", "y")), lax.axis_index(LINE)]).astype(jnp.int32)
     d_user, d_part = pl.pallas_call(
         functools.partial(softmax_kernel, users, near, scale),
         out_shape=(shape((PAD, width), F32), shape((near * 8, width), BF)),
-        in_specs=[SMEM, VMEM, VMEM],
+        in_specs=[SMEM, VMEM, VMEM, VMEM],
         out_specs=(VMEM, VMEM),
         scratch_shapes=[pltpu.VMEM((rows, 2 * owners // near * users), F32)],
         compiler_params=params(32),
         name="softmax",
-    )(place, gathered, swapped)
+    )(place, gathered, own_users, swapped)
     parts = exchange(d_part, LINE)
 
     loads = (mixed, out_gain, w_out, w_value, normed, weights, qk)

time: 156 us -> 156 us (level)
  no operation moved by 1% of the time
where the time goes in v16:
time: 156 us
  blocking collectives  105 us (67%)
  Pallas kernels  23.9 us (15%)
  starting transfers between devices  19.1 us (12%)
  waiting for transfers between devices  6.27 us (4%)
    all_to_all x1, blocking collectives, shards(): returned = exchange(outgoing, SHARD)  27 us
    all_to_all x1, blocking collectives, shards(): asked = exchange(request, SHARD)  26.7 us
    all_to_all x1, blocking collectives, shards(): fetched = exchange(served, SHARD)  23.6 us
    all_to_all x1, blocking collectives, shards(): gathered = exchange(spread, ('x', 'y'))  16.2 us
    all_to_all x1, blocking collectives, shards(): sums = exchange(mine, GROUP)  11 us
    pallas_call x1, Pallas kernels, shards(): pl.pallas_call(functools.partial(user_backward_kernel, users), out_shape=...  6.34 us
    pallas_call x1, Pallas kernels, shards(): pl.pallas_call(functools.partial(user_forward_kernel, users), out_shape=(...  5.81 us
    ppermute x1, starting transfers between devices, shards(): swapped = lax.ppermute(gathered, 'tower', swap)  5.71 us
  transfers between devices with their start and end apart: 6, of which 5 were waited for; matrix products, arithmetic and copies ran while one was open for 1% of the time, Pallas kernels for 8%

profile of v16, /device:TPU:1, one launch (start us, length us, event | category | flops | bytes accessed | tf_op | source)
XLA Modules:
  0.0 155.5 jit_solution(113195146618909625)
XLA Ops:
  0.6 1.4 index.1
  2.1 26.7 %all_to_all.77 = s32[128,1,128]{2,1,0:T(1,128)S(1)} all-to-all(s32[128,1,128]{2,1,0:T(1,128)S(1)} %bitcast.39), channel_id=1, replica_groups=mesh['tower'=2,'x'=4,'y'=4,'zh'=4,'zl'=2] {'x','y','zh','zl'}, dimensions={0} | all-to-all | bytes 131072 | tf_op jit(solution)/shard_map/all_to_all | solution.py:569
  28.8 1.4 serve.1
  30.1 23.6 %all_to_all.78 = bf16[128,8,256]{2,1,0:T(8,128)(2,1)S(1)} all-to-all(bf16[128,8,256]{2,1,0:T(8,128)(2,1)S(1)} %bitcast.33), channel_id=1, replica_groups=mesh['tower'=2,'x'=4,'y'=4,'zh'=4,'zl'=2] {'x','y','zh','zl'}, dimensions={0} | all-to-all | bytes 1048576 | tf_op jit(solution)/shard_map/all_to_all | solution.py:589
  53.7 2.5 %item_forward.1 = (bf16[64,1024]{1,0:T(8,128)(2,1)}, f32[16,1024]{1,0:T(8,128)S(1)}, f32[16,1024]{1,0:T(8,128)S(1)}) custom-call(bf16[1024,256]{1,0:T(8,128)(2,1)S(1)} %bitcast.27, bf16[128,256]{1,0:T(8,128)(2,1)S(1)} %get-tuple-element.46.hot_ref, s32[16,128]{1,0:T(8,128)S(1)} %get-tuple-element.47.column_ref, bf16[1024,1024]{1,0:T(8,128)(2,1)S(1)} %copy-done, ...), custom_call_target="tpu_custom_call" | custom-call | tf_op jit(solution)/shard_map/item_forward/pallas_call | solution.py:593
  56.3 3.4 %all-to-all-start.2 = ((bf16[8,8,1024]{2,1,0:T(8,128)(2,1)}), bf16[8,8,1024]{2,1,0:T(8,128)(2,1)S(1)}, u32[]{:S(2)}, u32[]{:S(2)}) async-start(bf16[8,8,1024]{2,1,0:T(8,128)(2,1)} %bitcast.10), calls=%async_computation.2 | async-start | bytes 262144 | tf_op jit(solution)/shard_map/all_to_all | solution.py:606
  59.7 5.8 %user_forward.1 = (bf16[16,1024]{1,0:T(8,128)(2,1)S(1)}, f32[256,1024]{1,0:T(8,128)}, bf16[256,1024]{1,0:T(8,128)(2,1)}, bf16[64,1024]{1,0:T(8,128)(2,1)}, f32[6...) custom-call(bf16[1024,256]{1,0:T(8,128)(2,1)S(1)} %bitcast.28, ...), custom_call_target="tpu_custom_call" | custom-call | tf_op jit(solution)/shard_map/user_forward/pallas_call | solution.py:617
  65.5 2.0 %all-to-all-done.2 = bf16[8,8,1024]{2,1,0:T(8,128)(2,1)S(1)} async-done(((bf16[8,8,1024]{2,1,0:T(8,128)(2,1)}), bf16[8,8,1024]{2,1,0:T(8,128)(2,1)S(1)}, u32[]{:S(2)}, u32[]{:S(2)}) %all-to-all-start.2) | async-done | bytes 131104 | tf_op jit(solution)/shard_map/all_to_all | solution.py:606
  67.7 16.2 %all_to_all.79 = bf16[16,32,1152]{2,1,0:T(8,128)(2,1)S(1)} all-to-all(bf16[16,32,1152]{2,1,0:T(8,128)(2,1)S(1)} %bitcast.29), channel_id=1, replica_groups=mesh['tower'=2,'x'=4,'y'=4,'zh'=4,'zl'=2] {'x','y'}, dimensions={0} | all-to-all | bytes 2359296 | tf_op jit(solution)/shard_map/all_to_all | solution.py:636
  83.9 5.7 %collective-permute-start = (bf16[512,1152]{1,0:T(8,128)(2,1)S(1)}, bf16[512,1152]{1,0:T(8,128)(2,1)S(1)}, u32[]{:S(2)}, u32[]{:S(2)}) collective-permute-start(bf16[512,1152]{1,0:T(8,128)(2,1)S(1)} %bitcast.24), channel_id=1, source_target_pairs={{0,128},{128,0},{1,129},{129,1},{2,130},{130,2},{3,131},{131,3},{4... | collective-permute-start | bytes 3538952 | tf_op jit(solution)/shard_map/ppermute | solution.py:637
  90.0 2.1 %collective-permute-done.swapped_ref = bf16[512,1152]{1,0:T(8,128)(2,1)S(1)} collective-permute-done((bf16[512,1152]{1,0:T(8,128)(2,1)S(1)}, bf16[512,1152]{1,0:T(8,128)(2,1)S(1)}, u32[]{:S(2)}, u32[]{:S(2)}) %collective-permute-start) | collective-permute-done | bytes 1179680 | tf_op jit(solution)/shard_map/ppermute | solution.py:637
  92.1 2.7 %softmax.1 = (f32[16,1024]{1,0:T(8,128)S(1)}, bf16[64,1024]{1,0:T(8,128)(2,1)}) custom-call(s32[2]{0:T(128)S(1)} %pad_add_fusion.place_ref, bf16[512,1152]{1,0:T(8,128)(2,1)S(1)} %bitcast.26, bf16[64,1024]{1,0:T(8,128)(2,1)S(1)} %own_users.1.own_users_ref, bf16[512,1152]{1,0:T(8,128)(2,1)S(1)} %collective-permute-done.swapped_ref), custom_call_target="tpu_custom_call" | custom-call | tf_op jit(solution)/shard_map/softmax/pallas_call | solution.py:647
  94.8 4.5 %all-to-all-start.4 = ((bf16[8,8,1024]{2,1,0:T(8,128)(2,1)}), bf16[8,8,1024]{2,1,0:T(8,128)(2,1)S(1)}, u32[]{:S(2)}, u32[]{:S(2)}) async-start(bf16[8,8,1024]{2,1,0:T(8,128)(2,1)} %bitcast.16), calls=%async_computation.4 | async-start | bytes 262144 | tf_op jit(solution)/shard_map/all_to_all | solution.py:656
  99.3 6.3 %user_backward.1 = (bf16[256,256]{1,0:T(8,128)(2,1)S(1)}, s32[8,384]{1,0:T(8,128)S(1)}, f32[1,1024]{1,0:T(1,128)S(1)}, f32[16,1024]{1,0:T(8,128)S(1)}, bf16[1024...) custom-call(f32[16,1024]{1,0:T(8,128)S(1)} %get-tuple-element.54.d_user_ref, ...), custom_call_target="tpu_custom_call" | custom-call | tf_op jit(solution)/shard_map/user_backward/pallas_call | solution.py:661
  105.6 1.5 all-to-all-done.4
  107.2 1.2 item_backward.1
  108.5 2.2 %collective-permute-start.1 = (f32[64,256]{1,0:T(8,128)S(1)}, f32[64,256]{1,0:T(8,128)S(1)}, u32[]{:S(2)}, u32[]{:S(2)}) collective-permute-start(f32[64,256]{1,0:T(8,128)S(1)} %get-tuple-element.72), channel_id=1, source_target_pairs={{0,128},{128,0},{1,129},{129,1},{2,130},{130,2},{3,131},{131,3},{4... | collective-permute-start | bytes 196616 | tf_op jit(solution)/shard_map/ppermute | solution.py:685
  112.0 27.0 %all_to_all.80 = bf16[128,8,256]{2,1,0:T(8,128)(2,1)S(1)} all-to-all(bf16[128,8,256]{2,1,0:T(8,128)(2,1)S(1)} %bitcast.31), channel_id=1, replica_groups=mesh['tower'=2,'x'=4,'y'=4,'zh'=4,'zl'=2] {'x','y','zh','zl'}, dimensions={0} | all-to-all | bytes 1048576 | tf_op jit(solution)/shard_map/all_to_all | solution.py:703
  139.0 0.5 scatter.1
  139.5 2.4 %collective-permute-start.3 = (bf16[512,256]{1,0:T(8,128)(2,1)S(1)}, bf16[512,256]{1,0:T(8,128)(2,1)S(1)}, u32[]{:S(2)}, u32[]{:S(2)}) collective-permute-start(bf16[512,256]{1,0:T(8,128)(2,1)S(1)} %get-tuple-element.77), channel_id=1, source_target_pairs={{0,128},{128,0},{1,129},{129,1},{2,130},{130,2},{3,131},{131,3},{4... | collective-permute-start | bytes 786440 | tf_op jit(solution)/shard_map/ppermute | solution.py:712
  141.9 11.0 %all_to_all.81 = f32[32,8,128]{2,1,0:T(8,128)S(1)} all-to-all(f32[32,8,128]{2,1,0:T(8,128)S(1)} %bitcast.38), channel_id=1, replica_groups=mesh['tower'=2,'x'=4,'y'=4,'zh'=4,'zl'=2] {'x','y','zl'}, dimensions={0} | all-to-all | bytes 262144 | tf_op jit(solution)/shard_map/all_to_all | solution.py:713
  153.0 0.9 collective-permute-start.2
  153.9 0.8 convert_add_fusion
  154.9 0.7 finish.1
  (12 shorter events, 2.1 us)
Async XLA Ops:
  0.6 53.1 %copy-start = (bf16[1024,1024]{1,0:T(8,128)(2,1)S(1)}, bf16[1024,1024]{1,0:T(8,128)(2,1)}, u32[]{:S(2)}) copy-start(bf16[1024,1024]{1,0:T(8,128)(2,1)} %refs_15_.1) | copy-start | bytes 6291460
  56.3 11.2 %all-to-all-start.2 = ((bf16[8,8,1024]{2,1,0:T(8,128)(2,1)}), bf16[8,8,1024]{2,1,0:T(8,128)(2,1)S(1)}, u32[]{:S(2)}, u32[]{:S(2)}) async-start(bf16[8,8,1024]{2,1,0:T(8,128)(2,1)} %bitcast.10), calls=%async_computation.2 | async-start | bytes 262144 | tf_op jit(solution)/shard_map/all_to_all | solution.py:606
  83.9 8.2 %collective-permute-start = (bf16[512,1152]{1,0:T(8,128)(2,1)S(1)}, bf16[512,1152]{1,0:T(8,128)(2,1)S(1)}, u32[]{:S(2)}, u32[]{:S(2)}) collective-permute-start(bf16[512,1152]{1,0:T(8,128)(2,1)S(1)} %bitcast.24), channel_id=1, source_target_pairs={{0,128},{128,0},{1,129},{129,1},{2,130},{130,2},{3,131},{131,3},{4... | collective-permute-start | bytes 3538952 | tf_op jit(solution)/shard_map/ppermute | solution.py:637
  94.8 12.4 %all-to-all-start.4 = ((bf16[8,8,1024]{2,1,0:T(8,128)(2,1)}), bf16[8,8,1024]{2,1,0:T(8,128)(2,1)S(1)}, u32[]{:S(2)}, u32[]{:S(2)}) async-start(bf16[8,8,1024]{2,1,0:T(8,128)(2,1)} %bitcast.16), calls=%async_computation.4 | async-start | bytes 262144 | tf_op jit(solution)/shard_map/all_to_all | solution.py:656
  108.4 30.6 %copy-start.1 = (s32[8,1024]{1,0:T(8,128)S(1)}, s32[8,1024]{1,0:T(8,128)}, u32[]{:S(2)}) copy-start(s32[8,1024]{1,0:T(8,128)} %get-tuple-element.73.row_ref) | copy-start | bytes 98308
  108.5 3.1 %collective-permute-start.1 = (f32[64,256]{1,0:T(8,128)S(1)}, f32[64,256]{1,0:T(8,128)S(1)}, u32[]{:S(2)}, u32[]{:S(2)}) collective-permute-start(f32[64,256]{1,0:T(8,128)S(1)} %get-tuple-element.72), channel_id=1, source_target_pairs={{0,128},{128,0},{1,129},{129,1},{2,130},{130,2},{3,131},{131,3},{4... | collective-permute-start | bytes 196616 | tf_op jit(solution)/shard_map/ppermute | solution.py:685
  139.5 14.3 %collective-permute-start.3 = (bf16[512,256]{1,0:T(8,128)(2,1)S(1)}, bf16[512,256]{1,0:T(8,128)(2,1)S(1)}, u32[]{:S(2)}, u32[]{:S(2)}) collective-permute-start(bf16[512,256]{1,0:T(8,128)(2,1)S(1)} %get-tuple-element.77), channel_id=1, source_target_pairs={{0,128},{128,0},{1,129},{129,1},{2,130},{130,2},{3,131},{131,3},{4... | collective-permute-start | bytes 786440 | tf_op jit(solution)/shard_map/ppermute | solution.py:712
  153.0 1.9 %collective-permute-start.2 = (f32[256,128]{1,0:T(8,128)S(1)}, f32[256,128]{1,0:T(8,128)S(1)}, u32[]{:S(2)}, u32[]{:S(2)}) collective-permute-start(f32[256,128]{1,0:T(8,128)S(1)} %bitcast.34), channel_id=1, source_target_pairs={{0,128},{128,0},{1,129},{129,1},{2,130},{130,2},{3,131},{131,3},{4... | collective-permute-start | bytes 393224 | tf_op jit(solution)/shard_map/ppermute | solution.py:714

commit v17 on v16

--- a/solution.py
+++ b/solution.py
@@ -238,7 +238,7 @@
         copy.wait()
     pos = pos_of[...].astype(F32)
     hidden = dot(rows, in_proj[...]) + jnp.concatenate([pos] * users, axis=0)
-    hidden_ref[...] = hidden
+    hidden_ref[...] = hidden.astype(BF)
     saves[0].start()
     scale = lax.rsqrt(jnp.mean(hidden * hidden, axis=-1, keepdims=True) + EPS)
     normed = (hidden * scale * norm_gain_ref[...]).astype(BF)
@@ -425,7 +425,7 @@
         d_normed[at, :] = d_normed[at, :] + d_last[u : u + 1]
     copies[9].wait()
     copies[10].wait()
-    d_normed[...] = norm_backward(hidden_ref[...], d_normed[...], norm_gain_ref[...])
+    d_normed[...] = norm_backward(hidden_ref[...].astype(F32), d_normed[...], norm_gain_ref[...])
     for u in range(users):
         at = slice((u + 1) * hist - 1, (u + 1) * hist)
         d_normed[at, :] = d_normed[at, :] + d_mixed[u : u + 1]
@@ -463,7 +463,7 @@
     d_items = jnp.concatenate([d_items, jnp.zeros((wide - span - PAD, emb), F32)], axis=0).astype(BF)
     d_all_ref[span:, :] = d_items
     keep_ref[...] = keep + dot(picks[:, span:], d_items)
-    send_ref[...] = send + dot(other_picks[:, span:], d_items)
+    send_ref[...] = (send + dot(other_picks[:, span:], d_items)).astype(BF)
 
 
 def rare_kernel(d_all_ref, row_ref, rare_ref):
@@ -479,7 +479,7 @@
     owner, slot = line // SLOTS, line % SLOTS - HOT_SLOT
     held = owner // 8 * 2 + owner % 2 + slot * (half // 2)
     held = one_hot((slot >= 0) & (slot < 2) & (iota(shape, 1) == held))
-    hot = dot(held, (keep_ref[...] + got_ref[...]).astype(BF))
+    hot = dot(held, (keep_ref[...] + got_ref[...].astype(F32)).astype(BF))
     outgoing_ref[...] = (rare_ref[...].astype(F32) + hot).astype(BF)
 
 
@@ -608,7 +608,7 @@
     loads = (column, hot_table, pos_embed, norm_gain, out_gain)
     loads += (in_proj, w_query, w_key, w_value, w_out)
     kept = (
-        shape((span, width), F32),
+        shape((span, width), BF),
         shape((span, width), BF),
         shape((users * heads, width), BF),
         shape((users * heads, span), F32),
@@ -673,7 +673,7 @@
         functools.partial(item_backward_kernel, users),
         out_shape=(
             shape((wide, emb), BF),
-            shape((owners // 2, emb), F32),
+            shape((owners // 2, emb), BF),
             shape((owners // 2, emb), F32),
             shape((8, 128), F32),
         ),

time: 156 us -> 156 us (level)
  no operation moved by 1% of the time
where the time goes in v17:
time: 156 us
  blocking collectives  105 us (67%)
  Pallas kernels  24 us (15%)
  starting transfers between devices  19.1 us (12%)
  waiting for transfers between devices  6.17 us (4%)
    all_to_all x1, blocking collectives, shards(): returned = exchange(outgoing, SHARD)  27.1 us
    all_to_all x1, blocking collectives, shards(): asked = exchange(request, SHARD)  26.7 us
    all_to_all x1, blocking collectives, shards(): fetched = exchange(served, SHARD)  23.6 us
    all_to_all x1, blocking collectives, shards(): gathered = exchange(spread, ('x', 'y'))  16.2 us
    all_to_all x1, blocking collectives, shards(): sums = exchange(mine, GROUP)  11 us
    pallas_call x1, Pallas kernels, shards(): pl.pallas_call(functools.partial(user_backward_kernel, users), out_shape=...  6.38 us
    pallas_call x1, Pallas kernels, shards(): pl.pallas_call(functools.partial(user_forward_kernel, users), out_shape=(...  5.82 us
    ppermute x1, starting transfers between devices, shards(): swapped = lax.ppermute(gathered, 'tower', swap)  5.71 us
  transfers between devices with their start and end apart: 6, of which 5 were waited for; matrix products, arithmetic and copies ran while one was open for 1% of the time, Pallas kernels for 8%

profile of v17, /device:TPU:1, one launch (start us, length us, event | category | flops | bytes accessed | tf_op | source)
XLA Modules:
  0.0 155.6 jit_solution(7271992727888278289)
XLA Ops:
  0.6 1.4 index.1
  2.1 26.7 %all_to_all.77 = s32[128,1,128]{2,1,0:T(1,128)S(1)} all-to-all(s32[128,1,128]{2,1,0:T(1,128)S(1)} %bitcast.39), channel_id=1, replica_groups=mesh['tower'=2,'x'=4,'y'=4,'zh'=4,'zl'=2] {'x','y','zh','zl'}, dimensions={0} | all-to-all | bytes 131072 | tf_op jit(solution)/shard_map/all_to_all | solution.py:569
  28.8 1.4 serve.1
  30.1 23.6 %all_to_all.78 = bf16[128,8,256]{2,1,0:T(8,128)(2,1)S(1)} all-to-all(bf16[128,8,256]{2,1,0:T(8,128)(2,1)S(1)} %bitcast.33), channel_id=1, replica_groups=mesh['tower'=2,'x'=4,'y'=4,'zh'=4,'zl'=2] {'x','y','zh','zl'}, dimensions={0} | all-to-all | bytes 1048576 | tf_op jit(solution)/shard_map/all_to_all | solution.py:589
  53.7 2.5 %item_forward.1 = (bf16[64,1024]{1,0:T(8,128)(2,1)}, f32[16,1024]{1,0:T(8,128)S(1)}, f32[16,1024]{1,0:T(8,128)S(1)}) custom-call(bf16[1024,256]{1,0:T(8,128)(2,1)S(1)} %bitcast.27, bf16[128,256]{1,0:T(8,128)(2,1)S(1)} %get-tuple-element.46.hot_ref, s32[16,128]{1,0:T(8,128)S(1)} %get-tuple-element.47.column_ref, bf16[1024,1024]{1,0:T(8,128)(2,1)S(1)} %copy-done, ...), custom_call_target="tpu_custom_call" | custom-call | tf_op jit(solution)/shard_map/item_forward/pallas_call | solution.py:593
  56.3 3.4 %all-to-all-start.2 = ((bf16[8,8,1024]{2,1,0:T(8,128)(2,1)}), bf16[8,8,1024]{2,1,0:T(8,128)(2,1)S(1)}, u32[]{:S(2)}, u32[]{:S(2)}) async-start(bf16[8,8,1024]{2,1,0:T(8,128)(2,1)} %bitcast.10), calls=%async_computation.2 | async-start | bytes 262144 | tf_op jit(solution)/shard_map/all_to_all | solution.py:606
  59.7 5.8 %user_forward.1 = (bf16[16,1024]{1,0:T(8,128)(2,1)S(1)}, bf16[256,1024]{1,0:T(8,128)(2,1)}, bf16[256,1024]{1,0:T(8,128)(2,1)}, bf16[64,1024]{1,0:T(8,128)(2,1)},...) custom-call(bf16[1024,256]{1,0:T(8,128)(2,1)S(1)} %bitcast.28, ...), custom_call_target="tpu_custom_call" | custom-call | tf_op jit(solution)/shard_map/user_forward/pallas_call | solution.py:617
  65.5 2.0 %all-to-all-done.2 = bf16[8,8,1024]{2,1,0:T(8,128)(2,1)S(1)} async-done(((bf16[8,8,1024]{2,1,0:T(8,128)(2,1)}), bf16[8,8,1024]{2,1,0:T(8,128)(2,1)S(1)}, u32[]{:S(2)}, u32[]{:S(2)}) %all-to-all-start.2) | async-done | bytes 131104 | tf_op jit(solution)/shard_map/all_to_all | solution.py:606
  67.7 16.2 %all_to_all.79 = bf16[16,32,1152]{2,1,0:T(8,128)(2,1)S(1)} all-to-all(bf16[16,32,1152]{2,1,0:T(8,128)(2,1)S(1)} %bitcast.29), channel_id=1, replica_groups=mesh['tower'=2,'x'=4,'y'=4,'zh'=4,'zl'=2] {'x','y'}, dimensions={0} | all-to-all | bytes 2359296 | tf_op jit(solution)/shard_map/all_to_all | solution.py:636
  83.9 5.7 %collective-permute-start = (bf16[512,1152]{1,0:T(8,128)(2,1)S(1)}, bf16[512,1152]{1,0:T(8,128)(2,1)S(1)}, u32[]{:S(2)}, u32[]{:S(2)}) collective-permute-start(bf16[512,1152]{1,0:T(8,128)(2,1)S(1)} %bitcast.24), channel_id=1, source_target_pairs={{0,128},{128,0},{1,129},{129,1},{2,130},{130,2},{3,131},{131,3},{4... | collective-permute-start | bytes 3538952 | tf_op jit(solution)/shard_map/ppermute | solution.py:637
  90.0 2.1 %collective-permute-done.swapped_ref = bf16[512,1152]{1,0:T(8,128)(2,1)S(1)} collective-permute-done((bf16[512,1152]{1,0:T(8,128)(2,1)S(1)}, bf16[512,1152]{1,0:T(8,128)(2,1)S(1)}, u32[]{:S(2)}, u32[]{:S(2)}) %collective-permute-start) | collective-permute-done | bytes 1179680 | tf_op jit(solution)/shard_map/ppermute | solution.py:637
  92.1 2.7 %softmax.1 = (f32[16,1024]{1,0:T(8,128)S(1)}, bf16[64,1024]{1,0:T(8,128)(2,1)}) custom-call(s32[2]{0:T(128)S(1)} %pad_add_fusion.place_ref, bf16[512,1152]{1,0:T(8,128)(2,1)S(1)} %bitcast.26, bf16[64,1024]{1,0:T(8,128)(2,1)S(1)} %own_users.1.own_users_ref, bf16[512,1152]{1,0:T(8,128)(2,1)S(1)} %collective-permute-done.swapped_ref), custom_call_target="tpu_custom_call" | custom-call | tf_op jit(solution)/shard_map/softmax/pallas_call | solution.py:647
  94.8 4.5 %all-to-all-start.4 = ((bf16[8,8,1024]{2,1,0:T(8,128)(2,1)}), bf16[8,8,1024]{2,1,0:T(8,128)(2,1)S(1)}, u32[]{:S(2)}, u32[]{:S(2)}) async-start(bf16[8,8,1024]{2,1,0:T(8,128)(2,1)} %bitcast.16), calls=%async_computation.4 | async-start | bytes 262144 | tf_op jit(solution)/shard_map/all_to_all | solution.py:656
  99.3 6.4 %user_backward.1 = (bf16[256,256]{1,0:T(8,128)(2,1)S(1)}, s32[8,384]{1,0:T(8,128)S(1)}, f32[1,1024]{1,0:T(1,128)S(1)}, f32[16,1024]{1,0:T(8,128)S(1)}, bf16[1024...) custom-call(f32[16,1024]{1,0:T(8,128)S(1)} %get-tuple-element.54.d_user_ref, ...), custom_call_target="tpu_custom_call" | custom-call | tf_op jit(solution)/shard_map/user_backward/pallas_call | solution.py:661
  105.7 1.5 all-to-all-done.4
  107.2 1.3 item_backward.1
  108.5 2.2 %collective-permute-start.1 = (bf16[64,256]{1,0:T(8,128)(2,1)S(1)}, bf16[64,256]{1,0:T(8,128)(2,1)S(1)}, u32[]{:S(2)}, u32[]{:S(2)}) collective-permute-start(bf16[64,256]{1,0:T(8,128)(2,1)S(1)} %get-tuple-element.72), channel_id=1, source_target_pairs={{0,128},{128,0},{1,129},{129,1},{2,130},{130,2},{3,131},{131,3},{4... | collective-permute-start | bytes 98312 | tf_op jit(solution)/shard_map/ppermute | solution.py:685
  112.0 27.1 %all_to_all.80 = bf16[128,8,256]{2,1,0:T(8,128)(2,1)S(1)} all-to-all(bf16[128,8,256]{2,1,0:T(8,128)(2,1)S(1)} %bitcast.31), channel_id=1, replica_groups=mesh['tower'=2,'x'=4,'y'=4,'zh'=4,'zl'=2] {'x','y','zh','zl'}, dimensions={0} | all-to-all | bytes 1048576 | tf_op jit(solution)/shard_map/all_to_all | solution.py:703
  139.1 0.5 scatter.1
  139.6 2.4 %collective-permute-start.3 = (bf16[512,256]{1,0:T(8,128)(2,1)S(1)}, bf16[512,256]{1,0:T(8,128)(2,1)S(1)}, u32[]{:S(2)}, u32[]{:S(2)}) collective-permute-start(bf16[512,256]{1,0:T(8,128)(2,1)S(1)} %get-tuple-element.77), channel_id=1, source_target_pairs={{0,128},{128,0},{1,129},{129,1},{2,130},{130,2},{3,131},{131,3},{4... | collective-permute-start | bytes 786440 | tf_op jit(solution)/shard_map/ppermute | solution.py:712
  141.9 11.0 %all_to_all.81 = f32[32,8,128]{2,1,0:T(8,128)S(1)} all-to-all(f32[32,8,128]{2,1,0:T(8,128)S(1)} %bitcast.38), channel_id=1, replica_groups=mesh['tower'=2,'x'=4,'y'=4,'zh'=4,'zl'=2] {'x','y','zl'}, dimensions={0} | all-to-all | bytes 262144 | tf_op jit(solution)/shard_map/all_to_all | solution.py:713
  153.0 0.9 collective-permute-start.2
  153.9 0.8 convert_add_fusion
  154.9 0.7 finish.1
  (12 shorter events, 2.0 us)
Async XLA Ops:
  0.6 53.1 %copy-start = (bf16[1024,1024]{1,0:T(8,128)(2,1)S(1)}, bf16[1024,1024]{1,0:T(8,128)(2,1)}, u32[]{:S(2)}) copy-start(bf16[1024,1024]{1,0:T(8,128)(2,1)} %refs_15_.1) | copy-start | bytes 6291460
  56.3 11.2 %all-to-all-start.2 = ((bf16[8,8,1024]{2,1,0:T(8,128)(2,1)}), bf16[8,8,1024]{2,1,0:T(8,128)(2,1)S(1)}, u32[]{:S(2)}, u32[]{:S(2)}) async-start(bf16[8,8,1024]{2,1,0:T(8,128)(2,1)} %bitcast.10), calls=%async_computation.2 | async-start | bytes 262144 | tf_op jit(solution)/shard_map/all_to_all | solution.py:606
  83.9 8.2 %collective-permute-start = (bf16[512,1152]{1,0:T(8,128)(2,1)S(1)}, bf16[512,1152]{1,0:T(8,128)(2,1)S(1)}, u32[]{:S(2)}, u32[]{:S(2)}) collective-permute-start(bf16[512,1152]{1,0:T(8,128)(2,1)S(1)} %bitcast.24), channel_id=1, source_target_pairs={{0,128},{128,0},{1,129},{129,1},{2,130},{130,2},{3,131},{131,3},{4... | collective-permute-start | bytes 3538952 | tf_op jit(solution)/shard_map/ppermute | solution.py:637
  94.8 12.4 %all-to-all-start.4 = ((bf16[8,8,1024]{2,1,0:T(8,128)(2,1)}), bf16[8,8,1024]{2,1,0:T(8,128)(2,1)S(1)}, u32[]{:S(2)}, u32[]{:S(2)}) async-start(bf16[8,8,1024]{2,1,0:T(8,128)(2,1)} %bitcast.16), calls=%async_computation.4 | async-start | bytes 262144 | tf_op jit(solution)/shard_map/all_to_all | solution.py:656
  108.4 30.6 %copy-start.1 = (s32[8,1024]{1,0:T(8,128)S(1)}, s32[8,1024]{1,0:T(8,128)}, u32[]{:S(2)}) copy-start(s32[8,1024]{1,0:T(8,128)} %get-tuple-element.73.row_ref) | copy-start | bytes 98308
  108.5 3.1 %collective-permute-start.1 = (bf16[64,256]{1,0:T(8,128)(2,1)S(1)}, bf16[64,256]{1,0:T(8,128)(2,1)S(1)}, u32[]{:S(2)}, u32[]{:S(2)}) collective-permute-start(bf16[64,256]{1,0:T(8,128)(2,1)S(1)} %get-tuple-element.72), channel_id=1, source_target_pairs={{0,128},{128,0},{1,129},{129,1},{2,130},{130,2},{3,131},{131,3},{4... | collective-permute-start | bytes 98312 | tf_op jit(solution)/shard_map/ppermute | solution.py:685
  139.6 14.3 %collective-permute-start.3 = (bf16[512,256]{1,0:T(8,128)(2,1)S(1)}, bf16[512,256]{1,0:T(8,128)(2,1)S(1)}, u32[]{:S(2)}, u32[]{:S(2)}) collective-permute-start(bf16[512,256]{1,0:T(8,128)(2,1)S(1)} %get-tuple-element.77), channel_id=1, source_target_pairs={{0,128},{128,0},{1,129},{129,1},{2,130},{130,2},{3,131},{131,3},{4... | collective-permute-start | bytes 786440 | tf_op jit(solution)/shard_map/ppermute | solution.py:712
  153.0 1.9 %collective-permute-start.2 = (f32[256,128]{1,0:T(8,128)S(1)}, f32[256,128]{1,0:T(8,128)S(1)}, u32[]{:S(2)}, u32[]{:S(2)}) collective-permute-start(f32[256,128]{1,0:T(8,128)S(1)} %bitcast.34), channel_id=1, source_target_pairs={{0,128},{128,0},{1,129},{129,1},{2,130},{130,2},{3,131},{131,3},{4... | collective-permute-start | bytes 393224 | tf_op jit(solution)/shard_map/ppermute | solution.py:714
